TPU v7x, 32 devices: a whole 2x2x4 slice. The times are simulated.
32 devices in a mesh: groups: 2 (over x), tp: 4 (over y, core), rep: 4 (over z).
Axes of the slice: x: 2, y: 2, z: 4, core: 2. Of those that a mesh axis runs over, the one named last changes fastest.
Arguments:
- head_outputs: bfloat16 [8, 768, 8192], P(('groups', 'rep'), None, 'tp'), parts along dimension 0, may hold values from -6 to 6
- residual: bfloat16 [8, 768, 8192], P(('groups', 'rep'), 'tp'), parts along dimension 0, may hold values from -6 to 6
- projection: bfloat16 [8192, 8192], P('tp'), may hold values from -0.0625 to 0.0625
- shrink_pool: bfloat16 [128, 16, 8192], P(('groups', 'rep'), None, 'tp'), parts along dimension 0, may hold values from -0.0625 to 0.0625
- expand_pool: bfloat16 [128, 16, 8192], P(('groups', 'rep'), None, 'tp'), parts along dimension 0, may hold values from -0.75 to 0.75
- pool_slot: int32 [128], P('groups'), parts along dimension 0, may hold values from 0 to 63, as said below
- variant_list: int32 [8, 24], P('groups'), parts along dimension 0, may hold values from 0 to 63, as said below
- request_variant: int32 [8, 768], P(('groups', 'rep')), parts along dimension 0, may hold values from 0 to 63, as said below
Outputs:
- hidden_next: bfloat16 [8, 768, 8192], P(('groups', 'rep'), 'tp'), parts along dimension 0
There are 2 independent parts, one for each index of `groups`. A program takes and returns all parts, laid end to end along the dimension named above; an argument that names none is the same for every part. Nothing has to cross between parts.
Inputs may be any that keep to these rules, and one draw needn't show every extreme that they name: A permutation: the factors of variant v are entry pool_slot[v] of shrink_pool and expand_pool. `variant_list`: row r lists 24 distinct variants for replica r. In one row at most 6 entries have the same pool_slot // 16, and every row has some value of it held by exactly 6 entries. `request_variant`: every request's variant is in its replica's row of variant_list; an entry of a list may be named by no request.
All inputs are finite; a program needn't handle non-finite values.
Results may differ from a plain program's by a relative error of at most 0.009.
Values may be sent and summed in bfloat16 or wider, within the bound.
No kernel may reach another device: no remote copies, remote signals or barrier semaphores. Data moves between devices by JAX's collectives and lax.ppermute only.
A program may use at most 192 MiB of HBM per device.

v0:
```python
import jax
import jax.numpy as jnp
from jax import lax
from jax.sharding import PartitionSpec as P


def local(
    head_outputs,
    residual,
    projection,
    shrink_pool,
    expand_pool,
    pool_slot,
    variant_list,
    request_variant,
):
    split_count = lax.axis_size("tp")
    split_index = lax.axis_index("tp")
    replica_index = lax.axis_index("rep")
    row_count = head_outputs.shape[1]
    local_width = head_outputs.shape[2]
    rank_size = shrink_pool.shape[1]
    listed = variant_list.shape[1]
    own_rows = row_count // split_count
    flat_size = rank_size * local_width
    features = head_outputs[0]
    wanted = request_variant[0]
    all_positions = jnp.take(pool_slot, variant_list, axis=0)
    my_list = lax.dynamic_index_in_dim(variant_list, replica_index, 0, keepdims=False)
    my_positions = lax.dynamic_index_in_dim(all_positions, replica_index, 0, keepdims=False)
    pieces = (
        lax.all_gather(shrink_pool, "rep", axis=0, tiled=True),
        lax.all_gather(expand_pool, "rep", axis=0, tiled=True),
    )
    piece_rows = pieces[0].shape[0]
    matches = my_positions[:, None] == jnp.arange(piece_rows, dtype=jnp.int32)[None, :]
    matches = matches.astype(jnp.bfloat16)
    shrink_part = jnp.dot(
        matches, pieces[0].reshape(piece_rows, flat_size), preferred_element_type=jnp.float32
    )
    expand_part = jnp.dot(
        matches, pieces[1].reshape(piece_rows, flat_size), preferred_element_type=jnp.float32
    )
    shrink_sel = shrink_part
    expand_sel = expand_part
    shrink_sel = shrink_sel.astype(jnp.bfloat16).reshape(listed * rank_size, local_width)
    expand_sel = expand_sel.astype(jnp.bfloat16).reshape(listed, rank_size, local_width)
    member = wanted[:, None] == my_list[None, :]
    scores = lax.dot_general(
        features, shrink_sel, (((1,), (1,)), ((), ())), preferred_element_type=jnp.float32
    )
    shrunk = jnp.sum(scores.reshape(row_count, listed, rank_size) * member[:, :, None], axis=1)
    own_shrunk = lax.psum_scatter(
        shrunk.astype(jnp.bfloat16), "tp", scatter_dimension=0, tiled=True
    )
    own_member = lax.dynamic_slice_in_dim(member, split_index * own_rows, own_rows, 0)
    spread = own_member[:, :, None] * own_shrunk[:, None, :]
    spread = spread.reshape(own_rows, listed * rank_size)
    piece = lax.all_gather(expand_sel, "tp", axis=2, tiled=True)
    delta_rows = jnp.dot(
        spread,
        piece.reshape(listed * rank_size, piece.shape[2]),
        preferred_element_type=jnp.float32,
    )
    base_rows = lax.psum_scatter(
        jnp.dot(features, projection, preferred_element_type=jnp.float32).astype(jnp.bfloat16),
        "tp",
        scatter_dimension=0,
        tiled=True,
    ).astype(jnp.float32)
    mixed_rows = residual[0].astype(jnp.float32) + base_rows + delta_rows
    return mixed_rows.astype(jnp.bfloat16)[None]


def solution(mesh):
    in_specs = (
        P(("groups", "rep"), None, "tp"),
        P(("groups", "rep"), "tp", None),
        P("tp", None),
        P(("groups", "rep"), None, "tp"),
        P(("groups", "rep"), None, "tp"),
        P("groups"),
        P("groups", None),
        P(("groups", "rep"), None),
    )
    out_specs = P(("groups", "rep"), "tp", None)
    return jax.shard_map(local, mesh=mesh, in_specs=in_specs, out_specs=out_specs, check_vma=False)
```

profile of v0, /device:TPU:0, one launch (start us, length us, event | category | flops | bytes accessed | tf_op | source)
XLA Modules:
  0.0 370.5 jit_solution(6679742262601798734)
XLA Ops:
  6.6 0.7 all-gather.6.cloned.1.call-update
  7.3 0.7 all-gather.4.cloned.1.call-update
  8.1 0.7 compare_select_fusion
  8.8 0.1 reshape.71
  8.9 1.2 gather_fusion
  10.2 0.1 broadcast_compare_fusion
  10.3 82.1 %all-gather.6.cloned.1.call-done = bf16[64,16,2048]{2,1,0:T(8,128)(2,1)} async-done(((bf16[16,16,2048]{2,1,0:T(8,128)(2,1)}), bf16[64,16,2048]{2,1,0:T(8,128)(2,1)}) %all-gather.6.cloned.1.call-update) | async-done | bytes 4194320 | tf_op jit(solution)/shard_map/all_gather | solution.py:33
  92.4 6.8 %copy.16 = bf16[8,8,16,2048]{3,1,2,0:T(8,128)(2,1)} copy(bf16[8,8,16,2048]{3,2,1,0:T(8,128)(2,1)} %bitcast.43) | data formatting | bytes 8388608
  99.3 74.1 %all-gather.4.cloned.1.call-done = bf16[64,16,2048]{2,1,0:T(8,128)(2,1)} async-done(((bf16[16,16,2048]{2,1,0:T(8,128)(2,1)}), bf16[64,16,2048]{2,1,0:T(8,128)(2,1)}) %all-gather.4.cloned.1.call-update) | async-done | bytes 4194320 | tf_op jit(solution)/shard_map/all_gather | solution.py:32
  173.3 4.6 %copy.15 = bf16[8,8,16,2048]{3,1,2,0:T(8,128)(2,1)S(1)} copy(bf16[8,8,16,2048]{3,2,1,0:T(8,128)(2,1)} %bitcast.44) | data formatting | bytes 8388608
  177.9 1.9 convolution_convert_fusion.1
  179.8 3.8 %reshape.64 = bf16[384,2048]{1,0:T(8,128)(2,1)} reshape(bf16[24,32768]{1,0:T(8,128)(2,1)} %convolution_convert_fusion.1) | data formatting | bytes 3145728 | tf_op jit(solution)/shard_map/reshape | solution.py:46
  183.6 2.8 fusion.3
  186.4 0.1 multiply_reduce_fusion
  186.6 0.8 copy.12
  187.5 2.9 convolution_convert_fusion
  190.4 1.2 copy.18
  191.7 0.2 reduce-scatter.5.cloned.1.call-start
  191.9 31.8 %convolution_convert_fusion.2 = bf16[768,8192]{1,0:T(8,128)(2,1)} fusion(bf16[2048,8192]{1,0:T(8,128)(2,1)} %param.10, bf16[1,768,2048]{2,1,0:T(8,128)(2,1)S(1)} %copy-done), kind=kOutput, calls=%fused_computation.3 | convolution fusion | flops 25776095232 | bytes 49283072 | tf_op jit(solution)/shard_map/dot_general | solution.py:66
  223.7 0.1 dynamic-slice_convert_fusion
  223.8 0.9 copy.13
  224.7 29.0 %all-gather.8.cloned.1.call-done = bf16[24,16,8192]{2,0,1:T(8,128)(2,1)} async-done(((bf16[24,16,2048]{2,0,1:T(8,128)(2,1)}), bf16[24,16,8192]{2,0,1:T(8,128)(2,1)}) %all-gather.8.cloned.1.call-update) | async-done | bytes 6291472 | tf_op jit(solution)/shard_map/all_gather | solution.py:59
  253.7 101.5 %reduce-scatter.5.cloned.1.call-done = bf16[192,8192]{1,0:T(8,128)(2,1)} async-done(((bf16[768,8192]{1,0:T(8,128)(2,1)}), bf16[192,8192]{1,0:T(8,128)(2,1)}) %reduce-scatter.5.cloned.1.call-update) | async-done | bytes 3145744 | tf_op jit(solution)/shard_map/reduce_scatter | solution.py:65
  355.2 8.7 %fusion.2 = bf16[1,192,8192]{2,1,0:T(8,128)(2,1)} fusion(bf16[24,16,8192]{2,0,1:T(8,128)(2,1)} %all-gather.8.cloned.1.call-done, bf16[192,8192]{1,0:T(8,128)(2,1)} %reduce-scatter.5.cloned.1.call-done, bf16[1,192,8192]{2,1,0:T(8,128)(2,1)} %param.9, bf16[192,16]{0,1:T(8,128)(2,1)S(1)} %copy.13, bf16[192,24]{0,1:T(8,128)(2,1)S(1)} %dynamic-slice_convert_fusion), kind=kOutput, calls=%fused_computation.7 | convolution fusion | flops 1215897600 | bytes 15744000 | tf_op jit(solution)/shard_map/dot_general | solution.py:60
  (23 shorter events, 0.3 us)
Async XLA Ops:
  6.5 177.1 %copy-start = (bf16[1,768,2048]{2,1,0:T(8,128)(2,1)S(1)}, bf16[1,768,2048]{2,1,0:T(8,128)(2,1)}, u32[]{:S(2)}) copy-start(bf16[1,768,2048]{2,1,0:T(8,128)(2,1)} %param.8) | copy-start | bytes 9437188
  6.5 3.7 copy-start.3
  6.5 2.3 copy-start.2
  6.5 3.6 copy-start.4
  6.5 85.9 %all-gather.6.cloned.1.call-start = ((), (), s32[]{:S(2)}) async-start(), calls=%async_computation.4 | async-start | bytes 5242880 | tf_op jit(solution)/shard_map/all_gather | solution.py:33
  7.3 166.1 %all-gather.4.cloned.1.call-start = ((), (), s32[]{:S(2)}) async-start(), calls=%async_computation.3 | async-start | bytes 5242880 | tf_op jit(solution)/shard_map/all_gather | solution.py:32
  8.0 215.8 %reduce-scatter.7.cloned.1.call-start = ((), (), s32[]{:S(2)}) async-start(), calls=%async_computation.6 | async-start | bytes 245760
  187.4 66.3 %all-gather.8.cloned.1.call-start = ((), (), s32[]{:S(2)}) async-start(), calls=%async_computation.5 | async-start | bytes 7864320 | tf_op jit(solution)/shard_map/all_gather | solution.py:59
  191.7 163.6 %reduce-scatter.5.cloned.1.call-start = ((), (), s32[]{:S(2)}) async-start(), calls=%async_computation.2 | async-start | bytes 15728640 | tf_op jit(solution)/shard_map/reduce_scatter | solution.py:65
  355.2 8.7 %copy-start.1 = (bf16[1,768,2048]{2,1,0:T(8,128)(2,1)S(1)}, bf16[1,768,2048]{2,1,0:T(8,128)(2,1)}, u32[]{:S(2)}) copy-start(bf16[1,768,2048]{2,1,0:T(8,128)(2,1)} %param.8) | copy-start | bytes 9437188
Sparse Core Ops, SparseCore 0:
  8.9 83.4 all-gather.5
  94.0 79.2 all-gather.3
  187.5 18.2 reduce-scatter.6
  207.3 46.3 all-gather.7
  256.1 99.0 reduce-scatter.4
where the time goes:
time: 371 us; the launch traced here: 370 us
  waiting for transfers between devices  288 us (78%)
  matrix products  48.2 us (13%)
  local copies, waits for them, and re-layouts  19.6 us (5%)
  between operations  13.2 us (4%)
    reduce_scatter x1, waiting for transfers between devices, local(): lax.psum_scatter(jnp.dot(features, projection, preferred_element_type=jnp...  102 us
    all_gather x1, waiting for transfers between devices, local(): lax.all_gather(expand_pool, 'rep', axis=0, tiled=True)  82.1 us
    all_gather x1, waiting for transfers between devices, local(): lax.all_gather(shrink_pool, 'rep', axis=0, tiled=True)  74.1 us
    dot_general x1, matrix products, local(): jnp.dot(features, projection, preferred_element_type=jnp.float32)  31.8 us
    all_gather x1, waiting for transfers between devices, local(): piece = lax.all_gather(expand_sel, 'tp', axis=2, tiled=True)  29 us
    unnamed x14, local copies, waits for them, and re-layouts  13.1 us
    dot_general x1, matrix products, local(): jnp.dot(spread, piece.reshape(listed * rank_size, piece.shape[2]), prefer...  8.72 us
  transfers between devices with their start and end apart: 5, of which 4 were waited for; matrix products, arithmetic and copies ran while one was open for 12% of the time, Pallas kernels for 0%

commit v1 on v0

v1 whole, which is shorter than its diff:
```python
import functools
import math

import jax
import jax.numpy as jnp
from jax import lax
from jax.experimental import pallas as pl
from jax.experimental.pallas import tpu as pltpu
from jax.sharding import PartitionSpec as P

ANY = pl.BlockSpec(memory_space=pl.ANY)
SMEM = pl.BlockSpec(memory_space=pltpu.SMEM)
VMEM = pl.BlockSpec(memory_space=pltpu.VMEM)
BF16 = jnp.bfloat16
F32 = jnp.float32


def params(mib=48):
    return pltpu.CompilerParams(vmem_limit_bytes=mib * 2**20)


def sds(shape, dtype=BF16):
    return jax.ShapeDtypeStruct(shape, dtype)


def select_kernel(cuts, n_rep, cap, pool_dev, rank, slot, lists, pos, pool, *rest):
    outs, (idx, sems) = rest[:-2], rest[-2:]
    me = pos[2]
    listed = lists.shape[1]
    copies = []
    for shift in [*range(1, n_rep), 0]:
        target = lax.rem(me + shift, n_rep)
        for k in range(cap):
            idx[shift * cap + k] = 0

        def body(l, count):
            place = slot[lists[target, l]]
            mine = (place // pool_dev == me) & (count < cap)

            @pl.when(mine)
            def _():
                idx[shift * cap + count] = place - me * pool_dev

            return count + mine.astype(jnp.int32)

        lax.fori_loop(0, listed, body, jnp.int32(0), unroll=True)
        for k in range(cap):
            entry = pl.multiple_of(idx[shift * cap + k] * rank, rank)
            for c, (start, stop) in enumerate(cuts):
                copy = pltpu.make_async_copy(
                    pool.at[pl.ds(entry, rank), pl.ds(start, stop - start)],
                    outs[shift * len(cuts) + c].at[pl.ds(k * rank, rank), :],
                    sems.at[(shift * cap + k) * len(cuts) + c],
                )
                copy.start()
                copies.append(copy)
    for copy in copies:
        copy.wait()


def select(slot, lists, pos, pool, cuts, n_rep, cap):
    pool_dev, rank, width = pool.shape
    shapes = [sds((cap * rank, stop - start)) for _ in range(n_rep) for start, stop in cuts]
    return pl.pallas_call(
        functools.partial(select_kernel, cuts, n_rep, cap, pool_dev, rank),
        out_shape=shapes,
        in_specs=[SMEM, SMEM, SMEM, ANY],
        out_specs=[ANY] * len(shapes),
        scratch_shapes=[
            pltpu.SMEM((n_rep * cap,), jnp.int32),
            pltpu.SemaphoreType.DMA((n_rep * cap * len(cuts),)),
        ],
        name="select",
    )(slot, lists, pos, pool.reshape(pool_dev * rank, width))


def gate_kernel(n, *refs):
    pass


def gate(arrays, after):
    n = len(arrays)
    return pl.pallas_call(
        functools.partial(gate_kernel, n),
        out_shape=[sds(a.shape, a.dtype) for a in arrays],
        in_specs=[ANY] * (n + len(after)),
        out_specs=[ANY] * n,
        input_output_aliases={i: i for i in range(n)},
        name="gate",
    )(*arrays, *after)


def product_kernel(split, pos, features, weights, keep, send):
    own = features.shape[0] // 2
    result = jnp.dot(features[...], weights[...], preferred_element_type=F32).astype(BF16)
    low, high = result[:own], result[own:]
    if split:
        low, high = low[None], high[None]

    @pl.when(pos[1] == 0)
    def _():
        keep[...] = low
        send[...] = high

    @pl.when(pos[1] == 1)
    def _():
        keep[...] = high
        send[...] = low


def product(pos, features, projection, other_rows, other_cols, first, count, tile, blocks, after=()):
    rows, depth = features.shape
    width = projection.shape[1]
    half = rows // 2
    own = half // 2
    tiles = count // tile

    def row_block(j, pos):
        return ((1 - pos[0]) if other_rows else pos[0], 0)

    def col_block(j, pos):
        if other_cols is None:
            return (0, j + first // tile)
        chip = (1 - pos[0]) if other_cols else pos[0]
        return (0, chip * (width // 2 // tile) + j + first // tile)

    if blocks > 1:
        per = tiles // blocks
        shape = (blocks, own, count // blocks)
        out_spec = pl.BlockSpec((1, own, tile), lambda j, pos: (j // per, 0, j % per))
    else:
        shape = (own, count)
        out_spec = pl.BlockSpec((own, tile), lambda j, pos: (0, j))
    body = functools.partial(product_kernel, blocks > 1)

    def kernel(pos, features, weights, *rest):
        body(pos, features, weights, *rest[-2:])

    return pl.pallas_call(
        kernel,
        out_shape=[sds(shape)] * 2,
        grid_spec=pltpu.PrefetchScalarGridSpec(
            num_scalar_prefetch=1,
            grid=(tiles,),
            in_specs=[pl.BlockSpec((half, depth), row_block), pl.BlockSpec((depth, tile), col_block)]
            + [ANY] * len(after),
            out_specs=[out_spec] * 2,
        ),
        compiler_params=params(),
        cost_estimate=pl.CostEstimate(
            flops=2 * half * depth * count, bytes_accessed=2 * depth * count, transcendentals=0
        ),
        name="product",
    )(pos, features, projection, *after)


def walk_list(slot, lists, me, n_rep, cap, pool_dev, counts, visit):
    for s in range(n_rep):
        counts[s] = 0

    for l in range(lists.shape[1]):
        variant = lists[me, l]
        owner = slot[variant] // pool_dev
        shift = lax.rem(me - owner + n_rep, n_rep)
        k = counts[shift]
        counts[shift] = k + 1
        visit(variant, shift * cap + jnp.minimum(k, cap - 1))


def score_kernel(n_rep, cap, pool_dev, rank, slot, lists, pos, wanted, features, *rest):
    blocks, (out, scores, counts) = rest[:n_rep], rest[n_rep:]
    size = cap * rank
    for s in range(n_rep):
        scores[pl.ds(s * size, size), :] = lax.dot_general(
            blocks[s][...], features[...], (((1,), (1,)), ((), ())), preferred_element_type=F32
        )
    out[...] = jnp.zeros_like(out)

    def visit(variant, place):
        offset = pl.multiple_of(place * rank, rank)
        out[...] += jnp.where(wanted[...] == variant, scores[pl.ds(offset, rank), :], 0.0)

    walk_list(slot, lists, pos[2], n_rep, cap, pool_dev, counts, visit)


def score(slot, lists, pos, wanted, features, blocks, cap, pool_dev, rank):
    n_rep = len(blocks)
    rows = features.shape[0]
    return pl.pallas_call(
        functools.partial(score_kernel, n_rep, cap, pool_dev, rank),
        out_shape=sds((rank, rows), F32),
        in_specs=[SMEM] * 3 + [VMEM] * (2 + n_rep),
        out_specs=VMEM,
        scratch_shapes=[
            pltpu.VMEM((n_rep * cap * rank, rows), F32),
            pltpu.SMEM((n_rep,), jnp.int32),
        ],
        compiler_params=params(),
        name="score",
    )(slot, lists, pos, wanted, features, *blocks)


def delta_kernel(n_rep, cap, pool_dev, rank, slot, lists, pos, wanted, shrunk, *rest):
    blocks, (keep, send, spread, expand, result, variants, counts) = rest[:n_rep], rest[n_rep:]
    size = cap * rank
    own = keep.shape[1]
    for i in range(n_rep * cap):
        variants[i] = -1

    def visit(variant, place):
        variants[place] = variant

    walk_list(slot, lists, pos[2], n_rep, cap, pool_dev, counts, visit)
    total = jnp.sum(shrunk[...], axis=0).astype(BF16).astype(F32)
    for i in range(n_rep * cap):
        spread[pl.ds(i * rank, rank), :] = jnp.where(wanted[...] == variants[i], total, 0.0).astype(BF16)
    for s in range(n_rep):
        expand[pl.ds(s * size, size), :] = blocks[s][...]
    result[...] = lax.dot_general(
        spread[...], expand[...], (((0,), (0,)), ((), ())), preferred_element_type=F32
    )
    chip, core = pos[0], pos[1]
    for i, y in enumerate((1 - chip, chip)):
        keep[i] = result[pl.ds((2 * y + core) * own, own), :].astype(BF16)
        send[i] = result[pl.ds((2 * y + 1 - core) * own, own), :].astype(BF16)


def delta(slot, lists, pos, wanted, shrunk, blocks, cap, pool_dev, rank, own):
    n_rep = len(blocks)
    rows = wanted.shape[1]
    width = blocks[0].shape[1]
    return pl.pallas_call(
        functools.partial(delta_kernel, n_rep, cap, pool_dev, rank),
        out_shape=[sds((2, own, width))] * 2,
        in_specs=[SMEM] * 3 + [VMEM] * (2 + n_rep),
        out_specs=[VMEM] * 2,
        scratch_shapes=[
            pltpu.VMEM((n_rep * cap * rank, rows), BF16),
            pltpu.VMEM((n_rep * cap * rank, width), BF16),
            pltpu.VMEM((rows, width), F32),
            pltpu.SMEM((n_rep * cap,), jnp.int32),
            pltpu.SMEM((n_rep,), jnp.int32),
        ],
        compiler_params=params(),
        name="delta",
    )(slot, lists, pos, wanted, shrunk, *blocks)


def near_kernel(pos, residual, keep, recv, first, second, mine, theirs, *rest):
    out = rest[-1]
    block = pl.program_id(0)
    total = residual[...].astype(F32) + keep[...].astype(F32) + recv[...].astype(F32)
    total += jnp.where(block == 0, first[...], second[...]).astype(F32)
    total += jnp.where(block == pos[1], mine[0], theirs[0]).astype(F32)
    out[...] = total.astype(BF16)


def far_kernel(pos, residual, keep, recv, piece, *rest):
    out = rest[-1]
    total = residual[...].astype(F32) + keep[...].astype(F32) + recv[...].astype(F32)
    out[...] = (total + piece[0].astype(F32)).astype(BF16)


def finish(pos, out, residual, keep, recv, start, stop, near, pieces):
    own, full = residual.shape
    width = full // 4
    size = stop - start
    tile = math.gcd(size, start, width)

    def place(b, j, pos):
        chip = pos[0] if near else 1 - pos[0]
        return (0, (2 * chip + b) * (width // tile) + start // tile + j)

    whole = pl.BlockSpec((own, tile), place)
    if near:
        first = pl.BlockSpec((own, tile), lambda b, j, pos: (0, start // tile + j))
        second = pl.BlockSpec((1, own, tile), lambda b, j, pos: (1, 0, j))
        specs, kernel = [first, first, second, second], near_kernel
    else:
        specs, kernel = [pl.BlockSpec((1, own, tile), lambda b, j, pos: (b, 0, j))], far_kernel
    operands = [pos, residual, keep, recv, *pieces]
    aliases = {}
    if out is not None:
        specs = specs + [ANY]
        aliases = {len(operands): 0}
        operands.append(out)
    return pl.pallas_call(
        kernel,
        out_shape=sds((own, full)),
        grid_spec=pltpu.PrefetchScalarGridSpec(
            num_scalar_prefetch=1,
            grid=(2, size // tile),
            in_specs=[whole] * 3 + specs,
            out_specs=whole,
        ),
        input_output_aliases=aliases,
        compiler_params=params(),
        cost_estimate=pl.CostEstimate(flops=own * size * 8, bytes_accessed=own * size * 20, transcendentals=0),
        name="near" if near else "far",
    )(*operands)


def paired(
    head_outputs, residual, projection, shrink_pool, expand_pool, pool_slot, variant_list, request_variant
):
    n_rep = lax.axis_size("rep")
    index = lax.axis_index("tp")
    chip, core = index // 2, index % 2
    pos = jnp.stack([chip, core, lax.axis_index("rep")]).astype(jnp.int32)
    features = head_outputs[0]
    rows = features.shape[0]
    own = rows // 4
    pool_dev, rank, width = shrink_pool.shape
    cap = pool_dev // 4 + 2
    stream = residual[0]
    lists = (pool_slot, variant_list, pos)
    sizes = (cap, pool_dev, rank)
    cuts = tuple((width * a // 8, width * b // 8) for a, b in ((0, 3), (3, 6), (6, 8)))
    tile = min(512, width)

    def over_core(x):
        return lax.ppermute(x, "tp", [(0, 1), (1, 0), (2, 3), (3, 2)])

    def over_chip(x):
        return lax.ppermute(x, "tp", [(0, 2), (2, 0), (1, 3), (3, 1)])

    def over_rep(x, shift):
        return lax.ppermute(x, "rep", [(i, (i + shift) % n_rep) for i in range(n_rep)])

    shifts = [s for s in range(1, n_rep) if s != n_rep // 2] + [n_rep // 2]
    chosen = select(*lists, shrink_pool, ((0, width),), n_rep, cap)
    shrink = [chosen[0]] + [None] * (n_rep - 1)
    for s in shifts:
        shrink[s] = over_rep(chosen[s], s)
    chosen_expand = select(*lists, expand_pool, cuts, n_rep, cap)

    early = []
    for b in range(2):
        keep, send = product(pos, features, projection, True, True, b * width, width, tile, 1)
        early.append(over_chip(keep + over_core(send)))
    keep, send = product(pos, features, projection, True, False, 0, 2 * width, tile, 2)
    late = keep + over_core(send)
    base_keep, base_send = product(pos, features, projection, False, None, 0, 4 * width, tile, 1)
    base_recv = over_core(base_send)

    part = score(*lists, request_variant, features, shrink, *sizes)
    shrunk = lax.all_gather(part, "tp")

    done = shrink[1:]
    expands = []
    for c in range(len(cuts)):
        sends = gate([chosen_expand[s * len(cuts) + c] for s in shifts], done)
        block = [chosen_expand[c]] + [None] * (n_rep - 1)
        for s, x in zip(shifts, sends):
            block[s] = over_rep(x, s)
        done = block[1:]
        expands.append(block)

    out = None
    far = []
    for c, (start, stop) in enumerate(cuts):
        mine, send = delta(*lists, request_variant, shrunk, expands[c], *sizes, own)
        theirs = over_core(send)
        first = jnp.where(core == 0, mine[0], theirs[0])
        second = jnp.where(core == 0, theirs[0], mine[0])
        far.append(over_chip(late[:, :, start:stop] + jnp.stack([first, second])))
        out = finish(pos, out, stream, base_keep, base_recv, start, stop, True, [*early, mine, theirs])
    for c, (start, stop) in enumerate(cuts):
        out = finish(pos, out, stream, base_keep, base_recv, start, stop, False, [far[c]])
    return out[None]


def general(
    head_outputs, residual, projection, shrink_pool, expand_pool, pool_slot, variant_list, request_variant
):
    split_count = lax.axis_size("tp")
    split_index = lax.axis_index("tp")
    replica_index = lax.axis_index("rep")
    row_count = head_outputs.shape[1]
    local_width = head_outputs.shape[2]
    rank_size = shrink_pool.shape[1]
    listed = variant_list.shape[1]
    own_rows = row_count // split_count
    flat_size = rank_size * local_width
    features = head_outputs[0]
    wanted = request_variant[0]
    my_list = lax.dynamic_index_in_dim(variant_list, replica_index, 0, keepdims=False)
    my_positions = jnp.take(pool_slot, my_list, axis=0)
    pieces = (
        lax.all_gather(shrink_pool, "rep", axis=0, tiled=True),
        lax.all_gather(expand_pool, "rep", axis=0, tiled=True),
    )
    piece_rows = pieces[0].shape[0]
    matches = (my_positions[:, None] == jnp.arange(piece_rows, dtype=jnp.int32)[None, :]).astype(BF16)
    shrink_sel = jnp.dot(matches, pieces[0].reshape(piece_rows, flat_size), preferred_element_type=F32)
    expand_sel = jnp.dot(matches, pieces[1].reshape(piece_rows, flat_size), preferred_element_type=F32)
    shrink_sel = shrink_sel.astype(BF16).reshape(listed * rank_size, local_width)
    expand_sel = expand_sel.astype(BF16).reshape(listed, rank_size, local_width)
    member = wanted[:, None] == my_list[None, :]
    scores = lax.dot_general(
        features, shrink_sel, (((1,), (1,)), ((), ())), preferred_element_type=F32
    )
    shrunk = jnp.sum(scores.reshape(row_count, listed, rank_size) * member[:, :, None], axis=1)
    own_shrunk = lax.psum_scatter(shrunk.astype(BF16), "tp", scatter_dimension=0, tiled=True)
    own_member = lax.dynamic_slice_in_dim(member, split_index * own_rows, own_rows, 0)
    spread = own_member[:, :, None] * own_shrunk[:, None, :]
    spread = spread.reshape(own_rows, listed * rank_size)
    piece = lax.all_gather(expand_sel, "tp", axis=2, tiled=True)
    delta_rows = jnp.dot(
        spread, piece.reshape(listed * rank_size, piece.shape[2]), preferred_element_type=F32
    )
    base_rows = lax.psum_scatter(
        jnp.dot(features, projection, preferred_element_type=F32).astype(BF16),
        "tp",
        scatter_dimension=0,
        tiled=True,
    ).astype(F32)
    return (residual[0].astype(F32) + base_rows + delta_rows).astype(BF16)[None]


def solution(mesh):
    in_specs = (
        P(("groups", "rep"), None, "tp"),
        P(("groups", "rep"), "tp", None),
        P("tp", None),
        P(("groups", "rep"), None, "tp"),
        P(("groups", "rep"), None, "tp"),
        P("groups"),
        P("groups", None),
        P(("groups", "rep"), None),
    )
    out_specs = P(("groups", "rep"), "tp", None)
    local = paired if mesh.shape["tp"] == 4 else general
    return jax.shard_map(local, mesh=mesh, in_specs=in_specs, out_specs=out_specs, check_vma=False)
```

time: 371 us -> 293 us (0.79)
  waiting for transfers between devices: 288 us -> 49.4 us
  Pallas kernels: 0 us -> 195 us
  matrix products: 48.2 us -> 0 us
  starting transfers between devices: 0.37 us -> 27.3 us
  local copies, waits for them, and re-layouts: 19.6 us -> 5.59 us
  between operations: 13.2 us -> 0.35 us
  other arithmetic: 1.03 us -> 8.17 us
  blocking collectives: 0 us -> 5.79 us
    pallas_call x0 -> x19, Pallas kernels: none -> 195 us  [the longest x2 100 us: select(): pl.pallas_call(functools.partial(select_kernel, cuts, n_rep, cap, pool_de...]
    all_gather x3 -> x0, waiting for transfers between devices: 185 us -> none  [the longest x1 82.1 us: local(): lax.all_gather(expand_pool, 'rep', axis=0, tiled=True)]
    reduce_scatter x1 -> x0, waiting for transfers between devices: 102 us -> none  [local(): lax.psum_scatter(jnp.dot(features, projection, preferred_element_type=jnp...]
    ppermute x0 -> x24, waiting for transfers between devices: none -> 49.4 us  [the longest x5 37.2 us: over_chip(): return lax.ppermute(x, 'tp', [(0, 2), (2, 0), (1, 3), (3, 1)])]
    dot_general x5 -> x0, matrix products: 48.2 us -> none  [the longest x1 31.8 us: local(): jnp.dot(features, projection, preferred_element_type=jnp.float32)]
    ppermute x0 -> x24, starting transfers between devices: none -> 27.3 us  [the longest x12 20.6 us: over_rep(): lax.ppermute(x, 'rep', [(i, (i + shift) % n_rep) for i in range(n_rep)])]
    unnamed x14 -> x58, local copies, waits for them, and re-layouts: 13.1 us -> 5.59 us
    all_gather x0 -> x1, blocking collectives: none -> 5.79 us  [paired(): shrunk = lax.all_gather(part, 'tp')]
  transfers between devices with their start and end apart: 5 -> 24, of which waited for: 4 -> 7; matrix products, arithmetic and copies ran while one was open for 12% -> 3% of each run, Pallas kernels for 0% -> 49%
where the time goes in v1:
time: 293 us; the launch traced here: 291 us
  Pallas kernels  195 us (67%)
  waiting for transfers between devices  49.4 us (17%)
  starting transfers between devices  27.3 us (9%)
  other arithmetic  8.17 us (3%)
  blocking collectives  5.79 us (2%)
  local copies, waits for them, and re-layouts  5.59 us (2%)
    pallas_call x2, Pallas kernels, select(): pl.pallas_call(functools.partial(select_kernel, cuts, n_rep, cap, pool_de...  100 us
    pallas_call x4, Pallas kernels, product(): pl.pallas_call(kernel, out_shape=[sds(shape)] * 2, grid_spec=pltpu.Prefet...  55.4 us
    ppermute x5, waiting for transfers between devices, over_chip(): return lax.ppermute(x, 'tp', [(0, 2), (2, 0), (1, 3), (3, 1)])  37.2 us
    pallas_call x6, Pallas kernels, finish(): pl.pallas_call(kernel, out_shape=sds((own, full)), grid_spec=pltpu.Prefet...  25.6 us
    ppermute x12, starting transfers between devices, over_rep(): lax.ppermute(x, 'rep', [(i, (i + shift) % n_rep) for i in range(n_rep)])  20.6 us
    ppermute x12, waiting for transfers between devices, over_rep(): lax.ppermute(x, 'rep', [(i, (i + shift) % n_rep) for i in range(n_rep)])  12.2 us
    pallas_call x3, Pallas kernels, delta(): pl.pallas_call(functools.partial(delta_kernel, n_rep, cap, pool_dev, rank...  8.14 us
  transfers between devices with their start and end apart: 24, of which 7 were waited for; matrix products, arithmetic and copies ran while one was open for 3% of the time, Pallas kernels for 49%

profile of v1, /device:TPU:0, one launch (start us, length us, event | category | flops | bytes accessed | tf_op | source)
XLA Modules:
  0.0 291.2 jit_solution(9129459237433695107)
XLA Ops:
  0.6 49.9 %select.8 = (bf16[96,2048]{1,0:T(8,128)(2,1)}, bf16[96,2048]{1,0:T(8,128)(2,1)}, bf16[96,2048]{1,0:T(8,128)(2,1)}, bf16[96,2048]{1,0:T(8,128)(2,1)}) custom-call(s32[64]{0:T(128)} %slot.11, s32[4,24]{1,0:T(4,128)} %lists.11, s32[3]{0:T(128)} %pad_add_fusion.pos, bf16[256,2048]{1,0:T(8,128)(2,1)} %bitcast.23), custom_call_target="tpu_custom_call" | custom-call | tf_op jit(solution)/shard_map/select/pallas_call | solution.py:64
  50.5 3.1 %collective-permute-start.2 = (bf16[96,2048]{1,0:T(8,128)(2,1)}, bf16[96,2048]{1,0:T(8,128)(2,1)S(1)}, u32[]{:S(2)}, u32[]{:S(2)}) collective-permute-start(bf16[96,2048]{1,0:T(8,128)(2,1)} %get-tuple-element.49), channel_id=1, source_target_pairs={{0,1},{1,2},{2,3},{3,0},{4,5},{5,6},{6,7},{7,4},{8,9},{9,10},{10,1... | collective-permute-start | bytes 1179656 | tf_op jit(solution)/shard_map/ppermute | solution.py:328
  58.2 25.4 %product.4 = (bf16[192,8192]{1,0:T(8,128)(2,1)S(1)}, bf16[192,8192]{1,0:T(8,128)(2,1)}) custom-call(s32[3]{0:T(128)S(1)} %copy-done.21, bf16[768,2048]{1,0:T(8,128)(2,1)} %bitcast.15, bf16[2048,8192]{1,0:T(8,128)(2,1)} %weights.7), custom_call_target="tpu_custom_call" | custom-call | flops 12884901888 | bytes 33554432 | tf_op jit(solution)/shard_map/product/pallas_call | solution.py:139
  85.2 50.3 %select.9 = (bf16[96,768]{1,0:T(8,128)(2,1)}, bf16[96,768]{1,0:T(8,128)(2,1)}, bf16[96,512]{1,0:T(8,128)(2,1)}, bf16[96,768]{1,0:T(8,128)(2,1)}, bf16[96,768]{1,...) custom-call(s32[64]{0:T(128)} %slot.11, ...), custom_call_target="tpu_custom_call" | custom-call | tf_op jit(solution)/shard_map/select/pallas_call | solution.py:64
  137.3 2.8 collective-permute-start.7
  140.1 7.9 %product.6 = (bf16[192,2048]{1,0:T(8,128)(2,1)S(1)}, bf16[192,2048]{1,0:T(8,128)(2,1)}) custom-call(s32[3]{0:T(128)S(1)} %copy-done.22, bf16[768,2048]{1,0:T(8,128)(2,1)S(1)} %bitcast.17, bf16[2048,8192]{1,0:T(8,128)(2,1)} %weights.7), custom_call_target="tpu_custom_call" | custom-call | flops 3221225472 | bytes 8388608 | tf_op jit(solution)/shard_map/product/pallas_call | solution.py:139
  155.7 7.8 %product.7 = (bf16[192,2048]{1,0:T(8,128)(2,1)S(1)}, bf16[192,2048]{1,0:T(8,128)(2,1)}) custom-call(s32[3]{0:T(128)S(1)} %copy-done.22, bf16[768,2048]{1,0:T(8,128)(2,1)S(1)} %bitcast.18, bf16[2048,8192]{1,0:T(8,128)(2,1)} %weights.7), custom_call_target="tpu_custom_call" | custom-call | flops 3221225472 | bytes 8388608 | tf_op jit(solution)/shard_map/product/pallas_call | solution.py:139
  164.5 4.3 %collective-permute-done.9.refs_4_.rest_2_ = bf16[96,768]{1,0:T(8,128)(2,1)} collective-permute-done((bf16[96,768]{1,0:T(8,128)(2,1)}, bf16[96,768]{1,0:T(8,128)(2,1)}, u32[]{:S(2)}, u32[]{:S(2)}) %collective-permute-start.9) | collective-permute-done | bytes 147488 | tf_op jit(solution)/shard_map/ppermute | solution.py:328
  168.9 14.4 %product.5 = (bf16[2,192,2048]{2,1,0:T(8,128)(2,1)S(1)}, bf16[2,192,2048]{2,1,0:T(8,128)(2,1)}) custom-call(s32[3]{0:T(128)S(1)} %copy-done.22, bf16[768,2048]{1,0:T(8,128)(2,1)} %bitcast.16, bf16[2048,8192]{1,0:T(8,128)(2,1)} %weights.7), custom_call_target="tpu_custom_call" | custom-call | flops 6442450944 | bytes 16777216 | tf_op jit(solution)/shard_map/product/pallas_call | solution.py:139
  185.8 5.8 %collective-permute-done.12.rest_2_ = bf16[96,512]{1,0:T(8,128)(2,1)S(1)} collective-permute-done((bf16[96,512]{1,0:T(8,128)(2,1)S(1)}, bf16[96,512]{1,0:T(8,128)(2,1)S(1)}, u32[]{:S(2)}, u32[]{:S(2)}) %collective-permute-start.12) | collective-permute-done | bytes 98336 | tf_op jit(solution)/shard_map/ppermute | solution.py:328
  191.6 3.2 %collective-permute-start.13 = (bf16[96,512]{1,0:T(8,128)(2,1)S(1)}, bf16[96,512]{1,0:T(8,128)(2,1)S(1)}, u32[]{:S(2)}, u32[]{:S(2)}) collective-permute-start(bf16[96,512]{1,0:T(8,128)(2,1)S(1)} %copy-done.28), channel_id=1, source_target_pairs={{0,3},{1,0},{2,1},{3,2},{4,7},{5,4},{6,5},{7,6},{8,11},{9,8},{10,9... | collective-permute-start | bytes 294920 | tf_op jit(solution)/shard_map/ppermute | solution.py:328
  194.9 5.3 %score.1 = f32[16,768]{1,0:T(8,128)S(1)} custom-call(s32[64]{0:T(128)S(1)} %copy-done.26, s32[4,24]{1,0:T(4,128)S(1)} %copy-done.24, s32[3]{0:T(128)S(1)} %copy-done.22, s32[1,768]{1,0:T(1,128)S(1)} %copy-done.25, bf16[768,2048]{1,0:T(8,128)(2,1)S(1)} %bitcast.19, bf16[96,2048]{1,0:T(8,128)(2,1)S(1)} %copy-done.18, bf16[96,2048]{1,0:T(8,128)(2,1)S(1)} %copy-done.5, ...), custom_call_target="tpu_custom_call" | custom-call | tf_op jit(solution)/shard_map/score/pallas_call | solution.py:189
  200.2 5.8 %all-gather = f32[64,768]{1,0:T(8,128)S(1)} all-gather(f32[16,768]{1,0:T(8,128)S(1)} %score.1), channel_id=2, replica_groups=mesh['groups'=2,'tp'=4,'rep'=4] {'tp'}, dimensions={0}, use_global_device_ids=true | all-gather | bytes 245760 | tf_op jit(solution)/shard_map/all_gather | solution.py:347
  206.0 2.9 %delta.5 = (bf16[2,192,768]{2,1,0:T(8,128)(2,1)S(1)}, bf16[2,192,768]{2,1,0:T(8,128)(2,1)}) custom-call(s32[64]{0:T(128)S(1)} %copy-done.26, s32[4,24]{1,0:T(4,128)S(1)} %copy-done.24, s32[3]{0:T(128)S(1)} %copy-done.22, s32[1,768]{1,0:T(1,128)S(1)} %copy-done.25, f32[4,16,768]{2,1,0:T(8,128)S(1)} %bitcast.20, bf16[96,768]{1,0:T(8,128)(2,1)S(1)} %copy-done.20, ...), custom_call_target="tpu_custom_call" | custom-call | tf_op jit(solution)/shard_map/delta/pallas_call | solution.py:232
  211.7 2.9 %delta.4 = (bf16[2,192,768]{2,1,0:T(8,128)(2,1)S(1)}, bf16[2,192,768]{2,1,0:T(8,128)(2,1)}) custom-call(s32[64]{0:T(128)S(1)} %copy-done.26, s32[4,24]{1,0:T(4,128)S(1)} %copy-done.24, s32[3]{0:T(128)S(1)} %copy-done.22, s32[1,768]{1,0:T(1,128)S(1)} %copy-done.25, f32[4,16,768]{2,1,0:T(8,128)S(1)} %bitcast.22, bf16[96,768]{1,0:T(8,128)(2,1)S(1)} %copy-done.19, ...), custom_call_target="tpu_custom_call" | custom-call | tf_op jit(solution)/shard_map/delta/pallas_call | solution.py:232
  226.9 11.9 %collective-permute-done.21.first = bf16[192,2048]{1,0:T(8,128)(2,1)S(1)} collective-permute-done((bf16[192,2048]{1,0:T(8,128)(2,1)S(1)}, bf16[192,2048]{1,0:T(8,128)(2,1)S(1)}, u32[]{:S(2)}, u32[]{:S(2)}) %collective-permute-start.21) | collective-permute-done | bytes 786464 | tf_op jit(solution)/shard_map/ppermute | solution.py:325
  240.3 15.4 %collective-permute-done.23.second = bf16[192,2048]{1,0:T(8,128)(2,1)S(1)} collective-permute-done((bf16[192,2048]{1,0:T(8,128)(2,1)S(1)}, bf16[192,2048]{1,0:T(8,128)(2,1)S(1)}, u32[]{:S(2)}, u32[]{:S(2)}) %collective-permute-start.23) | collective-permute-done | bytes 786464 | tf_op jit(solution)/shard_map/ppermute | solution.py:325
  255.7 5.0 %near.3.rest_0_ = bf16[192,8192]{1,0:T(8,128)(2,1)} custom-call(s32[3]{0:T(128)S(1)} %copy-done.22, bf16[192,8192]{1,0:T(8,128)(2,1)S(1)} %bitcast.9, bf16[192,8192]{1,0:T(8,128)(2,1)} %copy-done.1, bf16[192,8192]{1,0:T(8,128)(2,1)} %collective-permute-done.recv, bf16[192,2048]{1,0:T(8,128)(2,1)S(1)} %collective-permute-done.21.first, ...), custom_call_target="tpu_custom_call" | custom-call | flops 1179648 | bytes 2949120 | tf_op jit(solution)/shard_map/near/pallas_call | solution.py:287
  260.7 5.2 %near.4.rest_0_ = bf16[192,8192]{1,0:T(8,128)(2,1)} custom-call(s32[3]{0:T(128)S(1)} %copy-done.22, bf16[192,8192]{1,0:T(8,128)(2,1)S(1)} %bitcast.10, bf16[192,8192]{1,0:T(8,128)(2,1)} %copy-done.1, bf16[192,8192]{1,0:T(8,128)(2,1)} %collective-permute-done.recv, ...), custom_call_target="tpu_custom_call", output_to_operand_aliasing={{}: (8, {})} | custom-call | flops 1179648 | bytes 2949120 | tf_op jit(solution)/shard_map/near/pallas_call | solution.py:287
  266.0 2.8 near.5.rest_0_
  268.7 5.0 %far.3.rest_0_ = bf16[192,8192]{1,0:T(8,128)(2,1)} custom-call(s32[3]{0:T(128)S(1)} %copy-done.22, bf16[192,8192]{1,0:T(8,128)(2,1)S(1)} %bitcast.12, bf16[192,8192]{1,0:T(8,128)(2,1)} %copy-done.1, bf16[192,8192]{1,0:T(8,128)(2,1)} %collective-permute-done.recv, ...), custom_call_target="tpu_custom_call", output_to_operand_aliasing={{}: (5, {})} | custom-call | flops 1179648 | bytes 2949120 | tf_op jit(solution)/shard_map/far/pallas_call | solution.py:287
  273.7 7.2 %collective-permute-done.17.piece = bf16[2,192,768]{2,1,0:T(8,128)(2,1)S(1)} collective-permute-done((bf16[2,192,768]{2,1,0:T(8,128)(2,1)S(1)}, bf16[2,192,768]{2,1,0:T(8,128)(2,1)S(1)}, u32[]{:S(2)}, u32[]{:S(2)}) %collective-permute-start.17) | collective-permute-done | bytes 589856 | tf_op jit(solution)/shard_map/ppermute | solution.py:325
  281.0 5.0 %far.4.rest_0_ = bf16[192,8192]{1,0:T(8,128)(2,1)} custom-call(s32[3]{0:T(128)S(1)} %copy-done.22, bf16[192,8192]{1,0:T(8,128)(2,1)S(1)} %bitcast.13, bf16[192,8192]{1,0:T(8,128)(2,1)} %copy-done.1, bf16[192,8192]{1,0:T(8,128)(2,1)} %collective-permute-done.recv, ...), custom_call_target="tpu_custom_call", output_to_operand_aliasing={{}: (5, {})} | custom-call | flops 1179648 | bytes 2949120 | tf_op jit(solution)/shard_map/far/pallas_call | solution.py:287
  285.9 2.7 collective-permute-done.15.piece
  (111 shorter events, 38.9 us)
Async XLA Ops:
  50.5 85.0 %collective-permute-start.2 = (bf16[96,2048]{1,0:T(8,128)(2,1)}, bf16[96,2048]{1,0:T(8,128)(2,1)S(1)}, u32[]{:S(2)}, u32[]{:S(2)}) collective-permute-start(bf16[96,2048]{1,0:T(8,128)(2,1)} %get-tuple-element.49), channel_id=1, source_target_pairs={{0,1},{1,2},{2,3},{3,0},{4,5},{5,6},{6,7},{7,4},{8,9},{9,10},{10,1... | collective-permute-start | bytes 1179656 | tf_op jit(solution)/shard_map/ppermute | solution.py:328
  53.6 81.9 %collective-permute-start.3 = (bf16[96,2048]{1,0:T(8,128)(2,1)}, bf16[96,2048]{1,0:T(8,128)(2,1)}, u32[]{:S(2)}, u32[]{:S(2)}) collective-permute-start(bf16[96,2048]{1,0:T(8,128)(2,1)} %get-tuple-element.50), channel_id=1, source_target_pairs={{0,2},{1,3},{2,0},{3,1},{4,6},{5,7},{6,4},{7,5},{8,10},{9,11},{10,... | collective-permute-start | bytes 1179656 | tf_op jit(solution)/shard_map/ppermute | solution.py:328
  56.2 79.4 %collective-permute-start.4 = (bf16[96,2048]{1,0:T(8,128)(2,1)}, bf16[96,2048]{1,0:T(8,128)(2,1)}, u32[]{:S(2)}, u32[]{:S(2)}) collective-permute-start(bf16[96,2048]{1,0:T(8,128)(2,1)} %get-tuple-element.51), channel_id=1, source_target_pairs={{0,3},{1,0},{2,1},{3,2},{4,7},{5,4},{6,5},{7,6},{8,11},{9,8},{10,9... | collective-permute-start | bytes 1179656 | tf_op jit(solution)/shard_map/ppermute | solution.py:328
  85.2 170.5 %collective-permute-start = (bf16[192,8192]{1,0:T(8,128)(2,1)}, bf16[192,8192]{1,0:T(8,128)(2,1)}, u32[]{:S(2)}, u32[]{:S(2)}) collective-permute-start(bf16[192,8192]{1,0:T(8,128)(2,1)} %get-tuple-element.45), channel_id=1, source_target_pairs={{0,4},{4,0},{8,12},{12,8},{1,5},{5,1},{9,13},{13,9},{2,6},{6,2},{1... | collective-permute-start | bytes 9437192 | tf_op jit(solution)/shard_map/ppermute | solution.py:322
  136.3 12.6 %collective-permute-start.5 = (bf16[96,768]{1,0:T(8,128)(2,1)}, bf16[96,768]{1,0:T(8,128)(2,1)S(1)}, u32[]{:S(2)}, u32[]{:S(2)}) collective-permute-start(bf16[96,768]{1,0:T(8,128)(2,1)} %get-tuple-element.62), channel_id=1, source_target_pairs={{0,1},{1,2},{2,3},{3,0},{4,5},{5,6},{6,7},{7,4},{8,9},{9,10},{10,1... | collective-permute-start | bytes 442376 | tf_op jit(solution)/shard_map/ppermute | solution.py:328
  137.0 14.0 %collective-permute-start.6 = (bf16[96,768]{1,0:T(8,128)(2,1)}, bf16[96,768]{1,0:T(8,128)(2,1)S(1)}, u32[]{:S(2)}, u32[]{:S(2)}) collective-permute-start(bf16[96,768]{1,0:T(8,128)(2,1)} %get-tuple-element.63), channel_id=1, source_target_pairs={{0,2},{1,3},{2,0},{3,1},{4,6},{5,7},{6,4},{7,5},{8,10},{9,11},{10,... | collective-permute-start | bytes 442376 | tf_op jit(solution)/shard_map/ppermute | solution.py:328
  137.3 13.7 %collective-permute-start.7 = (bf16[96,768]{1,0:T(8,128)(2,1)}, bf16[96,768]{1,0:T(8,128)(2,1)}, u32[]{:S(2)}, u32[]{:S(2)}) collective-permute-start(bf16[96,768]{1,0:T(8,128)(2,1)} %get-tuple-element.64), channel_id=1, source_target_pairs={{0,3},{1,0},{2,1},{3,2},{4,7},{5,4},{6,5},{7,6},{8,11},{9,8},{10,9... | collective-permute-start | bytes 442376 | tf_op jit(solution)/shard_map/ppermute | solution.py:328
  148.9 62.7 %collective-permute-start.20 = (bf16[192,2048]{1,0:T(8,128)(2,1)}, bf16[192,2048]{1,0:T(8,128)(2,1)}, u32[]{:S(2)}, u32[]{:S(2)}) collective-permute-start(bf16[192,2048]{1,0:T(8,128)(2,1)} %get-tuple-element.80), channel_id=1, source_target_pairs={{0,4},{4,0},{8,12},{12,8},{1,5},{5,1},{9,13},{13,9},{2,6},{6,2},{1... | collective-permute-start | bytes 2359304 | tf_op jit(solution)/shard_map/ppermute | solution.py:322
  151.6 12.9 %collective-permute-start.10 = (bf16[96,768]{1,0:T(8,128)(2,1)}, bf16[96,768]{1,0:T(8,128)(2,1)S(1)}, u32[]{:S(2)}, u32[]{:S(2)}) collective-permute-start(bf16[96,768]{1,0:T(8,128)(2,1)} %get-tuple-element.67), channel_id=1, source_target_pairs={{0,3},{1,0},{2,1},{3,2},{4,7},{5,4},{6,5},{7,6},{8,11},{9,8},{10,9... | collective-permute-start | bytes 442376 | tf_op jit(solution)/shard_map/ppermute | solution.py:328
  154.2 10.3 %collective-permute-start.8 = (bf16[96,768]{1,0:T(8,128)(2,1)}, bf16[96,768]{1,0:T(8,128)(2,1)S(1)}, u32[]{:S(2)}, u32[]{:S(2)}) collective-permute-start(bf16[96,768]{1,0:T(8,128)(2,1)} %get-tuple-element.65), channel_id=1, source_target_pairs={{0,1},{1,2},{2,3},{3,0},{4,5},{5,6},{6,7},{7,4},{8,9},{9,10},{10,1... | collective-permute-start | bytes 442376 | tf_op jit(solution)/shard_map/ppermute | solution.py:328
  154.3 14.5 %collective-permute-start.9 = (bf16[96,768]{1,0:T(8,128)(2,1)}, bf16[96,768]{1,0:T(8,128)(2,1)}, u32[]{:S(2)}, u32[]{:S(2)}) collective-permute-start(bf16[96,768]{1,0:T(8,128)(2,1)} %get-tuple-element.66), channel_id=1, source_target_pairs={{0,2},{1,3},{2,0},{3,1},{4,6},{5,7},{6,4},{7,5},{8,10},{9,11},{10,... | collective-permute-start | bytes 442376 | tf_op jit(solution)/shard_map/ppermute | solution.py:328
  164.5 50.2 %collective-permute-start.22 = (bf16[192,2048]{1,0:T(8,128)(2,1)}, bf16[192,2048]{1,0:T(8,128)(2,1)}, u32[]{:S(2)}, u32[]{:S(2)}) collective-permute-start(bf16[192,2048]{1,0:T(8,128)(2,1)} %get-tuple-element.82), channel_id=1, source_target_pairs={{0,4},{4,0},{8,12},{12,8},{1,5},{5,1},{9,13},{13,9},{2,6},{6,2},{1... | collective-permute-start | bytes 2359304 | tf_op jit(solution)/shard_map/ppermute | solution.py:322
  168.9 14.5 %collective-permute-start.11 = (bf16[96,512]{1,0:T(8,128)(2,1)}, bf16[96,512]{1,0:T(8,128)(2,1)S(1)}, u32[]{:S(2)}, u32[]{:S(2)}) collective-permute-start(bf16[96,512]{1,0:T(8,128)(2,1)} %get-tuple-element.68), channel_id=1, source_target_pairs={{0,1},{1,2},{2,3},{3,0},{4,5},{5,6},{6,7},{7,4},{8,9},{9,10},{10,1... | collective-permute-start | bytes 294920 | tf_op jit(solution)/shard_map/ppermute | solution.py:328
  183.3 39.3 %collective-permute-start.1 = (bf16[2,192,2048]{2,1,0:T(8,128)(2,1)}, bf16[2,192,2048]{2,1,0:T(8,128)(2,1)}, u32[]{:S(2)}, u32[]{:S(2)}) collective-permute-start(bf16[2,192,2048]{2,1,0:T(8,128)(2,1)} %get-tuple-element.47), channel_id=1, source_target_pairs={{0,4},{4,0},{8,12},{12,8},{1,5},{5,1},{9,13},{13,9},{2,6},{6,2},{1... | collective-permute-start | bytes 4718600 | tf_op jit(solution)/shard_map/ppermute | solution.py:322
  183.4 8.2 %collective-permute-start.12 = (bf16[96,512]{1,0:T(8,128)(2,1)S(1)}, bf16[96,512]{1,0:T(8,128)(2,1)S(1)}, u32[]{:S(2)}, u32[]{:S(2)}) collective-permute-start(bf16[96,512]{1,0:T(8,128)(2,1)S(1)} %copy-done.27), channel_id=1, source_target_pairs={{0,2},{1,3},{2,0},{3,1},{4,6},{5,7},{6,4},{7,5},{8,10},{9,11},{10,... | collective-permute-start | bytes 294920 | tf_op jit(solution)/shard_map/ppermute | solution.py:328
  191.6 17.3 %collective-permute-start.13 = (bf16[96,512]{1,0:T(8,128)(2,1)S(1)}, bf16[96,512]{1,0:T(8,128)(2,1)S(1)}, u32[]{:S(2)}, u32[]{:S(2)}) collective-permute-start(bf16[96,512]{1,0:T(8,128)(2,1)S(1)} %copy-done.28), channel_id=1, source_target_pairs={{0,3},{1,0},{2,1},{3,2},{4,7},{5,4},{6,5},{7,6},{8,11},{9,8},{10,9... | collective-permute-start | bytes 294920 | tf_op jit(solution)/shard_map/ppermute | solution.py:328
  209.0 9.4 %collective-permute-start.18 = (bf16[2,192,768]{2,1,0:T(8,128)(2,1)}, bf16[2,192,768]{2,1,0:T(8,128)(2,1)S(1)}, u32[]{:S(2)}, u32[]{:S(2)}) collective-permute-start(bf16[2,192,768]{2,1,0:T(8,128)(2,1)} %get-tuple-element.78), channel_id=1, source_target_pairs={{0,4},{4,0},{8,12},{12,8},{1,5},{5,1},{9,13},{13,9},{2,6},{6,2},{1... | collective-permute-start | bytes 1769480 | tf_op jit(solution)/shard_map/ppermute | solution.py:322
  211.6 8.4 %collective-permute-start.14 = (bf16[2,192,512]{2,1,0:T(8,128)(2,1)}, bf16[2,192,512]{2,1,0:T(8,128)(2,1)}, u32[]{:S(2)}, u32[]{:S(2)}) collective-permute-start(bf16[2,192,512]{2,1,0:T(8,128)(2,1)} %get-tuple-element.72), channel_id=1, source_target_pairs={{0,4},{4,0},{8,12},{12,8},{1,5},{5,1},{9,13},{13,9},{2,6},{6,2},{1... | collective-permute-start | bytes 1179656 | tf_op jit(solution)/shard_map/ppermute | solution.py:322
  214.7 6.9 %collective-permute-start.16 = (bf16[2,192,768]{2,1,0:T(8,128)(2,1)}, bf16[2,192,768]{2,1,0:T(8,128)(2,1)}, u32[]{:S(2)}, u32[]{:S(2)}) collective-permute-start(bf16[2,192,768]{2,1,0:T(8,128)(2,1)} %get-tuple-element.75), channel_id=1, source_target_pairs={{0,4},{4,0},{8,12},{12,8},{1,5},{5,1},{9,13},{13,9},{2,6},{6,2},{1... | collective-permute-start | bytes 1769480 | tf_op jit(solution)/shard_map/ppermute | solution.py:322
  218.4 20.4 %collective-permute-start.21 = (bf16[192,2048]{1,0:T(8,128)(2,1)S(1)}, bf16[192,2048]{1,0:T(8,128)(2,1)S(1)}, u32[]{:S(2)}, u32[]{:S(2)}) collective-permute-start(bf16[192,2048]{1,0:T(8,128)(2,1)S(1)} %add.28), channel_id=1, source_target_pairs={{0,8},{8,0},{4,12},{12,4},{1,9},{9,1},{5,13},{13,5},{2,10},{10,2},... | collective-permute-start | bytes 2359304 | tf_op jit(solution)/shard_map/ppermute | solution.py:325
  220.0 35.7 %collective-permute-start.23 = (bf16[192,2048]{1,0:T(8,128)(2,1)S(1)}, bf16[192,2048]{1,0:T(8,128)(2,1)S(1)}, u32[]{:S(2)}, u32[]{:S(2)}) collective-permute-start(bf16[192,2048]{1,0:T(8,128)(2,1)S(1)} %add.29), channel_id=1, source_target_pairs={{0,8},{8,0},{4,12},{12,4},{1,9},{9,1},{5,13},{13,5},{2,10},{10,2},... | collective-permute-start | bytes 2359304 | tf_op jit(solution)/shard_map/ppermute | solution.py:325
  224.8 44.0 %collective-permute-start.19 = (bf16[2,192,768]{2,1,0:T(8,128)(2,1)S(1)}, bf16[2,192,768]{2,1,0:T(8,128)(2,1)S(1)}, u32[]{:S(2)}, u32[]{:S(2)}) collective-permute-start(bf16[2,192,768]{2,1,0:T(8,128)(2,1)S(1)} %get-tuple-element.83), channel_id=1, source_target_pairs={{0,8},{8,0},{4,12},{12,4},{1,9},{9,1},{5,13},{13,5},{2,10},{10,2},... | collective-permute-start | bytes 1769480 | tf_op jit(solution)/shard_map/ppermute | solution.py:325
  226.3 54.6 %collective-permute-start.17 = (bf16[2,192,768]{2,1,0:T(8,128)(2,1)S(1)}, bf16[2,192,768]{2,1,0:T(8,128)(2,1)S(1)}, u32[]{:S(2)}, u32[]{:S(2)}) collective-permute-start(bf16[2,192,768]{2,1,0:T(8,128)(2,1)S(1)} %get-tuple-element.84), channel_id=1, source_target_pairs={{0,8},{8,0},{4,12},{12,4},{1,9},{9,1},{5,13},{13,5},{2,10},{10,2},... | collective-permute-start | bytes 1769480 | tf_op jit(solution)/shard_map/ppermute | solution.py:325
  238.8 49.8 %collective-permute-start.15 = (bf16[2,192,512]{2,1,0:T(8,128)(2,1)S(1)}, bf16[2,192,512]{2,1,0:T(8,128)(2,1)S(1)}, u32[]{:S(2)}, u32[]{:S(2)}) collective-permute-start(bf16[2,192,512]{2,1,0:T(8,128)(2,1)S(1)} %slice_add_fusion.2), channel_id=1, source_target_pairs={{0,8},{8,0},{4,12},{12,4},{1,9},{9,1},{5,13},{13,5},{2,10},{10,2},... | collective-permute-start | bytes 1179656 | tf_op jit(solution)/shard_map/ppermute | solution.py:325
  (29 other events, 558.1 us)

commit v2 on v1

v2 whole, which is shorter than its diff:
```python
import functools
import math

import jax
import jax.numpy as jnp
from jax import lax
from jax.experimental import pallas as pl
from jax.experimental.pallas import tpu as pltpu
from jax.sharding import PartitionSpec as P

ANY = pl.BlockSpec(memory_space=pl.ANY)
HBM = pl.BlockSpec(memory_space=pltpu.HBM)
SMEM = pl.BlockSpec(memory_space=pltpu.SMEM)
VMEM = pl.BlockSpec(memory_space=pltpu.VMEM)
BF16 = jnp.bfloat16
F32 = jnp.float32


def order(us):
    return pl.CostEstimate(flops=int(us * 1.15e9) + 1, bytes_accessed=1, transcendentals=0)


def params(mib=48):
    return pltpu.CompilerParams(vmem_limit_bytes=mib * 2**20)


def sds(shape, dtype=BF16):
    return jax.ShapeDtypeStruct(shape, dtype)


TOKEN = sds((8, 128), F32)


def select_kernel(cuts, by_target, n_rep, cap, pool_dev, rank, slot, lists, pos, pool, *rest):
    n_outs = len(cuts) if by_target else n_rep * len(cuts)
    outs, (token, idx, sems) = rest[-3 - n_outs : -3], rest[-3:]
    token[...] = jnp.zeros_like(token)
    me = pos[2]
    listed = lists.shape[1]
    copies = []
    for shift in range(n_rep):
        target = shift if by_target else lax.rem(me + shift, n_rep)
        for k in range(cap):
            idx[shift * cap + k] = 0

        def body(l, count):
            place = slot[lists[target, l]]
            mine = (place // pool_dev == me) & (count < cap)

            @pl.when(mine)
            def _():
                idx[shift * cap + count] = place - me * pool_dev

            return count + mine.astype(jnp.int32)

        lax.fori_loop(0, listed, body, jnp.int32(0), unroll=True)
        for k in range(cap):
            entry = pl.multiple_of(idx[shift * cap + k] * rank, rank)
            for c, (start, stop) in enumerate(cuts):
                if by_target:
                    into = outs[c].at[shift, pl.ds(k * rank, rank), :]
                else:
                    into = outs[shift * len(cuts) + c].at[pl.ds(k * rank, rank), :]
                copy = pltpu.make_async_copy(
                    pool.at[pl.ds(entry, rank), pl.ds(start, stop - start)],
                    into,
                    sems.at[(shift * cap + k) * len(cuts) + c],
                )
                copy.start()
                copies.append(copy)
    for copy in copies:
        copy.wait()


def select(slot, lists, pos, pool, cuts, by_target, n_rep, cap, after=()):
    pool_dev, rank, width = pool.shape
    if by_target:
        shapes = [sds((n_rep, cap * rank, stop - start)) for start, stop in cuts]
    else:
        shapes = [sds((cap * rank, stop - start)) for _ in range(n_rep) for start, stop in cuts]
    return pl.pallas_call(
        functools.partial(select_kernel, cuts, by_target, n_rep, cap, pool_dev, rank),
        out_shape=[*shapes, TOKEN],
        in_specs=[SMEM, SMEM, SMEM, ANY] + [ANY] * len(after),
        out_specs=[HBM] * len(shapes) + [VMEM],
        scratch_shapes=[
            pltpu.SMEM((n_rep * cap,), jnp.int32),
            pltpu.SemaphoreType.DMA((n_rep * cap * len(cuts),)),
        ],
        cost_estimate=order(0),
        name="select",
    )(slot, lists, pos, pool.reshape(pool_dev * rank, width), *after)


def product_columns_kernel(pos, features, weights, out, token):
    token[...] = jnp.zeros_like(token)
    out[...] = jnp.dot(features[...], weights[...], preferred_element_type=F32).astype(BF16)[None]


def product_columns(pos, features, projection, tile, after=()):
    rows, depth = features.shape
    width = projection.shape[1]
    half = rows // 2
    per = width // 4 // tile
    return pl.pallas_call(
        lambda pos, features, weights, *rest: product_columns_kernel(pos, features, weights, *rest[-2:]),
        out_shape=[sds((2, half, width // 4)), TOKEN],
        grid_spec=pltpu.PrefetchScalarGridSpec(
            num_scalar_prefetch=1,
            grid=(2 * per,),
            in_specs=[
                pl.BlockSpec((half, depth), lambda j, pos: (1 - pos[0], 0)),
                pl.BlockSpec(
                    (depth, tile),
                    lambda j, pos: (
                        0,
                        (2 * pos[0] + jnp.where(j < per, pos[1], 1 - pos[1])) * per + lax.rem(j, per),
                    ),
                ),
            ]
            + [ANY] * len(after),
            out_specs=[
                pl.BlockSpec((1, half, tile), lambda j, pos: (j // per, 0, j % per)),
                pl.BlockSpec((8, 128), lambda j, pos: (0, 0)),
            ],
        ),
        compiler_params=params(),
        cost_estimate=order(0),
        name="product",
    )(pos, features, projection, *after)


def product_kernel(split, pos, features, weights, keep, send, token):
    token[...] = jnp.zeros_like(token)
    own = features.shape[0] // 2
    result = jnp.dot(features[...], weights[...], preferred_element_type=F32).astype(BF16)
    low, high = result[:own], result[own:]
    if split:
        low, high = low[None], high[None]

    @pl.when(pos[1] == 0)
    def _():
        keep[...] = low
        send[...] = high

    @pl.when(pos[1] == 1)
    def _():
        keep[...] = high
        send[...] = low


def product(pos, features, projection, other_rows, other_cols, first, count, tile, blocks, after=()):
    rows, depth = features.shape
    width = projection.shape[1]
    half = rows // 2
    own = half // 2
    tiles = count // tile

    def row_block(j, pos):
        return ((1 - pos[0]) if other_rows else pos[0], 0)

    def col_block(j, pos):
        if other_cols is None:
            return (0, j + first // tile)
        chip = (1 - pos[0]) if other_cols else pos[0]
        return (0, chip * (width // 2 // tile) + j + first // tile)

    if blocks > 1:
        per = tiles // blocks
        shape = (blocks, own, count // blocks)
        out_spec = pl.BlockSpec((1, own, tile), lambda j, pos: (j // per, 0, j % per))
    else:
        shape = (own, count)
        out_spec = pl.BlockSpec((own, tile), lambda j, pos: (0, j))
    body = functools.partial(product_kernel, blocks > 1)

    def kernel(pos, features, weights, *rest):
        body(pos, features, weights, *rest[-3:])

    return pl.pallas_call(
        kernel,
        out_shape=[sds(shape), sds(shape), TOKEN],
        grid_spec=pltpu.PrefetchScalarGridSpec(
            num_scalar_prefetch=1,
            grid=(tiles,),
            in_specs=[pl.BlockSpec((half, depth), row_block), pl.BlockSpec((depth, tile), col_block)]
            + [ANY] * len(after),
            out_specs=[out_spec] * 2 + [pl.BlockSpec((8, 128), lambda j, pos: (0, 0))],
        ),
        compiler_params=params(),
        cost_estimate=order(0),
        name="product",
    )(pos, features, projection, *after)


def walk_list(slot, lists, me, n_rep, cap, pool_dev, counts, by_owner, visit):
    for s in range(n_rep):
        counts[s] = 0

    for l in range(lists.shape[1]):
        variant = lists[me, l]
        owner = slot[variant] // pool_dev
        group = owner if by_owner else lax.rem(me - owner + n_rep, n_rep)
        k = counts[group]
        counts[group] = k + 1
        visit(variant, group * cap + jnp.minimum(k, cap - 1))


def score_kernel(n_rep, cap, pool_dev, rank, slot, lists, pos, wanted, features, factors, *rest):
    out, scores, counts = rest[-3:]
    scores[...] = lax.dot_general(
        factors[...], features[...], (((1,), (1,)), ((), ())), preferred_element_type=F32
    )
    out[...] = jnp.zeros_like(out)

    def visit(variant, place):
        offset = pl.multiple_of(place * rank, rank)
        out[...] += jnp.where(wanted[...] == variant, scores[pl.ds(offset, rank), :], 0.0)

    walk_list(slot, lists, pos[2], n_rep, cap, pool_dev, counts, True, visit)


def score(slot, lists, pos, wanted, features, factors, n_rep, cap, pool_dev, rank, after=()):
    rows = features.shape[0]
    return pl.pallas_call(
        functools.partial(score_kernel, n_rep, cap, pool_dev, rank),
        out_shape=sds((rank, rows), F32),
        in_specs=[SMEM] * 3 + [VMEM] * 3 + [ANY] * len(after),
        out_specs=VMEM,
        scratch_shapes=[
            pltpu.VMEM((n_rep * cap * rank, rows), F32),
            pltpu.SMEM((n_rep,), jnp.int32),
        ],
        compiler_params=params(),
        cost_estimate=order(15),
        name="score",
    )(slot, lists, pos, wanted, features, factors, *after)


def delta_kernel(
    n_blocks, n_rep, cap, pool_dev, rank, n_before, slot, lists, pos, wanted, shrunk, late_own, late_recv, *rest
):
    blocks, before = rest[:n_blocks], rest[n_blocks : n_blocks + n_before]
    straight, cross, mine, send, spread, expand, result, variants, counts = rest[-9:]
    size = n_rep * cap * rank // n_blocks
    own, width = straight.shape
    for i in range(n_rep * cap):
        variants[i] = -1

    def visit(variant, place):
        variants[place] = variant

    walk_list(slot, lists, pos[2], n_rep, cap, pool_dev, counts, n_blocks == 1, visit)
    total = jnp.sum(shrunk[...], axis=0).astype(BF16).astype(F32)
    for i in range(n_rep * cap):
        spread[pl.ds(i * rank, rank), :] = jnp.where(wanted[...] == variants[i], total, 0.0).astype(BF16)
    for s in range(n_blocks):
        expand[pl.ds(s * size, size), :] = blocks[s][...]
    result[...] = lax.dot_general(
        spread[...], expand[...], (((0,), (0,)), ((), ())), preferred_element_type=F32
    )
    chip, core = pos[0], pos[1]
    for out, c in ((straight, core), (cross, 1 - core)):
        rows = pl.ds(pl.multiple_of(c * own, own), own)
        base = late_own[rows, :].astype(F32) + late_recv[rows, :].astype(F32)
        out[...] = (base + result[pl.ds((2 - 2 * chip + c) * own, own), :]).astype(BF16)
    start = mine.shape[1] - width
    if before:
        mine[:, :start] = before[0][...]
        send[:, :start] = before[1][...]
    mine[:, start:] = result[pl.ds((2 * chip + core) * own, own), :].astype(BF16)
    send[:, start:] = result[pl.ds((2 * chip + 1 - core) * own, own), :].astype(BF16)


def delta(slot, lists, pos, wanted, shrunk, late, blocks, cut, n_rep, cap, pool_dev, rank, own, before=(), after=()):
    rows = wanted.shape[1]
    start, stop = cut
    width = stop - start
    late_own, late_recv = late
    return pl.pallas_call(
        functools.partial(delta_kernel, len(blocks), n_rep, cap, pool_dev, rank, len(before)),
        out_shape=[sds((own, width))] * 2 + [sds((own, stop))] * 2,
        in_specs=[SMEM] * 3 + [VMEM] * (4 + len(blocks) + len(before)) + [ANY] * len(after),
        out_specs=[VMEM] * 4,
        scratch_shapes=[
            pltpu.VMEM((n_rep * cap * rank, rows), BF16),
            pltpu.VMEM((n_rep * cap * rank, width), BF16),
            pltpu.VMEM((rows, width), F32),
            pltpu.SMEM((n_rep * cap,), jnp.int32),
            pltpu.SMEM((n_rep,), jnp.int32),
        ],
        compiler_params=params(),
        cost_estimate=order(0),
        name="delta",
    )(
        slot, lists, pos, wanted, shrunk, late_own[:, start:stop], late_recv[:, start:stop], *blocks, *before, *after
    )


def gate_kernel(*refs):
    pass


def gate(arrays, after):
    n = len(arrays)
    return pl.pallas_call(
        gate_kernel,
        out_shape=[sds(x.shape, x.dtype) for x in arrays],
        in_specs=[ANY] * (n + len(after)),
        out_specs=[ANY] * n,
        input_output_aliases={i: i for i in range(n)},
        cost_estimate=order(100),
        name="gate",
    )(*arrays, *after)


def near_kernel(pos, residual, keep, recv, first, mine, theirs, *rest):
    out = rest[-1]
    total = residual[...].astype(F32) + keep[...].astype(F32) + recv[...].astype(F32)
    total += first[0].astype(F32)
    total += jnp.where(pl.program_id(0) == pos[1], mine[...], theirs[...]).astype(F32)
    out[...] = total.astype(BF16)


def far_kernel(pos, residual, keep, recv, straight, cross, *rest):
    out = rest[-1]
    total = residual[...].astype(F32) + keep[...].astype(F32) + recv[...].astype(F32)
    total += jnp.where(pl.program_id(0) == pos[1], straight[...], cross[...]).astype(F32)
    out[...] = total.astype(BF16)


def finish(pos, out, residual, base, start, stop, near, pieces, after=()):
    own, full = residual.shape
    width = full // 4
    size = stop - start
    tile = min(1024, math.gcd(size, start, width))

    def place(b, j, pos):
        chip = pos[0] if near else 1 - pos[0]
        return (0, (2 * chip + b) * (width // tile) + start // tile + j)

    whole = pl.BlockSpec((own, tile), place)
    piece = pl.BlockSpec((own, tile), lambda b, j, pos: (0, j))
    if near:
        first = pl.BlockSpec((1, own, tile), lambda b, j, pos: (b, 0, start // tile + j))
        specs, kernel = [first, piece, piece], near_kernel
    else:
        specs, kernel = [piece, piece], far_kernel
    specs = specs + [ANY] * len(after)
    operands = [pos, residual, *base, *pieces, *after]
    aliases = {}
    if out is not None:
        specs = specs + [ANY]
        aliases = {len(operands): 0}
        operands.append(out)
    return pl.pallas_call(
        kernel,
        out_shape=sds((own, full)),
        grid_spec=pltpu.PrefetchScalarGridSpec(
            num_scalar_prefetch=1,
            grid=(2, size // tile),
            in_specs=[whole] * 3 + specs,
            out_specs=whole,
        ),
        input_output_aliases=aliases,
        compiler_params=params(),
        cost_estimate=order(60),
        name="near" if near else "far",
    )(*operands)


def paired(
    head_outputs, residual, projection, shrink_pool, expand_pool, pool_slot, variant_list, request_variant
):
    n_rep = lax.axis_size("rep")
    index = lax.axis_index("tp")
    chip, core = index // 2, index % 2
    pos = jnp.stack([chip, core, lax.axis_index("rep")]).astype(jnp.int32)
    features = head_outputs[0]
    rows = features.shape[0]
    own = rows // 4
    pool_dev, rank, width = shrink_pool.shape
    cap = pool_dev // 4 + 2
    stream = residual[0]
    lists = (pool_slot, variant_list, pos)
    sizes = (cap, pool_dev, rank)
    tile = min(512, width)
    cut = width // 2
    cuts = ((0, cut), (cut, width))

    def over_core(x):
        return lax.ppermute(x, "tp", [(0, 1), (1, 0), (2, 3), (3, 2)])

    def over_chip(x):
        return lax.ppermute(x, "tp", [(0, 2), (2, 0), (1, 3), (3, 1)])

    def over_both(x):
        return lax.ppermute(x, "tp", [(0, 3), (3, 0), (1, 2), (2, 1)])

    def over_rep(x, shift):
        return lax.ppermute(x, "rep", [(i, (i + shift) % n_rep) for i in range(n_rep)])

    shifts = [s for s in range(1, n_rep) if s != n_rep // 2] + [n_rep // 2]
    chosen, token = select(*lists, shrink_pool, ((0, width),), True, n_rep, cap)
    shrink = lax.all_to_all(chosen, "rep", 0, 0, tiled=True).reshape(n_rep * cap * rank, width)

    keep, send, token = product(pos, features, projection, True, True, 0, 2 * width, tile, 2, [token])
    early = keep + over_core(send)
    early_recv = over_chip(early)

    *chosen, token = select(*lists, expand_pool, cuts[:1], False, n_rep, cap, [token])
    first = [chosen[0]] + [None] * (n_rep - 1)
    for s in shifts:
        first[s] = over_rep(chosen[s], s)
    chosen, token = select(*lists, expand_pool, cuts[1:], True, n_rep, cap, [token])
    second = lax.all_to_all(chosen, "rep", 0, 0, tiled=True).reshape(n_rep * cap * rank, cut)

    both, token = product_columns(pos, features, projection, tile, [early, token])
    late = (both[0], over_core(both[1]))
    keep, send, token = product(pos, features, projection, False, None, 0, 4 * width, tile, 1, [token])
    base = (keep, over_core(send))

    part = score(*lists, request_variant, features, shrink, n_rep, *sizes, [token])
    shrunk = lax.all_gather(part, "tp")

    common = (*lists, request_variant, shrunk, late)
    straight, cross, *before = delta(*common, first, cuts[0], n_rep, *sizes, own, (), [early_recv])
    far = [over_chip(straight), over_both(cross)]
    straight, cross, mine, send = delta(*common, [second], cuts[1], n_rep, *sizes, own, before)
    last = [over_chip(straight), over_both(cross)]
    theirs = over_core(send)
    far = gate(far, [mine])
    out = finish(pos, None, stream, base, 0, width, True, [early_recv, mine, theirs], far)
    out = finish(pos, out, stream, base, *cuts[0], False, far)
    out = finish(pos, out, stream, base, *cuts[1], False, last)
    return out[None]


def general(
    head_outputs, residual, projection, shrink_pool, expand_pool, pool_slot, variant_list, request_variant
):
    split_count = lax.axis_size("tp")
    split_index = lax.axis_index("tp")
    replica_index = lax.axis_index("rep")
    row_count = head_outputs.shape[1]
    local_width = head_outputs.shape[2]
    rank_size = shrink_pool.shape[1]
    listed = variant_list.shape[1]
    own_rows = row_count // split_count
    flat_size = rank_size * local_width
    features = head_outputs[0]
    wanted = request_variant[0]
    my_list = lax.dynamic_index_in_dim(variant_list, replica_index, 0, keepdims=False)
    my_positions = jnp.take(pool_slot, my_list, axis=0)
    pieces = (
        lax.all_gather(shrink_pool, "rep", axis=0, tiled=True),
        lax.all_gather(expand_pool, "rep", axis=0, tiled=True),
    )
    piece_rows = pieces[0].shape[0]
    matches = (my_positions[:, None] == jnp.arange(piece_rows, dtype=jnp.int32)[None, :]).astype(BF16)
    shrink_sel = jnp.dot(matches, pieces[0].reshape(piece_rows, flat_size), preferred_element_type=F32)
    expand_sel = jnp.dot(matches, pieces[1].reshape(piece_rows, flat_size), preferred_element_type=F32)
    shrink_sel = shrink_sel.astype(BF16).reshape(listed * rank_size, local_width)
    expand_sel = expand_sel.astype(BF16).reshape(listed, rank_size, local_width)
    member = wanted[:, None] == my_list[None, :]
    scores = lax.dot_general(
        features, shrink_sel, (((1,), (1,)), ((), ())), preferred_element_type=F32
    )
    shrunk = jnp.sum(scores.reshape(row_count, listed, rank_size) * member[:, :, None], axis=1)
    own_shrunk = lax.psum_scatter(shrunk.astype(BF16), "tp", scatter_dimension=0, tiled=True)
    own_member = lax.dynamic_slice_in_dim(member, split_index * own_rows, own_rows, 0)
    spread = own_member[:, :, None] * own_shrunk[:, None, :]
    spread = spread.reshape(own_rows, listed * rank_size)
    piece = lax.all_gather(expand_sel, "tp", axis=2, tiled=True)
    delta_rows = jnp.dot(
        spread, piece.reshape(listed * rank_size, piece.shape[2]), preferred_element_type=F32
    )
    base_rows = lax.psum_scatter(
        jnp.dot(features, projection, preferred_element_type=F32).astype(BF16),
        "tp",
        scatter_dimension=0,
        tiled=True,
    ).astype(F32)
    return (residual[0].astype(F32) + base_rows + delta_rows).astype(BF16)[None]


def solution(mesh):
    in_specs = (
        P(("groups", "rep"), None, "tp"),
        P(("groups", "rep"), "tp", None),
        P("tp", None),
        P(("groups", "rep"), None, "tp"),
        P(("groups", "rep"), None, "tp"),
        P("groups"),
        P("groups", None),
        P(("groups", "rep"), None),
    )
    out_specs = P(("groups", "rep"), "tp", None)
    local = paired if mesh.shape["tp"] == 4 else general
    return jax.shard_map(local, mesh=mesh, in_specs=in_specs, out_specs=out_specs, check_vma=False)
```

time: 293 us -> 239 us (0.82)
  waiting for transfers between devices: 49.4 us -> 17.8 us
  Pallas kernels: 195 us -> 177 us
  local copies, waits for them, and re-layouts: 5.59 us -> 11.2 us
  starting transfers between devices: 27.3 us -> 22.1 us
  other arithmetic: 8.17 us -> 3.8 us
    ppermute x5 -> x3, waiting for transfers between devices: 37.2 us -> 0.29 us  [over_chip(): return lax.ppermute(x, 'tp', [(0, 2), (2, 0), (1, 3), (3, 1)])]
    ppermute x12 -> x3, starting transfers between devices: 20.6 us -> 5.9 us  [over_rep(): lax.ppermute(x, 'rep', [(i, (i + shift) % n_rep) for i in range(n_rep)])]
    pallas_call x6 -> x3, Pallas kernels: 25.6 us -> 12.1 us  [finish(): pl.pallas_call(kernel, out_shape=sds((own, full)), grid_spec=pltpu.Prefet...]
    ppermute x0 -> x2, waiting for transfers between devices: none -> 13.3 us  [over_both(): return lax.ppermute(x, 'tp', [(0, 3), (3, 0), (1, 2), (2, 1)])]
    ppermute x12 -> x3, waiting for transfers between devices: 12.2 us -> 0.01 us  [over_rep(): lax.ppermute(x, 'rep', [(i, (i + shift) % n_rep) for i in range(n_rep)])]
    all_to_all x0 -> x2, starting transfers between devices: none -> 10.2 us  [paired(): lax.all_to_all(chosen, 'rep', 0, 0, tiled=True)]
    all_to_all x0 -> x2, waiting for transfers between devices: none -> 4.23 us  [paired(): lax.all_to_all(chosen, 'rep', 0, 0, tiled=True)]
    ppermute x5 -> x3, starting transfers between devices: 5.74 us -> 2.53 us  [over_chip(): return lax.ppermute(x, 'tp', [(0, 2), (2, 0), (1, 3), (3, 1)])]
  transfers between devices with their start and end apart: 24 -> 14, of which waited for: 7 -> 4; matrix products, arithmetic and copies ran while one was open for 3% -> 3% of each run, Pallas kernels for 49% -> 46%
where the time goes in v2:
time: 239 us; the launch traced here: 238 us
  Pallas kernels  177 us (74%)
  starting transfers between devices  22.1 us (9%)
  waiting for transfers between devices  17.8 us (7%)
  local copies, waits for them, and re-layouts  11.2 us (5%)
  blocking collectives  5.8 us (2%)
  other arithmetic  3.8 us (2%)
    pallas_call x3, Pallas kernels, select(): pl.pallas_call(functools.partial(select_kernel, cuts, by_target, n_rep, c...  104 us
    pallas_call x2, Pallas kernels, product(): pl.pallas_call(kernel, out_shape=[sds(shape), sds(shape), TOKEN], grid_sp...  38.2 us
    ppermute x2, waiting for transfers between devices, over_both(): return lax.ppermute(x, 'tp', [(0, 3), (3, 0), (1, 2), (2, 1)])  13.3 us
    pallas_call x1, Pallas kernels, product_columns(): pl.pallas_call(lambda pos, features, weights, *rest: product_columns_kern...  13 us
    pallas_call x3, Pallas kernels, finish(): pl.pallas_call(kernel, out_shape=sds((own, full)), grid_spec=pltpu.Prefet...  12.1 us
    all_to_all x2, starting transfers between devices, paired(): lax.all_to_all(chosen, 'rep', 0, 0, tiled=True)  10.2 us
    pallas_call x2, Pallas kernels, delta(): pl.pallas_call(functools.partial(delta_kernel, len(blocks), n_rep, cap, p...  7.22 us
    unnamed x36, local copies, waits for them, and re-layouts  6.88 us
  transfers between devices with their start and end apart: 14, of which 4 were waited for; matrix products, arithmetic and copies ran while one was open for 3% of the time, Pallas kernels for 46%

profile of v2, /device:TPU:0, one launch (start us, length us, event | category | flops | bytes accessed | tf_op | source)
XLA Modules:
  0.0 238.0 jit_solution(8287449769427735697)
XLA Ops:
  0.6 50.4 %select.9 = (bf16[4,96,2048]{2,1,0:T(8,128)(2,1)}, f32[8,128]{1,0:T(8,128)}) custom-call(s32[64]{0:T(128)} %slot.11, s32[4,24]{1,0:T(4,128)} %lists.11, s32[3]{0:T(128)} %pad_add_fusion.pos, bf16[256,2048]{1,0:T(8,128)(2,1)} %bitcast.26), custom_call_target="tpu_custom_call" | custom-call | flops 1 | bytes 1 | tf_op jit(solution)/shard_map/select/pallas_call | solution.py:81
  52.4 13.2 %product.3 = (bf16[2,192,2048]{2,1,0:T(8,128)(2,1)S(1)}, bf16[2,192,2048]{2,1,0:T(8,128)(2,1)S(1)}, f32[8,128]{1,0:T(8,128)S(1)}) custom-call(s32[3]{0:T(128)S(1)} %copy-done.5, bf16[768,2048]{1,0:T(8,128)(2,1)} %bitcast.15, bf16[2048,8192]{1,0:T(8,128)(2,1)} %weights.5, f32[8,128]{1,0:T(8,128)S(1)} %copy-done.10), custom_call_target="tpu_custom_call" | custom-call | flops 1 | bytes 1 | tf_op jit(solution)/shard_map/product/pallas_call | solution.py:180
  66.6 5.9 %all-to-all-start = ((bf16[4,96,2048]{2,1,0:T(8,128)(2,1)}), bf16[4,96,2048]{2,1,0:T(8,128)(2,1)}, u32[]{:S(2)}, u32[]{:S(2)}) async-start(bf16[4,96,2048]{2,1,0:T(8,128)(2,1)} %get-tuple-element.41), calls=%async_computation | async-start | bytes 3145728 | tf_op jit(solution)/shard_map/all_to_all | solution.py:405
  72.5 26.6 %select.10 = (bf16[96,1024]{1,0:T(8,128)(2,1)}, bf16[96,1024]{1,0:T(8,128)(2,1)}, bf16[96,1024]{1,0:T(8,128)(2,1)}, bf16[96,1024]{1,0:T(8,128)(2,1)}, f32[8,128]{1,0:T(8,128)}) custom-call(s32[64]{0:T(128)} %slot.11, s32[4,24]{1,0:T(4,128)} %lists.11, s32[3]{0:T(128)} %pad_add_fusion.pos, bf16[256,2048]{1,0:T(8,128)(2,1)} %bitcast.24, f32[8,128]{1,0:T(8,128)} %copy-done.9), custom_call_target="tpu_custom_call" | custom-call | flops 1 | bytes 1 | tf_op jit(solution)/shard_map/select/pallas_call | solution.py:81
  99.1 2.1 collective-permute-start.3
  101.2 2.4 collective-permute-start.4
  105.0 26.6 %select.11 = (bf16[4,96,1024]{2,1,0:T(8,128)(2,1)}, f32[8,128]{1,0:T(8,128)}) custom-call(s32[64]{0:T(128)} %slot.11, s32[4,24]{1,0:T(4,128)} %lists.11, s32[3]{0:T(128)} %pad_add_fusion.pos, bf16[256,2048]{1,0:T(8,128)(2,1)} %bitcast.25, f32[8,128]{1,0:T(8,128)} %get-tuple-element.36.rest_0_), custom_call_target="tpu_custom_call" | custom-call | flops 1 | bytes 1 | tf_op jit(solution)/shard_map/select/pallas_call | solution.py:81
  131.6 3.2 %add.9.rest_0_ = bf16[2,192,2048]{2,1,0:T(8,128)(2,1)} add(bf16[2,192,2048]{2,1,0:T(8,128)(2,1)S(1)} %get-tuple-element.33, bf16[2,192,2048]{2,1,0:T(8,128)(2,1)} %collective-permute-done) | non-fusion elementwise | flops 786432 | bytes 4718592 | tf_op jit(solution)/shard_map/add | solution.py:408
  134.8 1.5 collective-permute-start.6
  136.4 13.0 %product.4 = (bf16[2,384,2048]{2,1,0:T(8,128)(2,1)S(1)}, f32[8,128]{1,0:T(8,128)S(1)}) custom-call(s32[3]{0:T(128)S(1)} %copy-done.6, bf16[768,2048]{1,0:T(8,128)(2,1)} %bitcast.16, bf16[2048,8192]{1,0:T(8,128)(2,1)} %weights.5, bf16[2,192,2048]{2,1,0:T(8,128)(2,1)} %add.9.rest_0_, f32[8,128]{1,0:T(8,128)S(1)} %copy-done.11), custom_call_target="tpu_custom_call" | custom-call | flops 1 | bytes 1 | tf_op jit(solution)/shard_map/product/pallas_call | solution.py:105
  150.8 25.1 %product.5 = (bf16[192,8192]{1,0:T(8,128)(2,1)S(1)}, bf16[192,8192]{1,0:T(8,128)(2,1)}, f32[8,128]{1,0:T(8,128)S(1)}) custom-call(s32[3]{0:T(128)S(1)} %copy-done.6, bf16[768,2048]{1,0:T(8,128)(2,1)} %bitcast.17, bf16[2048,8192]{1,0:T(8,128)(2,1)} %weights.5, f32[8,128]{1,0:T(8,128)S(1)} %get-tuple-element.38.rest_0_), custom_call_target="tpu_custom_call" | custom-call | flops 1 | bytes 1 | tf_op jit(solution)/shard_map/product/pallas_call | solution.py:180
  175.8 1.6 copy-done.13
  179.4 4.3 %all-to-all-start.1 = ((bf16[4,96,1024]{2,1,0:T(8,128)(2,1)}), bf16[4,96,1024]{2,1,0:T(8,128)(2,1)}, u32[]{:S(2)}, u32[]{:S(2)}) async-start(bf16[4,96,1024]{2,1,0:T(8,128)(2,1)} %get-tuple-element.44), calls=%async_computation.1 | async-start | bytes 1572864 | tf_op jit(solution)/shard_map/all_to_all | solution.py:416
  184.5 3.0 %score.1 = f32[16,768]{1,0:T(8,128)S(1)} custom-call(s32[64]{0:T(128)S(1)} %copy-done.7, s32[4,24]{1,0:T(4,128)S(1)} %copy-done.4, s32[3]{0:T(128)S(1)} %copy-done.6, s32[1,768]{1,0:T(1,128)S(1)} %copy-done.8, bf16[768,2048]{1,0:T(8,128)(2,1)S(1)} %bitcast.18, bf16[384,2048]{1,0:T(8,128)(2,1)} %bitcast.7.factors, f32[8,128]{1,0:T(8,128)S(1)} %copy-done.17), custom_call_target="tpu_custom_call" | custom-call | flops 17250000896 | bytes 1 | tf_op jit(solution)/shard_map/score/pallas_call | solution.py:225
  187.4 5.8 %all-gather = f32[64,768]{1,0:T(8,128)S(1)} all-gather(f32[16,768]{1,0:T(8,128)S(1)} %score.1), channel_id=2, replica_groups=mesh['groups'=2,'tp'=4,'rep'=4] {'tp'}, dimensions={0}, use_global_device_ids=true | all-gather | bytes 245760 | tf_op jit(solution)/shard_map/all_gather | solution.py:424
  193.2 1.6 fusion
  194.9 3.6 %delta.2 = (bf16[192,1024]{1,0:T(8,128)(2,1)}, bf16[192,1024]{1,0:T(8,128)(2,1)}, bf16[192,1024]{1,0:T(8,128)(2,1)S(1)}, bf16[192,1024]{1,0:T(8,128)(2,1)S(1)}) custom-call(s32[64]{0:T(128)S(1)} %copy-done.7, s32[4,24]{1,0:T(4,128)S(1)} %copy-done.4, s32[3]{0:T(128)S(1)} %copy-done.6, s32[1,768]{1,0:T(1,128)S(1)} %copy-done.8, f32[4,16,768]{2,1,0:T(8,128)S(1)} %bitcast.19, ...), custom_call_target="tpu_custom_call" | custom-call | flops 1 | bytes 1 | tf_op jit(solution)/shard_map/delta/pallas_call | solution.py:280
  200.6 4.2 %all-to-all-done.1 = bf16[4,96,1024]{2,1,0:T(8,128)(2,1)} async-done(((bf16[4,96,1024]{2,1,0:T(8,128)(2,1)}), bf16[4,96,1024]{2,1,0:T(8,128)(2,1)}, u32[]{:S(2)}, u32[]{:S(2)}) %all-to-all-start.1) | async-done | bytes 786464 | tf_op jit(solution)/shard_map/all_to_all | solution.py:416
  204.8 3.7 %delta.3 = (bf16[192,1024]{1,0:T(8,128)(2,1)}, bf16[192,1024]{1,0:T(8,128)(2,1)}, bf16[192,2048]{1,0:T(8,128)(2,1)S(1)}, bf16[192,2048]{1,0:T(8,128)(2,1)S(1)}) custom-call(s32[64]{0:T(128)S(1)} %copy-done.7, s32[4,24]{1,0:T(4,128)S(1)} %copy-done.4, s32[3]{0:T(128)S(1)} %copy-done.6, s32[1,768]{1,0:T(1,128)S(1)} %copy-done.8, f32[4,16,768]{2,1,0:T(8,128)S(1)} %bitcast.20, ...), custom_call_target="tpu_custom_call" | custom-call | flops 1 | bytes 1 | tf_op jit(solution)/shard_map/delta/pallas_call | solution.py:280
  211.5 6.4 %collective-permute-done.10.refs_1_ = bf16[192,1024]{1,0:T(8,128)(2,1)} collective-permute-done((bf16[192,1024]{1,0:T(8,128)(2,1)}, bf16[192,1024]{1,0:T(8,128)(2,1)}, u32[]{:S(2)}, u32[]{:S(2)}) %collective-permute-start.10) | collective-permute-done | bytes 393248 | tf_op jit(solution)/shard_map/ppermute | solution.py:398
  219.1 5.7 %near.1.rest_0_ = bf16[192,8192]{1,0:T(8,128)(2,1)} custom-call(s32[3]{0:T(128)S(1)} %copy-done.6, bf16[192,8192]{1,0:T(8,128)(2,1)} %bitcast.21, bf16[192,8192]{1,0:T(8,128)(2,1)} %copy-done.13, bf16[192,8192]{1,0:T(8,128)(2,1)} %collective-permute-done.1.recv, bf16[2,192,2048]{2,1,0:T(8,128)(2,1)} %collective-permute-done.6.rest_4_.first, ...), custom_call_target="tpu_custom_call" | custom-call | flops 69000003584 | bytes 1 | tf_op jit(solution)/shard_map/near/pallas_call | solution.py:356
  224.8 3.2 %far.2.rest_0_ = bf16[192,8192]{1,0:T(8,128)(2,1)} custom-call(s32[3]{0:T(128)S(1)} %copy-done.6, bf16[192,8192]{1,0:T(8,128)(2,1)S(1)} %bitcast.22, bf16[192,8192]{1,0:T(8,128)(2,1)} %copy-done.13, bf16[192,8192]{1,0:T(8,128)(2,1)} %collective-permute-done.1.recv, ...), custom_call_target="tpu_custom_call", output_to_operand_aliasing={{}: (6, {})} | custom-call | flops 69000003584 | bytes 1 | tf_op jit(solution)/shard_map/far/pallas_call | solution.py:356
  228.0 6.8 %collective-permute-done.8.cross = bf16[192,1024]{1,0:T(8,128)(2,1)} collective-permute-done((bf16[192,1024]{1,0:T(8,128)(2,1)}, bf16[192,1024]{1,0:T(8,128)(2,1)}, u32[]{:S(2)}, u32[]{:S(2)}) %collective-permute-start.8) | collective-permute-done | bytes 393248 | tf_op jit(solution)/shard_map/ppermute | solution.py:398
  234.8 3.2 %far.3 = bf16[192,8192]{1,0:T(8,128)(2,1)} custom-call(s32[3]{0:T(128)S(1)} %copy-done.6, bf16[192,8192]{1,0:T(8,128)(2,1)S(1)} %bitcast.23, bf16[192,8192]{1,0:T(8,128)(2,1)} %copy-done.13, bf16[192,8192]{1,0:T(8,128)(2,1)} %collective-permute-done.1.recv, bf16[192,1024]{1,0:T(8,128)(2,1)} %collective-permute-done.7.straight, ...), custom_call_target="tpu_custom_call", output_to_operand_aliasing={{}: (6, {})} | custom-call | flops 69000003584 | bytes 1 | tf_op jit(solution)/shard_map/far/pallas_call | solution.py:356
  (59 shorter events, 14.8 us)
Async XLA Ops:
  66.1 65.5 %collective-permute-start = (bf16[2,192,2048]{2,1,0:T(8,128)(2,1)S(1)}, bf16[2,192,2048]{2,1,0:T(8,128)(2,1)}, u32[]{:S(2)}, u32[]{:S(2)}) collective-permute-start(bf16[2,192,2048]{2,1,0:T(8,128)(2,1)S(1)} %get-tuple-element.34), channel_id=1, source_target_pairs={{0,4},{4,0},{8,12},{12,8},{1,5},{5,1},{9,13},{13,9},{2,6},{6,2},{1... | collective-permute-start | bytes 4718600 | tf_op jit(solution)/shard_map/ppermute | solution.py:392
  66.6 112.8 %all-to-all-start = ((bf16[4,96,2048]{2,1,0:T(8,128)(2,1)}), bf16[4,96,2048]{2,1,0:T(8,128)(2,1)}, u32[]{:S(2)}, u32[]{:S(2)}) async-start(bf16[4,96,2048]{2,1,0:T(8,128)(2,1)} %get-tuple-element.41), calls=%async_computation | async-start | bytes 3145728 | tf_op jit(solution)/shard_map/all_to_all | solution.py:405
  99.1 95.7 %collective-permute-start.3 = (bf16[96,1024]{1,0:T(8,128)(2,1)}, bf16[96,1024]{1,0:T(8,128)(2,1)S(1)}, u32[]{:S(2)}, u32[]{:S(2)}) collective-permute-start(bf16[96,1024]{1,0:T(8,128)(2,1)} %get-tuple-element.46), channel_id=1, source_target_pairs={{0,1},{1,2},{2,3},{3,0},{4,5},{5,6},{6,7},{7,4},{8,9},{9,10},{10,1... | collective-permute-start | bytes 589832 | tf_op jit(solution)/shard_map/ppermute | solution.py:401
  101.2 93.7 %collective-permute-start.4 = (bf16[96,1024]{1,0:T(8,128)(2,1)}, bf16[96,1024]{1,0:T(8,128)(2,1)S(1)}, u32[]{:S(2)}, u32[]{:S(2)}) collective-permute-start(bf16[96,1024]{1,0:T(8,128)(2,1)} %get-tuple-element.47), channel_id=1, source_target_pairs={{0,2},{1,3},{2,0},{3,1},{4,6},{5,7},{6,4},{7,5},{8,10},{9,11},{10,... | collective-permute-start | bytes 589832 | tf_op jit(solution)/shard_map/ppermute | solution.py:401
  103.5 91.3 %collective-permute-start.5 = (bf16[96,1024]{1,0:T(8,128)(2,1)}, bf16[96,1024]{1,0:T(8,128)(2,1)}, u32[]{:S(2)}, u32[]{:S(2)}) collective-permute-start(bf16[96,1024]{1,0:T(8,128)(2,1)} %get-tuple-element.48), channel_id=1, source_target_pairs={{0,3},{1,0},{2,1},{3,2},{4,7},{5,4},{6,5},{7,6},{8,11},{9,8},{10,9... | collective-permute-start | bytes 589832 | tf_op jit(solution)/shard_map/ppermute | solution.py:401
  131.6 4.7 %copy-start.6 = (s32[3]{0:T(128)S(1)}, s32[3]{0:T(128)}, u32[]{:S(2)}) copy-start(s32[3]{0:T(128)} %pad_add_fusion.pos) | copy-start | bytes 40
  131.6 4.7 %copy-start.11 = (f32[8,128]{1,0:T(8,128)S(1)}, f32[8,128]{1,0:T(8,128)}, u32[]{:S(2)}) copy-start(f32[8,128]{1,0:T(8,128)} %get-tuple-element.37.rest_1_) | copy-start | bytes 12292
  134.8 60.0 %collective-permute-start.6 = (bf16[2,192,2048]{2,1,0:T(8,128)(2,1)}, bf16[2,192,2048]{2,1,0:T(8,128)(2,1)}, u32[]{:S(2)}, u32[]{:S(2)}) collective-permute-start(bf16[2,192,2048]{2,1,0:T(8,128)(2,1)} %add.9.rest_0_), channel_id=1, source_target_pairs={{0,8},{8,0},{4,12},{12,4},{1,9},{9,1},{5,13},{13,5},{2,10},{10,2},... | collective-permute-start | bytes 4718600 | tf_op jit(solution)/shard_map/ppermute | solution.py:395
  150.8 42.5 %collective-permute-start.2 = (bf16[384,2048]{1,0:T(8,128)(2,1)}, bf16[384,2048]{1,0:T(8,128)(2,1)}, u32[]{:S(2)}, u32[]{:S(2)}) collective-permute-start(bf16[384,2048]{1,0:T(8,128)(2,1)} %get-tuple-element.59), channel_id=1, source_target_pairs={{0,4},{4,0},{8,12},{12,8},{1,5},{5,1},{9,13},{13,9},{2,6},{6,2},{1... | collective-permute-start | bytes 4718600 | tf_op jit(solution)/shard_map/ppermute | solution.py:392
  175.8 1.7 copy-start.13
  178.1 5.6 %copy-start = (bf16[1,768,2048]{2,1,0:T(8,128)(2,1)S(1)}, bf16[1,768,2048]{2,1,0:T(8,128)(2,1)}, u32[]{:S(2)}) copy-start(bf16[1,768,2048]{2,1,0:T(8,128)(2,1)} %param.8) | copy-start | bytes 9437188
  179.4 4.4 %copy-start.4 = (s32[4,24]{1,0:T(4,128)S(1)}, s32[4,24]{1,0:T(4,128)}, u32[]{:S(2)}) copy-start(s32[4,24]{1,0:T(4,128)} %lists.11) | copy-start | bytes 1156
  179.4 4.4 %copy-start.7 = (s32[64]{0:T(128)S(1)}, s32[64]{0:T(128)}, u32[]{:S(2)}) copy-start(s32[64]{0:T(128)} %slot.11) | copy-start | bytes 772
  179.4 4.4 %copy-start.8 = (s32[1,768]{1,0:T(1,128)S(1)}, s32[1,768]{1,0:T(1,128)}, u32[]{:S(2)}) copy-start(s32[1,768]{1,0:T(1,128)} %wanted.5) | copy-start | bytes 9220
  179.4 25.4 %all-to-all-start.1 = ((bf16[4,96,1024]{2,1,0:T(8,128)(2,1)}), bf16[4,96,1024]{2,1,0:T(8,128)(2,1)}, u32[]{:S(2)}, u32[]{:S(2)}) async-start(bf16[4,96,1024]{2,1,0:T(8,128)(2,1)} %get-tuple-element.44), calls=%async_computation.1 | async-start | bytes 1572864 | tf_op jit(solution)/shard_map/all_to_all | solution.py:416
  193.2 1.6 copy-start.3
  194.9 9.9 %copy-start.2 = (bf16[384,1024]{1,0:T(8,128)(2,1)S(1)}, bf16[384,1024]{1,0:T(8,128)(2,1)}, u32[]{:S(2)}) copy-start(bf16[384,1024]{1,0:T(8,128)(2,1)} %get-tuple-element.64.late_own) | copy-start | bytes 2359300
  198.4 12.2 %collective-permute-start.9 = (bf16[192,1024]{1,0:T(8,128)(2,1)}, bf16[192,1024]{1,0:T(8,128)(2,1)}, u32[]{:S(2)}, u32[]{:S(2)}) collective-permute-start(bf16[192,1024]{1,0:T(8,128)(2,1)} %get-tuple-element.53), channel_id=1, source_target_pairs={{0,8},{8,0},{4,12},{12,4},{1,9},{9,1},{5,13},{13,5},{2,10},{10,2},... | collective-permute-start | bytes 1179656 | tf_op jit(solution)/shard_map/ppermute | solution.py:395
  198.9 19.0 %collective-permute-start.10 = (bf16[192,1024]{1,0:T(8,128)(2,1)}, bf16[192,1024]{1,0:T(8,128)(2,1)}, u32[]{:S(2)}, u32[]{:S(2)}) collective-permute-start(bf16[192,1024]{1,0:T(8,128)(2,1)} %get-tuple-element.54), channel_id=1, source_target_pairs={{0,12},{12,0},{4,8},{8,4},{1,13},{13,1},{5,9},{9,5},{2,14},{14,2},... | collective-permute-start | bytes 1179656 | tf_op jit(solution)/shard_map/ppermute | solution.py:398
  200.1 17.8 %collective-permute-start.1 = (bf16[192,8192]{1,0:T(8,128)(2,1)}, bf16[192,8192]{1,0:T(8,128)(2,1)}, u32[]{:S(2)}, u32[]{:S(2)}) collective-permute-start(bf16[192,8192]{1,0:T(8,128)(2,1)} %get-tuple-element.40), channel_id=1, source_target_pairs={{0,4},{4,0},{8,12},{12,8},{1,5},{5,1},{9,13},{13,9},{2,6},{6,2},{1... | collective-permute-start | bytes 9437192 | tf_op jit(solution)/shard_map/ppermute | solution.py:392
  209.4 18.6 %collective-permute-start.7 = (bf16[192,1024]{1,0:T(8,128)(2,1)}, bf16[192,1024]{1,0:T(8,128)(2,1)}, u32[]{:S(2)}, u32[]{:S(2)}) collective-permute-start(bf16[192,1024]{1,0:T(8,128)(2,1)} %get-tuple-element.51), channel_id=1, source_target_pairs={{0,8},{8,0},{4,12},{12,4},{1,9},{9,1},{5,13},{13,5},{2,10},{10,2},... | collective-permute-start | bytes 1179656 | tf_op jit(solution)/shard_map/ppermute | solution.py:395
  209.9 24.9 %collective-permute-start.8 = (bf16[192,1024]{1,0:T(8,128)(2,1)}, bf16[192,1024]{1,0:T(8,128)(2,1)}, u32[]{:S(2)}, u32[]{:S(2)}) collective-permute-start(bf16[192,1024]{1,0:T(8,128)(2,1)} %get-tuple-element.52), channel_id=1, source_target_pairs={{0,12},{12,0},{4,8},{8,4},{1,13},{13,1},{5,9},{9,5},{2,14},{14,2},... | collective-permute-start | bytes 1179656 | tf_op jit(solution)/shard_map/ppermute | solution.py:398
  210.7 7.3 %collective-permute-start.11 = (bf16[192,2048]{1,0:T(8,128)(2,1)S(1)}, bf16[192,2048]{1,0:T(8,128)(2,1)S(1)}, u32[]{:S(2)}, u32[]{:S(2)}) collective-permute-start(bf16[192,2048]{1,0:T(8,128)(2,1)S(1)} %get-tuple-element.58), channel_id=1, source_target_pairs={{0,4},{4,0},{8,12},{12,8},{1,5},{5,1},{9,13},{13,9},{2,6},{6,2},{1... | collective-permute-start | bytes 2359304 | tf_op jit(solution)/shard_map/ppermute | solution.py:392
  219.1 5.7 %copy-start.12 = (bf16[1,192,8192]{2,1,0:T(8,128)(2,1)S(1)}, bf16[1,192,8192]{2,1,0:T(8,128)(2,1)}, u32[]{:S(2)}) copy-start(bf16[1,192,8192]{2,1,0:T(8,128)(2,1)} %param.9) | copy-start | bytes 9437188
  (8 other events, 6.9 us)

commit v3 on v2

--- a/solution.py
+++ b/solution.py
@@ -33,15 +33,14 @@
 
 def select_kernel(cuts, by_target, n_rep, cap, pool_dev, rank, slot, lists, pos, pool, *rest):
     n_outs = len(cuts) if by_target else n_rep * len(cuts)
-    outs, (token, idx, sems) = rest[-3 - n_outs : -3], rest[-3:]
+    outs, (token, idx) = rest[-2 - n_outs : -2], rest[-2:]
     token[...] = jnp.zeros_like(token)
     me = pos[2]
     listed = lists.shape[1]
-    copies = []
     for shift in range(n_rep):
         target = shift if by_target else lax.rem(me + shift, n_rep)
         for k in range(cap):
-            idx[shift * cap + k] = 0
+            idx[k] = 0
 
         def body(l, count):
             place = slot[lists[target, l]]
@@ -49,27 +48,18 @@
 
             @pl.when(mine)
             def _():
-                idx[shift * cap + count] = place - me * pool_dev
+                idx[count] = place - me * pool_dev
 
             return count + mine.astype(jnp.int32)
 
         lax.fori_loop(0, listed, body, jnp.int32(0), unroll=True)
         for k in range(cap):
-            entry = pl.multiple_of(idx[shift * cap + k] * rank, rank)
+            entry = idx[k]
             for c, (start, stop) in enumerate(cuts):
                 if by_target:
-                    into = outs[c].at[shift, pl.ds(k * rank, rank), :]
+                    outs[c][shift, pl.ds(k * rank, rank), :] = pool[entry, :, start:stop]
                 else:
-                    into = outs[shift * len(cuts) + c].at[pl.ds(k * rank, rank), :]
-                copy = pltpu.make_async_copy(
-                    pool.at[pl.ds(entry, rank), pl.ds(start, stop - start)],
-                    into,
-                    sems.at[(shift * cap + k) * len(cuts) + c],
-                )
-                copy.start()
-                copies.append(copy)
-    for copy in copies:
-        copy.wait()
+                    outs[shift * len(cuts) + c][pl.ds(k * rank, rank), :] = pool[entry, :, start:stop]
 
 
 def select(slot, lists, pos, pool, cuts, by_target, n_rep, cap, after=()):
@@ -81,46 +71,71 @@
     return pl.pallas_call(
         functools.partial(select_kernel, cuts, by_target, n_rep, cap, pool_dev, rank),
         out_shape=[*shapes, TOKEN],
-        in_specs=[SMEM, SMEM, SMEM, ANY] + [ANY] * len(after),
-        out_specs=[HBM] * len(shapes) + [VMEM],
-        scratch_shapes=[
-            pltpu.SMEM((n_rep * cap,), jnp.int32),
-            pltpu.SemaphoreType.DMA((n_rep * cap * len(cuts),)),
-        ],
+        in_specs=[SMEM, SMEM, SMEM, VMEM] + [ANY] * len(after),
+        out_specs=[VMEM] * len(shapes) + [VMEM],
+        scratch_shapes=[pltpu.SMEM((cap,), jnp.int32)],
+        compiler_params=params(),
         cost_estimate=order(0),
         name="select",
-    )(slot, lists, pos, pool.reshape(pool_dev * rank, width), *after)
-
-
-def product_columns_kernel(pos, features, weights, out, token):
+    )(slot, lists, pos, pool, *after)
+
+
+def product_columns_kernel(per, pos, features, weights, late, late_send, keep, send, token):
     token[...] = jnp.zeros_like(token)
-    out[...] = jnp.dot(features[...], weights[...], preferred_element_type=F32).astype(BF16)[None]
+    j = pl.program_id(0)
+    half = features.shape[0] // 2
+    own = half // 2
+    result = jnp.dot(features[...], weights[...], preferred_element_type=F32).astype(BF16)
+    for chip in range(2):
+        here = pos[0] == chip
+        other = result[(1 - chip) * half : (2 - chip) * half]
+
+        @pl.when(here & (j < per))
+        def _():
+            late[...] = other
+
+        @pl.when(here & (j >= per))
+        def _():
+            late_send[...] = other
+
+        for core in range(2):
+
+            @pl.when(here & (pos[1] == core))
+            def _():
+                keep[...] = result[chip * half + core * own : chip * half + (core + 1) * own][None]
+                send[...] = result[chip * half + (1 - core) * own : chip * half + (2 - core) * own][None]
 
 
 def product_columns(pos, features, projection, tile, after=()):
     rows, depth = features.shape
-    width = projection.shape[1]
+    width = projection.shape[1] // 4
     half = rows // 2
-    per = width // 4 // tile
-    return pl.pallas_call(
-        lambda pos, features, weights, *rest: product_columns_kernel(pos, features, weights, *rest[-2:]),
-        out_shape=[sds((2, half, width // 4)), TOKEN],
+    per = width // tile
+
+    def block(j, pos):
+        return jnp.where(j < per, pos[1], 1 - pos[1])
+
+    rest = pl.BlockSpec((1, half // 2, tile), lambda j, pos: (block(j, pos), 0, lax.rem(j, per)))
+
+    def kernel(pos, features, weights, *rest):
+        product_columns_kernel(per, pos, features, weights, *rest[-5:])
+
+    return pl.pallas_call(
+        kernel,
+        out_shape=[sds((half, width))] * 2 + [sds((2, half // 2, width))] * 2 + [TOKEN],
         grid_spec=pltpu.PrefetchScalarGridSpec(
             num_scalar_prefetch=1,
             grid=(2 * per,),
             in_specs=[
-                pl.BlockSpec((half, depth), lambda j, pos: (1 - pos[0], 0)),
-                pl.BlockSpec(
-                    (depth, tile),
-                    lambda j, pos: (
-                        0,
-                        (2 * pos[0] + jnp.where(j < per, pos[1], 1 - pos[1])) * per + lax.rem(j, per),
-                    ),
-                ),
+                pl.BlockSpec((rows, depth), lambda j, pos: (0, 0)),
+                pl.BlockSpec((depth, tile), lambda j, pos: (0, (2 * pos[0] + block(j, pos)) * per + lax.rem(j, per))),
             ]
             + [ANY] * len(after),
             out_specs=[
-                pl.BlockSpec((1, half, tile), lambda j, pos: (j // per, 0, j % per)),
+                pl.BlockSpec((half, tile), lambda j, pos: (0, jnp.minimum(j, per - 1))),
+                pl.BlockSpec((half, tile), lambda j, pos: (0, jnp.maximum(j - per, 0))),
+                rest,
+                rest,
                 pl.BlockSpec((8, 128), lambda j, pos: (0, 0)),
             ],
         ),
@@ -232,7 +247,7 @@
             pltpu.SMEM((n_rep,), jnp.int32),
         ],
         compiler_params=params(),
-        cost_estimate=order(15),
+        cost_estimate=order(40),
         name="score",
     )(slot, lists, pos, wanted, features, factors, *after)
 
@@ -314,17 +329,18 @@
     )(*arrays, *after)
 
 
-def near_kernel(pos, residual, keep, recv, first, mine, theirs, *rest):
+def near_kernel(pos, residual, keep, recv, first, second, mine, theirs, *rest):
     out = rest[-1]
-    total = residual[...].astype(F32) + keep[...].astype(F32) + recv[...].astype(F32)
-    total += first[0].astype(F32)
-    total += jnp.where(pl.program_id(0) == pos[1], mine[...], theirs[...]).astype(F32)
+    block = pl.program_id(0)
+    total = residual[...].astype(F32) + keep[0].astype(F32) + recv[0].astype(F32)
+    total += jnp.where(block == 0, first[...], second[...]).astype(F32)
+    total += jnp.where(block == pos[1], mine[...], theirs[...]).astype(F32)
     out[...] = total.astype(BF16)
 
 
 def far_kernel(pos, residual, keep, recv, straight, cross, *rest):
     out = rest[-1]
-    total = residual[...].astype(F32) + keep[...].astype(F32) + recv[...].astype(F32)
+    total = residual[...].astype(F32) + keep[0].astype(F32) + recv[0].astype(F32)
     total += jnp.where(pl.program_id(0) == pos[1], straight[...], cross[...]).astype(F32)
     out[...] = total.astype(BF16)
 
@@ -340,26 +356,22 @@
         return (0, (2 * chip + b) * (width // tile) + start // tile + j)
 
     whole = pl.BlockSpec((own, tile), place)
+    part = pl.BlockSpec((1, own, tile), lambda b, j, pos: (b, 0, start // tile + j))
     piece = pl.BlockSpec((own, tile), lambda b, j, pos: (0, j))
-    if near:
-        first = pl.BlockSpec((1, own, tile), lambda b, j, pos: (b, 0, start // tile + j))
-        specs, kernel = [first, piece, piece], near_kernel
-    else:
-        specs, kernel = [piece, piece], far_kernel
-    specs = specs + [ANY] * len(after)
     operands = [pos, residual, *base, *pieces, *after]
+    specs = [piece] * len(pieces) + [ANY] * len(after)
     aliases = {}
     if out is not None:
         specs = specs + [ANY]
         aliases = {len(operands): 0}
         operands.append(out)
     return pl.pallas_call(
-        kernel,
+        near_kernel if near else far_kernel,
         out_shape=sds((own, full)),
         grid_spec=pltpu.PrefetchScalarGridSpec(
             num_scalar_prefetch=1,
             grid=(2, size // tile),
-            in_specs=[whole] * 3 + specs,
+            in_specs=[whole, part, part] + specs,
             out_specs=whole,
         ),
         input_output_aliases=aliases,
@@ -384,7 +396,7 @@
     stream = residual[0]
     lists = (pool_slot, variant_list, pos)
     sizes = (cap, pool_dev, rank)
-    tile = min(512, width)
+    tile = min(1024, width)
     cut = width // 2
     cuts = ((0, cut), (cut, width))
 
@@ -404,9 +416,12 @@
     chosen, token = select(*lists, shrink_pool, ((0, width),), True, n_rep, cap)
     shrink = lax.all_to_all(chosen, "rep", 0, 0, tiled=True).reshape(n_rep * cap * rank, width)
 
-    keep, send, token = product(pos, features, projection, True, True, 0, 2 * width, tile, 2, [token])
-    early = keep + over_core(send)
-    early_recv = over_chip(early)
+    early = []
+    sums = []
+    for b in range(2):
+        keep, send, token = product(pos, features, projection, True, True, b * width, width, tile, 1, [token])
+        sums.append(keep + over_core(send))
+        early.append(over_chip(sums[-1]))
 
     *chosen, token = select(*lists, expand_pool, cuts[:1], False, n_rep, cap, [token])
     first = [chosen[0]] + [None] * (n_rep - 1)
@@ -415,24 +430,25 @@
     chosen, token = select(*lists, expand_pool, cuts[1:], True, n_rep, cap, [token])
     second = lax.all_to_all(chosen, "rep", 0, 0, tiled=True).reshape(n_rep * cap * rank, cut)
 
-    both, token = product_columns(pos, features, projection, tile, [early, token])
-    late = (both[0], over_core(both[1]))
-    keep, send, token = product(pos, features, projection, False, None, 0, 4 * width, tile, 1, [token])
-    base = (keep, over_core(send))
-
-    part = score(*lists, request_variant, features, shrink, n_rep, *sizes, [token])
+    late_keep, late_send, keep, send, token = product_columns(pos, features, projection, tile, [*sums, token])
+    late = (late_keep, over_core(late_send))
+    near_base = (keep, over_core(send))
+
+    part = score(*lists, request_variant, features, shrink, n_rep, *sizes, [token, early[0]])
     shrunk = lax.all_gather(part, "tp")
 
     common = (*lists, request_variant, shrunk, late)
-    straight, cross, *before = delta(*common, first, cuts[0], n_rep, *sizes, own, (), [early_recv])
+    straight, cross, *before = delta(*common, first, cuts[0], n_rep, *sizes, own, (), [early[1]])
     far = [over_chip(straight), over_both(cross)]
-    straight, cross, mine, send = delta(*common, [second], cuts[1], n_rep, *sizes, own, before)
+    keep, send, token = product(pos, features, projection, False, True, 0, 2 * width, tile, 2, [before[0]])
+    far_base = (keep, over_core(send))
+    straight, cross, mine, send = delta(*common, [second], cuts[1], n_rep, *sizes, own, before, [token])
     last = [over_chip(straight), over_both(cross)]
     theirs = over_core(send)
     far = gate(far, [mine])
-    out = finish(pos, None, stream, base, 0, width, True, [early_recv, mine, theirs], far)
-    out = finish(pos, out, stream, base, *cuts[0], False, far)
-    out = finish(pos, out, stream, base, *cuts[1], False, last)
+    out = finish(pos, None, stream, near_base, 0, width, True, [*early, mine, theirs], far)
+    out = finish(pos, out, stream, far_base, *cuts[0], False, far)
+    out = finish(pos, out, stream, far_base, *cuts[1], False, last)
     return out[None]
 
 

time: 239 us -> 124 us (0.52)
  Pallas kernels: 177 us -> 72.1 us
  waiting for transfers between devices: 17.8 us -> 7.07 us
    pallas_call x3, Pallas kernels: 104 us -> 4.76 us  [select(): pl.pallas_call(functools.partial(select_kernel, cuts, by_target, n_rep, c...]
    pallas_call x2 -> x3, Pallas kernels: 38.2 us -> 25.5 us  [product(): pl.pallas_call(kernel, out_shape=[sds(shape), sds(shape), TOKEN], grid_sp...]
    ppermute x2, waiting for transfers between devices: 13.3 us -> 4.73 us  [over_both(): return lax.ppermute(x, 'tp', [(0, 3), (3, 0), (1, 2), (2, 1)])]
    pallas_call x4, Pallas kernels: 25 us -> 31.2 us  [the longest x1 19.5 us: product_columns(): pl.pallas_call(kernel, out_shape=[sds((half, width))] * 2 + [sds((2, half...]
    all_to_all x2, waiting for transfers between devices: 4.23 us -> 0.01 us  [paired(): lax.all_to_all(chosen, 'rep', 0, 0, tiled=True)]
    unnamed x36 -> x46, local copies, waits for them, and re-layouts: 6.88 us -> 10.3 us
    ppermute x3 -> x4, starting transfers between devices: 2.53 us -> 4.99 us  [over_chip(): return lax.ppermute(x, 'tp', [(0, 2), (2, 0), (1, 3), (3, 1)])]
  transfers between devices with their start and end apart: 14 -> 17, of which waited for: 4 -> 2; matrix products, arithmetic and copies ran while one was open for 3% -> 3% of each run, Pallas kernels for 46% -> 55%
where the time goes in v3:
time: 124 us; the launch traced here: 123 us
  Pallas kernels  72.1 us (58%)
  starting transfers between devices  23.8 us (19%)
  local copies, waits for them, and re-layouts  11.7 us (9%)
  waiting for transfers between devices  7.07 us (6%)
  blocking collectives  5.83 us (5%)
  other arithmetic  2.45 us (2%)
    pallas_call x3, Pallas kernels, product(): pl.pallas_call(kernel, out_shape=[sds(shape), sds(shape), TOKEN], grid_sp...  25.5 us
    pallas_call x1, Pallas kernels, product_columns(): pl.pallas_call(kernel, out_shape=[sds((half, width))] * 2 + [sds((2, half...  19.5 us
    pallas_call x3, Pallas kernels, finish(): pl.pallas_call(near_kernel if near else far_kernel, out_shape=sds((own, f...  11.7 us
    all_to_all x2, starting transfers between devices, paired(): lax.all_to_all(chosen, 'rep', 0, 0, tiled=True)  10.9 us
    unnamed x46, local copies, waits for them, and re-layouts  10.3 us
    pallas_call x2, Pallas kernels, delta(): pl.pallas_call(functools.partial(delta_kernel, len(blocks), n_rep, cap, p...  7.6 us
    ppermute x3, starting transfers between devices, over_rep(): lax.ppermute(x, 'rep', [(i, (i + shift) % n_rep) for i in range(n_rep)])  5.84 us
    all_gather x1, blocking collectives, paired(): shrunk = lax.all_gather(part, 'tp')  5.83 us
  transfers between devices with their start and end apart: 17, of which 2 were waited for; matrix products, arithmetic and copies ran while one was open for 3% of the time, Pallas kernels for 55%

profile of v3, /device:TPU:0, one launch (start us, length us, event | category | flops | bytes accessed | tf_op | source)
XLA Modules:
  0.0 123.2 jit_solution(7249516843199772685)
XLA Ops:
  2.6 1.3 %select.9 = (bf16[4,96,2048]{2,1,0:T(8,128)(2,1)S(1)}, f32[8,128]{1,0:T(8,128)S(1)}) custom-call(s32[64]{0:T(128)S(1)} %copy-done.10, s32[4,24]{1,0:T(4,128)S(1)} %copy-done.8, s32[3]{0:T(128)S(1)} %pad_add_fusion.pos, bf16[16,16,2048]{2,1,0:T(8,128)(2,1)S(1)} %copy-done.6), custom_call_target="tpu_custom_call" | custom-call | flops 1 | bytes 1 | tf_op jit(solution)/shard_map/select/pallas_call | solution.py:71
  5.1 6.6 %all-to-all-start = ((bf16[4,96,2048]{2,1,0:T(8,128)(2,1)}), bf16[4,96,2048]{2,1,0:T(8,128)(2,1)}, u32[]{:S(2)}, u32[]{:S(2)}) async-start(bf16[4,96,2048]{2,1,0:T(8,128)(2,1)} %copy-done.5), calls=%async_computation | async-start | bytes 3145728 | tf_op jit(solution)/shard_map/all_to_all | solution.py:417
  11.7 6.6 %product.4 = (bf16[192,2048]{1,0:T(8,128)(2,1)S(1)}, bf16[192,2048]{1,0:T(8,128)(2,1)S(1)}, f32[8,128]{1,0:T(8,128)S(1)}) custom-call(s32[3]{0:T(128)S(1)} %pad_add_fusion.pos, bf16[768,2048]{1,0:T(8,128)(2,1)S(1)} %bitcast.11, bf16[2048,8192]{1,0:T(8,128)(2,1)} %weights.7, f32[8,128]{1,0:T(8,128)S(1)} %get-tuple-element.39.rest_0_), custom_call_target="tpu_custom_call" | custom-call | flops 1 | bytes 1 | tf_op jit(solution)/shard_map/product/pallas_call | solution.py:195
  18.4 6.7 %product.5 = (bf16[192,2048]{1,0:T(8,128)(2,1)S(1)}, bf16[192,2048]{1,0:T(8,128)(2,1)S(1)}, f32[8,128]{1,0:T(8,128)S(1)}) custom-call(s32[3]{0:T(128)S(1)} %pad_add_fusion.pos, bf16[768,2048]{1,0:T(8,128)(2,1)S(1)} %bitcast.12, bf16[2048,8192]{1,0:T(8,128)(2,1)} %weights.7, f32[8,128]{1,0:T(8,128)S(1)} %get-tuple-element.42.rest_0_), custom_call_target="tpu_custom_call" | custom-call | flops 1 | bytes 1 | tf_op jit(solution)/shard_map/product/pallas_call | solution.py:195
  26.9 1.5 %collective-permute-start.2 = (bf16[192,2048]{1,0:T(8,128)(2,1)}, bf16[192,2048]{1,0:T(8,128)(2,1)}, u32[]{:S(2)}, u32[]{:S(2)}) collective-permute-start(bf16[192,2048]{1,0:T(8,128)(2,1)} %add.12.rest_0_), channel_id=1, source_target_pairs={{0,8},{8,0},{4,12},{12,4},{1,9},{9,1},{5,13},{13,5},{2,10},{10,2},... | collective-permute-start | bytes 2359304 | tf_op jit(solution)/shard_map/ppermute | solution.py:407
  28.4 2.2 %select.10 = (bf16[96,1024]{1,0:T(8,128)(2,1)S(1)}, bf16[96,1024]{1,0:T(8,128)(2,1)}, bf16[96,1024]{1,0:T(8,128)(2,1)}, bf16[96,1024]{1,0:T(8,128)(2,1)}, f32[8,128]{1,0:T(8,128)S(1)}) custom-call(s32[64]{0:T(128)S(1)} %copy-done.11, s32[4,24]{1,0:T(4,128)S(1)} %copy-done.9, s32[3]{0:T(128)S(1)} %pad_add_fusion.pos, bf16[16,16,2048]{2,1,0:T(8,128)(2,1)S(1)} %copy-done.2, ...), custom_call_target="tpu_custom_call" | custom-call | flops 1 | bytes 1 | tf_op jit(solution)/shard_map/select/pallas_call | solution.py:71
  30.6 2.0 %collective-permute-start.4 = (bf16[96,1024]{1,0:T(8,128)(2,1)}, bf16[96,1024]{1,0:T(8,128)(2,1)S(1)}, u32[]{:S(2)}, u32[]{:S(2)}) collective-permute-start(bf16[96,1024]{1,0:T(8,128)(2,1)} %get-tuple-element.52), channel_id=1, source_target_pairs={{0,1},{1,2},{2,3},{3,0},{4,5},{5,6},{6,7},{7,4},{8,9},{9,10},{10,1... | collective-permute-start | bytes 589832 | tf_op jit(solution)/shard_map/ppermute | solution.py:413
  32.6 2.4 %collective-permute-start.5 = (bf16[96,1024]{1,0:T(8,128)(2,1)}, bf16[96,1024]{1,0:T(8,128)(2,1)}, u32[]{:S(2)}, u32[]{:S(2)}) collective-permute-start(bf16[96,1024]{1,0:T(8,128)(2,1)} %get-tuple-element.53), channel_id=1, source_target_pairs={{0,2},{1,3},{2,0},{3,1},{4,6},{5,7},{6,4},{7,5},{8,10},{9,11},{10,... | collective-permute-start | bytes 589832 | tf_op jit(solution)/shard_map/ppermute | solution.py:413
  35.0 1.5 %collective-permute-start.6 = (bf16[96,1024]{1,0:T(8,128)(2,1)}, bf16[96,1024]{1,0:T(8,128)(2,1)}, u32[]{:S(2)}, u32[]{:S(2)}) collective-permute-start(bf16[96,1024]{1,0:T(8,128)(2,1)} %get-tuple-element.54), channel_id=1, source_target_pairs={{0,3},{1,0},{2,1},{3,2},{4,7},{5,4},{6,5},{7,6},{8,11},{9,8},{10,9... | collective-permute-start | bytes 589832 | tf_op jit(solution)/shard_map/ppermute | solution.py:413
  39.4 19.5 %product.6 = (bf16[384,2048]{1,0:T(8,128)(2,1)S(1)}, bf16[384,2048]{1,0:T(8,128)(2,1)S(1)}, bf16[2,192,2048]{2,1,0:T(8,128)(2,1)}, bf16[2,192,2048]{2,1,0:T(8,128)(2,1)}, f32[8,128]{1,0:T(8,128)S(1)}) custom-call(s32[3]{0:T(128)S(1)} %pad_add_fusion.pos, bf16[768,2048]{1,0:T(8,128)(2,1)} %bitcast.9, bf16[2048,8192]{1,0:T(8,128)(2,1)} %weights.7, ...), custom_call_target="tpu_custom_call" | custom-call | flops 1 | bytes 1 | tf_op jit(solution)/shard_map/product/pallas_call | solution.py:123
  60.7 1.3 %fusion.1 = (bf16[384,1024]{1,0:T(8,128)(2,1)}, bf16[384,1024]{1,0:T(8,128)(2,1)}) fusion(bf16[384,2048]{1,0:T(8,128)(2,1)S(1)} %get-tuple-element.49), kind=kLoop, calls=%fused_computation.2 | loop fusion | bytes 3145728 | tf_op jit(solution)/shard_map/slice | solution.py:311
  62.0 4.3 %all-to-all-start.1 = ((bf16[4,96,1024]{2,1,0:T(8,128)(2,1)}), bf16[4,96,1024]{2,1,0:T(8,128)(2,1)}, u32[]{:S(2)}, u32[]{:S(2)}) async-start(bf16[4,96,1024]{2,1,0:T(8,128)(2,1)} %copy-done.7), calls=%async_computation.1 | async-start | bytes 1572864 | tf_op jit(solution)/shard_map/all_to_all | solution.py:431
  67.1 3.0 %score.1 = f32[16,768]{1,0:T(8,128)S(1)} custom-call(s32[64]{0:T(128)S(1)} %copy-done.11, s32[4,24]{1,0:T(4,128)S(1)} %copy-done.9, s32[3]{0:T(128)S(1)} %pad_add_fusion.pos, s32[1,768]{1,0:T(1,128)S(1)} %copy-done.12, bf16[768,2048]{1,0:T(8,128)(2,1)S(1)} %bitcast.13, bf16[384,2048]{1,0:T(8,128)(2,1)} %bitcast.5.factors, f32[8,128]{1,0:T(8,128)S(1)} %copy-done.22, ...), custom_call_target="tpu_custom_call" | custom-call | flops 46000001024 | bytes 1 | tf_op jit(solution)/shard_map/score/pallas_call | solution.py:240
  70.1 5.8 %all-gather = f32[64,768]{1,0:T(8,128)S(1)} all-gather(f32[16,768]{1,0:T(8,128)S(1)} %score.1), channel_id=2, replica_groups=mesh['groups'=2,'tp'=4,'rep'=4] {'tp'}, dimensions={0}, use_global_device_ids=true | all-gather | bytes 245760 | tf_op jit(solution)/shard_map/all_gather | solution.py:438
  77.1 3.7 %delta.2 = (bf16[192,1024]{1,0:T(8,128)(2,1)}, bf16[192,1024]{1,0:T(8,128)(2,1)}, bf16[192,1024]{1,0:T(8,128)(2,1)S(1)}, bf16[192,1024]{1,0:T(8,128)(2,1)S(1)}) custom-call(s32[64]{0:T(128)S(1)} %copy-done.11, s32[4,24]{1,0:T(4,128)S(1)} %copy-done.9, s32[3]{0:T(128)S(1)} %pad_add_fusion.pos, s32[1,768]{1,0:T(1,128)S(1)} %copy-done.12, ...), custom_call_target="tpu_custom_call" | custom-call | flops 1 | bytes 1 | tf_op jit(solution)/shard_map/delta/pallas_call | solution.py:295
  80.7 1.5 %collective-permute-start.11 = (bf16[192,1024]{1,0:T(8,128)(2,1)}, bf16[192,1024]{1,0:T(8,128)(2,1)S(1)}, u32[]{:S(2)}, u32[]{:S(2)}) collective-permute-start(bf16[192,1024]{1,0:T(8,128)(2,1)} %get-tuple-element.63), channel_id=1, source_target_pairs={{0,8},{8,0},{4,12},{12,4},{1,9},{9,1},{5,13},{13,5},{2,10},{10,2},... | collective-permute-start | bytes 1179656 | tf_op jit(solution)/shard_map/ppermute | solution.py:407
  82.9 12.2 %product.7 = (bf16[2,192,2048]{2,1,0:T(8,128)(2,1)S(1)}, bf16[2,192,2048]{2,1,0:T(8,128)(2,1)}, f32[8,128]{1,0:T(8,128)S(1)}) custom-call(s32[3]{0:T(128)S(1)} %pad_add_fusion.pos, bf16[768,2048]{1,0:T(8,128)(2,1)} %bitcast.10, bf16[2048,8192]{1,0:T(8,128)(2,1)} %weights.7, bf16[192,1024]{1,0:T(8,128)(2,1)S(1)} %get-tuple-element.55.rest_0_.rest_1_), custom_call_target="tpu_custom_call" | custom-call | flops 1 | bytes 1 | tf_op jit(solution)/shard_map/product/pallas_call | solution.py:195
  96.3 3.9 %delta.3 = (bf16[192,1024]{1,0:T(8,128)(2,1)}, bf16[192,1024]{1,0:T(8,128)(2,1)}, bf16[192,2048]{1,0:T(8,128)(2,1)S(1)}, bf16[192,2048]{1,0:T(8,128)(2,1)}) custom-call(s32[64]{0:T(128)S(1)} %copy-done.11, s32[4,24]{1,0:T(4,128)S(1)} %copy-done.9, s32[3]{0:T(128)S(1)} %pad_add_fusion.pos, s32[1,768]{1,0:T(1,128)S(1)} %copy-done.12, ...), custom_call_target="tpu_custom_call" | custom-call | flops 1 | bytes 1 | tf_op jit(solution)/shard_map/delta/pallas_call | solution.py:295
  101.2 1.5 %collective-permute-start.9 = (bf16[192,1024]{1,0:T(8,128)(2,1)}, bf16[192,1024]{1,0:T(8,128)(2,1)}, u32[]{:S(2)}, u32[]{:S(2)}) collective-permute-start(bf16[192,1024]{1,0:T(8,128)(2,1)} %get-tuple-element.61), channel_id=1, source_target_pairs={{0,8},{8,0},{4,12},{12,4},{1,9},{9,1},{5,13},{13,5},{2,10},{10,2},... | collective-permute-start | bytes 1179656 | tf_op jit(solution)/shard_map/ppermute | solution.py:407
  103.5 2.3 %collective-permute-done.14.theirs = bf16[192,2048]{1,0:T(8,128)(2,1)S(1)} collective-permute-done((bf16[192,2048]{1,0:T(8,128)(2,1)}, bf16[192,2048]{1,0:T(8,128)(2,1)S(1)}, u32[]{:S(2)}, u32[]{:S(2)}) %collective-permute-start.14) | collective-permute-done | bytes 786464 | tf_op jit(solution)/shard_map/ppermute | solution.py:404
  106.8 5.5 %near.1.rest_0_ = bf16[192,8192]{1,0:T(8,128)(2,1)} custom-call(s32[3]{0:T(128)S(1)} %pad_add_fusion.pos, bf16[192,8192]{1,0:T(8,128)(2,1)} %bitcast.16, bf16[2,192,2048]{2,1,0:T(8,128)(2,1)S(1)} %copy-done.13, bf16[2,192,2048]{2,1,0:T(8,128)(2,1)} %collective-permute-done.13.recv, bf16[192,2048]{1,0:T(8,128)(2,1)} %collective-permute-done.2.rest_1_.first, ...), custom_call_target="tpu_custom_call" | custom-call | flops 69000003584 | bytes 1 | tf_op jit(solution)/shard_map/near/pallas_call | solution.py:368
  112.2 3.1 %far.2.rest_0_ = bf16[192,8192]{1,0:T(8,128)(2,1)} custom-call(s32[3]{0:T(128)S(1)} %pad_add_fusion.pos, bf16[192,8192]{1,0:T(8,128)(2,1)} %bitcast.17, bf16[2,192,2048]{2,1,0:T(8,128)(2,1)S(1)} %copy-done.15, bf16[2,192,2048]{2,1,0:T(8,128)(2,1)} %collective-permute-done.8.recv, bf16[192,1024]{1,0:T(8,128)(2,1)S(1)} %copy-done.20, ...), custom_call_target="tpu_custom_call", output_to_operand_aliasing={{}: (6, {})} | custom-call | flops 69000003584 | bytes 1 | tf_op jit(solution)/shard_map/far/pallas_call | solution.py:368
  115.4 4.7 %collective-permute-done.10.cross = bf16[192,1024]{1,0:T(8,128)(2,1)} collective-permute-done((bf16[192,1024]{1,0:T(8,128)(2,1)}, bf16[192,1024]{1,0:T(8,128)(2,1)}, u32[]{:S(2)}, u32[]{:S(2)}) %collective-permute-start.10) | collective-permute-done | bytes 393248 | tf_op jit(solution)/shard_map/ppermute | solution.py:410
  120.1 3.1 %far.3 = bf16[192,8192]{1,0:T(8,128)(2,1)} custom-call(s32[3]{0:T(128)S(1)} %pad_add_fusion.pos, bf16[192,8192]{1,0:T(8,128)(2,1)} %bitcast.18, bf16[2,192,2048]{2,1,0:T(8,128)(2,1)S(1)} %copy-done.15, bf16[2,192,2048]{2,1,0:T(8,128)(2,1)} %collective-permute-done.8.recv, ...), custom_call_target="tpu_custom_call", output_to_operand_aliasing={{}: (6, {})} | custom-call | flops 69000003584 | bytes 1 | tf_op jit(solution)/shard_map/far/pallas_call | solution.py:368
  (76 shorter events, 16.8 us)
Async XLA Ops:
  5.1 6.6 %copy-start = (bf16[1,768,2048]{2,1,0:T(8,128)(2,1)S(1)}, bf16[1,768,2048]{2,1,0:T(8,128)(2,1)}, u32[]{:S(2)}) copy-start(bf16[1,768,2048]{2,1,0:T(8,128)(2,1)} %param.8) | copy-start | bytes 9437188
  5.1 56.9 %all-to-all-start = ((bf16[4,96,2048]{2,1,0:T(8,128)(2,1)}), bf16[4,96,2048]{2,1,0:T(8,128)(2,1)}, u32[]{:S(2)}, u32[]{:S(2)}) async-start(bf16[4,96,2048]{2,1,0:T(8,128)(2,1)} %copy-done.5), calls=%async_computation | async-start | bytes 3145728 | tf_op jit(solution)/shard_map/all_to_all | solution.py:417
  18.3 7.3 %collective-permute-start = (bf16[192,2048]{1,0:T(8,128)(2,1)S(1)}, bf16[192,2048]{1,0:T(8,128)(2,1)S(1)}, u32[]{:S(2)}, u32[]{:S(2)}) collective-permute-start(bf16[192,2048]{1,0:T(8,128)(2,1)S(1)} %get-tuple-element.41), channel_id=1, source_target_pairs={{0,4},{4,0},{8,12},{12,8},{1,5},{5,1},{9,13},{13,9},{2,6},{6,2},{1... | collective-permute-start | bytes 2359304 | tf_op jit(solution)/shard_map/ppermute | solution.py:404
  25.1 3.3 %copy-start.2 = (bf16[16,16,2048]{2,1,0:T(8,128)(2,1)S(1)}, bf16[16,16,2048]{2,1,0:T(8,128)(2,1)}, u32[]{:S(2)}) copy-start(bf16[16,16,2048]{2,1,0:T(8,128)(2,1)} %pool.5) | copy-start | bytes 3145732
  25.1 3.3 %copy-start.9 = (s32[4,24]{1,0:T(4,128)S(1)}, s32[4,24]{1,0:T(4,128)}, u32[]{:S(2)}) copy-start(s32[4,24]{1,0:T(4,128)} %lists.11) | copy-start | bytes 1156
  25.1 12.6 %collective-permute-start.1 = (bf16[192,2048]{1,0:T(8,128)(2,1)S(1)}, bf16[192,2048]{1,0:T(8,128)(2,1)S(1)}, u32[]{:S(2)}, u32[]{:S(2)}) collective-permute-start(bf16[192,2048]{1,0:T(8,128)(2,1)S(1)} %get-tuple-element.44), channel_id=1, source_target_pairs={{0,4},{4,0},{8,12},{12,8},{1,5},{5,1},{9,13},{13,9},{2,6},{6,2},{1... | collective-permute-start | bytes 2359304 | tf_op jit(solution)/shard_map/ppermute | solution.py:404
  26.9 39.5 %collective-permute-start.2 = (bf16[192,2048]{1,0:T(8,128)(2,1)}, bf16[192,2048]{1,0:T(8,128)(2,1)}, u32[]{:S(2)}, u32[]{:S(2)}) collective-permute-start(bf16[192,2048]{1,0:T(8,128)(2,1)} %add.12.rest_0_), channel_id=1, source_target_pairs={{0,8},{8,0},{4,12},{12,4},{1,9},{9,1},{5,13},{13,5},{2,10},{10,2},... | collective-permute-start | bytes 2359304 | tf_op jit(solution)/shard_map/ppermute | solution.py:407
  30.6 45.5 %collective-permute-start.4 = (bf16[96,1024]{1,0:T(8,128)(2,1)}, bf16[96,1024]{1,0:T(8,128)(2,1)S(1)}, u32[]{:S(2)}, u32[]{:S(2)}) collective-permute-start(bf16[96,1024]{1,0:T(8,128)(2,1)} %get-tuple-element.52), channel_id=1, source_target_pairs={{0,1},{1,2},{2,3},{3,0},{4,5},{5,6},{6,7},{7,4},{8,9},{9,10},{10,1... | collective-permute-start | bytes 589832 | tf_op jit(solution)/shard_map/ppermute | solution.py:413
  32.6 43.5 %collective-permute-start.5 = (bf16[96,1024]{1,0:T(8,128)(2,1)}, bf16[96,1024]{1,0:T(8,128)(2,1)}, u32[]{:S(2)}, u32[]{:S(2)}) collective-permute-start(bf16[96,1024]{1,0:T(8,128)(2,1)} %get-tuple-element.53), channel_id=1, source_target_pairs={{0,2},{1,3},{2,0},{3,1},{4,6},{5,7},{6,4},{7,5},{8,10},{9,11},{10,... | collective-permute-start | bytes 589832 | tf_op jit(solution)/shard_map/ppermute | solution.py:413
  35.0 41.1 %collective-permute-start.6 = (bf16[96,1024]{1,0:T(8,128)(2,1)}, bf16[96,1024]{1,0:T(8,128)(2,1)}, u32[]{:S(2)}, u32[]{:S(2)}) collective-permute-start(bf16[96,1024]{1,0:T(8,128)(2,1)} %get-tuple-element.54), channel_id=1, source_target_pairs={{0,3},{1,0},{2,1},{3,2},{4,7},{5,4},{6,5},{7,6},{8,11},{9,8},{10,9... | collective-permute-start | bytes 589832 | tf_op jit(solution)/shard_map/ppermute | solution.py:413
  38.9 37.2 %collective-permute-start.7 = (bf16[192,2048]{1,0:T(8,128)(2,1)}, bf16[192,2048]{1,0:T(8,128)(2,1)}, u32[]{:S(2)}, u32[]{:S(2)}) collective-permute-start(bf16[192,2048]{1,0:T(8,128)(2,1)} %add.13.rest_1_), channel_id=1, source_target_pairs={{0,8},{8,0},{4,12},{12,4},{1,9},{9,1},{5,13},{13,5},{2,10},{10,2},... | collective-permute-start | bytes 2359304 | tf_op jit(solution)/shard_map/ppermute | solution.py:407
  60.7 5.7 %copy-start.1 = (bf16[1,768,2048]{2,1,0:T(8,128)(2,1)S(1)}, bf16[1,768,2048]{2,1,0:T(8,128)(2,1)}, u32[]{:S(2)}) copy-start(bf16[1,768,2048]{2,1,0:T(8,128)(2,1)} %param.8) | copy-start | bytes 9437188
  62.0 4.4 %copy-start.12 = (s32[1,768]{1,0:T(1,128)S(1)}, s32[1,768]{1,0:T(1,128)}, u32[]{:S(2)}) copy-start(s32[1,768]{1,0:T(1,128)} %wanted.5) | copy-start | bytes 9220
  62.0 34.3 %all-to-all-start.1 = ((bf16[4,96,1024]{2,1,0:T(8,128)(2,1)}), bf16[4,96,1024]{2,1,0:T(8,128)(2,1)}, u32[]{:S(2)}, u32[]{:S(2)}) async-start(bf16[4,96,1024]{2,1,0:T(8,128)(2,1)} %copy-done.7), calls=%async_computation.1 | async-start | bytes 1572864 | tf_op jit(solution)/shard_map/all_to_all | solution.py:431
  66.4 9.6 %collective-permute-start.3 = (bf16[384,2048]{1,0:T(8,128)(2,1)}, bf16[384,2048]{1,0:T(8,128)(2,1)S(1)}, u32[]{:S(2)}, u32[]{:S(2)}) collective-permute-start(bf16[384,2048]{1,0:T(8,128)(2,1)} %copy-done.16), channel_id=1, source_target_pairs={{0,4},{4,0},{8,12},{12,8},{1,5},{5,1},{9,13},{13,9},{2,6},{6,2},{1... | collective-permute-start | bytes 4718600 | tf_op jit(solution)/shard_map/ppermute | solution.py:404
  80.7 22.0 %collective-permute-start.11 = (bf16[192,1024]{1,0:T(8,128)(2,1)}, bf16[192,1024]{1,0:T(8,128)(2,1)S(1)}, u32[]{:S(2)}, u32[]{:S(2)}) collective-permute-start(bf16[192,1024]{1,0:T(8,128)(2,1)} %get-tuple-element.63), channel_id=1, source_target_pairs={{0,8},{8,0},{4,12},{12,4},{1,9},{9,1},{5,13},{13,5},{2,10},{10,2},... | collective-permute-start | bytes 1179656 | tf_op jit(solution)/shard_map/ppermute | solution.py:407
  82.2 21.1 %collective-permute-start.12 = (bf16[192,1024]{1,0:T(8,128)(2,1)}, bf16[192,1024]{1,0:T(8,128)(2,1)}, u32[]{:S(2)}, u32[]{:S(2)}) collective-permute-start(bf16[192,1024]{1,0:T(8,128)(2,1)} %get-tuple-element.64), channel_id=1, source_target_pairs={{0,12},{12,0},{4,8},{8,4},{1,13},{13,1},{5,9},{9,5},{2,14},{14,2},... | collective-permute-start | bytes 1179656 | tf_op jit(solution)/shard_map/ppermute | solution.py:410
  82.4 21.0 %collective-permute-start.13 = (bf16[2,192,2048]{2,1,0:T(8,128)(2,1)}, bf16[2,192,2048]{2,1,0:T(8,128)(2,1)}, u32[]{:S(2)}, u32[]{:S(2)}) collective-permute-start(bf16[2,192,2048]{2,1,0:T(8,128)(2,1)} %get-tuple-element.69), channel_id=1, source_target_pairs={{0,4},{4,0},{8,12},{12,8},{1,5},{5,1},{9,13},{13,9},{2,6},{6,2},{1... | collective-permute-start | bytes 4718600 | tf_op jit(solution)/shard_map/ppermute | solution.py:404
  82.9 13.5 %copy-start.3 = (bf16[384,1024]{1,0:T(8,128)(2,1)S(1)}, bf16[384,1024]{1,0:T(8,128)(2,1)}, u32[]{:S(2)}) copy-start(bf16[384,1024]{1,0:T(8,128)(2,1)} %get-tuple-element.73.late_own) | copy-start | bytes 2359300
  101.2 14.2 %collective-permute-start.9 = (bf16[192,1024]{1,0:T(8,128)(2,1)}, bf16[192,1024]{1,0:T(8,128)(2,1)}, u32[]{:S(2)}, u32[]{:S(2)}) collective-permute-start(bf16[192,1024]{1,0:T(8,128)(2,1)} %get-tuple-element.61), channel_id=1, source_target_pairs={{0,8},{8,0},{4,12},{12,4},{1,9},{9,1},{5,13},{13,5},{2,10},{10,2},... | collective-permute-start | bytes 1179656 | tf_op jit(solution)/shard_map/ppermute | solution.py:407
  102.7 17.4 %collective-permute-start.10 = (bf16[192,1024]{1,0:T(8,128)(2,1)}, bf16[192,1024]{1,0:T(8,128)(2,1)}, u32[]{:S(2)}, u32[]{:S(2)}) collective-permute-start(bf16[192,1024]{1,0:T(8,128)(2,1)} %get-tuple-element.62), channel_id=1, source_target_pairs={{0,12},{12,0},{4,8},{8,4},{1,13},{13,1},{5,9},{9,5},{2,14},{14,2},... | collective-permute-start | bytes 1179656 | tf_op jit(solution)/shard_map/ppermute | solution.py:410
  102.7 3.1 %collective-permute-start.14 = (bf16[192,2048]{1,0:T(8,128)(2,1)}, bf16[192,2048]{1,0:T(8,128)(2,1)S(1)}, u32[]{:S(2)}, u32[]{:S(2)}) collective-permute-start(bf16[192,2048]{1,0:T(8,128)(2,1)} %get-tuple-element.70), channel_id=1, source_target_pairs={{0,4},{4,0},{8,12},{12,8},{1,5},{5,1},{9,13},{13,9},{2,6},{6,2},{1... | collective-permute-start | bytes 2359304 | tf_op jit(solution)/shard_map/ppermute | solution.py:404
  103.3 8.9 %collective-permute-start.8 = (bf16[2,192,2048]{2,1,0:T(8,128)(2,1)}, bf16[2,192,2048]{2,1,0:T(8,128)(2,1)}, u32[]{:S(2)}, u32[]{:S(2)}) collective-permute-start(bf16[2,192,2048]{2,1,0:T(8,128)(2,1)} %get-tuple-element.57), channel_id=1, source_target_pairs={{0,4},{4,0},{8,12},{12,8},{1,5},{5,1},{9,13},{13,9},{2,6},{6,2},{1... | collective-permute-start | bytes 4718600 | tf_op jit(solution)/shard_map/ppermute | solution.py:404
  106.8 5.5 %copy-start.15 = (bf16[2,192,2048]{2,1,0:T(8,128)(2,1)S(1)}, bf16[2,192,2048]{2,1,0:T(8,128)(2,1)}, u32[]{:S(2)}) copy-start(bf16[2,192,2048]{2,1,0:T(8,128)(2,1)} %copy-done.14) | copy-start | bytes 4718596
  (16 other events, 20.9 us)

commit v4 on v3

--- a/solution.py
+++ b/solution.py
@@ -31,14 +31,13 @@
 TOKEN = sds((8, 128), F32)
 
 
-def select_kernel(cuts, by_target, n_rep, cap, pool_dev, rank, slot, lists, pos, pool, *rest):
-    n_outs = len(cuts) if by_target else n_rep * len(cuts)
-    outs, (token, idx) = rest[-2 - n_outs : -2], rest[-2:]
+def select_kernel(by_shift, by_target, n_rep, cap, pool_dev, rank, slot, lists, pos, pool, *rest):
+    token, idx = rest[-2:]
+    outs = rest[-2 - n_rep * len(by_shift) - len(by_target) : -2]
     token[...] = jnp.zeros_like(token)
     me = pos[2]
-    listed = lists.shape[1]
     for shift in range(n_rep):
-        target = shift if by_target else lax.rem(me + shift, n_rep)
+        target = lax.rem(me + shift, n_rep)
         for k in range(cap):
             idx[k] = 0
 
@@ -52,58 +51,44 @@
 
             return count + mine.astype(jnp.int32)
 
-        lax.fori_loop(0, listed, body, jnp.int32(0), unroll=True)
+        lax.fori_loop(0, lists.shape[1], body, jnp.int32(0), unroll=True)
         for k in range(cap):
             entry = idx[k]
-            for c, (start, stop) in enumerate(cuts):
-                if by_target:
-                    outs[c][shift, pl.ds(k * rank, rank), :] = pool[entry, :, start:stop]
-                else:
-                    outs[shift * len(cuts) + c][pl.ds(k * rank, rank), :] = pool[entry, :, start:stop]
-
-
-def select(slot, lists, pos, pool, cuts, by_target, n_rep, cap, after=()):
+            rows = pl.ds(k * rank, rank)
+            for c, (start, stop) in enumerate(by_shift):
+                outs[c * n_rep + shift][rows, :] = pool[entry, :, start:stop]
+            for c, (start, stop) in enumerate(by_target):
+                outs[len(by_shift) * n_rep + c][target, rows, :] = pool[entry, :, start:stop]
+
+
+def select(slot, lists, pos, pool, by_shift, by_target, n_rep, cap, after=()):
     pool_dev, rank, width = pool.shape
-    if by_target:
-        shapes = [sds((n_rep, cap * rank, stop - start)) for start, stop in cuts]
-    else:
-        shapes = [sds((cap * rank, stop - start)) for _ in range(n_rep) for start, stop in cuts]
-    return pl.pallas_call(
-        functools.partial(select_kernel, cuts, by_target, n_rep, cap, pool_dev, rank),
+    shapes = [sds((cap * rank, stop - start)) for start, stop in by_shift for _ in range(n_rep)]
+    shapes += [sds((n_rep, cap * rank, stop - start)) for start, stop in by_target]
+    return pl.pallas_call(
+        functools.partial(select_kernel, by_shift, by_target, n_rep, cap, pool_dev, rank),
         out_shape=[*shapes, TOKEN],
         in_specs=[SMEM, SMEM, SMEM, VMEM] + [ANY] * len(after),
         out_specs=[VMEM] * len(shapes) + [VMEM],
         scratch_shapes=[pltpu.SMEM((cap,), jnp.int32)],
-        compiler_params=params(),
+        compiler_params=params(16),
         cost_estimate=order(0),
         name="select",
     )(slot, lists, pos, pool, *after)
 
 
-def product_columns_kernel(per, pos, features, weights, late, late_send, keep, send, token):
+def product_columns_kernel(per, pos, features, weights, late, late_send, token):
     token[...] = jnp.zeros_like(token)
     j = pl.program_id(0)
-    half = features.shape[0] // 2
-    own = half // 2
     result = jnp.dot(features[...], weights[...], preferred_element_type=F32).astype(BF16)
-    for chip in range(2):
-        here = pos[0] == chip
-        other = result[(1 - chip) * half : (2 - chip) * half]
-
-        @pl.when(here & (j < per))
-        def _():
-            late[...] = other
-
-        @pl.when(here & (j >= per))
-        def _():
-            late_send[...] = other
-
-        for core in range(2):
-
-            @pl.when(here & (pos[1] == core))
-            def _():
-                keep[...] = result[chip * half + core * own : chip * half + (core + 1) * own][None]
-                send[...] = result[chip * half + (1 - core) * own : chip * half + (2 - core) * own][None]
+
+    @pl.when(j < per)
+    def _():
+        late[...] = result
+
+    @pl.when(j >= per)
+    def _():
+        late_send[...] = result
 
 
 def product_columns(pos, features, projection, tile, after=()):
@@ -112,30 +97,29 @@
     half = rows // 2
     per = width // tile
 
-    def block(j, pos):
-        return jnp.where(j < per, pos[1], 1 - pos[1])
-
-    rest = pl.BlockSpec((1, half // 2, tile), lambda j, pos: (block(j, pos), 0, lax.rem(j, per)))
-
     def kernel(pos, features, weights, *rest):
-        product_columns_kernel(per, pos, features, weights, *rest[-5:])
+        product_columns_kernel(per, pos, features, weights, *rest[-3:])
 
     return pl.pallas_call(
         kernel,
-        out_shape=[sds((half, width))] * 2 + [sds((2, half // 2, width))] * 2 + [TOKEN],
+        out_shape=[sds((half, width))] * 2 + [TOKEN],
         grid_spec=pltpu.PrefetchScalarGridSpec(
             num_scalar_prefetch=1,
             grid=(2 * per,),
             in_specs=[
-                pl.BlockSpec((rows, depth), lambda j, pos: (0, 0)),
-                pl.BlockSpec((depth, tile), lambda j, pos: (0, (2 * pos[0] + block(j, pos)) * per + lax.rem(j, per))),
+                pl.BlockSpec((half, depth), lambda j, pos: (1 - pos[0], 0)),
+                pl.BlockSpec(
+                    (depth, tile),
+                    lambda j, pos: (
+                        0,
+                        (2 * pos[0] + jnp.where(j < per, pos[1], 1 - pos[1])) * per + lax.rem(j, per),
+                    ),
+                ),
             ]
             + [ANY] * len(after),
             out_specs=[
                 pl.BlockSpec((half, tile), lambda j, pos: (0, jnp.minimum(j, per - 1))),
                 pl.BlockSpec((half, tile), lambda j, pos: (0, jnp.maximum(j - per, 0))),
-                rest,
-                rest,
                 pl.BlockSpec((8, 128), lambda j, pos: (0, 0)),
             ],
         ),
@@ -291,11 +275,15 @@
     rows = wanted.shape[1]
     start, stop = cut
     width = stop - start
-    late_own, late_recv = late
     return pl.pallas_call(
         functools.partial(delta_kernel, len(blocks), n_rep, cap, pool_dev, rank, len(before)),
         out_shape=[sds((own, width))] * 2 + [sds((own, stop))] * 2,
-        in_specs=[SMEM] * 3 + [VMEM] * (4 + len(blocks) + len(before)) + [ANY] * len(after),
+        grid=(1,),
+        in_specs=[SMEM] * 3
+        + [VMEM] * 2
+        + [pl.BlockSpec((2 * own, width), lambda i: (0, start // width))] * 2
+        + [VMEM] * (len(blocks) + len(before))
+        + [ANY] * len(after),
         out_specs=[VMEM] * 4,
         scratch_shapes=[
             pltpu.VMEM((n_rep * cap * rank, rows), BF16),
@@ -307,9 +295,7 @@
         compiler_params=params(),
         cost_estimate=order(0),
         name="delta",
-    )(
-        slot, lists, pos, wanted, shrunk, late_own[:, start:stop], late_recv[:, start:stop], *blocks, *before, *after
-    )
+    )(slot, lists, pos, wanted, shrunk, *late, *blocks, *before, *after)
 
 
 def gate_kernel(*refs):
@@ -413,7 +399,7 @@
         return lax.ppermute(x, "rep", [(i, (i + shift) % n_rep) for i in range(n_rep)])
 
     shifts = [s for s in range(1, n_rep) if s != n_rep // 2] + [n_rep // 2]
-    chosen, token = select(*lists, shrink_pool, ((0, width),), True, n_rep, cap)
+    chosen, token = select(*lists, shrink_pool, (), ((0, width),), n_rep, cap)
     shrink = lax.all_to_all(chosen, "rep", 0, 0, tiled=True).reshape(n_rep * cap * rank, width)
 
     early = []
@@ -423,16 +409,14 @@
         sums.append(keep + over_core(send))
         early.append(over_chip(sums[-1]))
 
-    *chosen, token = select(*lists, expand_pool, cuts[:1], False, n_rep, cap, [token])
+    *chosen, second, token = select(*lists, expand_pool, cuts[:1], cuts[1:], n_rep, cap, [token])
     first = [chosen[0]] + [None] * (n_rep - 1)
     for s in shifts:
         first[s] = over_rep(chosen[s], s)
-    chosen, token = select(*lists, expand_pool, cuts[1:], True, n_rep, cap, [token])
-    second = lax.all_to_all(chosen, "rep", 0, 0, tiled=True).reshape(n_rep * cap * rank, cut)
-
-    late_keep, late_send, keep, send, token = product_columns(pos, features, projection, tile, [*sums, token])
-    late = (late_keep, over_core(late_send))
-    near_base = (keep, over_core(send))
+    second = lax.all_to_all(second, "rep", 0, 0, tiled=True).reshape(n_rep * cap * rank, cut)
+
+    keep, send, token = product_columns(pos, features, projection, tile, [*sums, token])
+    late = (keep, over_core(send))
 
     part = score(*lists, request_variant, features, shrink, n_rep, *sizes, [token, early[0]])
     shrunk = lax.all_gather(part, "tp")
@@ -440,12 +424,14 @@
     common = (*lists, request_variant, shrunk, late)
     straight, cross, *before = delta(*common, first, cuts[0], n_rep, *sizes, own, (), [early[1]])
     far = [over_chip(straight), over_both(cross)]
-    keep, send, token = product(pos, features, projection, False, True, 0, 2 * width, tile, 2, [before[0]])
-    far_base = (keep, over_core(send))
+    keep, send, token = product(pos, features, projection, False, False, 0, 2 * width, tile, 2, [before[0]])
+    near_base = (keep, over_core(send))
     straight, cross, mine, send = delta(*common, [second], cuts[1], n_rep, *sizes, own, before, [token])
     last = [over_chip(straight), over_both(cross)]
     theirs = over_core(send)
-    far = gate(far, [mine])
+    keep, send, token = product(pos, features, projection, False, True, 0, 2 * width, tile, 2, [mine])
+    far_base = (keep, over_core(send))
+    far = gate(far, [token])
     out = finish(pos, None, stream, near_base, 0, width, True, [*early, mine, theirs], far)
     out = finish(pos, out, stream, far_base, *cuts[0], False, far)
     out = finish(pos, out, stream, far_base, *cuts[1], False, last)

time: 124 us -> 131 us (1.056)
  Pallas kernels: 72.1 us -> 76 us
  waiting for transfers between devices: 7.07 us -> 8.74 us
    pallas_call x3 -> x4, Pallas kernels: 25.5 us -> 37.8 us  [product(): pl.pallas_call(kernel, out_shape=[sds(shape), sds(shape), TOKEN], grid_sp...]
    pallas_call x4 -> x3, Pallas kernels: 24.3 us -> 15.2 us  [the longest x1 11.7 us: product_columns(): pl.pallas_call(kernel, out_shape=[sds((half, width))] * 2 + [TOKEN], grid...]
    all_to_all x2 -> x1, waiting for transfers between devices: 0.01 us -> 5.47 us  [paired(): lax.all_to_all(chosen, 'rep', 0, 0, tiled=True)]
    ppermute x2, waiting for transfers between devices: 4.73 us -> 0.01 us  [over_both(): return lax.ppermute(x, 'tp', [(0, 3), (3, 0), (1, 2), (2, 1)])]
    all_to_all x2 -> x1, starting transfers between devices: 10.9 us -> 6.58 us  [paired(): lax.all_to_all(chosen, 'rep', 0, 0, tiled=True)]
    all_to_all x0 -> x1, starting transfers between devices: none -> 4.2 us  [paired(): lax.all_to_all(second, 'rep', 0, 0, tiled=True)]
    unnamed x46 -> x50, local copies, waits for them, and re-layouts: 10.3 us -> 13 us
    slice x2 -> x0, local copies, waits for them, and re-layouts: 1.42 us -> none  [the longest x1 1.3 us: delta(): late_own[:, start:stop]]
  transfers between devices with their start and end apart: 17 -> 17, of which waited for: 2 -> 2; matrix products, arithmetic and copies ran while one was open for 3% -> 2% of each run, Pallas kernels for 55% -> 55%
where the time goes in v4:
time: 131 us; the launch traced here: 130 us
  Pallas kernels  76 us (58%)
  starting transfers between devices  23.7 us (18%)
  local copies, waits for them, and re-layouts  13 us (10%)
  waiting for transfers between devices  8.74 us (7%)
  blocking collectives  5.83 us (4%)
  other arithmetic  2.46 us (2%)
    pallas_call x4, Pallas kernels, product(): pl.pallas_call(kernel, out_shape=[sds(shape), sds(shape), TOKEN], grid_sp...  37.8 us
    unnamed x50, local copies, waits for them, and re-layouts  13 us
    pallas_call x3, Pallas kernels, finish(): pl.pallas_call(near_kernel if near else far_kernel, out_shape=sds((own, f...  11.7 us
    pallas_call x1, Pallas kernels, product_columns(): pl.pallas_call(kernel, out_shape=[sds((half, width))] * 2 + [TOKEN], grid...  11.7 us
    pallas_call x2, Pallas kernels, delta(): pl.pallas_call(functools.partial(delta_kernel, len(blocks), n_rep, cap, p...  8.13 us
    all_to_all x1, starting transfers between devices, paired(): lax.all_to_all(chosen, 'rep', 0, 0, tiled=True)  6.58 us
    ppermute x3, starting transfers between devices, over_rep(): lax.ppermute(x, 'rep', [(i, (i + shift) % n_rep) for i in range(n_rep)])  5.85 us
    all_gather x1, blocking collectives, paired(): shrunk = lax.all_gather(part, 'tp')  5.83 us
  transfers between devices with their start and end apart: 17, of which 2 were waited for; matrix products, arithmetic and copies ran while one was open for 2% of the time, Pallas kernels for 55%

profile of v4, /device:TPU:0, one launch (start us, length us, event | category | flops | bytes accessed | tf_op | source)
XLA Modules:
  0.0 129.9 jit_solution(7408233794167979751)
XLA Ops:
  2.6 1.3 %select.8 = (bf16[4,96,2048]{2,1,0:T(8,128)(2,1)S(1)}, f32[8,128]{1,0:T(8,128)S(1)}) custom-call(s32[64]{0:T(128)S(1)} %copy-done.14, s32[4,24]{1,0:T(4,128)S(1)} %copy-done.11, s32[3]{0:T(128)S(1)} %pad_add_fusion.pos, bf16[16,16,2048]{2,1,0:T(8,128)(2,1)S(1)} %copy-done.6), custom_call_target="tpu_custom_call" | custom-call | flops 1 | bytes 1 | tf_op jit(solution)/shard_map/select/pallas_call | solution.py:68
  5.1 6.6 %all-to-all-start = ((bf16[4,96,2048]{2,1,0:T(8,128)(2,1)}), bf16[4,96,2048]{2,1,0:T(8,128)(2,1)}, u32[]{:S(2)}, u32[]{:S(2)}) async-start(bf16[4,96,2048]{2,1,0:T(8,128)(2,1)} %copy-done.5), calls=%async_computation | async-start | bytes 3145728 | tf_op jit(solution)/shard_map/all_to_all | solution.py:403
  11.7 6.6 %product.5 = (bf16[192,2048]{1,0:T(8,128)(2,1)S(1)}, bf16[192,2048]{1,0:T(8,128)(2,1)S(1)}, f32[8,128]{1,0:T(8,128)S(1)}) custom-call(s32[3]{0:T(128)S(1)} %pad_add_fusion.pos, bf16[768,2048]{1,0:T(8,128)(2,1)S(1)} %bitcast.12, bf16[2048,8192]{1,0:T(8,128)(2,1)} %weights.9, f32[8,128]{1,0:T(8,128)S(1)} %get-tuple-element.39.rest_0_), custom_call_target="tpu_custom_call" | custom-call | flops 1 | bytes 1 | tf_op jit(solution)/shard_map/product/pallas_call | solution.py:179
  18.5 6.7 %product.6 = (bf16[192,2048]{1,0:T(8,128)(2,1)S(1)}, bf16[192,2048]{1,0:T(8,128)(2,1)S(1)}, f32[8,128]{1,0:T(8,128)S(1)}) custom-call(s32[3]{0:T(128)S(1)} %pad_add_fusion.pos, bf16[768,2048]{1,0:T(8,128)(2,1)S(1)} %bitcast.13, bf16[2048,8192]{1,0:T(8,128)(2,1)} %weights.9, f32[8,128]{1,0:T(8,128)S(1)} %get-tuple-element.42.rest_0_), custom_call_target="tpu_custom_call" | custom-call | flops 1 | bytes 1 | tf_op jit(solution)/shard_map/product/pallas_call | solution.py:179
  26.9 1.5 %collective-permute-start.2 = (bf16[192,2048]{1,0:T(8,128)(2,1)}, bf16[192,2048]{1,0:T(8,128)(2,1)}, u32[]{:S(2)}, u32[]{:S(2)}) collective-permute-start(bf16[192,2048]{1,0:T(8,128)(2,1)} %add.12.rest_0_), channel_id=1, source_target_pairs={{0,8},{8,0},{4,12},{12,4},{1,9},{9,1},{5,13},{13,5},{2,10},{10,2},... | collective-permute-start | bytes 2359304 | tf_op jit(solution)/shard_map/ppermute | solution.py:393
  28.4 2.2 %select.9 = (bf16[96,1024]{1,0:T(8,128)(2,1)S(1)}, bf16[96,1024]{1,0:T(8,128)(2,1)}, bf16[96,1024]{1,0:T(8,128)(2,1)}, bf16[96,1024]{1,0:T(8,128)(2,1)}, bf16[4,...) custom-call(s32[64]{0:T(128)S(1)} %copy-done.15, s32[4,24]{1,0:T(4,128)S(1)} %copy-done.12, s32[3]{0:T(128)S(1)} %pad_add_fusion.pos, ...), custom_call_target="tpu_custom_call" | custom-call | flops 1 | bytes 1 | tf_op jit(solution)/shard_map/select/pallas_call | solution.py:68
  30.6 2.0 %collective-permute-start.4 = (bf16[96,1024]{1,0:T(8,128)(2,1)}, bf16[96,1024]{1,0:T(8,128)(2,1)S(1)}, u32[]{:S(2)}, u32[]{:S(2)}) collective-permute-start(bf16[96,1024]{1,0:T(8,128)(2,1)} %get-tuple-element.52), channel_id=1, source_target_pairs={{0,1},{1,2},{2,3},{3,0},{4,5},{5,6},{6,7},{7,4},{8,9},{9,10},{10,1... | collective-permute-start | bytes 589832 | tf_op jit(solution)/shard_map/ppermute | solution.py:399
  32.6 2.4 %collective-permute-start.5 = (bf16[96,1024]{1,0:T(8,128)(2,1)}, bf16[96,1024]{1,0:T(8,128)(2,1)}, u32[]{:S(2)}, u32[]{:S(2)}) collective-permute-start(bf16[96,1024]{1,0:T(8,128)(2,1)} %get-tuple-element.53), channel_id=1, source_target_pairs={{0,2},{1,3},{2,0},{3,1},{4,6},{5,7},{6,4},{7,5},{8,10},{9,11},{10,... | collective-permute-start | bytes 589832 | tf_op jit(solution)/shard_map/ppermute | solution.py:399
  35.0 1.5 %collective-permute-start.6 = (bf16[96,1024]{1,0:T(8,128)(2,1)}, bf16[96,1024]{1,0:T(8,128)(2,1)}, u32[]{:S(2)}, u32[]{:S(2)}) collective-permute-start(bf16[96,1024]{1,0:T(8,128)(2,1)} %get-tuple-element.54), channel_id=1, source_target_pairs={{0,3},{1,0},{2,1},{3,2},{4,7},{5,4},{6,5},{7,6},{8,11},{9,8},{10,9... | collective-permute-start | bytes 589832 | tf_op jit(solution)/shard_map/ppermute | solution.py:399
  38.2 11.7 %product.7 = (bf16[384,2048]{1,0:T(8,128)(2,1)S(1)}, bf16[384,2048]{1,0:T(8,128)(2,1)S(1)}, f32[8,128]{1,0:T(8,128)S(1)}) custom-call(s32[3]{0:T(128)S(1)} %pad_add_fusion.pos, bf16[768,2048]{1,0:T(8,128)(2,1)} %bitcast.9, bf16[2048,8192]{1,0:T(8,128)(2,1)} %weights.9, bf16[192,2048]{1,0:T(8,128)(2,1)} %add.12.rest_0_, bf16[192,2048]{1,0:T(8,128)(2,1)} %add.13.rest_1_, ...), custom_call_target="tpu_custom_call" | custom-call | flops 1 | bytes 1 | tf_op jit(solution)/shard_map/product/pallas_call | solution.py:103
  52.8 5.5 %all-to-all-done = bf16[4,96,2048]{2,1,0:T(8,128)(2,1)} async-done(((bf16[4,96,2048]{2,1,0:T(8,128)(2,1)}), bf16[4,96,2048]{2,1,0:T(8,128)(2,1)}, u32[]{:S(2)}, u32[]{:S(2)}) %all-to-all-start) | async-done | bytes 1572896 | tf_op jit(solution)/shard_map/all_to_all | solution.py:403
  58.3 4.2 %all-to-all-start.1 = ((bf16[4,96,1024]{2,1,0:T(8,128)(2,1)}), bf16[4,96,1024]{2,1,0:T(8,128)(2,1)}, u32[]{:S(2)}, u32[]{:S(2)}) async-start(bf16[4,96,1024]{2,1,0:T(8,128)(2,1)} %copy-done.8), calls=%async_computation.1 | async-start | bytes 1572864 | tf_op jit(solution)/shard_map/all_to_all | solution.py:416
  63.3 3.1 %score.1 = f32[16,768]{1,0:T(8,128)S(1)} custom-call(s32[64]{0:T(128)S(1)} %copy-done.15, s32[4,24]{1,0:T(4,128)S(1)} %copy-done.12, s32[3]{0:T(128)S(1)} %pad_add_fusion.pos, s32[1,768]{1,0:T(1,128)S(1)} %copy-done.13, bf16[768,2048]{1,0:T(8,128)(2,1)S(1)} %bitcast.14, bf16[384,2048]{1,0:T(8,128)(2,1)} %bitcast.5.factors, f32[8,128]{1,0:T(8,128)S(1)} %copy-done.22, ...), custom_call_target="tpu_custom_call" | custom-call | flops 46000001024 | bytes 1 | tf_op jit(solution)/shard_map/score/pallas_call | solution.py:224
  66.3 5.8 %all-gather = f32[64,768]{1,0:T(8,128)S(1)} all-gather(f32[16,768]{1,0:T(8,128)S(1)} %score.1), channel_id=2, replica_groups=mesh['groups'=2,'tp'=4,'rep'=4] {'tp'}, dimensions={0}, use_global_device_ids=true | all-gather | bytes 245760 | tf_op jit(solution)/shard_map/all_gather | solution.py:422
  75.0 3.9 %delta.2 = (bf16[192,1024]{1,0:T(8,128)(2,1)}, bf16[192,1024]{1,0:T(8,128)(2,1)}, bf16[192,1024]{1,0:T(8,128)(2,1)S(1)}, bf16[192,1024]{1,0:T(8,128)(2,1)S(1)}) custom-call(s32[64]{0:T(128)S(1)} %copy-done.15, s32[4,24]{1,0:T(4,128)S(1)} %copy-done.12, s32[3]{0:T(128)S(1)} %pad_add_fusion.pos, s32[1,768]{1,0:T(1,128)S(1)} %copy-done.13, ...), custom_call_target="tpu_custom_call" | custom-call | flops 1 | bytes 1 | tf_op jit(solution)/shard_map/delta/pallas_call | solution.py:278
  78.8 1.5 %collective-permute-start.11 = (bf16[192,1024]{1,0:T(8,128)(2,1)}, bf16[192,1024]{1,0:T(8,128)(2,1)}, u32[]{:S(2)}, u32[]{:S(2)}) collective-permute-start(bf16[192,1024]{1,0:T(8,128)(2,1)} %get-tuple-element.63), channel_id=1, source_target_pairs={{0,8},{8,0},{4,12},{12,4},{1,9},{9,1},{5,13},{13,5},{2,10},{10,2},... | collective-permute-start | bytes 1179656 | tf_op jit(solution)/shard_map/ppermute | solution.py:393
  80.5 12.3 %product.8 = (bf16[2,192,2048]{2,1,0:T(8,128)(2,1)S(1)}, bf16[2,192,2048]{2,1,0:T(8,128)(2,1)}, f32[8,128]{1,0:T(8,128)S(1)}) custom-call(s32[3]{0:T(128)S(1)} %pad_add_fusion.pos, bf16[768,2048]{1,0:T(8,128)(2,1)} %bitcast.10, bf16[2048,8192]{1,0:T(8,128)(2,1)} %weights.9, bf16[192,1024]{1,0:T(8,128)(2,1)S(1)} %get-tuple-element.55.rest_0_.rest_1_), custom_call_target="tpu_custom_call" | custom-call | flops 1 | bytes 1 | tf_op jit(solution)/shard_map/product/pallas_call | solution.py:179
  93.9 4.3 %delta.3 = (bf16[192,1024]{1,0:T(8,128)(2,1)}, bf16[192,1024]{1,0:T(8,128)(2,1)}, bf16[192,2048]{1,0:T(8,128)(2,1)S(1)}, bf16[192,2048]{1,0:T(8,128)(2,1)}) custom-call(s32[64]{0:T(128)S(1)} %copy-done.15, s32[4,24]{1,0:T(4,128)S(1)} %copy-done.12, s32[3]{0:T(128)S(1)} %pad_add_fusion.pos, s32[1,768]{1,0:T(1,128)S(1)} %copy-done.13, ...), custom_call_target="tpu_custom_call" | custom-call | flops 1 | bytes 1 | tf_op jit(solution)/shard_map/delta/pallas_call | solution.py:278
  98.2 1.5 %collective-permute-start.9 = (bf16[192,1024]{1,0:T(8,128)(2,1)}, bf16[192,1024]{1,0:T(8,128)(2,1)}, u32[]{:S(2)}, u32[]{:S(2)}) collective-permute-start(bf16[192,1024]{1,0:T(8,128)(2,1)} %get-tuple-element.61), channel_id=1, source_target_pairs={{0,8},{8,0},{4,12},{12,4},{1,9},{9,1},{5,13},{13,5},{2,10},{10,2},... | collective-permute-start | bytes 1179656 | tf_op jit(solution)/shard_map/ppermute | solution.py:393
  100.4 12.3 %product.9 = (bf16[2,192,2048]{2,1,0:T(8,128)(2,1)S(1)}, bf16[2,192,2048]{2,1,0:T(8,128)(2,1)}, f32[8,128]{1,0:T(8,128)S(1)}) custom-call(s32[3]{0:T(128)S(1)} %pad_add_fusion.pos, bf16[768,2048]{1,0:T(8,128)(2,1)} %bitcast.11, bf16[2048,8192]{1,0:T(8,128)(2,1)} %weights.9, bf16[192,2048]{1,0:T(8,128)(2,1)S(1)} %get-tuple-element.58.rest_0_.mine), custom_call_target="tpu_custom_call" | custom-call | flops 1 | bytes 1 | tf_op jit(solution)/shard_map/product/pallas_call | solution.py:179
  114.9 3.2 %collective-permute-done.13.recv = bf16[2,192,2048]{2,1,0:T(8,128)(2,1)} collective-permute-done((bf16[2,192,2048]{2,1,0:T(8,128)(2,1)}, bf16[2,192,2048]{2,1,0:T(8,128)(2,1)}, u32[]{:S(2)}, u32[]{:S(2)}) %collective-permute-start.13) | collective-permute-done | bytes 1572896 | tf_op jit(solution)/shard_map/ppermute | solution.py:390
  118.2 5.5 %near.1.rest_0_ = bf16[192,8192]{1,0:T(8,128)(2,1)} custom-call(s32[3]{0:T(128)S(1)} %pad_add_fusion.pos, bf16[192,8192]{1,0:T(8,128)(2,1)} %bitcast.17, bf16[2,192,2048]{2,1,0:T(8,128)(2,1)S(1)} %copy-done.17, bf16[2,192,2048]{2,1,0:T(8,128)(2,1)} %collective-permute-done.13.recv, bf16[192,2048]{1,0:T(8,128)(2,1)} %collective-permute-done.2.rest_1_.first, ...), custom_call_target="tpu_custom_call" | custom-call | flops 69000003584 | bytes 1 | tf_op jit(solution)/shard_map/near/pallas_call | solution.py:354
  123.6 3.1 %far.2.rest_0_ = bf16[192,8192]{1,0:T(8,128)(2,1)} custom-call(s32[3]{0:T(128)S(1)} %pad_add_fusion.pos, bf16[192,8192]{1,0:T(8,128)(2,1)} %bitcast.18, bf16[2,192,2048]{2,1,0:T(8,128)(2,1)S(1)} %copy-done.19, bf16[2,192,2048]{2,1,0:T(8,128)(2,1)} %collective-permute-done.8.recv, ...), custom_call_target="tpu_custom_call", output_to_operand_aliasing={{}: (6, {})} | custom-call | flops 69000003584 | bytes 1 | tf_op jit(solution)/shard_map/far/pallas_call | solution.py:354
  126.8 3.1 %far.3 = bf16[192,8192]{1,0:T(8,128)(2,1)} custom-call(s32[3]{0:T(128)S(1)} %pad_add_fusion.pos, bf16[192,8192]{1,0:T(8,128)(2,1)} %bitcast.19, bf16[2,192,2048]{2,1,0:T(8,128)(2,1)S(1)} %copy-done.19, bf16[2,192,2048]{2,1,0:T(8,128)(2,1)} %collective-permute-done.8.recv, ...), custom_call_target="tpu_custom_call", output_to_operand_aliasing={{}: (6, {})} | custom-call | flops 69000003584 | bytes 1 | tf_op jit(solution)/shard_map/far/pallas_call | solution.py:354
  (78 shorter events, 18.1 us)
Async XLA Ops:
  5.1 6.6 %copy-start = (bf16[1,768,2048]{2,1,0:T(8,128)(2,1)S(1)}, bf16[1,768,2048]{2,1,0:T(8,128)(2,1)}, u32[]{:S(2)}) copy-start(bf16[1,768,2048]{2,1,0:T(8,128)(2,1)} %param.8) | copy-start | bytes 9437188
  5.1 53.1 %all-to-all-start = ((bf16[4,96,2048]{2,1,0:T(8,128)(2,1)}), bf16[4,96,2048]{2,1,0:T(8,128)(2,1)}, u32[]{:S(2)}, u32[]{:S(2)}) async-start(bf16[4,96,2048]{2,1,0:T(8,128)(2,1)} %copy-done.5), calls=%async_computation | async-start | bytes 3145728 | tf_op jit(solution)/shard_map/all_to_all | solution.py:403
  18.4 7.3 %collective-permute-start = (bf16[192,2048]{1,0:T(8,128)(2,1)S(1)}, bf16[192,2048]{1,0:T(8,128)(2,1)S(1)}, u32[]{:S(2)}, u32[]{:S(2)}) collective-permute-start(bf16[192,2048]{1,0:T(8,128)(2,1)S(1)} %get-tuple-element.41), channel_id=1, source_target_pairs={{0,4},{4,0},{8,12},{12,8},{1,5},{5,1},{9,13},{13,9},{2,6},{6,2},{1... | collective-permute-start | bytes 2359304 | tf_op jit(solution)/shard_map/ppermute | solution.py:390
  25.1 11.3 %collective-permute-start.1 = (bf16[192,2048]{1,0:T(8,128)(2,1)S(1)}, bf16[192,2048]{1,0:T(8,128)(2,1)S(1)}, u32[]{:S(2)}, u32[]{:S(2)}) collective-permute-start(bf16[192,2048]{1,0:T(8,128)(2,1)S(1)} %get-tuple-element.44), channel_id=1, source_target_pairs={{0,4},{4,0},{8,12},{12,8},{1,5},{5,1},{9,13},{13,9},{2,6},{6,2},{1... | collective-permute-start | bytes 2359304 | tf_op jit(solution)/shard_map/ppermute | solution.py:390
  26.9 35.6 %collective-permute-start.2 = (bf16[192,2048]{1,0:T(8,128)(2,1)}, bf16[192,2048]{1,0:T(8,128)(2,1)}, u32[]{:S(2)}, u32[]{:S(2)}) collective-permute-start(bf16[192,2048]{1,0:T(8,128)(2,1)} %add.12.rest_0_), channel_id=1, source_target_pairs={{0,8},{8,0},{4,12},{12,4},{1,9},{9,1},{5,13},{13,5},{2,10},{10,2},... | collective-permute-start | bytes 2359304 | tf_op jit(solution)/shard_map/ppermute | solution.py:393
  30.6 7.6 %copy-start.8 = (bf16[4,96,1024]{2,1,0:T(8,128)(2,1)}, bf16[4,96,1024]{2,1,0:T(8,128)(2,1)S(1)}, u32[]{:S(2)}) copy-start(bf16[4,96,1024]{2,1,0:T(8,128)(2,1)S(1)} %get-tuple-element.50) | copy-start | bytes 2359300
  30.6 41.6 %collective-permute-start.4 = (bf16[96,1024]{1,0:T(8,128)(2,1)}, bf16[96,1024]{1,0:T(8,128)(2,1)S(1)}, u32[]{:S(2)}, u32[]{:S(2)}) collective-permute-start(bf16[96,1024]{1,0:T(8,128)(2,1)} %get-tuple-element.52), channel_id=1, source_target_pairs={{0,1},{1,2},{2,3},{3,0},{4,5},{5,6},{6,7},{7,4},{8,9},{9,10},{10,1... | collective-permute-start | bytes 589832 | tf_op jit(solution)/shard_map/ppermute | solution.py:399
  32.6 40.3 %collective-permute-start.5 = (bf16[96,1024]{1,0:T(8,128)(2,1)}, bf16[96,1024]{1,0:T(8,128)(2,1)}, u32[]{:S(2)}, u32[]{:S(2)}) collective-permute-start(bf16[96,1024]{1,0:T(8,128)(2,1)} %get-tuple-element.53), channel_id=1, source_target_pairs={{0,2},{1,3},{2,0},{3,1},{4,6},{5,7},{6,4},{7,5},{8,10},{9,11},{10,... | collective-permute-start | bytes 589832 | tf_op jit(solution)/shard_map/ppermute | solution.py:399
  35.0 37.9 %collective-permute-start.6 = (bf16[96,1024]{1,0:T(8,128)(2,1)}, bf16[96,1024]{1,0:T(8,128)(2,1)}, u32[]{:S(2)}, u32[]{:S(2)}) collective-permute-start(bf16[96,1024]{1,0:T(8,128)(2,1)} %get-tuple-element.54), channel_id=1, source_target_pairs={{0,3},{1,0},{2,1},{3,2},{4,7},{5,4},{6,5},{7,6},{8,11},{9,8},{10,9... | collective-permute-start | bytes 589832 | tf_op jit(solution)/shard_map/ppermute | solution.py:399
  37.7 35.2 %collective-permute-start.7 = (bf16[192,2048]{1,0:T(8,128)(2,1)}, bf16[192,2048]{1,0:T(8,128)(2,1)}, u32[]{:S(2)}, u32[]{:S(2)}) collective-permute-start(bf16[192,2048]{1,0:T(8,128)(2,1)} %add.13.rest_1_), channel_id=1, source_target_pairs={{0,8},{8,0},{4,12},{12,4},{1,9},{9,1},{5,13},{13,5},{2,10},{10,2},... | collective-permute-start | bytes 2359304 | tf_op jit(solution)/shard_map/ppermute | solution.py:393
  38.2 24.4 %copy-start.1 = (bf16[1,768,2048]{2,1,0:T(8,128)(2,1)S(1)}, bf16[1,768,2048]{2,1,0:T(8,128)(2,1)}, u32[]{:S(2)}) copy-start(bf16[1,768,2048]{2,1,0:T(8,128)(2,1)} %param.8) | copy-start | bytes 9437188
  52.8 9.8 %copy-start.13 = (s32[1,768]{1,0:T(1,128)S(1)}, s32[1,768]{1,0:T(1,128)}, u32[]{:S(2)}) copy-start(s32[1,768]{1,0:T(1,128)} %wanted.5) | copy-start | bytes 9220
  58.3 35.7 %all-to-all-start.1 = ((bf16[4,96,1024]{2,1,0:T(8,128)(2,1)}), bf16[4,96,1024]{2,1,0:T(8,128)(2,1)}, u32[]{:S(2)}, u32[]{:S(2)}) async-start(bf16[4,96,1024]{2,1,0:T(8,128)(2,1)} %copy-done.8), calls=%async_computation.1 | async-start | bytes 1572864 | tf_op jit(solution)/shard_map/all_to_all | solution.py:416
  62.5 10.4 %collective-permute-start.3 = (bf16[384,2048]{1,0:T(8,128)(2,1)}, bf16[384,2048]{1,0:T(8,128)(2,1)S(1)}, u32[]{:S(2)}, u32[]{:S(2)}) collective-permute-start(bf16[384,2048]{1,0:T(8,128)(2,1)} %copy-done.20), channel_id=1, source_target_pairs={{0,4},{4,0},{8,12},{12,8},{1,5},{5,1},{9,13},{13,9},{2,6},{6,2},{1... | collective-permute-start | bytes 4718600 | tf_op jit(solution)/shard_map/ppermute | solution.py:390
  63.3 10.8 %copy-start.3 = (bf16[384,2048]{1,0:T(8,128)(2,1)S(1)}, bf16[384,2048]{1,0:T(8,128)(2,1)}, u32[]{:S(2)}) copy-start(bf16[384,2048]{1,0:T(8,128)(2,1)} %copy-done.2) | copy-start | bytes 4718596
  78.8 35.6 %collective-permute-start.11 = (bf16[192,1024]{1,0:T(8,128)(2,1)}, bf16[192,1024]{1,0:T(8,128)(2,1)}, u32[]{:S(2)}, u32[]{:S(2)}) collective-permute-start(bf16[192,1024]{1,0:T(8,128)(2,1)} %get-tuple-element.63), channel_id=1, source_target_pairs={{0,8},{8,0},{4,12},{12,4},{1,9},{9,1},{5,13},{13,5},{2,10},{10,2},... | collective-permute-start | bytes 1179656 | tf_op jit(solution)/shard_map/ppermute | solution.py:393
  80.4 34.2 %collective-permute-start.12 = (bf16[192,1024]{1,0:T(8,128)(2,1)}, bf16[192,1024]{1,0:T(8,128)(2,1)}, u32[]{:S(2)}, u32[]{:S(2)}) collective-permute-start(bf16[192,1024]{1,0:T(8,128)(2,1)} %get-tuple-element.64), channel_id=1, source_target_pairs={{0,12},{12,0},{4,8},{8,4},{1,13},{13,1},{5,9},{9,5},{2,14},{14,2},... | collective-permute-start | bytes 1179656 | tf_op jit(solution)/shard_map/ppermute | solution.py:396
  80.5 13.4 %copy-start.4 = (bf16[384,2048]{1,0:T(8,128)(2,1)S(1)}, bf16[384,2048]{1,0:T(8,128)(2,1)}, u32[]{:S(2)}) copy-start(bf16[384,2048]{1,0:T(8,128)(2,1)} %copy-done.2) | copy-start | bytes 4718596
  98.2 28.6 %collective-permute-start.9 = (bf16[192,1024]{1,0:T(8,128)(2,1)}, bf16[192,1024]{1,0:T(8,128)(2,1)}, u32[]{:S(2)}, u32[]{:S(2)}) collective-permute-start(bf16[192,1024]{1,0:T(8,128)(2,1)} %get-tuple-element.61), channel_id=1, source_target_pairs={{0,8},{8,0},{4,12},{12,4},{1,9},{9,1},{5,13},{13,5},{2,10},{10,2},... | collective-permute-start | bytes 1179656 | tf_op jit(solution)/shard_map/ppermute | solution.py:393
  99.7 27.1 %collective-permute-start.10 = (bf16[192,1024]{1,0:T(8,128)(2,1)}, bf16[192,1024]{1,0:T(8,128)(2,1)}, u32[]{:S(2)}, u32[]{:S(2)}) collective-permute-start(bf16[192,1024]{1,0:T(8,128)(2,1)} %get-tuple-element.62), channel_id=1, source_target_pairs={{0,12},{12,0},{4,8},{8,4},{1,13},{13,1},{5,9},{9,5},{2,14},{14,2},... | collective-permute-start | bytes 1179656 | tf_op jit(solution)/shard_map/ppermute | solution.py:396
  100.0 14.9 %collective-permute-start.14 = (bf16[192,2048]{1,0:T(8,128)(2,1)}, bf16[192,2048]{1,0:T(8,128)(2,1)S(1)}, u32[]{:S(2)}, u32[]{:S(2)}) collective-permute-start(bf16[192,2048]{1,0:T(8,128)(2,1)} %get-tuple-element.70), channel_id=1, source_target_pairs={{0,4},{4,0},{8,12},{12,8},{1,5},{5,1},{9,13},{13,9},{2,6},{6,2},{1... | collective-permute-start | bytes 2359304 | tf_op jit(solution)/shard_map/ppermute | solution.py:390
  114.4 3.8 %collective-permute-start.13 = (bf16[2,192,2048]{2,1,0:T(8,128)(2,1)}, bf16[2,192,2048]{2,1,0:T(8,128)(2,1)}, u32[]{:S(2)}, u32[]{:S(2)}) collective-permute-start(bf16[2,192,2048]{2,1,0:T(8,128)(2,1)} %get-tuple-element.69), channel_id=1, source_target_pairs={{0,4},{4,0},{8,12},{12,8},{1,5},{5,1},{9,13},{13,9},{2,6},{6,2},{1... | collective-permute-start | bytes 4718600 | tf_op jit(solution)/shard_map/ppermute | solution.py:390
  114.6 9.1 %collective-permute-start.8 = (bf16[2,192,2048]{2,1,0:T(8,128)(2,1)}, bf16[2,192,2048]{2,1,0:T(8,128)(2,1)}, u32[]{:S(2)}, u32[]{:S(2)}) collective-permute-start(bf16[2,192,2048]{2,1,0:T(8,128)(2,1)} %get-tuple-element.60), channel_id=1, source_target_pairs={{0,4},{4,0},{8,12},{12,8},{1,5},{5,1},{9,13},{13,9},{2,6},{6,2},{1... | collective-permute-start | bytes 4718600 | tf_op jit(solution)/shard_map/ppermute | solution.py:390
  118.2 5.5 %copy-start.19 = (bf16[2,192,2048]{2,1,0:T(8,128)(2,1)S(1)}, bf16[2,192,2048]{2,1,0:T(8,128)(2,1)}, u32[]{:S(2)}) copy-start(bf16[2,192,2048]{2,1,0:T(8,128)(2,1)} %copy-done.18) | copy-start | bytes 4718596
  (18 other events, 26.0 us)

commit v5 on v3

--- a/solution.py
+++ b/solution.py
@@ -28,17 +28,24 @@
     return jax.ShapeDtypeStruct(shape, dtype)
 
 
-TOKEN = sds((8, 128), F32)
-
-
-def select_kernel(cuts, by_target, n_rep, cap, pool_dev, rank, slot, lists, pos, pool, *rest):
-    n_outs = len(cuts) if by_target else n_rep * len(cuts)
-    outs, (token, idx) = rest[-2 - n_outs : -2], rest[-2:]
+def in_hbm(shape, dtype=BF16):
+    return pltpu.HBM(shape, dtype)
+
+
+def pin(*arrays):
+    return [pltpu.with_memory_space_constraint(x, pltpu.HBM) for x in arrays]
+
+
+TOKEN = in_hbm((8, 128), F32)
+
+
+def select_kernel(by_shift, by_target, n_rep, cap, pool_dev, rank, slot, lists, pos, pool, *rest):
+    token, idx = rest[-2:]
+    outs = rest[-2 - n_rep * len(by_shift) - len(by_target) : -2]
     token[...] = jnp.zeros_like(token)
     me = pos[2]
-    listed = lists.shape[1]
     for shift in range(n_rep):
-        target = shift if by_target else lax.rem(me + shift, n_rep)
+        target = lax.rem(me + shift, n_rep)
         for k in range(cap):
             idx[k] = 0
 
@@ -52,32 +59,30 @@
 
             return count + mine.astype(jnp.int32)
 
-        lax.fori_loop(0, listed, body, jnp.int32(0), unroll=True)
+        lax.fori_loop(0, lists.shape[1], body, jnp.int32(0), unroll=True)
         for k in range(cap):
             entry = idx[k]
-            for c, (start, stop) in enumerate(cuts):
-                if by_target:
-                    outs[c][shift, pl.ds(k * rank, rank), :] = pool[entry, :, start:stop]
-                else:
-                    outs[shift * len(cuts) + c][pl.ds(k * rank, rank), :] = pool[entry, :, start:stop]
-
-
-def select(slot, lists, pos, pool, cuts, by_target, n_rep, cap, after=()):
+            rows = pl.ds(k * rank, rank)
+            for c, (start, stop) in enumerate(by_shift):
+                outs[c * n_rep + shift][rows, :] = pool[entry, :, start:stop]
+            for c, (start, stop) in enumerate(by_target):
+                outs[len(by_shift) * n_rep + c][target, rows, :] = pool[entry, :, start:stop]
+
+
+def select(slot, lists, pos, pool, by_shift, by_target, n_rep, cap, after=()):
     pool_dev, rank, width = pool.shape
-    if by_target:
-        shapes = [sds((n_rep, cap * rank, stop - start)) for start, stop in cuts]
-    else:
-        shapes = [sds((cap * rank, stop - start)) for _ in range(n_rep) for start, stop in cuts]
-    return pl.pallas_call(
-        functools.partial(select_kernel, cuts, by_target, n_rep, cap, pool_dev, rank),
+    shapes = [in_hbm((cap * rank, stop - start)) for start, stop in by_shift for _ in range(n_rep)]
+    shapes += [in_hbm((n_rep, cap * rank, stop - start)) for start, stop in by_target]
+    return pl.pallas_call(
+        functools.partial(select_kernel, by_shift, by_target, n_rep, cap, pool_dev, rank),
         out_shape=[*shapes, TOKEN],
         in_specs=[SMEM, SMEM, SMEM, VMEM] + [ANY] * len(after),
         out_specs=[VMEM] * len(shapes) + [VMEM],
         scratch_shapes=[pltpu.SMEM((cap,), jnp.int32)],
-        compiler_params=params(),
+        compiler_params=params(16),
         cost_estimate=order(0),
         name="select",
-    )(slot, lists, pos, pool, *after)
+    )(*pin(slot, lists, pos, pool), *pin(*after))
 
 
 def product_columns_kernel(per, pos, features, weights, late, late_send, keep, send, token):
@@ -122,7 +127,7 @@
 
     return pl.pallas_call(
         kernel,
-        out_shape=[sds((half, width))] * 2 + [sds((2, half // 2, width))] * 2 + [TOKEN],
+        out_shape=[in_hbm((half, width))] * 2 + [in_hbm((2, half // 2, width))] * 2 + [TOKEN],
         grid_spec=pltpu.PrefetchScalarGridSpec(
             num_scalar_prefetch=1,
             grid=(2 * per,),
@@ -142,7 +147,7 @@
         compiler_params=params(),
         cost_estimate=order(0),
         name="product",
-    )(pos, features, projection, *after)
+    )(*pin(pos), features, projection, *pin(*after))
 
 
 def product_kernel(split, pos, features, weights, keep, send, token):
@@ -194,7 +199,7 @@
 
     return pl.pallas_call(
         kernel,
-        out_shape=[sds(shape), sds(shape), TOKEN],
+        out_shape=[in_hbm(shape) if blocks > 1 else sds(shape)] * 2 + [TOKEN],
         grid_spec=pltpu.PrefetchScalarGridSpec(
             num_scalar_prefetch=1,
             grid=(tiles,),
@@ -205,7 +210,7 @@
         compiler_params=params(),
         cost_estimate=order(0),
         name="product",
-    )(pos, features, projection, *after)
+    )(*pin(pos), features, projection, *pin(*after))
 
 
 def walk_list(slot, lists, me, n_rep, cap, pool_dev, counts, by_owner, visit):
@@ -249,7 +254,7 @@
         compiler_params=params(),
         cost_estimate=order(40),
         name="score",
-    )(slot, lists, pos, wanted, features, factors, *after)
+    )(*pin(slot, lists, pos, wanted), features, *pin(factors), *pin(*after))
 
 
 def delta_kernel(
@@ -291,11 +296,15 @@
     rows = wanted.shape[1]
     start, stop = cut
     width = stop - start
-    late_own, late_recv = late
     return pl.pallas_call(
         functools.partial(delta_kernel, len(blocks), n_rep, cap, pool_dev, rank, len(before)),
-        out_shape=[sds((own, width))] * 2 + [sds((own, stop))] * 2,
-        in_specs=[SMEM] * 3 + [VMEM] * (4 + len(blocks) + len(before)) + [ANY] * len(after),
+        out_shape=[in_hbm((own, width))] * 2 + [in_hbm((own, stop))] * 2,
+        grid=(1,),
+        in_specs=[SMEM] * 3
+        + [VMEM] * 2
+        + [pl.BlockSpec((2 * own, width), lambda i: (0, start // width))] * 2
+        + [VMEM] * (len(blocks) + len(before))
+        + [ANY] * len(after),
         out_specs=[VMEM] * 4,
         scratch_shapes=[
             pltpu.VMEM((n_rep * cap * rank, rows), BF16),
@@ -307,9 +316,7 @@
         compiler_params=params(),
         cost_estimate=order(0),
         name="delta",
-    )(
-        slot, lists, pos, wanted, shrunk, late_own[:, start:stop], late_recv[:, start:stop], *blocks, *before, *after
-    )
+    )(*pin(slot, lists, pos, wanted), shrunk, *pin(late[0]), late[1], *pin(blocks[0]), *blocks[1:], *pin(*before), *pin(*after))
 
 
 def gate_kernel(*refs):
@@ -326,7 +333,7 @@
         input_output_aliases={i: i for i in range(n)},
         cost_estimate=order(100),
         name="gate",
-    )(*arrays, *after)
+    )(*arrays, *pin(*after))
 
 
 def near_kernel(pos, residual, keep, recv, first, second, mine, theirs, *rest):
@@ -358,7 +365,7 @@
     whole = pl.BlockSpec((own, tile), place)
     part = pl.BlockSpec((1, own, tile), lambda b, j, pos: (b, 0, start // tile + j))
     piece = pl.BlockSpec((own, tile), lambda b, j, pos: (0, j))
-    operands = [pos, residual, *base, *pieces, *after]
+    operands = [*pin(pos, residual, *base), *pieces, *pin(*after)]
     specs = [piece] * len(pieces) + [ANY] * len(after)
     aliases = {}
     if out is not None:
@@ -413,7 +420,7 @@
         return lax.ppermute(x, "rep", [(i, (i + shift) % n_rep) for i in range(n_rep)])
 
     shifts = [s for s in range(1, n_rep) if s != n_rep // 2] + [n_rep // 2]
-    chosen, token = select(*lists, shrink_pool, ((0, width),), True, n_rep, cap)
+    chosen, token = select(*lists, shrink_pool, (), ((0, width),), n_rep, cap)
     shrink = lax.all_to_all(chosen, "rep", 0, 0, tiled=True).reshape(n_rep * cap * rank, width)
 
     early = []
@@ -423,12 +430,11 @@
         sums.append(keep + over_core(send))
         early.append(over_chip(sums[-1]))
 
-    *chosen, token = select(*lists, expand_pool, cuts[:1], False, n_rep, cap, [token])
+    *chosen, second, token = select(*lists, expand_pool, cuts[:1], cuts[1:], n_rep, cap, [token])
     first = [chosen[0]] + [None] * (n_rep - 1)
     for s in shifts:
         first[s] = over_rep(chosen[s], s)
-    chosen, token = select(*lists, expand_pool, cuts[1:], True, n_rep, cap, [token])
-    second = lax.all_to_all(chosen, "rep", 0, 0, tiled=True).reshape(n_rep * cap * rank, cut)
+    second = lax.all_to_all(second, "rep", 0, 0, tiled=True).reshape(n_rep * cap * rank, cut)
 
     late_keep, late_send, keep, send, token = product_columns(pos, features, projection, tile, [*sums, token])
     late = (late_keep, over_core(late_send))

time: 124 us -> 119 us (0.960)
  local copies, waits for them, and re-layouts: 11.7 us -> 1.42 us
  Pallas kernels: 72.1 us -> 77 us
    unnamed x46 -> x8, local copies, waits for them, and re-layouts: 10.3 us -> 1.42 us
    all_to_all x2 -> x1, starting transfers between devices: 10.9 us -> 6.58 us  [paired(): lax.all_to_all(chosen, 'rep', 0, 0, tiled=True)]
    all_to_all x0 -> x1, starting transfers between devices: none -> 4.19 us  [paired(): lax.all_to_all(second, 'rep', 0, 0, tiled=True)]
    pallas_call x7 -> x6, Pallas kernels: 49.8 us -> 52 us  [the longest x3 26.7 us: product(): pl.pallas_call(kernel, out_shape=[in_hbm(shape) if blocks > 1 else sds(sh...]
    pallas_call x2, Pallas kernels: 7.6 us -> 9.19 us  [delta(): pl.pallas_call(functools.partial(delta_kernel, len(blocks), n_rep, cap, p...]
    slice x2 -> x0, local copies, waits for them, and re-layouts: 1.42 us -> none  [the longest x1 1.3 us: delta(): late_own[:, start:stop]]
  transfers between devices with their start and end apart: 17 -> 17, of which waited for: 2 -> 2; matrix products, arithmetic and copies ran while one was open for 3% -> 2% of each run, Pallas kernels for 55% -> 60%
where the time goes in v5:
time: 119 us; the launch traced here: 118 us
  Pallas kernels  77 us (65%)
  starting transfers between devices  23.6 us (20%)
  waiting for transfers between devices  7.28 us (6%)
  blocking collectives  5.84 us (5%)
  other arithmetic  2.95 us (2%)
  local copies, waits for them, and re-layouts  1.42 us (1%)
    pallas_call x3, Pallas kernels, product(): pl.pallas_call(kernel, out_shape=[in_hbm(shape) if blocks > 1 else sds(sh...  26.7 us
    pallas_call x1, Pallas kernels, product_columns(): pl.pallas_call(kernel, out_shape=[in_hbm((half, width))] * 2 + [in_hbm((2...  19 us
    pallas_call x3, Pallas kernels, finish(): pl.pallas_call(near_kernel if near else far_kernel, out_shape=sds((own, f...  12.9 us
    pallas_call x2, Pallas kernels, delta(): pl.pallas_call(functools.partial(delta_kernel, len(blocks), n_rep, cap, p...  9.19 us
    all_to_all x1, starting transfers between devices, paired(): lax.all_to_all(chosen, 'rep', 0, 0, tiled=True)  6.58 us
    pallas_call x2, Pallas kernels, select(): pl.pallas_call(functools.partial(select_kernel, by_shift, by_target, n_re...  6.27 us
    ppermute x3, starting transfers between devices, over_rep(): lax.ppermute(x, 'rep', [(i, (i + shift) % n_rep) for i in range(n_rep)])  5.85 us
    all_gather x1, blocking collectives, paired(): shrunk = lax.all_gather(part, 'tp')  5.84 us
  transfers between devices with their start and end apart: 17, of which 2 were waited for; matrix products, arithmetic and copies ran while one was open for 2% of the time, Pallas kernels for 60%

profile of v5, /device:TPU:0, one launch (start us, length us, event | category | flops | bytes accessed | tf_op | source)
XLA Modules:
  0.0 118.2 jit_solution(404164502950153191)
XLA Ops:
  0.6 3.1 %select.8 = (bf16[4,96,2048]{2,1,0:T(8,128)(2,1)}, f32[8,128]{1,0:T(8,128)}) custom-call(s32[64]{0:T(128)} %slot.9, s32[4,24]{1,0:T(4,128)} %lists.9, s32[3]{0:T(128)} %pad_add_fusion.pos, bf16[16,16,2048]{2,1,0:T(8,128)(2,1)} %pool.2), custom_call_target="tpu_custom_call" | custom-call | flops 1 | bytes 1 | tf_op jit(solution)/shard_map/select/pallas_call | solution.py:76
  3.7 6.6 %all-to-all-start = ((bf16[4,96,2048]{2,1,0:T(8,128)(2,1)}), bf16[4,96,2048]{2,1,0:T(8,128)(2,1)}, u32[]{:S(2)}, u32[]{:S(2)}) async-start(bf16[4,96,2048]{2,1,0:T(8,128)(2,1)} %get-tuple-element.37), calls=%async_computation | async-start | bytes 3145728 | tf_op jit(solution)/shard_map/all_to_all | solution.py:424
  10.3 7.3 %product.4 = (bf16[192,2048]{1,0:T(8,128)(2,1)S(1)}, bf16[192,2048]{1,0:T(8,128)(2,1)S(1)}, f32[8,128]{1,0:T(8,128)}) custom-call(s32[3]{0:T(128)} %pad_add_fusion.pos, bf16[768,2048]{1,0:T(8,128)(2,1)S(1)} %bitcast.9, bf16[2048,8192]{1,0:T(8,128)(2,1)} %weights.7, f32[8,128]{1,0:T(8,128)} %get-tuple-element.38.rest_0_), custom_call_target="tpu_custom_call" | custom-call | flops 1 | bytes 1 | tf_op jit(solution)/shard_map/product/pallas_call | solution.py:200
  17.6 7.3 %product.5 = (bf16[192,2048]{1,0:T(8,128)(2,1)S(1)}, bf16[192,2048]{1,0:T(8,128)(2,1)S(1)}, f32[8,128]{1,0:T(8,128)}) custom-call(s32[3]{0:T(128)} %pad_add_fusion.pos, bf16[768,2048]{1,0:T(8,128)(2,1)S(1)} %bitcast.10, bf16[2048,8192]{1,0:T(8,128)(2,1)} %weights.7, f32[8,128]{1,0:T(8,128)} %get-tuple-element.41.rest_0_), custom_call_target="tpu_custom_call" | custom-call | flops 1 | bytes 1 | tf_op jit(solution)/shard_map/product/pallas_call | solution.py:200
  26.6 1.5 %collective-permute-start.2 = (bf16[192,2048]{1,0:T(8,128)(2,1)}, bf16[192,2048]{1,0:T(8,128)(2,1)}, u32[]{:S(2)}, u32[]{:S(2)}) collective-permute-start(bf16[192,2048]{1,0:T(8,128)(2,1)} %add.12.rest_0_), channel_id=1, source_target_pairs={{0,8},{8,0},{4,12},{12,4},{1,9},{9,1},{5,13},{13,5},{2,10},{10,2},... | collective-permute-start | bytes 2359304 | tf_op jit(solution)/shard_map/ppermute | solution.py:414
  28.1 3.1 %select.9 = (bf16[96,1024]{1,0:T(8,128)(2,1)}, bf16[96,1024]{1,0:T(8,128)(2,1)}, bf16[96,1024]{1,0:T(8,128)(2,1)}, bf16[96,1024]{1,0:T(8,128)(2,1)}, bf16[4,96,1024]{2,1,0:T(8,128)(2,1)}, /*index=5*/f32[8,128]{1,0:T(8,128)}) custom-call(s32[64]{0:T(128)} %slot.9, s32[4,24]{1,0:T(4,128)} %lists.9, s32[3]{0:T(128)} %pad_add_fusion.pos, ...), custom_call_target="tpu_custom_call" | custom-call | flops 1 | bytes 1 | tf_op jit(solution)/shard_map/select/pallas_call | solution.py:76
  31.3 2.0 %collective-permute-start.4 = (bf16[96,1024]{1,0:T(8,128)(2,1)}, bf16[96,1024]{1,0:T(8,128)(2,1)S(1)}, u32[]{:S(2)}, u32[]{:S(2)}) collective-permute-start(bf16[96,1024]{1,0:T(8,128)(2,1)} %get-tuple-element.50), channel_id=1, source_target_pairs={{0,1},{1,2},{2,3},{3,0},{4,5},{5,6},{6,7},{7,4},{8,9},{9,10},{10,1... | collective-permute-start | bytes 589832 | tf_op jit(solution)/shard_map/ppermute | solution.py:420
  33.3 2.4 %collective-permute-start.5 = (bf16[96,1024]{1,0:T(8,128)(2,1)}, bf16[96,1024]{1,0:T(8,128)(2,1)}, u32[]{:S(2)}, u32[]{:S(2)}) collective-permute-start(bf16[96,1024]{1,0:T(8,128)(2,1)} %get-tuple-element.51), channel_id=1, source_target_pairs={{0,2},{1,3},{2,0},{3,1},{4,6},{5,7},{6,4},{7,5},{8,10},{9,11},{10,... | collective-permute-start | bytes 589832 | tf_op jit(solution)/shard_map/ppermute | solution.py:420
  35.6 1.5 %collective-permute-start.6 = (bf16[96,1024]{1,0:T(8,128)(2,1)}, bf16[96,1024]{1,0:T(8,128)(2,1)}, u32[]{:S(2)}, u32[]{:S(2)}) collective-permute-start(bf16[96,1024]{1,0:T(8,128)(2,1)} %get-tuple-element.52), channel_id=1, source_target_pairs={{0,3},{1,0},{2,1},{3,2},{4,7},{5,4},{6,5},{7,6},{8,11},{9,8},{10,9... | collective-permute-start | bytes 589832 | tf_op jit(solution)/shard_map/ppermute | solution.py:420
  38.8 19.0 %product.6 = (bf16[384,2048]{1,0:T(8,128)(2,1)}, bf16[384,2048]{1,0:T(8,128)(2,1)}, bf16[2,192,2048]{2,1,0:T(8,128)(2,1)}, bf16[2,192,2048]{2,1,0:T(8,128)(2,1)}, f32[8,128]{1,0:T(8,128)}) custom-call(s32[3]{0:T(128)} %pad_add_fusion.pos, bf16[768,2048]{1,0:T(8,128)(2,1)S(1)} %bitcast.11, bf16[2048,8192]{1,0:T(8,128)(2,1)} %weights.7, ...), custom_call_target="tpu_custom_call" | custom-call | flops 1 | bytes 1 | tf_op jit(solution)/shard_map/product/pallas_call | solution.py:128
  57.8 4.2 %all-to-all-start.1 = ((bf16[4,96,1024]{2,1,0:T(8,128)(2,1)}), bf16[4,96,1024]{2,1,0:T(8,128)(2,1)}, u32[]{:S(2)}, u32[]{:S(2)}) async-start(bf16[4,96,1024]{2,1,0:T(8,128)(2,1)} %get-tuple-element.56), calls=%async_computation.1 | async-start | bytes 1572864 | tf_op jit(solution)/shard_map/all_to_all | solution.py:437
  62.1 3.0 %score.1 = f32[16,768]{1,0:T(8,128)S(1)} custom-call(s32[64]{0:T(128)} %slot.9, s32[4,24]{1,0:T(4,128)} %lists.9, s32[3]{0:T(128)} %pad_add_fusion.pos, s32[1,768]{1,0:T(1,128)} %wanted.5, bf16[768,2048]{1,0:T(8,128)(2,1)S(1)} %bitcast.12, bf16[384,2048]{1,0:T(8,128)(2,1)} %bitcast.5.factors, f32[8,128]{1,0:T(8,128)} %get-tuple-element.46.rest_0_, ...), custom_call_target="tpu_custom_call" | custom-call | flops 46000001024 | bytes 1 | tf_op jit(solution)/shard_map/score/pallas_call | solution.py:245
  65.1 5.8 %all-gather = f32[64,768]{1,0:T(8,128)S(1)} all-gather(f32[16,768]{1,0:T(8,128)S(1)} %score.1), channel_id=2, replica_groups=mesh['groups'=2,'tp'=4,'rep'=4] {'tp'}, dimensions={0}, use_global_device_ids=true | all-gather | bytes 245760 | tf_op jit(solution)/shard_map/all_gather | solution.py:444
  71.0 4.6 %delta.2 = (bf16[192,1024]{1,0:T(8,128)(2,1)}, bf16[192,1024]{1,0:T(8,128)(2,1)}, bf16[192,1024]{1,0:T(8,128)(2,1)}, bf16[192,1024]{1,0:T(8,128)(2,1)}) custom-call(s32[64]{0:T(128)} %slot.9, s32[4,24]{1,0:T(4,128)} %lists.9, s32[3]{0:T(128)} %pad_add_fusion.pos, s32[1,768]{1,0:T(1,128)} %wanted.5, f32[4,16,768]{2,1,0:T(8,128)S(1)} %bitcast.14, ...), custom_call_target="tpu_custom_call" | custom-call | flops 1 | bytes 1 | tf_op jit(solution)/shard_map/delta/pallas_call | solution.py:299
  75.6 1.5 %collective-permute-start.11 = (bf16[192,1024]{1,0:T(8,128)(2,1)}, bf16[192,1024]{1,0:T(8,128)(2,1)}, u32[]{:S(2)}, u32[]{:S(2)}) collective-permute-start(bf16[192,1024]{1,0:T(8,128)(2,1)} %get-tuple-element.61), channel_id=1, source_target_pairs={{0,8},{8,0},{4,12},{12,4},{1,9},{9,1},{5,13},{13,5},{2,10},{10,2},... | collective-permute-start | bytes 1179656 | tf_op jit(solution)/shard_map/ppermute | solution.py:414
  77.7 12.1 %product.7 = (bf16[2,192,2048]{2,1,0:T(8,128)(2,1)}, bf16[2,192,2048]{2,1,0:T(8,128)(2,1)}, f32[8,128]{1,0:T(8,128)}) custom-call(s32[3]{0:T(128)} %pad_add_fusion.pos, bf16[768,2048]{1,0:T(8,128)(2,1)S(1)} %bitcast.13, bf16[2048,8192]{1,0:T(8,128)(2,1)} %weights.7, bf16[192,1024]{1,0:T(8,128)(2,1)} %get-tuple-element.53.rest_0_.rest_1_), custom_call_target="tpu_custom_call" | custom-call | flops 1 | bytes 1 | tf_op jit(solution)/shard_map/product/pallas_call | solution.py:200
  89.8 1.4 %copy-done.2 = bf16[384,2048]{1,0:T(8,128)(2,1)S(1)} copy-done((bf16[384,2048]{1,0:T(8,128)(2,1)S(1)}, bf16[384,2048]{1,0:T(8,128)(2,1)}, u32[]{:S(2)}) %copy-start.2) | copy-done | bytes 1572888
  91.2 4.6 %delta.3 = (bf16[192,1024]{1,0:T(8,128)(2,1)}, bf16[192,1024]{1,0:T(8,128)(2,1)}, bf16[192,2048]{1,0:T(8,128)(2,1)}, bf16[192,2048]{1,0:T(8,128)(2,1)}) custom-call(s32[64]{0:T(128)} %slot.9, s32[4,24]{1,0:T(4,128)} %lists.9, s32[3]{0:T(128)} %pad_add_fusion.pos, s32[1,768]{1,0:T(1,128)} %wanted.5, f32[4,16,768]{2,1,0:T(8,128)S(1)} %bitcast.15, ...), custom_call_target="tpu_custom_call" | custom-call | flops 1 | bytes 1 | tf_op jit(solution)/shard_map/delta/pallas_call | solution.py:299
  95.8 1.5 %collective-permute-start.9 = (bf16[192,1024]{1,0:T(8,128)(2,1)}, bf16[192,1024]{1,0:T(8,128)(2,1)}, u32[]{:S(2)}, u32[]{:S(2)}) collective-permute-start(bf16[192,1024]{1,0:T(8,128)(2,1)} %get-tuple-element.59), channel_id=1, source_target_pairs={{0,8},{8,0},{4,12},{12,4},{1,9},{9,1},{5,13},{13,5},{2,10},{10,2},... | collective-permute-start | bytes 1179656 | tf_op jit(solution)/shard_map/ppermute | solution.py:414
  98.0 2.4 %collective-permute-done.14.theirs = bf16[192,2048]{1,0:T(8,128)(2,1)S(1)} collective-permute-done((bf16[192,2048]{1,0:T(8,128)(2,1)}, bf16[192,2048]{1,0:T(8,128)(2,1)S(1)}, u32[]{:S(2)}, u32[]{:S(2)}) %collective-permute-start.14) | collective-permute-done | bytes 786464 | tf_op jit(solution)/shard_map/ppermute | solution.py:411
  100.5 5.9 %near.1.rest_0_ = bf16[192,8192]{1,0:T(8,128)(2,1)} custom-call(s32[3]{0:T(128)} %pad_add_fusion.pos, bf16[192,8192]{1,0:T(8,128)(2,1)} %bitcast.16, bf16[2,192,2048]{2,1,0:T(8,128)(2,1)} %get-tuple-element.66.keep, bf16[2,192,2048]{2,1,0:T(8,128)(2,1)} %collective-permute-done.13.recv, bf16[192,2048]{1,0:T(8,128)(2,1)} %collective-permute-done.2.rest_1_.first, ...), custom_call_target="tpu_custom_call" | custom-call | flops 69000003584 | bytes 1 | tf_op jit(solution)/shard_map/near/pallas_call | solution.py:375
  106.4 3.5 %far.2.rest_0_ = bf16[192,8192]{1,0:T(8,128)(2,1)} custom-call(s32[3]{0:T(128)} %pad_add_fusion.pos, bf16[192,8192]{1,0:T(8,128)(2,1)} %bitcast.17, bf16[2,192,2048]{2,1,0:T(8,128)(2,1)} %get-tuple-element.54.keep, bf16[2,192,2048]{2,1,0:T(8,128)(2,1)} %collective-permute-done.8.recv, ...), custom_call_target="tpu_custom_call", output_to_operand_aliasing={{}: (6, {})} | custom-call | flops 69000003584 | bytes 1 | tf_op jit(solution)/shard_map/far/pallas_call | solution.py:375
  109.9 4.8 %collective-permute-done.10.cross = bf16[192,1024]{1,0:T(8,128)(2,1)} collective-permute-done((bf16[192,1024]{1,0:T(8,128)(2,1)}, bf16[192,1024]{1,0:T(8,128)(2,1)}, u32[]{:S(2)}, u32[]{:S(2)}) %collective-permute-start.10) | collective-permute-done | bytes 393248 | tf_op jit(solution)/shard_map/ppermute | solution.py:417
  114.7 3.5 %far.3 = bf16[192,8192]{1,0:T(8,128)(2,1)} custom-call(s32[3]{0:T(128)} %pad_add_fusion.pos, bf16[192,8192]{1,0:T(8,128)(2,1)} %bitcast.18, bf16[2,192,2048]{2,1,0:T(8,128)(2,1)} %get-tuple-element.54.keep, bf16[2,192,2048]{2,1,0:T(8,128)(2,1)} %collective-permute-done.8.recv, ...), custom_call_target="tpu_custom_call", output_to_operand_aliasing={{}: (6, {})} | custom-call | flops 69000003584 | bytes 1 | tf_op jit(solution)/shard_map/far/pallas_call | solution.py:375
  (35 shorter events, 5.5 us)
Async XLA Ops:
  3.7 6.6 %copy-start = (bf16[1,768,2048]{2,1,0:T(8,128)(2,1)S(1)}, bf16[1,768,2048]{2,1,0:T(8,128)(2,1)}, u32[]{:S(2)}) copy-start(bf16[1,768,2048]{2,1,0:T(8,128)(2,1)} %param.8) | copy-start | bytes 9437188
  3.7 54.1 %all-to-all-start = ((bf16[4,96,2048]{2,1,0:T(8,128)(2,1)}), bf16[4,96,2048]{2,1,0:T(8,128)(2,1)}, u32[]{:S(2)}, u32[]{:S(2)}) async-start(bf16[4,96,2048]{2,1,0:T(8,128)(2,1)} %get-tuple-element.37), calls=%async_computation | async-start | bytes 3145728 | tf_op jit(solution)/shard_map/all_to_all | solution.py:424
  17.6 7.8 %collective-permute-start = (bf16[192,2048]{1,0:T(8,128)(2,1)S(1)}, bf16[192,2048]{1,0:T(8,128)(2,1)S(1)}, u32[]{:S(2)}, u32[]{:S(2)}) collective-permute-start(bf16[192,2048]{1,0:T(8,128)(2,1)S(1)} %get-tuple-element.40), channel_id=1, source_target_pairs={{0,4},{4,0},{8,12},{12,8},{1,5},{5,1},{9,13},{13,9},{2,6},{6,2},{1... | collective-permute-start | bytes 2359304 | tf_op jit(solution)/shard_map/ppermute | solution.py:411
  24.9 12.2 %collective-permute-start.1 = (bf16[192,2048]{1,0:T(8,128)(2,1)S(1)}, bf16[192,2048]{1,0:T(8,128)(2,1)S(1)}, u32[]{:S(2)}, u32[]{:S(2)}) collective-permute-start(bf16[192,2048]{1,0:T(8,128)(2,1)S(1)} %get-tuple-element.43), channel_id=1, source_target_pairs={{0,4},{4,0},{8,12},{12,8},{1,5},{5,1},{9,13},{13,9},{2,6},{6,2},{1... | collective-permute-start | bytes 2359304 | tf_op jit(solution)/shard_map/ppermute | solution.py:411
  26.6 35.4 %collective-permute-start.2 = (bf16[192,2048]{1,0:T(8,128)(2,1)}, bf16[192,2048]{1,0:T(8,128)(2,1)}, u32[]{:S(2)}, u32[]{:S(2)}) collective-permute-start(bf16[192,2048]{1,0:T(8,128)(2,1)} %add.12.rest_0_), channel_id=1, source_target_pairs={{0,8},{8,0},{4,12},{12,4},{1,9},{9,1},{5,13},{13,5},{2,10},{10,2},... | collective-permute-start | bytes 2359304 | tf_op jit(solution)/shard_map/ppermute | solution.py:414
  31.3 39.7 %collective-permute-start.4 = (bf16[96,1024]{1,0:T(8,128)(2,1)}, bf16[96,1024]{1,0:T(8,128)(2,1)S(1)}, u32[]{:S(2)}, u32[]{:S(2)}) collective-permute-start(bf16[96,1024]{1,0:T(8,128)(2,1)} %get-tuple-element.50), channel_id=1, source_target_pairs={{0,1},{1,2},{2,3},{3,0},{4,5},{5,6},{6,7},{7,4},{8,9},{9,10},{10,1... | collective-permute-start | bytes 589832 | tf_op jit(solution)/shard_map/ppermute | solution.py:420
  33.3 37.6 %collective-permute-start.5 = (bf16[96,1024]{1,0:T(8,128)(2,1)}, bf16[96,1024]{1,0:T(8,128)(2,1)}, u32[]{:S(2)}, u32[]{:S(2)}) collective-permute-start(bf16[96,1024]{1,0:T(8,128)(2,1)} %get-tuple-element.51), channel_id=1, source_target_pairs={{0,2},{1,3},{2,0},{3,1},{4,6},{5,7},{6,4},{7,5},{8,10},{9,11},{10,... | collective-permute-start | bytes 589832 | tf_op jit(solution)/shard_map/ppermute | solution.py:420
  35.6 35.3 %collective-permute-start.6 = (bf16[96,1024]{1,0:T(8,128)(2,1)}, bf16[96,1024]{1,0:T(8,128)(2,1)}, u32[]{:S(2)}, u32[]{:S(2)}) collective-permute-start(bf16[96,1024]{1,0:T(8,128)(2,1)} %get-tuple-element.52), channel_id=1, source_target_pairs={{0,3},{1,0},{2,1},{3,2},{4,7},{5,4},{6,5},{7,6},{8,11},{9,8},{10,9... | collective-permute-start | bytes 589832 | tf_op jit(solution)/shard_map/ppermute | solution.py:420
  38.3 32.7 %collective-permute-start.7 = (bf16[192,2048]{1,0:T(8,128)(2,1)}, bf16[192,2048]{1,0:T(8,128)(2,1)}, u32[]{:S(2)}, u32[]{:S(2)}) collective-permute-start(bf16[192,2048]{1,0:T(8,128)(2,1)} %add.13.rest_1_), channel_id=1, source_target_pairs={{0,8},{8,0},{4,12},{12,4},{1,9},{9,1},{5,13},{13,5},{2,10},{10,2},... | collective-permute-start | bytes 2359304 | tf_op jit(solution)/shard_map/ppermute | solution.py:414
  57.8 32.0 %all-to-all-start.1 = ((bf16[4,96,1024]{2,1,0:T(8,128)(2,1)}), bf16[4,96,1024]{2,1,0:T(8,128)(2,1)}, u32[]{:S(2)}, u32[]{:S(2)}) async-start(bf16[4,96,1024]{2,1,0:T(8,128)(2,1)} %get-tuple-element.56), calls=%async_computation.1 | async-start | bytes 1572864 | tf_op jit(solution)/shard_map/all_to_all | solution.py:437
  62.0 8.9 %collective-permute-start.3 = (bf16[384,2048]{1,0:T(8,128)(2,1)}, bf16[384,2048]{1,0:T(8,128)(2,1)S(1)}, u32[]{:S(2)}, u32[]{:S(2)}) collective-permute-start(bf16[384,2048]{1,0:T(8,128)(2,1)} %get-tuple-element.48), channel_id=1, source_target_pairs={{0,4},{4,0},{8,12},{12,8},{1,5},{5,1},{9,13},{13,9},{2,6},{6,2},{1... | collective-permute-start | bytes 4718600 | tf_op jit(solution)/shard_map/ppermute | solution.py:411
  71.0 4.6 %copy-start.1 = (bf16[384,2048]{1,0:T(8,128)(2,1)}, bf16[384,2048]{1,0:T(8,128)(2,1)S(1)}, u32[]{:S(2)}) copy-start(bf16[384,2048]{1,0:T(8,128)(2,1)S(1)} %collective-permute-done.3.late_recv) | copy-start | bytes 4718596
  75.6 21.7 %collective-permute-start.11 = (bf16[192,1024]{1,0:T(8,128)(2,1)}, bf16[192,1024]{1,0:T(8,128)(2,1)}, u32[]{:S(2)}, u32[]{:S(2)}) collective-permute-start(bf16[192,1024]{1,0:T(8,128)(2,1)} %get-tuple-element.61), channel_id=1, source_target_pairs={{0,8},{8,0},{4,12},{12,4},{1,9},{9,1},{5,13},{13,5},{2,10},{10,2},... | collective-permute-start | bytes 1179656 | tf_op jit(solution)/shard_map/ppermute | solution.py:414
  77.1 20.9 %collective-permute-start.12 = (bf16[192,1024]{1,0:T(8,128)(2,1)}, bf16[192,1024]{1,0:T(8,128)(2,1)}, u32[]{:S(2)}, u32[]{:S(2)}) collective-permute-start(bf16[192,1024]{1,0:T(8,128)(2,1)} %get-tuple-element.62), channel_id=1, source_target_pairs={{0,12},{12,0},{4,8},{8,4},{1,13},{13,1},{5,9},{9,5},{2,14},{14,2},... | collective-permute-start | bytes 1179656 | tf_op jit(solution)/shard_map/ppermute | solution.py:417
  77.3 20.8 %collective-permute-start.13 = (bf16[2,192,2048]{2,1,0:T(8,128)(2,1)}, bf16[2,192,2048]{2,1,0:T(8,128)(2,1)}, u32[]{:S(2)}, u32[]{:S(2)}) collective-permute-start(bf16[2,192,2048]{2,1,0:T(8,128)(2,1)} %get-tuple-element.67), channel_id=1, source_target_pairs={{0,4},{4,0},{8,12},{12,8},{1,5},{5,1},{9,13},{13,9},{2,6},{6,2},{1... | collective-permute-start | bytes 4718600 | tf_op jit(solution)/shard_map/ppermute | solution.py:411
  89.8 1.4 %copy-start.2 = (bf16[384,2048]{1,0:T(8,128)(2,1)S(1)}, bf16[384,2048]{1,0:T(8,128)(2,1)}, u32[]{:S(2)}) copy-start(bf16[384,2048]{1,0:T(8,128)(2,1)} %copy-done.1) | copy-start | bytes 4718596
  95.8 14.1 %collective-permute-start.9 = (bf16[192,1024]{1,0:T(8,128)(2,1)}, bf16[192,1024]{1,0:T(8,128)(2,1)}, u32[]{:S(2)}, u32[]{:S(2)}) collective-permute-start(bf16[192,1024]{1,0:T(8,128)(2,1)} %get-tuple-element.59), channel_id=1, source_target_pairs={{0,8},{8,0},{4,12},{12,4},{1,9},{9,1},{5,13},{13,5},{2,10},{10,2},... | collective-permute-start | bytes 1179656 | tf_op jit(solution)/shard_map/ppermute | solution.py:414
  97.3 17.4 %collective-permute-start.10 = (bf16[192,1024]{1,0:T(8,128)(2,1)}, bf16[192,1024]{1,0:T(8,128)(2,1)}, u32[]{:S(2)}, u32[]{:S(2)}) collective-permute-start(bf16[192,1024]{1,0:T(8,128)(2,1)} %get-tuple-element.60), channel_id=1, source_target_pairs={{0,12},{12,0},{4,8},{8,4},{1,13},{13,1},{5,9},{9,5},{2,14},{14,2},... | collective-permute-start | bytes 1179656 | tf_op jit(solution)/shard_map/ppermute | solution.py:417
  97.3 3.2 %collective-permute-start.14 = (bf16[192,2048]{1,0:T(8,128)(2,1)}, bf16[192,2048]{1,0:T(8,128)(2,1)S(1)}, u32[]{:S(2)}, u32[]{:S(2)}) collective-permute-start(bf16[192,2048]{1,0:T(8,128)(2,1)} %get-tuple-element.68), channel_id=1, source_target_pairs={{0,4},{4,0},{8,12},{12,8},{1,5},{5,1},{9,13},{13,9},{2,6},{6,2},{1... | collective-permute-start | bytes 2359304 | tf_op jit(solution)/shard_map/ppermute | solution.py:411
  98.0 8.4 %collective-permute-start.8 = (bf16[2,192,2048]{2,1,0:T(8,128)(2,1)}, bf16[2,192,2048]{2,1,0:T(8,128)(2,1)}, u32[]{:S(2)}, u32[]{:S(2)}) collective-permute-start(bf16[2,192,2048]{2,1,0:T(8,128)(2,1)} %get-tuple-element.55), channel_id=1, source_target_pairs={{0,4},{4,0},{8,12},{12,8},{1,5},{5,1},{9,13},{13,9},{2,6},{6,2},{1... | collective-permute-start | bytes 4718600 | tf_op jit(solution)/shard_map/ppermute | solution.py:411
  98.0 2.4 %copy-start.3 = (bf16[192,2048]{1,0:T(8,128)(2,1)S(1)}, bf16[192,2048]{1,0:T(8,128)(2,1)}, u32[]{:S(2)}) copy-start(bf16[192,2048]{1,0:T(8,128)(2,1)} %get-tuple-element.63.refs_2_.mine) | copy-start | bytes 2359300

commit v6 on v4

--- a/solution.py
+++ b/solution.py
@@ -14,6 +14,7 @@
 VMEM = pl.BlockSpec(memory_space=pltpu.VMEM)
 BF16 = jnp.bfloat16
 F32 = jnp.float32
+TILE = 512
 
 
 def order(us):
@@ -28,7 +29,15 @@
     return jax.ShapeDtypeStruct(shape, dtype)
 
 
-TOKEN = sds((8, 128), F32)
+def in_hbm(shape, dtype=BF16):
+    return pltpu.HBM(shape, dtype)
+
+
+def pin(*arrays):
+    return [pltpu.with_memory_space_constraint(x, pltpu.HBM) for x in arrays]
+
+
+TOKEN = in_hbm((8, 128), F32)
 
 
 def select_kernel(by_shift, by_target, n_rep, cap, pool_dev, rank, slot, lists, pos, pool, *rest):
@@ -63,8 +72,8 @@
 
 def select(slot, lists, pos, pool, by_shift, by_target, n_rep, cap, after=()):
     pool_dev, rank, width = pool.shape
-    shapes = [sds((cap * rank, stop - start)) for start, stop in by_shift for _ in range(n_rep)]
-    shapes += [sds((n_rep, cap * rank, stop - start)) for start, stop in by_target]
+    shapes = [in_hbm((cap * rank, stop - start)) for start, stop in by_shift for _ in range(n_rep)]
+    shapes += [in_hbm((n_rep, cap * rank, stop - start)) for start, stop in by_target]
     return pl.pallas_call(
         functools.partial(select_kernel, by_shift, by_target, n_rep, cap, pool_dev, rank),
         out_shape=[*shapes, TOKEN],
@@ -74,7 +83,56 @@
         compiler_params=params(16),
         cost_estimate=order(0),
         name="select",
-    )(slot, lists, pos, pool, *after)
+    )(*pin(slot, lists, pos, pool), *pin(*after))
+
+
+def product_all_kernel(pos, features, weights, early, early_send, keep, send, token):
+    token[...] = jnp.zeros_like(token)
+    half = features.shape[0] // 2
+    own = half // 2
+    result = jnp.dot(features[...], weights[...], preferred_element_type=F32).astype(BF16)
+    for chip in range(2):
+        other, mine = (1 - chip) * half, chip * half
+        for core in range(2):
+            a, b = core * own, (1 - core) * own
+
+            @pl.when((pos[0] == chip) & (pos[1] == core))
+            def _():
+                early[...] = result[other + a : other + a + own]
+                early_send[...] = result[other + b : other + b + own]
+                keep[0] = result[mine + a : mine + a + own]
+                send[0] = result[mine + b : mine + b + own]
+
+
+def product_all(pos, features, projection, block, tile, filled=(), after=()):
+    rows, depth = features.shape
+    width = projection.shape[1] // 4
+    own = rows // 4
+    per = width // tile
+
+    def kernel(pos, features, weights, *rest):
+        product_all_kernel(pos, features, weights, *rest[-5:])
+
+    flat = pl.BlockSpec((own, tile), lambda j, pos: (0, j))
+    part = pl.BlockSpec((1, own, tile), lambda j, pos: (block, 0, j))
+    return pl.pallas_call(
+        kernel,
+        out_shape=[sds((own, width))] * 2 + [in_hbm((2, own, width))] * 2 + [TOKEN],
+        grid_spec=pltpu.PrefetchScalarGridSpec(
+            num_scalar_prefetch=1,
+            grid=(per,),
+            in_specs=[
+                pl.BlockSpec((rows, depth), lambda j, pos: (0, 0)),
+                pl.BlockSpec((depth, tile), lambda j, pos: (0, (2 * (1 - pos[0]) + block) * per + j)),
+            ]
+            + [ANY] * (len(filled) + len(after)),
+            out_specs=[flat, flat, part, part, pl.BlockSpec((8, 128), lambda j, pos: (0, 0))],
+        ),
+        input_output_aliases={3 + i: 2 + i for i in range(len(filled))},
+        compiler_params=params(),
+        cost_estimate=order(0),
+        name="product",
+    )(*pin(pos), features, projection, *pin(*filled, *after))
 
 
 def product_columns_kernel(per, pos, features, weights, late, late_send, token):
@@ -102,7 +160,7 @@
 
     return pl.pallas_call(
         kernel,
-        out_shape=[sds((half, width))] * 2 + [TOKEN],
+        out_shape=[in_hbm((half, width))] * 2 + [TOKEN],
         grid_spec=pltpu.PrefetchScalarGridSpec(
             num_scalar_prefetch=1,
             grid=(2 * per,),
@@ -126,7 +184,7 @@
         compiler_params=params(),
         cost_estimate=order(0),
         name="product",
-    )(pos, features, projection, *after)
+    )(*pin(pos), features, projection, *pin(*after))
 
 
 def product_kernel(split, pos, features, weights, keep, send, token):
@@ -178,7 +236,7 @@
 
     return pl.pallas_call(
         kernel,
-        out_shape=[sds(shape), sds(shape), TOKEN],
+        out_shape=[in_hbm(shape) if blocks > 1 else sds(shape)] * 2 + [TOKEN],
         grid_spec=pltpu.PrefetchScalarGridSpec(
             num_scalar_prefetch=1,
             grid=(tiles,),
@@ -189,7 +247,7 @@
         compiler_params=params(),
         cost_estimate=order(0),
         name="product",
-    )(pos, features, projection, *after)
+    )(*pin(pos), features, projection, *pin(*after))
 
 
 def walk_list(slot, lists, me, n_rep, cap, pool_dev, counts, by_owner, visit):
@@ -233,7 +291,7 @@
         compiler_params=params(),
         cost_estimate=order(40),
         name="score",
-    )(slot, lists, pos, wanted, features, factors, *after)
+    )(*pin(slot, lists, pos, wanted), features, *pin(factors), *pin(*after))
 
 
 def delta_kernel(
@@ -277,7 +335,7 @@
     width = stop - start
     return pl.pallas_call(
         functools.partial(delta_kernel, len(blocks), n_rep, cap, pool_dev, rank, len(before)),
-        out_shape=[sds((own, width))] * 2 + [sds((own, stop))] * 2,
+        out_shape=[in_hbm((own, width))] * 2 + [in_hbm((own, stop))] * 2,
         grid=(1,),
         in_specs=[SMEM] * 3
         + [VMEM] * 2
@@ -295,24 +353,24 @@
         compiler_params=params(),
         cost_estimate=order(0),
         name="delta",
-    )(slot, lists, pos, wanted, shrunk, *late, *blocks, *before, *after)
+    )(*pin(slot, lists, pos, wanted), shrunk, *pin(late[0]), late[1], *pin(blocks[0]), *blocks[1:], *pin(*before), *pin(*after))
 
 
 def gate_kernel(*refs):
     pass
 
 
-def gate(arrays, after):
+def gate(arrays, after, us=0):
     n = len(arrays)
     return pl.pallas_call(
         gate_kernel,
-        out_shape=[sds(x.shape, x.dtype) for x in arrays],
+        out_shape=[in_hbm(x.shape, x.dtype) for x in arrays],
         in_specs=[ANY] * (n + len(after)),
         out_specs=[ANY] * n,
         input_output_aliases={i: i for i in range(n)},
-        cost_estimate=order(100),
+        cost_estimate=order(us),
         name="gate",
-    )(*arrays, *after)
+    )(*pin(*arrays, *after))
 
 
 def near_kernel(pos, residual, keep, recv, first, second, mine, theirs, *rest):
@@ -335,17 +393,32 @@
     own, full = residual.shape
     width = full // 4
     size = stop - start
-    tile = min(1024, math.gcd(size, start, width))
+    tile = min(TILE, math.gcd(size, start, width))
+    count = size // tile
+    skip = start // tile
 
     def place(b, j, pos):
         chip = pos[0] if near else 1 - pos[0]
-        return (0, (2 * chip + b) * (width // tile) + start // tile + j)
+        return (0, (2 * chip + b) * (width // tile) + skip + j)
 
     whole = pl.BlockSpec((own, tile), place)
-    part = pl.BlockSpec((1, own, tile), lambda b, j, pos: (b, 0, start // tile + j))
-    piece = pl.BlockSpec((own, tile), lambda b, j, pos: (0, j))
-    operands = [pos, residual, *base, *pieces, *after]
-    specs = [piece] * len(pieces) + [ANY] * len(after)
+    halves = [
+        lambda b, j, pos: (0, skip + jnp.where(b == 0, j, count - 1)),
+        lambda b, j, pos: (0, skip + jnp.where(b == 1, j, 0)),
+    ]
+    by_block = [pl.BlockSpec((own, tile), f) for f in halves]
+
+    def by_core(offset):
+        def index(b, j, pos):
+            half = pos[1] ^ offset
+            return (0, jnp.where(b == half, j, jnp.where(half == 0, count - 1, 0)))
+
+        return pl.BlockSpec((own, tile), index)
+
+    part = pl.BlockSpec((1, own, tile), lambda b, j, pos: (b, 0, skip + j))
+    specs = [part, part, *(by_block if near else []), by_core(0), by_core(1)]
+    specs = specs + [ANY] * len(after)
+    operands = [*pin(pos, residual, *base), *pieces, *pin(*after)]
     aliases = {}
     if out is not None:
         specs = specs + [ANY]
@@ -356,8 +429,8 @@
         out_shape=sds((own, full)),
         grid_spec=pltpu.PrefetchScalarGridSpec(
             num_scalar_prefetch=1,
-            grid=(2, size // tile),
-            in_specs=[whole, part, part] + specs,
+            grid=(2, count),
+            in_specs=[whole, *specs],
             out_specs=whole,
         ),
         input_output_aliases=aliases,
@@ -404,8 +477,9 @@
 
     early = []
     sums = []
+    filled = ()
     for b in range(2):
-        keep, send, token = product(pos, features, projection, True, True, b * width, width, tile, 1, [token])
+        keep, send, *filled, token = product_all(pos, features, projection, b, tile, filled, [token])
         sums.append(keep + over_core(send))
         early.append(over_chip(sums[-1]))
 
@@ -424,14 +498,13 @@
     common = (*lists, request_variant, shrunk, late)
     straight, cross, *before = delta(*common, first, cuts[0], n_rep, *sizes, own, (), [early[1]])
     far = [over_chip(straight), over_both(cross)]
+    far_base = (filled[0], over_core(filled[1]))
     keep, send, token = product(pos, features, projection, False, False, 0, 2 * width, tile, 2, [before[0]])
     near_base = (keep, over_core(send))
     straight, cross, mine, send = delta(*common, [second], cuts[1], n_rep, *sizes, own, before, [token])
     last = [over_chip(straight), over_both(cross)]
     theirs = over_core(send)
-    keep, send, token = product(pos, features, projection, False, True, 0, 2 * width, tile, 2, [mine])
-    far_base = (keep, over_core(send))
-    far = gate(far, [token])
+    far = gate(far, [mine], 100)
     out = finish(pos, None, stream, near_base, 0, width, True, [*early, mine, theirs], far)
     out = finish(pos, out, stream, far_base, *cuts[0], False, far)
     out = finish(pos, out, stream, far_base, *cuts[1], False, last)

time: 131 us -> 122 us (0.931)
  local copies, waits for them, and re-layouts: 13 us -> 1.42 us
  Pallas kernels: 76 us -> 82.1 us
  waiting for transfers between devices: 8.74 us -> 4.37 us
    unnamed x50 -> x10, local copies, waits for them, and re-layouts: 13 us -> 1.42 us
    all_to_all x1, waiting for transfers between devices: 5.47 us -> 0.01 us  [paired(): lax.all_to_all(chosen, 'rep', 0, 0, tiled=True)]
    pallas_call x3, Pallas kernels: 11.7 us -> 17 us  [finish(): pl.pallas_call(near_kernel if near else far_kernel, out_shape=sds((own, f...]
    pallas_call x6 -> x5, Pallas kernels: 49.5 us -> 46.4 us  [the longest x2 22.2 us: product_all(): pl.pallas_call(kernel, out_shape=[sds((own, width))] * 2 + [in_hbm((2, ow...]
    pallas_call x2, Pallas kernels: 3.54 us -> 6.26 us  [select(): pl.pallas_call(functools.partial(select_kernel, by_shift, by_target, n_re...]
  transfers between devices with their start and end apart: 17 -> 17, of which waited for: 2 -> 3; matrix products, arithmetic and copies ran while one was open for 2% -> 2% of each run, Pallas kernels for 55% -> 61%
where the time goes in v6:
time: 122 us; the launch traced here: 121 us
  Pallas kernels  82.1 us (67%)
  starting transfers between devices  23.6 us (19%)
  blocking collectives  6.75 us (6%)
  waiting for transfers between devices  4.37 us (4%)
  other arithmetic  2.96 us (2%)
  local copies, waits for them, and re-layouts  1.42 us (1%)
    pallas_call x2, Pallas kernels, product_all(): pl.pallas_call(kernel, out_shape=[sds((own, width))] * 2 + [in_hbm((2, ow...  22.2 us
    pallas_call x3, Pallas kernels, finish(): pl.pallas_call(near_kernel if near else far_kernel, out_shape=sds((own, f...  17 us
    pallas_call x1, Pallas kernels, product_columns(): pl.pallas_call(kernel, out_shape=[in_hbm((half, width))] * 2 + [TOKEN], g...  12.2 us
    pallas_call x1, Pallas kernels, product(): pl.pallas_call(kernel, out_shape=[in_hbm(shape) if blocks > 1 else sds(sh...  12.1 us
    pallas_call x2, Pallas kernels, delta(): pl.pallas_call(functools.partial(delta_kernel, len(blocks), n_rep, cap, p...  9.33 us
    all_gather x1, blocking collectives, paired(): shrunk = lax.all_gather(part, 'tp')  6.75 us
    all_to_all x1, starting transfers between devices, paired(): lax.all_to_all(chosen, 'rep', 0, 0, tiled=True)  6.58 us
    pallas_call x2, Pallas kernels, select(): pl.pallas_call(functools.partial(select_kernel, by_shift, by_target, n_re...  6.26 us
  transfers between devices with their start and end apart: 17, of which 3 were waited for; matrix products, arithmetic and copies ran while one was open for 2% of the time, Pallas kernels for 61%

profile of v6, /device:TPU:0, one launch (start us, length us, event | category | flops | bytes accessed | tf_op | source)
XLA Modules:
  0.0 121.2 jit_solution(11948978348868733299)
XLA Ops:
  0.6 3.1 %select.8 = (bf16[4,96,2048]{2,1,0:T(8,128)(2,1)}, f32[8,128]{1,0:T(8,128)}) custom-call(s32[64]{0:T(128)} %slot.9, s32[4,24]{1,0:T(4,128)} %lists.9, s32[3]{0:T(128)} %pad_add_fusion.pos, bf16[16,16,2048]{2,1,0:T(8,128)(2,1)} %pool.2), custom_call_target="tpu_custom_call" | custom-call | flops 1 | bytes 1 | tf_op jit(solution)/shard_map/select/pallas_call | solution.py:77
  3.8 6.6 %all-to-all-start = ((bf16[4,96,2048]{2,1,0:T(8,128)(2,1)}), bf16[4,96,2048]{2,1,0:T(8,128)(2,1)}, u32[]{:S(2)}, u32[]{:S(2)}) async-start(bf16[4,96,2048]{2,1,0:T(8,128)(2,1)} %get-tuple-element.45), calls=%async_computation | async-start | bytes 3145728 | tf_op jit(solution)/shard_map/all_to_all | solution.py:476
  10.3 11.1 %product.4 = (bf16[192,2048]{1,0:T(8,128)(2,1)S(1)}, bf16[192,2048]{1,0:T(8,128)(2,1)S(1)}, bf16[2,192,2048]{2,1,0:T(8,128)(2,1)}, bf16[2,192,2048]{2,1,0:T(8,128)(2,1)}, f32[8,128]{1,0:T(8,128)}) custom-call(s32[3]{0:T(128)} %pad_add_fusion.pos, bf16[768,2048]{1,0:T(8,128)(2,1)S(1)} %bitcast.9, bf16[2048,8192]{1,0:T(8,128)(2,1)} %weights.7, ...), custom_call_target="tpu_custom_call" | custom-call | flops 1 | bytes 1 | tf_op jit(solution)/shard_map/product/pallas_call | solution.py:118
  21.4 11.1 %product.5 = (bf16[192,2048]{1,0:T(8,128)(2,1)S(1)}, bf16[192,2048]{1,0:T(8,128)(2,1)S(1)}, bf16[2,192,2048]{2,1,0:T(8,128)(2,1)}, bf16[2,192,2048]{2,1,0:T(8,128)(2,1)}, f32[8,128]{1,0:T(8,128)}) custom-call(s32[3]{0:T(128)} %pad_add_fusion.pos, bf16[768,2048]{1,0:T(8,128)(2,1)S(1)} %bitcast.10, ...), custom_call_target="tpu_custom_call", output_to_operand_aliasing={{2}: (3, {}), {3}: (4, {})} | custom-call | flops 1 | bytes 1 | tf_op jit(solution)/shard_map/product/pallas_call | solution.py:118
  34.2 1.5 %collective-permute-start.3 = (bf16[192,2048]{1,0:T(8,128)(2,1)}, bf16[192,2048]{1,0:T(8,128)(2,1)}, u32[]{:S(2)}, u32[]{:S(2)}) collective-permute-start(bf16[192,2048]{1,0:T(8,128)(2,1)} %add.12.rest_0_), channel_id=1, source_target_pairs={{0,8},{8,0},{4,12},{12,4},{1,9},{9,1},{5,13},{13,5},{2,10},{10,2},... | collective-permute-start | bytes 2359304 | tf_op jit(solution)/shard_map/ppermute | solution.py:466
  35.7 3.1 %select.9 = (bf16[96,1024]{1,0:T(8,128)(2,1)}, bf16[96,1024]{1,0:T(8,128)(2,1)}, bf16[96,1024]{1,0:T(8,128)(2,1)}, bf16[96,1024]{1,0:T(8,128)(2,1)}, bf16[4,96,1024]{2,1,0:T(8,128)(2,1)}, /*index=5*/f32[8,128]{1,0:T(8,128)}) custom-call(s32[64]{0:T(128)} %slot.9, s32[4,24]{1,0:T(4,128)} %lists.9, s32[3]{0:T(128)} %pad_add_fusion.pos, ...), custom_call_target="tpu_custom_call" | custom-call | flops 1 | bytes 1 | tf_op jit(solution)/shard_map/select/pallas_call | solution.py:77
  38.8 2.0 %collective-permute-start.5 = (bf16[96,1024]{1,0:T(8,128)(2,1)}, bf16[96,1024]{1,0:T(8,128)(2,1)S(1)}, u32[]{:S(2)}, u32[]{:S(2)}) collective-permute-start(bf16[96,1024]{1,0:T(8,128)(2,1)} %get-tuple-element.57), channel_id=1, source_target_pairs={{0,1},{1,2},{2,3},{3,0},{4,5},{5,6},{6,7},{7,4},{8,9},{9,10},{10,1... | collective-permute-start | bytes 589832 | tf_op jit(solution)/shard_map/ppermute | solution.py:472
  40.8 2.4 %collective-permute-start.6 = (bf16[96,1024]{1,0:T(8,128)(2,1)}, bf16[96,1024]{1,0:T(8,128)(2,1)}, u32[]{:S(2)}, u32[]{:S(2)}) collective-permute-start(bf16[96,1024]{1,0:T(8,128)(2,1)} %get-tuple-element.58), channel_id=1, source_target_pairs={{0,2},{1,3},{2,0},{3,1},{4,6},{5,7},{6,4},{7,5},{8,10},{9,11},{10,... | collective-permute-start | bytes 589832 | tf_op jit(solution)/shard_map/ppermute | solution.py:472
  43.2 1.5 %collective-permute-start.7 = (bf16[96,1024]{1,0:T(8,128)(2,1)}, bf16[96,1024]{1,0:T(8,128)(2,1)}, u32[]{:S(2)}, u32[]{:S(2)}) collective-permute-start(bf16[96,1024]{1,0:T(8,128)(2,1)} %get-tuple-element.59), channel_id=1, source_target_pairs={{0,3},{1,0},{2,1},{3,2},{4,7},{5,4},{6,5},{7,6},{8,11},{9,8},{10,9... | collective-permute-start | bytes 589832 | tf_op jit(solution)/shard_map/ppermute | solution.py:472
  46.4 12.2 %product.6 = (bf16[384,2048]{1,0:T(8,128)(2,1)}, bf16[384,2048]{1,0:T(8,128)(2,1)}, f32[8,128]{1,0:T(8,128)}) custom-call(s32[3]{0:T(128)} %pad_add_fusion.pos, bf16[768,2048]{1,0:T(8,128)(2,1)S(1)} %bitcast.11, bf16[2048,8192]{1,0:T(8,128)(2,1)} %weights.7, bf16[192,2048]{1,0:T(8,128)(2,1)} %add.12.rest_0_, bf16[192,2048]{1,0:T(8,128)(2,1)} %add.13.rest_1_, ...), custom_call_target="tpu_custom_call" | custom-call | flops 1 | bytes 1 | tf_op jit(solution)/shard_map/product/pallas_call | solution.py:161
  58.6 4.2 %all-to-all-start.1 = ((bf16[4,96,1024]{2,1,0:T(8,128)(2,1)}), bf16[4,96,1024]{2,1,0:T(8,128)(2,1)}, u32[]{:S(2)}, u32[]{:S(2)}) async-start(bf16[4,96,1024]{2,1,0:T(8,128)(2,1)} %get-tuple-element.55), calls=%async_computation.1 | async-start | bytes 1572864 | tf_op jit(solution)/shard_map/all_to_all | solution.py:490
  62.9 3.0 %score.1 = f32[16,768]{1,0:T(8,128)S(1)} custom-call(s32[64]{0:T(128)} %slot.9, s32[4,24]{1,0:T(4,128)} %lists.9, s32[3]{0:T(128)} %pad_add_fusion.pos, s32[1,768]{1,0:T(1,128)} %wanted.5, bf16[768,2048]{1,0:T(8,128)(2,1)S(1)} %bitcast.12, bf16[384,2048]{1,0:T(8,128)(2,1)} %bitcast.5.factors, f32[8,128]{1,0:T(8,128)} %get-tuple-element.52.rest_0_, ...), custom_call_target="tpu_custom_call" | custom-call | flops 46000001024 | bytes 1 | tf_op jit(solution)/shard_map/score/pallas_call | solution.py:282
  65.9 6.7 %all-gather = f32[64,768]{1,0:T(8,128)S(1)} all-gather(f32[16,768]{1,0:T(8,128)S(1)} %score.1), channel_id=2, replica_groups=mesh['groups'=2,'tp'=4,'rep'=4] {'tp'}, dimensions={0}, use_global_device_ids=true | all-gather | bytes 245760 | tf_op jit(solution)/shard_map/all_gather | solution.py:496
  72.6 4.6 %delta.2 = (bf16[192,1024]{1,0:T(8,128)(2,1)}, bf16[192,1024]{1,0:T(8,128)(2,1)}, bf16[192,1024]{1,0:T(8,128)(2,1)}, bf16[192,1024]{1,0:T(8,128)(2,1)}) custom-call(s32[64]{0:T(128)} %slot.9, s32[4,24]{1,0:T(4,128)} %lists.9, s32[3]{0:T(128)} %pad_add_fusion.pos, s32[1,768]{1,0:T(1,128)} %wanted.5, f32[4,16,768]{2,1,0:T(8,128)S(1)} %bitcast.14, ...), custom_call_target="tpu_custom_call" | custom-call | flops 1 | bytes 1 | tf_op jit(solution)/shard_map/delta/pallas_call | solution.py:336
  77.3 1.5 %collective-permute-start.11 = (bf16[192,1024]{1,0:T(8,128)(2,1)}, bf16[192,1024]{1,0:T(8,128)(2,1)}, u32[]{:S(2)}, u32[]{:S(2)}) collective-permute-start(bf16[192,1024]{1,0:T(8,128)(2,1)} %get-tuple-element.65), channel_id=1, source_target_pairs={{0,8},{8,0},{4,12},{12,4},{1,9},{9,1},{5,13},{13,5},{2,10},{10,2},... | collective-permute-start | bytes 1179656 | tf_op jit(solution)/shard_map/ppermute | solution.py:466
  79.4 12.1 %product.7 = (bf16[2,192,2048]{2,1,0:T(8,128)(2,1)}, bf16[2,192,2048]{2,1,0:T(8,128)(2,1)}, f32[8,128]{1,0:T(8,128)}) custom-call(s32[3]{0:T(128)} %pad_add_fusion.pos, bf16[768,2048]{1,0:T(8,128)(2,1)S(1)} %bitcast.13, bf16[2048,8192]{1,0:T(8,128)(2,1)} %weights.7, bf16[192,1024]{1,0:T(8,128)(2,1)} %get-tuple-element.60.rest_0_.rest_1_), custom_call_target="tpu_custom_call" | custom-call | flops 1 | bytes 1 | tf_op jit(solution)/shard_map/product/pallas_call | solution.py:237
  91.5 1.4 %copy-done.2 = bf16[384,2048]{1,0:T(8,128)(2,1)S(1)} copy-done((bf16[384,2048]{1,0:T(8,128)(2,1)S(1)}, bf16[384,2048]{1,0:T(8,128)(2,1)}, u32[]{:S(2)}) %copy-start.2) | copy-done | bytes 1572888
  92.9 4.7 %delta.3 = (bf16[192,1024]{1,0:T(8,128)(2,1)}, bf16[192,1024]{1,0:T(8,128)(2,1)}, bf16[192,2048]{1,0:T(8,128)(2,1)}, bf16[192,2048]{1,0:T(8,128)(2,1)}) custom-call(s32[64]{0:T(128)} %slot.9, s32[4,24]{1,0:T(4,128)} %lists.9, s32[3]{0:T(128)} %pad_add_fusion.pos, s32[1,768]{1,0:T(1,128)} %wanted.5, f32[4,16,768]{2,1,0:T(8,128)S(1)} %bitcast.15, ...), custom_call_target="tpu_custom_call" | custom-call | flops 1 | bytes 1 | tf_op jit(solution)/shard_map/delta/pallas_call | solution.py:336
  97.6 1.5 %collective-permute-start.9 = (bf16[192,1024]{1,0:T(8,128)(2,1)}, bf16[192,1024]{1,0:T(8,128)(2,1)}, u32[]{:S(2)}, u32[]{:S(2)}) collective-permute-start(bf16[192,1024]{1,0:T(8,128)(2,1)} %get-tuple-element.63), channel_id=1, source_target_pairs={{0,8},{8,0},{4,12},{12,4},{1,9},{9,1},{5,13},{13,5},{2,10},{10,2},... | collective-permute-start | bytes 1179656 | tf_op jit(solution)/shard_map/ppermute | solution.py:466
  99.8 2.3 %collective-permute-done.14.theirs = bf16[192,2048]{1,0:T(8,128)(2,1)S(1)} collective-permute-done((bf16[192,2048]{1,0:T(8,128)(2,1)}, bf16[192,2048]{1,0:T(8,128)(2,1)S(1)}, u32[]{:S(2)}, u32[]{:S(2)}) %collective-permute-start.14) | collective-permute-done | bytes 786464 | tf_op jit(solution)/shard_map/ppermute | solution.py:463
  102.2 1.9 %collective-permute-done.13.recv = bf16[2,192,2048]{2,1,0:T(8,128)(2,1)} collective-permute-done((bf16[2,192,2048]{2,1,0:T(8,128)(2,1)S(1)}, bf16[2,192,2048]{2,1,0:T(8,128)(2,1)}, u32[]{:S(2)}, u32[]{:S(2)}) %collective-permute-start.13) | collective-permute-done | bytes 1572896 | tf_op jit(solution)/shard_map/ppermute | solution.py:463
  104.1 7.6 %near.1.rest_0_ = bf16[192,8192]{1,0:T(8,128)(2,1)} custom-call(s32[3]{0:T(128)} %pad_add_fusion.pos, bf16[192,8192]{1,0:T(8,128)(2,1)} %bitcast.16, bf16[2,192,2048]{2,1,0:T(8,128)(2,1)} %get-tuple-element.70.keep, bf16[2,192,2048]{2,1,0:T(8,128)(2,1)} %collective-permute-done.13.recv, bf16[192,2048]{1,0:T(8,128)(2,1)} %collective-permute-done.3.rest_1_.first, ...), custom_call_target="tpu_custom_call" | custom-call | flops 69000003584 | bytes 1 | tf_op jit(solution)/shard_map/near/pallas_call | solution.py:427
  111.7 4.7 %far.2.rest_0_ = bf16[192,8192]{1,0:T(8,128)(2,1)} custom-call(s32[3]{0:T(128)} %pad_add_fusion.pos, bf16[192,8192]{1,0:T(8,128)(2,1)} %bitcast.17, bf16[2,192,2048]{2,1,0:T(8,128)(2,1)} %get-tuple-element.43.keep, bf16[2,192,2048]{2,1,0:T(8,128)(2,1)} %collective-permute-done.recv, ...), custom_call_target="tpu_custom_call", output_to_operand_aliasing={{}: (6, {})} | custom-call | flops 69000003584 | bytes 1 | tf_op jit(solution)/shard_map/far/pallas_call | solution.py:427
  116.5 4.7 %far.3 = bf16[192,8192]{1,0:T(8,128)(2,1)} custom-call(s32[3]{0:T(128)} %pad_add_fusion.pos, bf16[192,8192]{1,0:T(8,128)(2,1)} %bitcast.18, bf16[2,192,2048]{2,1,0:T(8,128)(2,1)} %get-tuple-element.43.keep, bf16[2,192,2048]{2,1,0:T(8,128)(2,1)} %collective-permute-done.recv, ...), custom_call_target="tpu_custom_call", output_to_operand_aliasing={{}: (6, {})} | custom-call | flops 69000003584 | bytes 1 | tf_op jit(solution)/shard_map/far/pallas_call | solution.py:427
  (37 shorter events, 5.6 us)
Async XLA Ops:
  3.8 6.6 %copy-start = (bf16[1,768,2048]{2,1,0:T(8,128)(2,1)S(1)}, bf16[1,768,2048]{2,1,0:T(8,128)(2,1)}, u32[]{:S(2)}) copy-start(bf16[1,768,2048]{2,1,0:T(8,128)(2,1)} %param.8) | copy-start | bytes 9437188
  3.8 54.8 %all-to-all-start = ((bf16[4,96,2048]{2,1,0:T(8,128)(2,1)}), bf16[4,96,2048]{2,1,0:T(8,128)(2,1)}, u32[]{:S(2)}, u32[]{:S(2)}) async-start(bf16[4,96,2048]{2,1,0:T(8,128)(2,1)} %get-tuple-element.45), calls=%async_computation | async-start | bytes 3145728 | tf_op jit(solution)/shard_map/all_to_all | solution.py:476
  21.4 11.6 %collective-permute-start.1 = (bf16[192,2048]{1,0:T(8,128)(2,1)S(1)}, bf16[192,2048]{1,0:T(8,128)(2,1)S(1)}, u32[]{:S(2)}, u32[]{:S(2)}) collective-permute-start(bf16[192,2048]{1,0:T(8,128)(2,1)S(1)} %get-tuple-element.47), channel_id=1, source_target_pairs={{0,4},{4,0},{8,12},{12,8},{1,5},{5,1},{9,13},{13,9},{2,6},{6,2},{1... | collective-permute-start | bytes 2359304 | tf_op jit(solution)/shard_map/ppermute | solution.py:463
  32.5 12.1 %collective-permute-start.2 = (bf16[192,2048]{1,0:T(8,128)(2,1)S(1)}, bf16[192,2048]{1,0:T(8,128)(2,1)S(1)}, u32[]{:S(2)}, u32[]{:S(2)}) collective-permute-start(bf16[192,2048]{1,0:T(8,128)(2,1)S(1)} %get-tuple-element.49), channel_id=1, source_target_pairs={{0,4},{4,0},{8,12},{12,8},{1,5},{5,1},{9,13},{13,9},{2,6},{6,2},{1... | collective-permute-start | bytes 2359304 | tf_op jit(solution)/shard_map/ppermute | solution.py:463
  34.2 28.6 %collective-permute-start.3 = (bf16[192,2048]{1,0:T(8,128)(2,1)}, bf16[192,2048]{1,0:T(8,128)(2,1)}, u32[]{:S(2)}, u32[]{:S(2)}) collective-permute-start(bf16[192,2048]{1,0:T(8,128)(2,1)} %add.12.rest_0_), channel_id=1, source_target_pairs={{0,8},{8,0},{4,12},{12,4},{1,9},{9,1},{5,13},{13,5},{2,10},{10,2},... | collective-permute-start | bytes 2359304 | tf_op jit(solution)/shard_map/ppermute | solution.py:466
  38.8 33.8 %collective-permute-start.5 = (bf16[96,1024]{1,0:T(8,128)(2,1)}, bf16[96,1024]{1,0:T(8,128)(2,1)S(1)}, u32[]{:S(2)}, u32[]{:S(2)}) collective-permute-start(bf16[96,1024]{1,0:T(8,128)(2,1)} %get-tuple-element.57), channel_id=1, source_target_pairs={{0,1},{1,2},{2,3},{3,0},{4,5},{5,6},{6,7},{7,4},{8,9},{9,10},{10,1... | collective-permute-start | bytes 589832 | tf_op jit(solution)/shard_map/ppermute | solution.py:472
  40.8 31.8 %collective-permute-start.6 = (bf16[96,1024]{1,0:T(8,128)(2,1)}, bf16[96,1024]{1,0:T(8,128)(2,1)}, u32[]{:S(2)}, u32[]{:S(2)}) collective-permute-start(bf16[96,1024]{1,0:T(8,128)(2,1)} %get-tuple-element.58), channel_id=1, source_target_pairs={{0,2},{1,3},{2,0},{3,1},{4,6},{5,7},{6,4},{7,5},{8,10},{9,11},{10,... | collective-permute-start | bytes 589832 | tf_op jit(solution)/shard_map/ppermute | solution.py:472
  43.2 29.4 %collective-permute-start.7 = (bf16[96,1024]{1,0:T(8,128)(2,1)}, bf16[96,1024]{1,0:T(8,128)(2,1)}, u32[]{:S(2)}, u32[]{:S(2)}) collective-permute-start(bf16[96,1024]{1,0:T(8,128)(2,1)} %get-tuple-element.59), channel_id=1, source_target_pairs={{0,3},{1,0},{2,1},{3,2},{4,7},{5,4},{6,5},{7,6},{8,11},{9,8},{10,9... | collective-permute-start | bytes 589832 | tf_op jit(solution)/shard_map/ppermute | solution.py:472
  45.8 26.8 %collective-permute-start.8 = (bf16[192,2048]{1,0:T(8,128)(2,1)}, bf16[192,2048]{1,0:T(8,128)(2,1)}, u32[]{:S(2)}, u32[]{:S(2)}) collective-permute-start(bf16[192,2048]{1,0:T(8,128)(2,1)} %add.13.rest_1_), channel_id=1, source_target_pairs={{0,8},{8,0},{4,12},{12,4},{1,9},{9,1},{5,13},{13,5},{2,10},{10,2},... | collective-permute-start | bytes 2359304 | tf_op jit(solution)/shard_map/ppermute | solution.py:466
  58.6 32.9 %all-to-all-start.1 = ((bf16[4,96,1024]{2,1,0:T(8,128)(2,1)}), bf16[4,96,1024]{2,1,0:T(8,128)(2,1)}, u32[]{:S(2)}, u32[]{:S(2)}) async-start(bf16[4,96,1024]{2,1,0:T(8,128)(2,1)} %get-tuple-element.55), calls=%async_computation.1 | async-start | bytes 1572864 | tf_op jit(solution)/shard_map/all_to_all | solution.py:490
  62.8 9.8 %collective-permute-start.4 = (bf16[384,2048]{1,0:T(8,128)(2,1)}, bf16[384,2048]{1,0:T(8,128)(2,1)S(1)}, u32[]{:S(2)}, u32[]{:S(2)}) collective-permute-start(bf16[384,2048]{1,0:T(8,128)(2,1)} %get-tuple-element.54), channel_id=1, source_target_pairs={{0,4},{4,0},{8,12},{12,8},{1,5},{5,1},{9,13},{13,9},{2,6},{6,2},{1... | collective-permute-start | bytes 4718600 | tf_op jit(solution)/shard_map/ppermute | solution.py:463
  72.6 4.6 %copy-start.1 = (bf16[384,2048]{1,0:T(8,128)(2,1)}, bf16[384,2048]{1,0:T(8,128)(2,1)S(1)}, u32[]{:S(2)}) copy-start(bf16[384,2048]{1,0:T(8,128)(2,1)S(1)} %collective-permute-done.4.late_recv) | copy-start | bytes 4718596
  77.3 21.8 %collective-permute-start.11 = (bf16[192,1024]{1,0:T(8,128)(2,1)}, bf16[192,1024]{1,0:T(8,128)(2,1)}, u32[]{:S(2)}, u32[]{:S(2)}) collective-permute-start(bf16[192,1024]{1,0:T(8,128)(2,1)} %get-tuple-element.65), channel_id=1, source_target_pairs={{0,8},{8,0},{4,12},{12,4},{1,9},{9,1},{5,13},{13,5},{2,10},{10,2},... | collective-permute-start | bytes 1179656 | tf_op jit(solution)/shard_map/ppermute | solution.py:466
  78.8 21.0 %collective-permute-start.12 = (bf16[192,1024]{1,0:T(8,128)(2,1)}, bf16[192,1024]{1,0:T(8,128)(2,1)}, u32[]{:S(2)}, u32[]{:S(2)}) collective-permute-start(bf16[192,1024]{1,0:T(8,128)(2,1)} %get-tuple-element.66), channel_id=1, source_target_pairs={{0,12},{12,0},{4,8},{8,4},{1,13},{13,1},{5,9},{9,5},{2,14},{14,2},... | collective-permute-start | bytes 1179656 | tf_op jit(solution)/shard_map/ppermute | solution.py:469
  79.0 32.7 %collective-permute-start = (bf16[2,192,2048]{2,1,0:T(8,128)(2,1)}, bf16[2,192,2048]{2,1,0:T(8,128)(2,1)}, u32[]{:S(2)}, u32[]{:S(2)}) collective-permute-start(bf16[2,192,2048]{2,1,0:T(8,128)(2,1)} %get-tuple-element.44), channel_id=1, source_target_pairs={{0,4},{4,0},{8,12},{12,8},{1,5},{5,1},{9,13},{13,9},{2,6},{6,2},{1... | collective-permute-start | bytes 4718600 | tf_op jit(solution)/shard_map/ppermute | solution.py:463
  91.5 1.4 %copy-start.2 = (bf16[384,2048]{1,0:T(8,128)(2,1)S(1)}, bf16[384,2048]{1,0:T(8,128)(2,1)}, u32[]{:S(2)}) copy-start(bf16[384,2048]{1,0:T(8,128)(2,1)} %copy-done.1) | copy-start | bytes 4718596
  92.9 6.8 %copy-start.4 = (bf16[2,192,2048]{2,1,0:T(8,128)(2,1)S(1)}, bf16[2,192,2048]{2,1,0:T(8,128)(2,1)}, u32[]{:S(2)}) copy-start(bf16[2,192,2048]{2,1,0:T(8,128)(2,1)} %get-tuple-element.71) | copy-start | bytes 4718596
  97.6 18.8 %collective-permute-start.9 = (bf16[192,1024]{1,0:T(8,128)(2,1)}, bf16[192,1024]{1,0:T(8,128)(2,1)}, u32[]{:S(2)}, u32[]{:S(2)}) collective-permute-start(bf16[192,1024]{1,0:T(8,128)(2,1)} %get-tuple-element.63), channel_id=1, source_target_pairs={{0,8},{8,0},{4,12},{12,4},{1,9},{9,1},{5,13},{13,5},{2,10},{10,2},... | collective-permute-start | bytes 1179656 | tf_op jit(solution)/shard_map/ppermute | solution.py:466
  99.1 17.4 %collective-permute-start.10 = (bf16[192,1024]{1,0:T(8,128)(2,1)}, bf16[192,1024]{1,0:T(8,128)(2,1)}, u32[]{:S(2)}, u32[]{:S(2)}) collective-permute-start(bf16[192,1024]{1,0:T(8,128)(2,1)} %get-tuple-element.64), channel_id=1, source_target_pairs={{0,12},{12,0},{4,8},{8,4},{1,13},{13,1},{5,9},{9,5},{2,14},{14,2},... | collective-permute-start | bytes 1179656 | tf_op jit(solution)/shard_map/ppermute | solution.py:469
  99.1 3.1 %collective-permute-start.14 = (bf16[192,2048]{1,0:T(8,128)(2,1)}, bf16[192,2048]{1,0:T(8,128)(2,1)S(1)}, u32[]{:S(2)}, u32[]{:S(2)}) collective-permute-start(bf16[192,2048]{1,0:T(8,128)(2,1)} %get-tuple-element.72), channel_id=1, source_target_pairs={{0,4},{4,0},{8,12},{12,8},{1,5},{5,1},{9,13},{13,9},{2,6},{6,2},{1... | collective-permute-start | bytes 2359304 | tf_op jit(solution)/shard_map/ppermute | solution.py:463
  99.8 4.3 %collective-permute-start.13 = (bf16[2,192,2048]{2,1,0:T(8,128)(2,1)S(1)}, bf16[2,192,2048]{2,1,0:T(8,128)(2,1)}, u32[]{:S(2)}, u32[]{:S(2)}) collective-permute-start(bf16[2,192,2048]{2,1,0:T(8,128)(2,1)S(1)} %copy-done.4), channel_id=1, source_target_pairs={{0,4},{4,0},{8,12},{12,8},{1,5},{5,1},{9,13},{13,9},{2,6},{6,2},{1... | collective-permute-start | bytes 4718600 | tf_op jit(solution)/shard_map/ppermute | solution.py:463
  99.8 4.2 %copy-start.3 = (bf16[192,2048]{1,0:T(8,128)(2,1)S(1)}, bf16[192,2048]{1,0:T(8,128)(2,1)}, u32[]{:S(2)}) copy-start(bf16[192,2048]{1,0:T(8,128)(2,1)} %get-tuple-element.67.refs_2_.mine) | copy-start | bytes 2359300

commit v7 on v5

--- a/solution.py
+++ b/solution.py
@@ -14,6 +14,7 @@
 VMEM = pl.BlockSpec(memory_space=pltpu.VMEM)
 BF16 = jnp.bfloat16
 F32 = jnp.float32
+TILE = 1024
 
 
 def order(us):
@@ -39,11 +40,11 @@
 TOKEN = in_hbm((8, 128), F32)
 
 
-def select_kernel(by_shift, by_target, n_rep, cap, pool_dev, rank, slot, lists, pos, pool, *rest):
+def select_kernel(by_shift, by_target, n_rep, cap, pool_dev, rank, slot, lists, pool, *rest):
     token, idx = rest[-2:]
     outs = rest[-2 - n_rep * len(by_shift) - len(by_target) : -2]
     token[...] = jnp.zeros_like(token)
-    me = pos[2]
+    me = lax.axis_index("rep")
     for shift in range(n_rep):
         target = lax.rem(me + shift, n_rep)
         for k in range(cap):
@@ -69,20 +70,65 @@
                 outs[len(by_shift) * n_rep + c][target, rows, :] = pool[entry, :, start:stop]
 
 
-def select(slot, lists, pos, pool, by_shift, by_target, n_rep, cap, after=()):
+def select(slot, lists, pool, by_shift, by_target, n_rep, cap, after=()):
     pool_dev, rank, width = pool.shape
     shapes = [in_hbm((cap * rank, stop - start)) for start, stop in by_shift for _ in range(n_rep)]
     shapes += [in_hbm((n_rep, cap * rank, stop - start)) for start, stop in by_target]
     return pl.pallas_call(
         functools.partial(select_kernel, by_shift, by_target, n_rep, cap, pool_dev, rank),
         out_shape=[*shapes, TOKEN],
-        in_specs=[SMEM, SMEM, SMEM, VMEM] + [ANY] * len(after),
+        in_specs=[SMEM, SMEM, VMEM] + [ANY] * len(after),
         out_specs=[VMEM] * len(shapes) + [VMEM],
         scratch_shapes=[pltpu.SMEM((cap,), jnp.int32)],
         compiler_params=params(16),
         cost_estimate=order(0),
         name="select",
-    )(*pin(slot, lists, pos, pool), *pin(*after))
+    )(*pin(slot, lists, pool), *pin(*after))
+
+
+def product_early_kernel(per, pos, features, weights, keep0, send0, keep1, send1, token):
+    token[...] = jnp.zeros_like(token)
+    j = pl.program_id(0)
+    own = features.shape[0] // 2
+    result = jnp.dot(features[...], weights[...], preferred_element_type=F32).astype(BF16)
+    for core in range(2):
+        a, b = core * own, (1 - core) * own
+        for block, keep, send in ((0, keep0, send0), (1, keep1, send1)):
+
+            @pl.when((pos[1] == core) & (j // per == block))
+            def _():
+                keep[...] = result[a : a + own]
+                send[...] = result[b : b + own]
+
+
+def product_early(pos, features, projection, tile, after=()):
+    rows, depth = features.shape
+    width = projection.shape[1] // 4
+    half = rows // 2
+    per = width // tile
+
+    def kernel(pos, features, weights, *rest):
+        product_early_kernel(per, pos, features, weights, *rest[-5:])
+
+    low = pl.BlockSpec((half // 2, tile), lambda j, pos: (0, jnp.minimum(j, per - 1)))
+    high = pl.BlockSpec((half // 2, tile), lambda j, pos: (0, jnp.maximum(j - per, 0)))
+    return pl.pallas_call(
+        kernel,
+        out_shape=[sds((half // 2, width))] * 4 + [TOKEN],
+        grid_spec=pltpu.PrefetchScalarGridSpec(
+            num_scalar_prefetch=1,
+            grid=(2 * per,),
+            in_specs=[
+                pl.BlockSpec((half, depth), lambda j, pos: (1 - pos[0], 0)),
+                pl.BlockSpec((depth, tile), lambda j, pos: (0, 2 * (1 - pos[0]) * per + j)),
+            ]
+            + [ANY] * len(after),
+            out_specs=[low, low, high, high, pl.BlockSpec((8, 128), lambda j, pos: (0, 0))],
+        ),
+        compiler_params=params(),
+        cost_estimate=order(0),
+        name="product",
+    )(*pin(pos), features, projection, *pin(*after))
 
 
 def product_columns_kernel(per, pos, features, weights, late, late_send, keep, send, token):
@@ -356,17 +402,32 @@
     own, full = residual.shape
     width = full // 4
     size = stop - start
-    tile = min(1024, math.gcd(size, start, width))
+    tile = min(TILE, math.gcd(size, start, width))
+    count = size // tile
+    skip = start // tile
 
     def place(b, j, pos):
         chip = pos[0] if near else 1 - pos[0]
-        return (0, (2 * chip + b) * (width // tile) + start // tile + j)
+        return (0, (2 * chip + b) * (width // tile) + skip + j)
 
     whole = pl.BlockSpec((own, tile), place)
-    part = pl.BlockSpec((1, own, tile), lambda b, j, pos: (b, 0, start // tile + j))
-    piece = pl.BlockSpec((own, tile), lambda b, j, pos: (0, j))
+    halves = [
+        lambda b, j, pos: (0, skip + jnp.where(b == 0, j, count - 1)),
+        lambda b, j, pos: (0, skip + jnp.where(b == 1, j, 0)),
+    ]
+    by_block = [pl.BlockSpec((own, tile), f) for f in halves]
+
+    def by_core(offset):
+        def index(b, j, pos):
+            half = pos[1] ^ offset
+            return (0, jnp.where(b == half, j, jnp.where(half == 0, count - 1, 0)))
+
+        return pl.BlockSpec((own, tile), index)
+
+    part = pl.BlockSpec((1, own, tile), lambda b, j, pos: (b, 0, skip + j))
+    specs = [part, part, *(by_block if near else []), by_core(0), by_core(1)]
+    specs = specs + [ANY] * len(after)
     operands = [*pin(pos, residual, *base), *pieces, *pin(*after)]
-    specs = [piece] * len(pieces) + [ANY] * len(after)
     aliases = {}
     if out is not None:
         specs = specs + [ANY]
@@ -377,8 +438,8 @@
         out_shape=sds((own, full)),
         grid_spec=pltpu.PrefetchScalarGridSpec(
             num_scalar_prefetch=1,
-            grid=(2, size // tile),
-            in_specs=[whole, part, part] + specs,
+            grid=(2, count),
+            in_specs=[whole, *specs],
             out_specs=whole,
         ),
         input_output_aliases=aliases,
@@ -420,17 +481,14 @@
         return lax.ppermute(x, "rep", [(i, (i + shift) % n_rep) for i in range(n_rep)])
 
     shifts = [s for s in range(1, n_rep) if s != n_rep // 2] + [n_rep // 2]
-    chosen, token = select(*lists, shrink_pool, (), ((0, width),), n_rep, cap)
+    chosen, token = select(pool_slot, variant_list, shrink_pool, (), ((0, width),), n_rep, cap)
     shrink = lax.all_to_all(chosen, "rep", 0, 0, tiled=True).reshape(n_rep * cap * rank, width)
 
-    early = []
-    sums = []
-    for b in range(2):
-        keep, send, token = product(pos, features, projection, True, True, b * width, width, tile, 1, [token])
-        sums.append(keep + over_core(send))
-        early.append(over_chip(sums[-1]))
-
-    *chosen, second, token = select(*lists, expand_pool, cuts[:1], cuts[1:], n_rep, cap, [token])
+    keep0, send0, keep1, send1, token = product_early(pos, features, projection, tile, [token])
+    sums = [keep0 + over_core(send0), keep1 + over_core(send1)]
+    early = [over_chip(x) for x in sums]
+
+    *chosen, second, token = select(pool_slot, variant_list, expand_pool, cuts[:1], cuts[1:], n_rep, cap, sums)
     first = [chosen[0]] + [None] * (n_rep - 1)
     for s in shifts:
         first[s] = over_rep(chosen[s], s)
@@ -446,12 +504,12 @@
     common = (*lists, request_variant, shrunk, late)
     straight, cross, *before = delta(*common, first, cuts[0], n_rep, *sizes, own, (), [early[1]])
     far = [over_chip(straight), over_both(cross)]
-    keep, send, token = product(pos, features, projection, False, True, 0, 2 * width, tile, 2, [before[0]])
-    far_base = (keep, over_core(send))
-    straight, cross, mine, send = delta(*common, [second], cuts[1], n_rep, *sizes, own, before, [token])
+    straight, cross, mine, send = delta(*common, [second], cuts[1], n_rep, *sizes, own, before)
     last = [over_chip(straight), over_both(cross)]
     theirs = over_core(send)
-    far = gate(far, [mine])
+    keep, send, token = product(pos, features, projection, False, True, 0, 2 * width, tile, 2, [mine])
+    far_base = (keep, over_core(send))
+    far = gate(far, [token])
     out = finish(pos, None, stream, near_base, 0, width, True, [*early, mine, theirs], far)
     out = finish(pos, out, stream, far_base, *cuts[0], False, far)
     out = finish(pos, out, stream, far_base, *cuts[1], False, last)

time: 119 us -> 116 us (0.975)
  Pallas kernels: 77 us -> 74.3 us
    pallas_call x3 -> x1, Pallas kernels: 26.7 us -> 12.1 us  [product(): pl.pallas_call(kernel, out_shape=[in_hbm(shape) if blocks > 1 else sds(sh...]
    pallas_call x0 -> x1, Pallas kernels: none -> 12.1 us  [product_early(): pl.pallas_call(kernel, out_shape=[sds((half // 2, width))] * 4 + [TOKEN],...]
    ppermute x2, waiting for transfers between devices: 4.81 us -> 0.01 us  [over_both(): return lax.ppermute(x, 'tp', [(0, 3), (3, 0), (1, 2), (2, 1)])]
    all_to_all x1, waiting for transfers between devices: 0.01 us -> 3.65 us  [paired(): lax.all_to_all(second, 'rep', 0, 0, tiled=True)]
    ppermute x6, waiting for transfers between devices: 2.44 us -> 4.05 us  [over_core(): return lax.ppermute(x, 'tp', [(0, 1), (1, 0), (2, 3), (3, 2)])]
  transfers between devices with their start and end apart: 17 -> 17, of which waited for: 2 -> 3; matrix products, arithmetic and copies ran while one was open for 2% -> 3% of each run, Pallas kernels for 60% -> 58%
where the time goes in v7:
time: 116 us
  Pallas kernels  74.3 us (64%)
  starting transfers between devices  23.4 us (20%)
  waiting for transfers between devices  7.73 us (7%)
  blocking collectives  5.84 us (5%)
  other arithmetic  2.99 us (3%)
  local copies, waits for them, and re-layouts  1.42 us (1%)
    pallas_call x1, Pallas kernels, product_columns(): pl.pallas_call(kernel, out_shape=[in_hbm((half, width))] * 2 + [in_hbm((2...  19 us
    pallas_call x3, Pallas kernels, finish(): pl.pallas_call(near_kernel if near else far_kernel, out_shape=sds((own, f...  12.6 us
    pallas_call x1, Pallas kernels, product_early(): pl.pallas_call(kernel, out_shape=[sds((half // 2, width))] * 4 + [TOKEN],...  12.1 us
    pallas_call x1, Pallas kernels, product(): pl.pallas_call(kernel, out_shape=[in_hbm(shape) if blocks > 1 else sds(sh...  12.1 us
    pallas_call x2, Pallas kernels, delta(): pl.pallas_call(functools.partial(delta_kernel, len(blocks), n_rep, cap, p...  9.2 us
    all_to_all x1, starting transfers between devices, paired(): lax.all_to_all(chosen, 'rep', 0, 0, tiled=True)  6.32 us
    pallas_call x2, Pallas kernels, select(): pl.pallas_call(functools.partial(select_kernel, by_shift, by_target, n_re...  6.32 us
    ppermute x3, starting transfers between devices, over_rep(): lax.ppermute(x, 'rep', [(i, (i + shift) % n_rep) for i in range(n_rep)])  5.85 us
  transfers between devices with their start and end apart: 17, of which 3 were waited for; matrix products, arithmetic and copies ran while one was open for 3% of the time, Pallas kernels for 58%

profile of v7, /device:TPU:0, one launch (start us, length us, event | category | flops | bytes accessed | tf_op | source)
XLA Modules:
  0.0 115.7 jit_solution(16692453313638928743)
XLA Ops:
  0.0 3.1 %select.8 = (bf16[4,96,2048]{2,1,0:T(8,128)(2,1)}, f32[8,128]{1,0:T(8,128)}) custom-call(s32[64]{0:T(128)} %slot.9, s32[4,24]{1,0:T(4,128)} %lists.9, bf16[16,16,2048]{2,1,0:T(8,128)(2,1)} %pool.2), custom_call_target="tpu_custom_call" | custom-call | flops 1 | bytes 1 | tf_op jit(solution)/shard_map/select/pallas_call | solution.py:77
  3.1 6.3 %all-to-all-start = ((bf16[4,96,2048]{2,1,0:T(8,128)(2,1)}), bf16[4,96,2048]{2,1,0:T(8,128)(2,1)}, u32[]{:S(2)}, u32[]{:S(2)}) async-start(bf16[4,96,2048]{2,1,0:T(8,128)(2,1)} %get-tuple-element.35), calls=%async_computation | async-start | bytes 3145728 | tf_op jit(solution)/shard_map/all_to_all | solution.py:485
  10.1 12.1 %product.3 = (bf16[192,2048]{1,0:T(8,128)(2,1)S(1)}, bf16[192,2048]{1,0:T(8,128)(2,1)S(1)}, bf16[192,2048]{1,0:T(8,128)(2,1)S(1)}, bf16[192,2048]{1,0:T(8,128)(2,1)S(1)}, f32[8,128]{1,0:T(8,128)}) custom-call(s32[3]{0:T(128)} %pad_add_fusion.pos, bf16[768,2048]{1,0:T(8,128)(2,1)} %bitcast.9, bf16[2048,8192]{1,0:T(8,128)(2,1)} %weights.5, ...), custom_call_target="tpu_custom_call" | custom-call | flops 1 | bytes 1 | tf_op jit(solution)/shard_map/product/pallas_call | solution.py:115
  22.8 1.8 %collective-permute-done = bf16[192,2048]{1,0:T(8,128)(2,1)S(1)} collective-permute-done((bf16[192,2048]{1,0:T(8,128)(2,1)S(1)}, bf16[192,2048]{1,0:T(8,128)(2,1)S(1)}, u32[]{:S(2)}, u32[]{:S(2)}) %collective-permute-start) | collective-permute-done | bytes 786464 | tf_op jit(solution)/shard_map/ppermute | solution.py:472
  25.7 1.5 %collective-permute-start.2 = (bf16[192,2048]{1,0:T(8,128)(2,1)}, bf16[192,2048]{1,0:T(8,128)(2,1)}, u32[]{:S(2)}, u32[]{:S(2)}) collective-permute-start(bf16[192,2048]{1,0:T(8,128)(2,1)} %add.12.rest_0_), channel_id=1, source_target_pairs={{0,8},{8,0},{4,12},{12,4},{1,9},{9,1},{5,13},{13,5},{2,10},{10,2},... | collective-permute-start | bytes 2359304 | tf_op jit(solution)/shard_map/ppermute | solution.py:475
  28.9 3.2 %select.9 = (bf16[96,1024]{1,0:T(8,128)(2,1)}, bf16[96,1024]{1,0:T(8,128)(2,1)}, bf16[96,1024]{1,0:T(8,128)(2,1)}, bf16[96,1024]{1,0:T(8,128)(2,1)}, bf16[4,96,1024]{2,1,0:T(8,128)(2,1)}, /*index=5*/f32[8,128]{1,0:T(8,128)}) custom-call(s32[64]{0:T(128)} %slot.9, s32[4,24]{1,0:T(4,128)} %lists.9, bf16[16,16,2048]{2,1,0:T(8,128)(2,1)} %pool.3, ...), custom_call_target="tpu_custom_call" | custom-call | flops 1 | bytes 1 | tf_op jit(solution)/shard_map/select/pallas_call | solution.py:77
  32.1 2.0 %collective-permute-start.4 = (bf16[96,1024]{1,0:T(8,128)(2,1)}, bf16[96,1024]{1,0:T(8,128)(2,1)S(1)}, u32[]{:S(2)}, u32[]{:S(2)}) collective-permute-start(bf16[96,1024]{1,0:T(8,128)(2,1)} %get-tuple-element.47), channel_id=1, source_target_pairs={{0,1},{1,2},{2,3},{3,0},{4,5},{5,6},{6,7},{7,4},{8,9},{9,10},{10,1... | collective-permute-start | bytes 589832 | tf_op jit(solution)/shard_map/ppermute | solution.py:481
  34.1 2.4 %collective-permute-start.5 = (bf16[96,1024]{1,0:T(8,128)(2,1)}, bf16[96,1024]{1,0:T(8,128)(2,1)}, u32[]{:S(2)}, u32[]{:S(2)}) collective-permute-start(bf16[96,1024]{1,0:T(8,128)(2,1)} %get-tuple-element.48), channel_id=1, source_target_pairs={{0,2},{1,3},{2,0},{3,1},{4,6},{5,7},{6,4},{7,5},{8,10},{9,11},{10,... | collective-permute-start | bytes 589832 | tf_op jit(solution)/shard_map/ppermute | solution.py:481
  36.5 1.5 %collective-permute-start.6 = (bf16[96,1024]{1,0:T(8,128)(2,1)}, bf16[96,1024]{1,0:T(8,128)(2,1)}, u32[]{:S(2)}, u32[]{:S(2)}) collective-permute-start(bf16[96,1024]{1,0:T(8,128)(2,1)} %get-tuple-element.49), channel_id=1, source_target_pairs={{0,3},{1,0},{2,1},{3,2},{4,7},{5,4},{6,5},{7,6},{8,11},{9,8},{10,9... | collective-permute-start | bytes 589832 | tf_op jit(solution)/shard_map/ppermute | solution.py:481
  37.9 19.0 %product.4 = (bf16[384,2048]{1,0:T(8,128)(2,1)}, bf16[384,2048]{1,0:T(8,128)(2,1)}, bf16[2,192,2048]{2,1,0:T(8,128)(2,1)}, bf16[2,192,2048]{2,1,0:T(8,128)(2,1)}, f32[8,128]{1,0:T(8,128)}) custom-call(s32[3]{0:T(128)} %pad_add_fusion.pos, bf16[768,2048]{1,0:T(8,128)(2,1)S(1)} %bitcast.10, bf16[2048,8192]{1,0:T(8,128)(2,1)} %weights.5, ...), custom_call_target="tpu_custom_call" | custom-call | flops 1 | bytes 1 | tf_op jit(solution)/shard_map/product/pallas_call | solution.py:174
  56.9 4.2 %all-to-all-start.1 = ((bf16[4,96,1024]{2,1,0:T(8,128)(2,1)}), bf16[4,96,1024]{2,1,0:T(8,128)(2,1)}, u32[]{:S(2)}, u32[]{:S(2)}) async-start(bf16[4,96,1024]{2,1,0:T(8,128)(2,1)} %get-tuple-element.45), calls=%async_computation.1 | async-start | bytes 1572864 | tf_op jit(solution)/shard_map/all_to_all | solution.py:495
  61.2 3.0 %score.1 = f32[16,768]{1,0:T(8,128)S(1)} custom-call(s32[64]{0:T(128)} %slot.9, s32[4,24]{1,0:T(4,128)} %lists.9, s32[3]{0:T(128)} %pad_add_fusion.pos, s32[1,768]{1,0:T(1,128)} %wanted.5, bf16[768,2048]{1,0:T(8,128)(2,1)S(1)} %bitcast.11, bf16[384,2048]{1,0:T(8,128)(2,1)} %bitcast.5.factors, f32[8,128]{1,0:T(8,128)} %get-tuple-element.42.rest_0_, ...), custom_call_target="tpu_custom_call" | custom-call | flops 46000001024 | bytes 1 | tf_op jit(solution)/shard_map/score/pallas_call | solution.py:291
  64.2 5.8 %all-gather = f32[64,768]{1,0:T(8,128)S(1)} all-gather(f32[16,768]{1,0:T(8,128)S(1)} %score.1), channel_id=2, replica_groups=mesh['groups'=2,'tp'=4,'rep'=4] {'tp'}, dimensions={0}, use_global_device_ids=true | all-gather | bytes 245760 | tf_op jit(solution)/shard_map/all_gather | solution.py:502
  70.1 4.6 %delta.2 = (bf16[192,1024]{1,0:T(8,128)(2,1)}, bf16[192,1024]{1,0:T(8,128)(2,1)}, bf16[192,1024]{1,0:T(8,128)(2,1)}, bf16[192,1024]{1,0:T(8,128)(2,1)}) custom-call(s32[64]{0:T(128)} %slot.9, s32[4,24]{1,0:T(4,128)} %lists.9, s32[3]{0:T(128)} %pad_add_fusion.pos, s32[1,768]{1,0:T(1,128)} %wanted.5, f32[4,16,768]{2,1,0:T(8,128)S(1)} %bitcast.13, ...), custom_call_target="tpu_custom_call" | custom-call | flops 1 | bytes 1 | tf_op jit(solution)/shard_map/delta/pallas_call | solution.py:345
  74.7 1.5 %collective-permute-start.11 = (bf16[192,1024]{1,0:T(8,128)(2,1)}, bf16[192,1024]{1,0:T(8,128)(2,1)}, u32[]{:S(2)}, u32[]{:S(2)}) collective-permute-start(bf16[192,1024]{1,0:T(8,128)(2,1)} %get-tuple-element.57), channel_id=1, source_target_pairs={{0,8},{8,0},{4,12},{12,4},{1,9},{9,1},{5,13},{13,5},{2,10},{10,2},... | collective-permute-start | bytes 1179656 | tf_op jit(solution)/shard_map/ppermute | solution.py:475
  76.8 3.7 %all-to-all-done.1 = bf16[4,96,1024]{2,1,0:T(8,128)(2,1)} async-done(((bf16[4,96,1024]{2,1,0:T(8,128)(2,1)}), bf16[4,96,1024]{2,1,0:T(8,128)(2,1)}, u32[]{:S(2)}, u32[]{:S(2)}) %all-to-all-start.1) | async-done | bytes 786464 | tf_op jit(solution)/shard_map/all_to_all | solution.py:495
  80.5 1.4 %copy-done.2 = bf16[384,2048]{1,0:T(8,128)(2,1)S(1)} copy-done((bf16[384,2048]{1,0:T(8,128)(2,1)S(1)}, bf16[384,2048]{1,0:T(8,128)(2,1)}, u32[]{:S(2)}) %copy-start.2) | copy-done | bytes 1572888
  81.9 4.6 %delta.3 = (bf16[192,1024]{1,0:T(8,128)(2,1)}, bf16[192,1024]{1,0:T(8,128)(2,1)}, bf16[192,2048]{1,0:T(8,128)(2,1)}, bf16[192,2048]{1,0:T(8,128)(2,1)}) custom-call(s32[64]{0:T(128)} %slot.9, s32[4,24]{1,0:T(4,128)} %lists.9, s32[3]{0:T(128)} %pad_add_fusion.pos, s32[1,768]{1,0:T(1,128)} %wanted.5, f32[4,16,768]{2,1,0:T(8,128)S(1)} %bitcast.14, ...), custom_call_target="tpu_custom_call" | custom-call | flops 1 | bytes 1 | tf_op jit(solution)/shard_map/delta/pallas_call | solution.py:345
  86.5 1.5 %collective-permute-start.9 = (bf16[192,1024]{1,0:T(8,128)(2,1)}, bf16[192,1024]{1,0:T(8,128)(2,1)}, u32[]{:S(2)}, u32[]{:S(2)}) collective-permute-start(bf16[192,1024]{1,0:T(8,128)(2,1)} %get-tuple-element.55), channel_id=1, source_target_pairs={{0,8},{8,0},{4,12},{12,4},{1,9},{9,1},{5,13},{13,5},{2,10},{10,2},... | collective-permute-start | bytes 1179656 | tf_op jit(solution)/shard_map/ppermute | solution.py:475
  88.0 12.1 %product.5 = (bf16[2,192,2048]{2,1,0:T(8,128)(2,1)}, bf16[2,192,2048]{2,1,0:T(8,128)(2,1)}, f32[8,128]{1,0:T(8,128)}) custom-call(s32[3]{0:T(128)} %pad_add_fusion.pos, bf16[768,2048]{1,0:T(8,128)(2,1)S(1)} %bitcast.12, bf16[2048,8192]{1,0:T(8,128)(2,1)} %weights.5, bf16[192,2048]{1,0:T(8,128)(2,1)} %get-tuple-element.52.rest_0_.mine), custom_call_target="tpu_custom_call" | custom-call | flops 1 | bytes 1 | tf_op jit(solution)/shard_map/product/pallas_call | solution.py:246
  100.8 2.3 %collective-permute-done.14.theirs = bf16[192,2048]{1,0:T(8,128)(2,1)S(1)} collective-permute-done((bf16[192,2048]{1,0:T(8,128)(2,1)}, bf16[192,2048]{1,0:T(8,128)(2,1)S(1)}, u32[]{:S(2)}, u32[]{:S(2)}) %collective-permute-start.14) | collective-permute-done | bytes 786464 | tf_op jit(solution)/shard_map/ppermute | solution.py:472
  103.1 5.7 %near.1.rest_0_ = bf16[192,8192]{1,0:T(8,128)(2,1)} custom-call(s32[3]{0:T(128)} %pad_add_fusion.pos, bf16[192,8192]{1,0:T(8,128)(2,1)} %bitcast.15, bf16[2,192,2048]{2,1,0:T(8,128)(2,1)} %get-tuple-element.62.keep, bf16[2,192,2048]{2,1,0:T(8,128)(2,1)} %collective-permute-done.13.recv, bf16[192,2048]{1,0:T(8,128)(2,1)} %collective-permute-done.2.rest_1_.first, ...), custom_call_target="tpu_custom_call" | custom-call | flops 69000003584 | bytes 1 | tf_op jit(solution)/shard_map/near/pallas_call | solution.py:436
  108.7 3.5 %far.2.rest_0_ = bf16[192,8192]{1,0:T(8,128)(2,1)} custom-call(s32[3]{0:T(128)} %pad_add_fusion.pos, bf16[192,8192]{1,0:T(8,128)(2,1)} %bitcast.16, bf16[2,192,2048]{2,1,0:T(8,128)(2,1)} %get-tuple-element.53.keep, bf16[2,192,2048]{2,1,0:T(8,128)(2,1)} %collective-permute-done.8.recv, ...), custom_call_target="tpu_custom_call", output_to_operand_aliasing={{}: (6, {})} | custom-call | flops 69000003584 | bytes 1 | tf_op jit(solution)/shard_map/far/pallas_call | solution.py:436
  112.2 3.5 %far.3 = bf16[192,8192]{1,0:T(8,128)(2,1)} custom-call(s32[3]{0:T(128)} %pad_add_fusion.pos, bf16[192,8192]{1,0:T(8,128)(2,1)} %bitcast.17, bf16[2,192,2048]{2,1,0:T(8,128)(2,1)} %get-tuple-element.53.keep, bf16[2,192,2048]{2,1,0:T(8,128)(2,1)} %collective-permute-done.8.recv, ...), custom_call_target="tpu_custom_call", output_to_operand_aliasing={{}: (6, {})} | custom-call | flops 69000003584 | bytes 1 | tf_op jit(solution)/shard_map/far/pallas_call | solution.py:436
  (34 shorter events, 5.5 us)
Async XLA Ops:
  3.1 53.7 %all-to-all-start = ((bf16[4,96,2048]{2,1,0:T(8,128)(2,1)}), bf16[4,96,2048]{2,1,0:T(8,128)(2,1)}, u32[]{:S(2)}, u32[]{:S(2)}) async-start(bf16[4,96,2048]{2,1,0:T(8,128)(2,1)} %get-tuple-element.35), calls=%async_computation | async-start | bytes 3145728 | tf_op jit(solution)/shard_map/all_to_all | solution.py:485
  22.2 2.3 %collective-permute-start = (bf16[192,2048]{1,0:T(8,128)(2,1)S(1)}, bf16[192,2048]{1,0:T(8,128)(2,1)S(1)}, u32[]{:S(2)}, u32[]{:S(2)}) collective-permute-start(bf16[192,2048]{1,0:T(8,128)(2,1)S(1)} %get-tuple-element.38), channel_id=1, source_target_pairs={{0,4},{4,0},{8,12},{12,8},{1,5},{5,1},{9,13},{13,9},{2,6},{6,2},{1... | collective-permute-start | bytes 2359304 | tf_op jit(solution)/shard_map/ppermute | solution.py:472
  22.2 5.0 %collective-permute-start.1 = (bf16[192,2048]{1,0:T(8,128)(2,1)S(1)}, bf16[192,2048]{1,0:T(8,128)(2,1)S(1)}, u32[]{:S(2)}, u32[]{:S(2)}) collective-permute-start(bf16[192,2048]{1,0:T(8,128)(2,1)S(1)} %get-tuple-element.40), channel_id=1, source_target_pairs={{0,4},{4,0},{8,12},{12,8},{1,5},{5,1},{9,13},{13,9},{2,6},{6,2},{1... | collective-permute-start | bytes 2359304 | tf_op jit(solution)/shard_map/ppermute | solution.py:472
  25.7 35.4 %collective-permute-start.2 = (bf16[192,2048]{1,0:T(8,128)(2,1)}, bf16[192,2048]{1,0:T(8,128)(2,1)}, u32[]{:S(2)}, u32[]{:S(2)}) collective-permute-start(bf16[192,2048]{1,0:T(8,128)(2,1)} %add.12.rest_0_), channel_id=1, source_target_pairs={{0,8},{8,0},{4,12},{12,4},{1,9},{9,1},{5,13},{13,5},{2,10},{10,2},... | collective-permute-start | bytes 2359304 | tf_op jit(solution)/shard_map/ppermute | solution.py:475
  27.2 10.7 %copy-start = (bf16[1,768,2048]{2,1,0:T(8,128)(2,1)S(1)}, bf16[1,768,2048]{2,1,0:T(8,128)(2,1)}, u32[]{:S(2)}) copy-start(bf16[1,768,2048]{2,1,0:T(8,128)(2,1)} %param.8) | copy-start | bytes 9437188
  28.4 41.6 %collective-permute-start.7 = (bf16[192,2048]{1,0:T(8,128)(2,1)}, bf16[192,2048]{1,0:T(8,128)(2,1)}, u32[]{:S(2)}, u32[]{:S(2)}) collective-permute-start(bf16[192,2048]{1,0:T(8,128)(2,1)} %add.13.rest_1_), channel_id=1, source_target_pairs={{0,8},{8,0},{4,12},{12,4},{1,9},{9,1},{5,13},{13,5},{2,10},{10,2},... | collective-permute-start | bytes 2359304 | tf_op jit(solution)/shard_map/ppermute | solution.py:475
  32.1 37.9 %collective-permute-start.4 = (bf16[96,1024]{1,0:T(8,128)(2,1)}, bf16[96,1024]{1,0:T(8,128)(2,1)S(1)}, u32[]{:S(2)}, u32[]{:S(2)}) collective-permute-start(bf16[96,1024]{1,0:T(8,128)(2,1)} %get-tuple-element.47), channel_id=1, source_target_pairs={{0,1},{1,2},{2,3},{3,0},{4,5},{5,6},{6,7},{7,4},{8,9},{9,10},{10,1... | collective-permute-start | bytes 589832 | tf_op jit(solution)/shard_map/ppermute | solution.py:481
  34.1 35.9 %collective-permute-start.5 = (bf16[96,1024]{1,0:T(8,128)(2,1)}, bf16[96,1024]{1,0:T(8,128)(2,1)}, u32[]{:S(2)}, u32[]{:S(2)}) collective-permute-start(bf16[96,1024]{1,0:T(8,128)(2,1)} %get-tuple-element.48), channel_id=1, source_target_pairs={{0,2},{1,3},{2,0},{3,1},{4,6},{5,7},{6,4},{7,5},{8,10},{9,11},{10,... | collective-permute-start | bytes 589832 | tf_op jit(solution)/shard_map/ppermute | solution.py:481
  36.5 33.6 %collective-permute-start.6 = (bf16[96,1024]{1,0:T(8,128)(2,1)}, bf16[96,1024]{1,0:T(8,128)(2,1)}, u32[]{:S(2)}, u32[]{:S(2)}) collective-permute-start(bf16[96,1024]{1,0:T(8,128)(2,1)} %get-tuple-element.49), channel_id=1, source_target_pairs={{0,3},{1,0},{2,1},{3,2},{4,7},{5,4},{6,5},{7,6},{8,11},{9,8},{10,9... | collective-permute-start | bytes 589832 | tf_op jit(solution)/shard_map/ppermute | solution.py:481
  56.9 23.6 %all-to-all-start.1 = ((bf16[4,96,1024]{2,1,0:T(8,128)(2,1)}), bf16[4,96,1024]{2,1,0:T(8,128)(2,1)}, u32[]{:S(2)}, u32[]{:S(2)}) async-start(bf16[4,96,1024]{2,1,0:T(8,128)(2,1)} %get-tuple-element.45), calls=%async_computation.1 | async-start | bytes 1572864 | tf_op jit(solution)/shard_map/all_to_all | solution.py:495
  61.1 8.9 %collective-permute-start.3 = (bf16[384,2048]{1,0:T(8,128)(2,1)}, bf16[384,2048]{1,0:T(8,128)(2,1)S(1)}, u32[]{:S(2)}, u32[]{:S(2)}) collective-permute-start(bf16[384,2048]{1,0:T(8,128)(2,1)} %get-tuple-element.44), channel_id=1, source_target_pairs={{0,4},{4,0},{8,12},{12,8},{1,5},{5,1},{9,13},{13,9},{2,6},{6,2},{1... | collective-permute-start | bytes 4718600 | tf_op jit(solution)/shard_map/ppermute | solution.py:472
  70.1 4.6 %copy-start.1 = (bf16[384,2048]{1,0:T(8,128)(2,1)}, bf16[384,2048]{1,0:T(8,128)(2,1)S(1)}, u32[]{:S(2)}) copy-start(bf16[384,2048]{1,0:T(8,128)(2,1)S(1)} %collective-permute-done.3.late_recv) | copy-start | bytes 4718596
  74.7 25.3 %collective-permute-start.11 = (bf16[192,1024]{1,0:T(8,128)(2,1)}, bf16[192,1024]{1,0:T(8,128)(2,1)}, u32[]{:S(2)}, u32[]{:S(2)}) collective-permute-start(bf16[192,1024]{1,0:T(8,128)(2,1)} %get-tuple-element.57), channel_id=1, source_target_pairs={{0,8},{8,0},{4,12},{12,4},{1,9},{9,1},{5,13},{13,5},{2,10},{10,2},... | collective-permute-start | bytes 1179656 | tf_op jit(solution)/shard_map/ppermute | solution.py:475
  76.2 24.5 %collective-permute-start.12 = (bf16[192,1024]{1,0:T(8,128)(2,1)}, bf16[192,1024]{1,0:T(8,128)(2,1)}, u32[]{:S(2)}, u32[]{:S(2)}) collective-permute-start(bf16[192,1024]{1,0:T(8,128)(2,1)} %get-tuple-element.58), channel_id=1, source_target_pairs={{0,12},{12,0},{4,8},{8,4},{1,13},{13,1},{5,9},{9,5},{2,14},{14,2},... | collective-permute-start | bytes 1179656 | tf_op jit(solution)/shard_map/ppermute | solution.py:478
  76.4 24.4 %collective-permute-start.13 = (bf16[2,192,2048]{2,1,0:T(8,128)(2,1)}, bf16[2,192,2048]{2,1,0:T(8,128)(2,1)}, u32[]{:S(2)}, u32[]{:S(2)}) collective-permute-start(bf16[2,192,2048]{2,1,0:T(8,128)(2,1)} %get-tuple-element.63), channel_id=1, source_target_pairs={{0,4},{4,0},{8,12},{12,8},{1,5},{5,1},{9,13},{13,9},{2,6},{6,2},{1... | collective-permute-start | bytes 4718600 | tf_op jit(solution)/shard_map/ppermute | solution.py:472
  80.5 1.4 %copy-start.2 = (bf16[384,2048]{1,0:T(8,128)(2,1)S(1)}, bf16[384,2048]{1,0:T(8,128)(2,1)}, u32[]{:S(2)}) copy-start(bf16[384,2048]{1,0:T(8,128)(2,1)} %copy-done.1) | copy-start | bytes 4718596
  86.5 25.7 %collective-permute-start.9 = (bf16[192,1024]{1,0:T(8,128)(2,1)}, bf16[192,1024]{1,0:T(8,128)(2,1)}, u32[]{:S(2)}, u32[]{:S(2)}) collective-permute-start(bf16[192,1024]{1,0:T(8,128)(2,1)} %get-tuple-element.55), channel_id=1, source_target_pairs={{0,8},{8,0},{4,12},{12,4},{1,9},{9,1},{5,13},{13,5},{2,10},{10,2},... | collective-permute-start | bytes 1179656 | tf_op jit(solution)/shard_map/ppermute | solution.py:475
  88.0 24.3 %collective-permute-start.10 = (bf16[192,1024]{1,0:T(8,128)(2,1)}, bf16[192,1024]{1,0:T(8,128)(2,1)}, u32[]{:S(2)}, u32[]{:S(2)}) collective-permute-start(bf16[192,1024]{1,0:T(8,128)(2,1)} %get-tuple-element.56), channel_id=1, source_target_pairs={{0,12},{12,0},{4,8},{8,4},{1,13},{13,1},{5,9},{9,5},{2,14},{14,2},... | collective-permute-start | bytes 1179656 | tf_op jit(solution)/shard_map/ppermute | solution.py:478
  100.0 3.0 %collective-permute-start.14 = (bf16[192,2048]{1,0:T(8,128)(2,1)}, bf16[192,2048]{1,0:T(8,128)(2,1)S(1)}, u32[]{:S(2)}, u32[]{:S(2)}) collective-permute-start(bf16[192,2048]{1,0:T(8,128)(2,1)} %get-tuple-element.64), channel_id=1, source_target_pairs={{0,4},{4,0},{8,12},{12,8},{1,5},{5,1},{9,13},{13,9},{2,6},{6,2},{1... | collective-permute-start | bytes 2359304 | tf_op jit(solution)/shard_map/ppermute | solution.py:472
  100.7 8.0 %collective-permute-start.8 = (bf16[2,192,2048]{2,1,0:T(8,128)(2,1)}, bf16[2,192,2048]{2,1,0:T(8,128)(2,1)}, u32[]{:S(2)}, u32[]{:S(2)}) collective-permute-start(bf16[2,192,2048]{2,1,0:T(8,128)(2,1)} %get-tuple-element.54), channel_id=1, source_target_pairs={{0,4},{4,0},{8,12},{12,8},{1,5},{5,1},{9,13},{13,9},{2,6},{6,2},{1... | collective-permute-start | bytes 4718600 | tf_op jit(solution)/shard_map/ppermute | solution.py:472
  100.8 2.3 %copy-start.3 = (bf16[192,2048]{1,0:T(8,128)(2,1)S(1)}, bf16[192,2048]{1,0:T(8,128)(2,1)}, u32[]{:S(2)}) copy-start(bf16[192,2048]{1,0:T(8,128)(2,1)} %get-tuple-element.52.rest_0_.mine) | copy-start | bytes 2359300

commit v8 on v7

--- a/solution.py
+++ b/solution.py
@@ -19,6 +19,27 @@
 
 def order(us):
     return pl.CostEstimate(flops=int(us * 1.15e9) + 1, bytes_accessed=1, transcendentals=0)
+
+
+def position():
+    index = lax.axis_index("tp")
+    return lax.div(index, 2), lax.rem(index, 2), lax.axis_index("rep")
+
+
+def placed(spec):
+    if spec.index_map is None:
+        return spec
+    return pl.BlockSpec(spec.block_shape, lambda *ids: spec.index_map(*ids, position()))
+
+
+def grid_spec(grid, in_specs, out_specs):
+    specs = out_specs if isinstance(out_specs, list) else [out_specs]
+    specs = [placed(x) for x in specs]
+    return pl.GridSpec(
+        grid=grid,
+        in_specs=[placed(x) for x in in_specs],
+        out_specs=specs if isinstance(out_specs, list) else specs[0],
+    )
 
 
 def params(mib=48):
@@ -101,22 +122,21 @@
                 send[...] = result[b : b + own]
 
 
-def product_early(pos, features, projection, tile, after=()):
+def product_early(features, projection, tile, after=()):
     rows, depth = features.shape
     width = projection.shape[1] // 4
     half = rows // 2
     per = width // tile
 
-    def kernel(pos, features, weights, *rest):
-        product_early_kernel(per, pos, features, weights, *rest[-5:])
+    def kernel(features, weights, *rest):
+        product_early_kernel(per, position(), features, weights, *rest[-5:])
 
     low = pl.BlockSpec((half // 2, tile), lambda j, pos: (0, jnp.minimum(j, per - 1)))
     high = pl.BlockSpec((half // 2, tile), lambda j, pos: (0, jnp.maximum(j - per, 0)))
     return pl.pallas_call(
         kernel,
         out_shape=[sds((half // 2, width))] * 4 + [TOKEN],
-        grid_spec=pltpu.PrefetchScalarGridSpec(
-            num_scalar_prefetch=1,
+        grid_spec=grid_spec(
             grid=(2 * per,),
             in_specs=[
                 pl.BlockSpec((half, depth), lambda j, pos: (1 - pos[0], 0)),
@@ -128,7 +148,7 @@
         compiler_params=params(),
         cost_estimate=order(0),
         name="product",
-    )(*pin(pos), features, projection, *pin(*after))
+    )(features, projection, *pin(*after))
 
 
 def product_columns_kernel(per, pos, features, weights, late, late_send, keep, send, token):
@@ -157,7 +177,7 @@
                 send[...] = result[chip * half + (1 - core) * own : chip * half + (2 - core) * own][None]
 
 
-def product_columns(pos, features, projection, tile, after=()):
+def product_columns(features, projection, tile, after=()):
     rows, depth = features.shape
     width = projection.shape[1] // 4
     half = rows // 2
@@ -168,14 +188,13 @@
 
     rest = pl.BlockSpec((1, half // 2, tile), lambda j, pos: (block(j, pos), 0, lax.rem(j, per)))
 
-    def kernel(pos, features, weights, *rest):
-        product_columns_kernel(per, pos, features, weights, *rest[-5:])
+    def kernel(features, weights, *rest):
+        product_columns_kernel(per, position(), features, weights, *rest[-5:])
 
     return pl.pallas_call(
         kernel,
         out_shape=[in_hbm((half, width))] * 2 + [in_hbm((2, half // 2, width))] * 2 + [TOKEN],
-        grid_spec=pltpu.PrefetchScalarGridSpec(
-            num_scalar_prefetch=1,
+        grid_spec=grid_spec(
             grid=(2 * per,),
             in_specs=[
                 pl.BlockSpec((rows, depth), lambda j, pos: (0, 0)),
@@ -193,7 +212,7 @@
         compiler_params=params(),
         cost_estimate=order(0),
         name="product",
-    )(*pin(pos), features, projection, *pin(*after))
+    )(features, projection, *pin(*after))
 
 
 def product_kernel(split, pos, features, weights, keep, send, token):
@@ -215,7 +234,7 @@
         send[...] = low
 
 
-def product(pos, features, projection, other_rows, other_cols, first, count, tile, blocks, after=()):
+def product(features, projection, other_rows, other_cols, first, count, tile, blocks, after=()):
     rows, depth = features.shape
     width = projection.shape[1]
     half = rows // 2
@@ -240,14 +259,13 @@
         out_spec = pl.BlockSpec((own, tile), lambda j, pos: (0, j))
     body = functools.partial(product_kernel, blocks > 1)
 
-    def kernel(pos, features, weights, *rest):
-        body(pos, features, weights, *rest[-3:])
+    def kernel(features, weights, *rest):
+        body(position(), features, weights, *rest[-3:])
 
     return pl.pallas_call(
         kernel,
         out_shape=[in_hbm(shape) if blocks > 1 else sds(shape)] * 2 + [TOKEN],
-        grid_spec=pltpu.PrefetchScalarGridSpec(
-            num_scalar_prefetch=1,
+        grid_spec=grid_spec(
             grid=(tiles,),
             in_specs=[pl.BlockSpec((half, depth), row_block), pl.BlockSpec((depth, tile), col_block)]
             + [ANY] * len(after),
@@ -256,7 +274,7 @@
         compiler_params=params(),
         cost_estimate=order(0),
         name="product",
-    )(*pin(pos), features, projection, *pin(*after))
+    )(features, projection, *pin(*after))
 
 
 def walk_list(slot, lists, me, n_rep, cap, pool_dev, counts, by_owner, visit):
@@ -272,7 +290,7 @@
         visit(variant, group * cap + jnp.minimum(k, cap - 1))
 
 
-def score_kernel(n_rep, cap, pool_dev, rank, slot, lists, pos, wanted, features, factors, *rest):
+def score_kernel(n_rep, cap, pool_dev, rank, slot, lists, wanted, features, factors, *rest):
     out, scores, counts = rest[-3:]
     scores[...] = lax.dot_general(
         factors[...], features[...], (((1,), (1,)), ((), ())), preferred_element_type=F32
@@ -283,15 +301,15 @@
         offset = pl.multiple_of(place * rank, rank)
         out[...] += jnp.where(wanted[...] == variant, scores[pl.ds(offset, rank), :], 0.0)
 
-    walk_list(slot, lists, pos[2], n_rep, cap, pool_dev, counts, True, visit)
-
-
-def score(slot, lists, pos, wanted, features, factors, n_rep, cap, pool_dev, rank, after=()):
+    walk_list(slot, lists, position()[2], n_rep, cap, pool_dev, counts, True, visit)
+
+
+def score(slot, lists, wanted, features, factors, n_rep, cap, pool_dev, rank, after=()):
     rows = features.shape[0]
     return pl.pallas_call(
         functools.partial(score_kernel, n_rep, cap, pool_dev, rank),
         out_shape=sds((rank, rows), F32),
-        in_specs=[SMEM] * 3 + [VMEM] * 3 + [ANY] * len(after),
+        in_specs=[SMEM] * 2 + [VMEM] * 3 + [ANY] * len(after),
         out_specs=VMEM,
         scratch_shapes=[
             pltpu.VMEM((n_rep * cap * rank, rows), F32),
@@ -300,11 +318,11 @@
         compiler_params=params(),
         cost_estimate=order(40),
         name="score",
-    )(*pin(slot, lists, pos, wanted), features, *pin(factors), *pin(*after))
+    )(*pin(slot, lists, wanted), features, *pin(factors), *pin(*after))
 
 
 def delta_kernel(
-    n_blocks, n_rep, cap, pool_dev, rank, n_before, slot, lists, pos, wanted, shrunk, late_own, late_recv, *rest
+    n_blocks, n_rep, cap, pool_dev, rank, n_before, slot, lists, wanted, shrunk, late_own, late_recv, *rest
 ):
     blocks, before = rest[:n_blocks], rest[n_blocks : n_blocks + n_before]
     straight, cross, mine, send, spread, expand, result, variants, counts = rest[-9:]
@@ -316,7 +334,7 @@
     def visit(variant, place):
         variants[place] = variant
 
-    walk_list(slot, lists, pos[2], n_rep, cap, pool_dev, counts, n_blocks == 1, visit)
+    walk_list(slot, lists, position()[2], n_rep, cap, pool_dev, counts, n_blocks == 1, visit)
     total = jnp.sum(shrunk[...], axis=0).astype(BF16).astype(F32)
     for i in range(n_rep * cap):
         spread[pl.ds(i * rank, rank), :] = jnp.where(wanted[...] == variants[i], total, 0.0).astype(BF16)
@@ -325,7 +343,7 @@
     result[...] = lax.dot_general(
         spread[...], expand[...], (((0,), (0,)), ((), ())), preferred_element_type=F32
     )
-    chip, core = pos[0], pos[1]
+    chip, core, _ = position()
     for out, c in ((straight, core), (cross, 1 - core)):
         rows = pl.ds(pl.multiple_of(c * own, own), own)
         base = late_own[rows, :].astype(F32) + late_recv[rows, :].astype(F32)
@@ -338,7 +356,7 @@
     send[:, start:] = result[pl.ds((2 * chip + 1 - core) * own, own), :].astype(BF16)
 
 
-def delta(slot, lists, pos, wanted, shrunk, late, blocks, cut, n_rep, cap, pool_dev, rank, own, before=(), after=()):
+def delta(slot, lists, wanted, shrunk, late, blocks, cut, n_rep, cap, pool_dev, rank, own, before=(), after=()):
     rows = wanted.shape[1]
     start, stop = cut
     width = stop - start
@@ -346,7 +364,7 @@
         functools.partial(delta_kernel, len(blocks), n_rep, cap, pool_dev, rank, len(before)),
         out_shape=[in_hbm((own, width))] * 2 + [in_hbm((own, stop))] * 2,
         grid=(1,),
-        in_specs=[SMEM] * 3
+        in_specs=[SMEM] * 2
         + [VMEM] * 2
         + [pl.BlockSpec((2 * own, width), lambda i: (0, start // width))] * 2
         + [VMEM] * (len(blocks) + len(before))
@@ -362,7 +380,7 @@
         compiler_params=params(),
         cost_estimate=order(0),
         name="delta",
-    )(*pin(slot, lists, pos, wanted), shrunk, *pin(late[0]), late[1], *pin(blocks[0]), *blocks[1:], *pin(*before), *pin(*after))
+    )(*pin(slot, lists, wanted), shrunk, *pin(late[0]), late[1], *pin(blocks[0]), *blocks[1:], *pin(*before), *pin(*after))
 
 
 def gate_kernel(*refs):
@@ -382,23 +400,23 @@
     )(*arrays, *pin(*after))
 
 
-def near_kernel(pos, residual, keep, recv, first, second, mine, theirs, *rest):
+def near_kernel(residual, keep, recv, first, second, mine, theirs, *rest):
     out = rest[-1]
     block = pl.program_id(0)
     total = residual[...].astype(F32) + keep[0].astype(F32) + recv[0].astype(F32)
     total += jnp.where(block == 0, first[...], second[...]).astype(F32)
-    total += jnp.where(block == pos[1], mine[...], theirs[...]).astype(F32)
+    total += jnp.where(block == position()[1], mine[...], theirs[...]).astype(F32)
     out[...] = total.astype(BF16)
 
 
-def far_kernel(pos, residual, keep, recv, straight, cross, *rest):
+def far_kernel(residual, keep, recv, straight, cross, *rest):
     out = rest[-1]
     total = residual[...].astype(F32) + keep[0].astype(F32) + recv[0].astype(F32)
-    total += jnp.where(pl.program_id(0) == pos[1], straight[...], cross[...]).astype(F32)
+    total += jnp.where(pl.program_id(0) == position()[1], straight[...], cross[...]).astype(F32)
     out[...] = total.astype(BF16)
 
 
-def finish(pos, out, residual, base, start, stop, near, pieces, after=()):
+def finish(out, residual, base, start, stop, near, pieces, after=()):
     own, full = residual.shape
     width = full // 4
     size = stop - start
@@ -427,7 +445,7 @@
     part = pl.BlockSpec((1, own, tile), lambda b, j, pos: (b, 0, skip + j))
     specs = [part, part, *(by_block if near else []), by_core(0), by_core(1)]
     specs = specs + [ANY] * len(after)
-    operands = [*pin(pos, residual, *base), *pieces, *pin(*after)]
+    operands = [*pin(residual, *base), *pieces, *pin(*after)]
     aliases = {}
     if out is not None:
         specs = specs + [ANY]
@@ -436,8 +454,7 @@
     return pl.pallas_call(
         near_kernel if near else far_kernel,
         out_shape=sds((own, full)),
-        grid_spec=pltpu.PrefetchScalarGridSpec(
-            num_scalar_prefetch=1,
+        grid_spec=grid_spec(
             grid=(2, count),
             in_specs=[whole, *specs],
             out_specs=whole,
@@ -453,16 +470,13 @@
     head_outputs, residual, projection, shrink_pool, expand_pool, pool_slot, variant_list, request_variant
 ):
     n_rep = lax.axis_size("rep")
-    index = lax.axis_index("tp")
-    chip, core = index // 2, index % 2
-    pos = jnp.stack([chip, core, lax.axis_index("rep")]).astype(jnp.int32)
     features = head_outputs[0]
     rows = features.shape[0]
     own = rows // 4
     pool_dev, rank, width = shrink_pool.shape
     cap = pool_dev // 4 + 2
     stream = residual[0]
-    lists = (pool_slot, variant_list, pos)
+    lists = (pool_slot, variant_list)
     sizes = (cap, pool_dev, rank)
     tile = min(1024, width)
     cut = width // 2
@@ -484,7 +498,7 @@
     chosen, token = select(pool_slot, variant_list, shrink_pool, (), ((0, width),), n_rep, cap)
     shrink = lax.all_to_all(chosen, "rep", 0, 0, tiled=True).reshape(n_rep * cap * rank, width)
 
-    keep0, send0, keep1, send1, token = product_early(pos, features, projection, tile, [token])
+    keep0, send0, keep1, send1, token = product_early(features, projection, tile, [token])
     sums = [keep0 + over_core(send0), keep1 + over_core(send1)]
     early = [over_chip(x) for x in sums]
 
@@ -494,7 +508,7 @@
         first[s] = over_rep(chosen[s], s)
     second = lax.all_to_all(second, "rep", 0, 0, tiled=True).reshape(n_rep * cap * rank, cut)
 
-    late_keep, late_send, keep, send, token = product_columns(pos, features, projection, tile, [*sums, token])
+    late_keep, late_send, keep, send, token = product_columns(features, projection, tile, [*sums, token])
     late = (late_keep, over_core(late_send))
     near_base = (keep, over_core(send))
 
@@ -504,15 +518,15 @@
     common = (*lists, request_variant, shrunk, late)
     straight, cross, *before = delta(*common, first, cuts[0], n_rep, *sizes, own, (), [early[1]])
     far = [over_chip(straight), over_both(cross)]
-    straight, cross, mine, send = delta(*common, [second], cuts[1], n_rep, *sizes, own, before)
+    straight, cross, mine, send = delta(*common, [second], cuts[1], n_rep, *sizes, own, before, [near_base[1]])
     last = [over_chip(straight), over_both(cross)]
     theirs = over_core(send)
-    keep, send, token = product(pos, features, projection, False, True, 0, 2 * width, tile, 2, [mine])
+    keep, send, token = product(features, projection, False, True, 0, 2 * width, tile, 2, [mine])
     far_base = (keep, over_core(send))
     far = gate(far, [token])
-    out = finish(pos, None, stream, near_base, 0, width, True, [*early, mine, theirs], far)
-    out = finish(pos, out, stream, far_base, *cuts[0], False, far)
-    out = finish(pos, out, stream, far_base, *cuts[1], False, last)
+    out = finish(None, stream, near_base, 0, width, True, [*early, mine, theirs], far)
+    out = finish(out, stream, far_base, *cuts[0], False, far)
+    out = finish(out, stream, far_base, *cuts[1], False, last)
     return out[None]
 
 

time: 116 us -> 114 us (0.983)
  Pallas kernels: 74.3 us -> 70.5 us
    ppermute x6, waiting for transfers between devices: 4.05 us -> 1.79 us  [over_core(): return lax.ppermute(x, 'tp', [(0, 1), (1, 0), (2, 3), (3, 2)])]
    pallas_call x3, Pallas kernels: 12.6 us -> 10.8 us  [finish(): pl.pallas_call(near_kernel if near else far_kernel, out_shape=sds((own, f...]
    ppermute x2, waiting for transfers between devices: 0.01 us -> 1.63 us  [over_both(): return lax.ppermute(x, 'tp', [(0, 3), (3, 0), (1, 2), (2, 1)])]
  transfers between devices with their start and end apart: 17 -> 17, of which waited for: 3 -> 4; matrix products, arithmetic and copies ran while one was open for 3% -> 2% of each run, Pallas kernels for 58% -> 57%
where the time goes in v8:
time: 114 us; the launch traced here: 113 us
  Pallas kernels  70.5 us (62%)
  starting transfers between devices  23.4 us (21%)
  waiting for transfers between devices  8.74 us (8%)
  blocking collectives  5.79 us (5%)
  local copies, waits for them, and re-layouts  2.53 us (2%)
  other arithmetic  2.4 us (2%)
    pallas_call x1, Pallas kernels, product_columns(): pl.pallas_call(kernel, out_shape=[in_hbm((half, width))] * 2 + [in_hbm((2...  18.4 us
    pallas_call x1, Pallas kernels, product_early(): pl.pallas_call(kernel, out_shape=[sds((half // 2, width))] * 4 + [TOKEN],...  11.5 us
    pallas_call x1, Pallas kernels, product(): pl.pallas_call(kernel, out_shape=[in_hbm(shape) if blocks > 1 else sds(sh...  11.4 us
    pallas_call x3, Pallas kernels, finish(): pl.pallas_call(near_kernel if near else far_kernel, out_shape=sds((own, f...  10.8 us
    pallas_call x2, Pallas kernels, delta(): pl.pallas_call(functools.partial(delta_kernel, len(blocks), n_rep, cap, p...  9.24 us
    all_to_all x1, starting transfers between devices, paired(): lax.all_to_all(chosen, 'rep', 0, 0, tiled=True)  6.32 us
    pallas_call x2, Pallas kernels, select(): pl.pallas_call(functools.partial(select_kernel, by_shift, by_target, n_re...  6.28 us
    ppermute x3, starting transfers between devices, over_rep(): lax.ppermute(x, 'rep', [(i, (i + shift) % n_rep) for i in range(n_rep)])  5.85 us
  transfers between devices with their start and end apart: 17, of which 4 were waited for; matrix products, arithmetic and copies ran while one was open for 2% of the time, Pallas kernels for 57%

profile of v8, /device:TPU:0, one launch (start us, length us, event | category | flops | bytes accessed | tf_op | source)
XLA Modules:
  0.0 113.5 jit_solution(4061854258103249484)
XLA Ops:
  0.0 3.1 %select.2 = (bf16[4,96,2048]{2,1,0:T(8,128)(2,1)}, f32[8,128]{1,0:T(8,128)}) custom-call(s32[64]{0:T(128)} %slot.9, s32[4,24]{1,0:T(4,128)} %lists.9, bf16[16,16,2048]{2,1,0:T(8,128)(2,1)} %pool.2), custom_call_target="tpu_custom_call" | custom-call | flops 1 | bytes 1 | tf_op jit(solution)/shard_map/select/pallas_call | solution.py:98
  3.1 6.3 %all-to-all-start = ((bf16[4,96,2048]{2,1,0:T(8,128)(2,1)}), bf16[4,96,2048]{2,1,0:T(8,128)(2,1)}, u32[]{:S(2)}, u32[]{:S(2)}) async-start(bf16[4,96,2048]{2,1,0:T(8,128)(2,1)} %get-tuple-element.35), calls=%async_computation | async-start | bytes 3145728 | tf_op jit(solution)/shard_map/all_to_all | solution.py:499
  9.5 11.5 %product.3 = (bf16[192,2048]{1,0:T(8,128)(2,1)S(1)}, bf16[192,2048]{1,0:T(8,128)(2,1)S(1)}, bf16[192,2048]{1,0:T(8,128)(2,1)S(1)}, bf16[192,2048]{1,0:T(8,128)(2,1)S(1)}, f32[8,128]{1,0:T(8,128)}) custom-call(bf16[768,2048]{1,0:T(8,128)(2,1)} %bitcast.6, bf16[2048,8192]{1,0:T(8,128)(2,1)} %weights.5, f32[8,128]{1,0:T(8,128)} %get-tuple-element.36.rest_0_), custom_call_target="tpu_custom_call" | custom-call | flops 1 | bytes 1 | tf_op jit(solution)/shard_map/product/pallas_call | solution.py:136
  21.4 1.8 %collective-permute-done = bf16[192,2048]{1,0:T(8,128)(2,1)S(1)} collective-permute-done((bf16[192,2048]{1,0:T(8,128)(2,1)S(1)}, bf16[192,2048]{1,0:T(8,128)(2,1)S(1)}, u32[]{:S(2)}, u32[]{:S(2)}) %collective-permute-start) | collective-permute-done | bytes 786464 | tf_op jit(solution)/shard_map/ppermute | solution.py:486
  24.4 1.5 %collective-permute-start.2 = (bf16[192,2048]{1,0:T(8,128)(2,1)}, bf16[192,2048]{1,0:T(8,128)(2,1)}, u32[]{:S(2)}, u32[]{:S(2)}) collective-permute-start(bf16[192,2048]{1,0:T(8,128)(2,1)} %add.6.rest_0_), channel_id=1, source_target_pairs={{0,8},{8,0},{4,12},{12,4},{1,9},{9,1},{5,13},{13,5},{2,10},{10,2},... | collective-permute-start | bytes 2359304 | tf_op jit(solution)/shard_map/ppermute | solution.py:489
  27.1 3.1 %select.3 = (bf16[96,1024]{1,0:T(8,128)(2,1)}, bf16[96,1024]{1,0:T(8,128)(2,1)}, bf16[96,1024]{1,0:T(8,128)(2,1)}, bf16[96,1024]{1,0:T(8,128)(2,1)}, bf16[4,96,1024]{2,1,0:T(8,128)(2,1)}, /*index=5*/f32[8,128]{1,0:T(8,128)}) custom-call(s32[64]{0:T(128)} %slot.9, s32[4,24]{1,0:T(4,128)} %lists.9, bf16[16,16,2048]{2,1,0:T(8,128)(2,1)} %pool.3, ...), custom_call_target="tpu_custom_call" | custom-call | flops 1 | bytes 1 | tf_op jit(solution)/shard_map/select/pallas_call | solution.py:98
  30.3 2.0 %collective-permute-start.4 = (bf16[96,1024]{1,0:T(8,128)(2,1)}, bf16[96,1024]{1,0:T(8,128)(2,1)S(1)}, u32[]{:S(2)}, u32[]{:S(2)}) collective-permute-start(bf16[96,1024]{1,0:T(8,128)(2,1)} %get-tuple-element.47), channel_id=1, source_target_pairs={{0,1},{1,2},{2,3},{3,0},{4,5},{5,6},{6,7},{7,4},{8,9},{9,10},{10,1... | collective-permute-start | bytes 589832 | tf_op jit(solution)/shard_map/ppermute | solution.py:495
  32.8 2.4 %collective-permute-start.5 = (bf16[96,1024]{1,0:T(8,128)(2,1)}, bf16[96,1024]{1,0:T(8,128)(2,1)}, u32[]{:S(2)}, u32[]{:S(2)}) collective-permute-start(bf16[96,1024]{1,0:T(8,128)(2,1)} %get-tuple-element.48), channel_id=1, source_target_pairs={{0,2},{1,3},{2,0},{3,1},{4,6},{5,7},{6,4},{7,5},{8,10},{9,11},{10,... | collective-permute-start | bytes 589832 | tf_op jit(solution)/shard_map/ppermute | solution.py:495
  35.2 1.5 %collective-permute-start.6 = (bf16[96,1024]{1,0:T(8,128)(2,1)}, bf16[96,1024]{1,0:T(8,128)(2,1)}, u32[]{:S(2)}, u32[]{:S(2)}) collective-permute-start(bf16[96,1024]{1,0:T(8,128)(2,1)} %get-tuple-element.49), channel_id=1, source_target_pairs={{0,3},{1,0},{2,1},{3,2},{4,7},{5,4},{6,5},{7,6},{8,11},{9,8},{10,9... | collective-permute-start | bytes 589832 | tf_op jit(solution)/shard_map/ppermute | solution.py:495
  36.6 18.4 %product.4 = (bf16[384,2048]{1,0:T(8,128)(2,1)}, bf16[384,2048]{1,0:T(8,128)(2,1)}, bf16[2,192,2048]{2,1,0:T(8,128)(2,1)}, bf16[2,192,2048]{2,1,0:T(8,128)(2,1)}, f32[8,128]{1,0:T(8,128)}) custom-call(bf16[768,2048]{1,0:T(8,128)(2,1)S(1)} %bitcast.7, bf16[2048,8192]{1,0:T(8,128)(2,1)} %weights.5, bf16[192,2048]{1,0:T(8,128)(2,1)} %add.6.rest_0_, ...), custom_call_target="tpu_custom_call" | custom-call | flops 1 | bytes 1 | tf_op jit(solution)/shard_map/product/pallas_call | solution.py:194
  56.0 4.2 %all-to-all-start.1 = ((bf16[4,96,1024]{2,1,0:T(8,128)(2,1)}), bf16[4,96,1024]{2,1,0:T(8,128)(2,1)}, u32[]{:S(2)}, u32[]{:S(2)}) async-start(bf16[4,96,1024]{2,1,0:T(8,128)(2,1)} %get-tuple-element.45), calls=%async_computation.1 | async-start | bytes 1572864 | tf_op jit(solution)/shard_map/all_to_all | solution.py:509
  60.8 3.0 %score.1 = f32[16,768]{1,0:T(8,128)S(1)} custom-call(s32[64]{0:T(128)} %slot.9, s32[4,24]{1,0:T(4,128)} %lists.9, s32[1,768]{1,0:T(1,128)} %wanted.5, bf16[768,2048]{1,0:T(8,128)(2,1)S(1)} %bitcast.8, bf16[384,2048]{1,0:T(8,128)(2,1)} %bitcast.2.factors, f32[8,128]{1,0:T(8,128)} %get-tuple-element.42.rest_0_, ...), custom_call_target="tpu_custom_call" | custom-call | flops 46000001024 | bytes 1 | tf_op jit(solution)/shard_map/score/pallas_call | solution.py:309
  63.8 5.8 %all-gather = f32[64,768]{1,0:T(8,128)S(1)} all-gather(f32[16,768]{1,0:T(8,128)S(1)} %score.1), channel_id=2, replica_groups=mesh['groups'=2,'tp'=4,'rep'=4] {'tp'}, dimensions={0}, use_global_device_ids=true | all-gather | bytes 245760 | tf_op jit(solution)/shard_map/all_gather | solution.py:516
  69.6 4.7 %delta.2 = (bf16[192,1024]{1,0:T(8,128)(2,1)}, bf16[192,1024]{1,0:T(8,128)(2,1)}, bf16[192,1024]{1,0:T(8,128)(2,1)}, bf16[192,1024]{1,0:T(8,128)(2,1)}) custom-call(s32[64]{0:T(128)} %slot.9, s32[4,24]{1,0:T(4,128)} %lists.9, s32[1,768]{1,0:T(1,128)} %wanted.5, f32[4,16,768]{2,1,0:T(8,128)S(1)} %bitcast.10, bf16[384,2048]{1,0:T(8,128)(2,1)} %get-tuple-element.43.late_own, ...), custom_call_target="tpu_custom_call" | custom-call | flops 1 | bytes 1 | tf_op jit(solution)/shard_map/delta/pallas_call | solution.py:363
  74.3 1.5 %collective-permute-start.12 = (bf16[192,1024]{1,0:T(8,128)(2,1)}, bf16[192,1024]{1,0:T(8,128)(2,1)}, u32[]{:S(2)}, u32[]{:S(2)}) collective-permute-start(bf16[192,1024]{1,0:T(8,128)(2,1)} %get-tuple-element.58), channel_id=1, source_target_pairs={{0,8},{8,0},{4,12},{12,4},{1,9},{9,1},{5,13},{13,5},{2,10},{10,2},... | collective-permute-start | bytes 1179656 | tf_op jit(solution)/shard_map/ppermute | solution.py:489
  76.0 4.3 %all-to-all-done.1 = bf16[4,96,1024]{2,1,0:T(8,128)(2,1)} async-done(((bf16[4,96,1024]{2,1,0:T(8,128)(2,1)}), bf16[4,96,1024]{2,1,0:T(8,128)(2,1)}, u32[]{:S(2)}, u32[]{:S(2)}) %all-to-all-start.1) | async-done | bytes 786464 | tf_op jit(solution)/shard_map/all_to_all | solution.py:509
  80.3 1.4 %copy-done.2 = bf16[384,2048]{1,0:T(8,128)(2,1)S(1)} copy-done((bf16[384,2048]{1,0:T(8,128)(2,1)S(1)}, bf16[384,2048]{1,0:T(8,128)(2,1)}, u32[]{:S(2)}) %copy-start.2) | copy-done | bytes 1572888
  81.7 4.6 %delta.3 = (bf16[192,1024]{1,0:T(8,128)(2,1)}, bf16[192,1024]{1,0:T(8,128)(2,1)}, bf16[192,2048]{1,0:T(8,128)(2,1)}, bf16[192,2048]{1,0:T(8,128)(2,1)}) custom-call(s32[64]{0:T(128)} %slot.9, s32[4,24]{1,0:T(4,128)} %lists.9, s32[1,768]{1,0:T(1,128)} %wanted.5, f32[4,16,768]{2,1,0:T(8,128)S(1)} %bitcast.11, bf16[384,2048]{1,0:T(8,128)(2,1)} %get-tuple-element.43.late_own, ...), custom_call_target="tpu_custom_call" | custom-call | flops 1 | bytes 1 | tf_op jit(solution)/shard_map/delta/pallas_call | solution.py:363
  86.3 1.5 %collective-permute-start.10 = (bf16[192,1024]{1,0:T(8,128)(2,1)}, bf16[192,1024]{1,0:T(8,128)(2,1)}, u32[]{:S(2)}, u32[]{:S(2)}) collective-permute-start(bf16[192,1024]{1,0:T(8,128)(2,1)} %get-tuple-element.56), channel_id=1, source_target_pairs={{0,8},{8,0},{4,12},{12,4},{1,9},{9,1},{5,13},{13,5},{2,10},{10,2},... | collective-permute-start | bytes 1179656 | tf_op jit(solution)/shard_map/ppermute | solution.py:489
  88.4 11.4 %product.5 = (bf16[2,192,2048]{2,1,0:T(8,128)(2,1)}, bf16[2,192,2048]{2,1,0:T(8,128)(2,1)}, f32[8,128]{1,0:T(8,128)}) custom-call(bf16[768,2048]{1,0:T(8,128)(2,1)S(1)} %bitcast.9, bf16[2048,8192]{1,0:T(8,128)(2,1)} %weights.5, bf16[192,2048]{1,0:T(8,128)(2,1)} %get-tuple-element.53.rest_0_.mine), custom_call_target="tpu_custom_call" | custom-call | flops 1 | bytes 1 | tf_op jit(solution)/shard_map/product/pallas_call | solution.py:265
  101.0 5.2 %near.1.rest_0_ = bf16[192,8192]{1,0:T(8,128)(2,1)} custom-call(bf16[192,8192]{1,0:T(8,128)(2,1)} %bitcast.12, bf16[2,192,2048]{2,1,0:T(8,128)(2,1)} %get-tuple-element.63.keep, bf16[2,192,2048]{2,1,0:T(8,128)(2,1)} %collective-permute-done.8.rest_3_.recv, bf16[192,2048]{1,0:T(8,128)(2,1)} %collective-permute-done.2.rest_1_.first, ...), custom_call_target="tpu_custom_call" | custom-call | flops 69000003584 | bytes 1 | tf_op jit(solution)/shard_map/near/pallas_call | solution.py:454
  106.2 2.8 %far.2.rest_0_ = bf16[192,8192]{1,0:T(8,128)(2,1)} custom-call(bf16[192,8192]{1,0:T(8,128)(2,1)} %bitcast.13, bf16[2,192,2048]{2,1,0:T(8,128)(2,1)} %get-tuple-element.54.keep, bf16[2,192,2048]{2,1,0:T(8,128)(2,1)} %collective-permute-done.9.recv, bf16[192,1024]{1,0:T(8,128)(2,1)} %get-tuple-element.61.rest_0_.straight, ...), custom_call_target="tpu_custom_call", output_to_operand_aliasing={{}: (5, {})} | custom-call | flops 69000003584 | bytes 1 | tf_op jit(solution)/shard_map/far/pallas_call | solution.py:454
  109.1 1.6 %collective-permute-done.11.cross = bf16[192,1024]{1,0:T(8,128)(2,1)} collective-permute-done((bf16[192,1024]{1,0:T(8,128)(2,1)}, bf16[192,1024]{1,0:T(8,128)(2,1)}, u32[]{:S(2)}, u32[]{:S(2)}) %collective-permute-start.11) | collective-permute-done | bytes 393248 | tf_op jit(solution)/shard_map/ppermute | solution.py:492
  110.7 2.8 %far.3 = bf16[192,8192]{1,0:T(8,128)(2,1)} custom-call(bf16[192,8192]{1,0:T(8,128)(2,1)} %bitcast.14, bf16[2,192,2048]{2,1,0:T(8,128)(2,1)} %get-tuple-element.54.keep, bf16[2,192,2048]{2,1,0:T(8,128)(2,1)} %collective-permute-done.9.recv, bf16[192,1024]{1,0:T(8,128)(2,1)} %collective-permute-done.10.straight, ...), custom_call_target="tpu_custom_call", output_to_operand_aliasing={{}: (5, {})} | custom-call | flops 69000003584 | bytes 1 | tf_op jit(solution)/shard_map/far/pallas_call | solution.py:454
  (33 shorter events, 7.0 us)
Async XLA Ops:
  3.1 52.9 %all-to-all-start = ((bf16[4,96,2048]{2,1,0:T(8,128)(2,1)}), bf16[4,96,2048]{2,1,0:T(8,128)(2,1)}, u32[]{:S(2)}, u32[]{:S(2)}) async-start(bf16[4,96,2048]{2,1,0:T(8,128)(2,1)} %get-tuple-element.35), calls=%async_computation | async-start | bytes 3145728 | tf_op jit(solution)/shard_map/all_to_all | solution.py:499
  20.9 2.3 %collective-permute-start = (bf16[192,2048]{1,0:T(8,128)(2,1)S(1)}, bf16[192,2048]{1,0:T(8,128)(2,1)S(1)}, u32[]{:S(2)}, u32[]{:S(2)}) collective-permute-start(bf16[192,2048]{1,0:T(8,128)(2,1)S(1)} %get-tuple-element.38), channel_id=1, source_target_pairs={{0,4},{4,0},{8,12},{12,8},{1,5},{5,1},{9,13},{13,9},{2,6},{6,2},{1... | collective-permute-start | bytes 2359304 | tf_op jit(solution)/shard_map/ppermute | solution.py:486
  20.9 5.0 %collective-permute-start.1 = (bf16[192,2048]{1,0:T(8,128)(2,1)S(1)}, bf16[192,2048]{1,0:T(8,128)(2,1)S(1)}, u32[]{:S(2)}, u32[]{:S(2)}) collective-permute-start(bf16[192,2048]{1,0:T(8,128)(2,1)S(1)} %get-tuple-element.40), channel_id=1, source_target_pairs={{0,4},{4,0},{8,12},{12,8},{1,5},{5,1},{9,13},{13,9},{2,6},{6,2},{1... | collective-permute-start | bytes 2359304 | tf_op jit(solution)/shard_map/ppermute | solution.py:486
  24.4 36.0 %collective-permute-start.2 = (bf16[192,2048]{1,0:T(8,128)(2,1)}, bf16[192,2048]{1,0:T(8,128)(2,1)}, u32[]{:S(2)}, u32[]{:S(2)}) collective-permute-start(bf16[192,2048]{1,0:T(8,128)(2,1)} %add.6.rest_0_), channel_id=1, source_target_pairs={{0,8},{8,0},{4,12},{12,4},{1,9},{9,1},{5,13},{13,5},{2,10},{10,2},... | collective-permute-start | bytes 2359304 | tf_op jit(solution)/shard_map/ppermute | solution.py:489
  25.9 10.7 %copy-start = (bf16[1,768,2048]{2,1,0:T(8,128)(2,1)S(1)}, bf16[1,768,2048]{2,1,0:T(8,128)(2,1)}, u32[]{:S(2)}) copy-start(bf16[1,768,2048]{2,1,0:T(8,128)(2,1)} %param.8) | copy-start | bytes 9437188
  30.3 30.0 %collective-permute-start.4 = (bf16[96,1024]{1,0:T(8,128)(2,1)}, bf16[96,1024]{1,0:T(8,128)(2,1)S(1)}, u32[]{:S(2)}, u32[]{:S(2)}) collective-permute-start(bf16[96,1024]{1,0:T(8,128)(2,1)} %get-tuple-element.47), channel_id=1, source_target_pairs={{0,1},{1,2},{2,3},{3,0},{4,5},{5,6},{6,7},{7,4},{8,9},{9,10},{10,1... | collective-permute-start | bytes 589832 | tf_op jit(solution)/shard_map/ppermute | solution.py:495
  32.3 37.3 %collective-permute-start.7 = (bf16[192,2048]{1,0:T(8,128)(2,1)}, bf16[192,2048]{1,0:T(8,128)(2,1)}, u32[]{:S(2)}, u32[]{:S(2)}) collective-permute-start(bf16[192,2048]{1,0:T(8,128)(2,1)} %add.7.rest_1_), channel_id=1, source_target_pairs={{0,8},{8,0},{4,12},{12,4},{1,9},{9,1},{5,13},{13,5},{2,10},{10,2},... | collective-permute-start | bytes 2359304 | tf_op jit(solution)/shard_map/ppermute | solution.py:489
  32.8 36.8 %collective-permute-start.5 = (bf16[96,1024]{1,0:T(8,128)(2,1)}, bf16[96,1024]{1,0:T(8,128)(2,1)}, u32[]{:S(2)}, u32[]{:S(2)}) collective-permute-start(bf16[96,1024]{1,0:T(8,128)(2,1)} %get-tuple-element.48), channel_id=1, source_target_pairs={{0,2},{1,3},{2,0},{3,1},{4,6},{5,7},{6,4},{7,5},{8,10},{9,11},{10,... | collective-permute-start | bytes 589832 | tf_op jit(solution)/shard_map/ppermute | solution.py:495
  35.2 34.4 %collective-permute-start.6 = (bf16[96,1024]{1,0:T(8,128)(2,1)}, bf16[96,1024]{1,0:T(8,128)(2,1)}, u32[]{:S(2)}, u32[]{:S(2)}) collective-permute-start(bf16[96,1024]{1,0:T(8,128)(2,1)} %get-tuple-element.49), channel_id=1, source_target_pairs={{0,3},{1,0},{2,1},{3,2},{4,7},{5,4},{6,5},{7,6},{8,11},{9,8},{10,9... | collective-permute-start | bytes 589832 | tf_op jit(solution)/shard_map/ppermute | solution.py:495
  56.0 24.2 %all-to-all-start.1 = ((bf16[4,96,1024]{2,1,0:T(8,128)(2,1)}), bf16[4,96,1024]{2,1,0:T(8,128)(2,1)}, u32[]{:S(2)}, u32[]{:S(2)}) async-start(bf16[4,96,1024]{2,1,0:T(8,128)(2,1)} %get-tuple-element.45), calls=%async_computation.1 | async-start | bytes 1572864 | tf_op jit(solution)/shard_map/all_to_all | solution.py:509
  60.3 9.4 %collective-permute-start.3 = (bf16[384,2048]{1,0:T(8,128)(2,1)}, bf16[384,2048]{1,0:T(8,128)(2,1)S(1)}, u32[]{:S(2)}, u32[]{:S(2)}) collective-permute-start(bf16[384,2048]{1,0:T(8,128)(2,1)} %get-tuple-element.44), channel_id=1, source_target_pairs={{0,4},{4,0},{8,12},{12,8},{1,5},{5,1},{9,13},{13,9},{2,6},{6,2},{1... | collective-permute-start | bytes 4718600 | tf_op jit(solution)/shard_map/ppermute | solution.py:486
  60.4 19.9 %collective-permute-start.8 = (bf16[2,192,2048]{2,1,0:T(8,128)(2,1)}, bf16[2,192,2048]{2,1,0:T(8,128)(2,1)}, u32[]{:S(2)}, u32[]{:S(2)}) collective-permute-start(bf16[2,192,2048]{2,1,0:T(8,128)(2,1)} %get-tuple-element.52), channel_id=1, source_target_pairs={{0,4},{4,0},{8,12},{12,8},{1,5},{5,1},{9,13},{13,9},{2,6},{6,2},{1... | collective-permute-start | bytes 4718600 | tf_op jit(solution)/shard_map/ppermute | solution.py:486
  69.6 4.7 %copy-start.1 = (bf16[384,2048]{1,0:T(8,128)(2,1)}, bf16[384,2048]{1,0:T(8,128)(2,1)S(1)}, u32[]{:S(2)}) copy-start(bf16[384,2048]{1,0:T(8,128)(2,1)S(1)} %collective-permute-done.3.late_recv) | copy-start | bytes 4718596
  74.3 25.5 %collective-permute-start.12 = (bf16[192,1024]{1,0:T(8,128)(2,1)}, bf16[192,1024]{1,0:T(8,128)(2,1)}, u32[]{:S(2)}, u32[]{:S(2)}) collective-permute-start(bf16[192,1024]{1,0:T(8,128)(2,1)} %get-tuple-element.58), channel_id=1, source_target_pairs={{0,8},{8,0},{4,12},{12,4},{1,9},{9,1},{5,13},{13,5},{2,10},{10,2},... | collective-permute-start | bytes 1179656 | tf_op jit(solution)/shard_map/ppermute | solution.py:489
  75.8 24.1 %collective-permute-start.13 = (bf16[192,1024]{1,0:T(8,128)(2,1)}, bf16[192,1024]{1,0:T(8,128)(2,1)}, u32[]{:S(2)}, u32[]{:S(2)}) collective-permute-start(bf16[192,1024]{1,0:T(8,128)(2,1)} %get-tuple-element.59), channel_id=1, source_target_pairs={{0,12},{12,0},{4,8},{8,4},{1,13},{13,1},{5,9},{9,5},{2,14},{14,2},... | collective-permute-start | bytes 1179656 | tf_op jit(solution)/shard_map/ppermute | solution.py:492
  80.3 1.4 %copy-start.2 = (bf16[384,2048]{1,0:T(8,128)(2,1)S(1)}, bf16[384,2048]{1,0:T(8,128)(2,1)}, u32[]{:S(2)}) copy-start(bf16[384,2048]{1,0:T(8,128)(2,1)} %copy-done.1) | copy-start | bytes 4718596
  86.3 22.8 %collective-permute-start.10 = (bf16[192,1024]{1,0:T(8,128)(2,1)}, bf16[192,1024]{1,0:T(8,128)(2,1)}, u32[]{:S(2)}, u32[]{:S(2)}) collective-permute-start(bf16[192,1024]{1,0:T(8,128)(2,1)} %get-tuple-element.56), channel_id=1, source_target_pairs={{0,8},{8,0},{4,12},{12,4},{1,9},{9,1},{5,13},{13,5},{2,10},{10,2},... | collective-permute-start | bytes 1179656 | tf_op jit(solution)/shard_map/ppermute | solution.py:489
  87.8 22.9 %collective-permute-start.11 = (bf16[192,1024]{1,0:T(8,128)(2,1)}, bf16[192,1024]{1,0:T(8,128)(2,1)}, u32[]{:S(2)}, u32[]{:S(2)}) collective-permute-start(bf16[192,1024]{1,0:T(8,128)(2,1)} %get-tuple-element.57), channel_id=1, source_target_pairs={{0,12},{12,0},{4,8},{8,4},{1,13},{13,1},{5,9},{9,5},{2,14},{14,2},... | collective-permute-start | bytes 1179656 | tf_op jit(solution)/shard_map/ppermute | solution.py:492
  87.8 12.2 %collective-permute-start.14 = (bf16[192,2048]{1,0:T(8,128)(2,1)}, bf16[192,2048]{1,0:T(8,128)(2,1)}, u32[]{:S(2)}, u32[]{:S(2)}) collective-permute-start(bf16[192,2048]{1,0:T(8,128)(2,1)} %get-tuple-element.64), channel_id=1, source_target_pairs={{0,4},{4,0},{8,12},{12,8},{1,5},{5,1},{9,13},{13,9},{2,6},{6,2},{1... | collective-permute-start | bytes 2359304 | tf_op jit(solution)/shard_map/ppermute | solution.py:486
  99.8 6.4 %collective-permute-start.9 = (bf16[2,192,2048]{2,1,0:T(8,128)(2,1)}, bf16[2,192,2048]{2,1,0:T(8,128)(2,1)}, u32[]{:S(2)}, u32[]{:S(2)}) collective-permute-start(bf16[2,192,2048]{2,1,0:T(8,128)(2,1)} %get-tuple-element.55), channel_id=1, source_target_pairs={{0,4},{4,0},{8,12},{12,8},{1,5},{5,1},{9,13},{13,9},{2,6},{6,2},{1... | collective-permute-start | bytes 4718600 | tf_op jit(solution)/shard_map/ppermute | solution.py:486
  99.9 1.1 %copy-start.3 = (bf16[192,2048]{1,0:T(8,128)(2,1)S(1)}, bf16[192,2048]{1,0:T(8,128)(2,1)}, u32[]{:S(2)}) copy-start(bf16[192,2048]{1,0:T(8,128)(2,1)} %get-tuple-element.53.rest_0_.mine) | copy-start | bytes 2359300

commit v9 on v8

--- a/solution.py
+++ b/solution.py
@@ -61,46 +61,57 @@
 TOKEN = in_hbm((8, 128), F32)
 
 
-def select_kernel(by_shift, by_target, n_rep, cap, pool_dev, rank, slot, lists, pool, *rest):
-    token, idx = rest[-2:]
-    outs = rest[-2 - n_rep * len(by_shift) - len(by_target) : -2]
+def select_kernel(by_shift, by_target, named, n_rep, cap, pool_dev, rank, slot, lists, pool, *rest):
+    token, idx, counts = rest[-3:]
+    outs = rest[: -3]
+    outs = outs[-(n_rep * len(by_shift) + len(by_target) + named) :]
     token[...] = jnp.zeros_like(token)
     me = lax.axis_index("rep")
+    base = me * pool_dev
     for shift in range(n_rep):
         target = lax.rem(me + shift, n_rep)
+        for k in range(cap + 1):
+            idx[k] = 0
+        count = jnp.int32(0)
+        for l in range(lists.shape[1]):
+            place = slot[lists[target, l]] - base
+            idx[jnp.minimum(count, cap)] = place
+            count = count + jnp.where((place >= 0) & (place < pool_dev), 1, 0)
         for k in range(cap):
-            idx[k] = 0
-
-        def body(l, count):
-            place = slot[lists[target, l]]
-            mine = (place // pool_dev == me) & (count < cap)
-
-            @pl.when(mine)
-            def _():
-                idx[count] = place - me * pool_dev
-
-            return count + mine.astype(jnp.int32)
-
-        lax.fori_loop(0, lists.shape[1], body, jnp.int32(0), unroll=True)
-        for k in range(cap):
-            entry = idx[k]
+            entry = jnp.clip(idx[k], 0, pool_dev - 1)
             rows = pl.ds(k * rank, rank)
             for c, (start, stop) in enumerate(by_shift):
                 outs[c * n_rep + shift][rows, :] = pool[entry, :, start:stop]
             for c, (start, stop) in enumerate(by_target):
                 outs[len(by_shift) * n_rep + c][target, rows, :] = pool[entry, :, start:stop]
-
-
-def select(slot, lists, pool, by_shift, by_target, n_rep, cap, after=()):
+    if named:
+        names = outs[-1]
+        for i in range(n_rep * cap):
+            names[i] = -1
+        for s in range(n_rep):
+            counts[s] = 0
+        for l in range(lists.shape[1]):
+            variant = lists[me, l]
+            owner = slot[variant] // pool_dev
+            k = counts[owner]
+            counts[owner] = k + 1
+            names[owner * cap + jnp.minimum(k, cap - 1)] = variant
+
+
+def select(slot, lists, pool, by_shift, by_target, named, n_rep, cap, after=()):
     pool_dev, rank, width = pool.shape
     shapes = [in_hbm((cap * rank, stop - start)) for start, stop in by_shift for _ in range(n_rep)]
     shapes += [in_hbm((n_rep, cap * rank, stop - start)) for start, stop in by_target]
-    return pl.pallas_call(
-        functools.partial(select_kernel, by_shift, by_target, n_rep, cap, pool_dev, rank),
+    specs = [VMEM] * len(shapes)
+    if named:
+        shapes.append(in_hbm((n_rep * cap,), jnp.int32))
+        specs.append(SMEM)
+    return pl.pallas_call(
+        functools.partial(select_kernel, by_shift, by_target, int(named), n_rep, cap, pool_dev, rank),
         out_shape=[*shapes, TOKEN],
         in_specs=[SMEM, SMEM, VMEM] + [ANY] * len(after),
-        out_specs=[VMEM] * len(shapes) + [VMEM],
-        scratch_shapes=[pltpu.SMEM((cap,), jnp.int32)],
+        out_specs=[*specs, VMEM],
+        scratch_shapes=[pltpu.SMEM((cap + 1,), jnp.int32), pltpu.SMEM((n_rep,), jnp.int32)],
         compiler_params=params(16),
         cost_estimate=order(0),
         name="select",
@@ -277,73 +288,59 @@
     )(features, projection, *pin(*after))
 
 
-def walk_list(slot, lists, me, n_rep, cap, pool_dev, counts, by_owner, visit):
-    for s in range(n_rep):
-        counts[s] = 0
-
-    for l in range(lists.shape[1]):
-        variant = lists[me, l]
-        owner = slot[variant] // pool_dev
-        group = owner if by_owner else lax.rem(me - owner + n_rep, n_rep)
-        k = counts[group]
-        counts[group] = k + 1
-        visit(variant, group * cap + jnp.minimum(k, cap - 1))
-
-
-def score_kernel(n_rep, cap, pool_dev, rank, slot, lists, wanted, features, factors, *rest):
-    out, scores, counts = rest[-3:]
+def score_kernel(rank, names, wanted, features, factors, *rest):
+    out, scores = rest[-2:]
     scores[...] = lax.dot_general(
         factors[...], features[...], (((1,), (1,)), ((), ())), preferred_element_type=F32
     )
-    out[...] = jnp.zeros_like(out)
-
-    def visit(variant, place):
-        offset = pl.multiple_of(place * rank, rank)
-        out[...] += jnp.where(wanted[...] == variant, scores[pl.ds(offset, rank), :], 0.0)
-
-    walk_list(slot, lists, position()[2], n_rep, cap, pool_dev, counts, True, visit)
-
-
-def score(slot, lists, wanted, features, factors, n_rep, cap, pool_dev, rank, after=()):
+    total = jnp.zeros(out.shape, F32)
+    for i in range(factors.shape[0] // rank):
+        total += jnp.where(wanted[...] == names[i], scores[i * rank : (i + 1) * rank, :], 0.0)
+    out[...] = total
+
+
+def score(names, wanted, features, factors, rank, after=()):
     rows = features.shape[0]
     return pl.pallas_call(
-        functools.partial(score_kernel, n_rep, cap, pool_dev, rank),
+        functools.partial(score_kernel, rank),
         out_shape=sds((rank, rows), F32),
-        in_specs=[SMEM] * 2 + [VMEM] * 3 + [ANY] * len(after),
+        in_specs=[SMEM] + [VMEM] * 3 + [ANY] * len(after),
         out_specs=VMEM,
-        scratch_shapes=[
-            pltpu.VMEM((n_rep * cap * rank, rows), F32),
-            pltpu.SMEM((n_rep,), jnp.int32),
-        ],
+        scratch_shapes=[pltpu.VMEM((factors.shape[0], rows), F32)],
         compiler_params=params(),
         cost_estimate=order(40),
         name="score",
-    )(*pin(slot, lists, wanted), features, *pin(factors), *pin(*after))
-
-
-def delta_kernel(
-    n_blocks, n_rep, cap, pool_dev, rank, n_before, slot, lists, wanted, shrunk, late_own, late_recv, *rest
-):
+    )(*pin(names, wanted), features, *pin(factors), *pin(*after))
+
+
+def delta_kernel(n_blocks, n_rep, cap, rank, n_before, names, wanted, shrunk, late_own, late_recv, *rest):
     blocks, before = rest[:n_blocks], rest[n_blocks : n_blocks + n_before]
-    straight, cross, mine, send, spread, expand, result, variants, counts = rest[-9:]
-    size = n_rep * cap * rank // n_blocks
+    straight, cross, mine, send, member, expand, result = rest[-7:]
+    chip, core, me = position()
+    listed = n_rep * cap
+    size = listed * rank // n_blocks
     own, width = straight.shape
-    for i in range(n_rep * cap):
-        variants[i] = -1
-
-    def visit(variant, place):
-        variants[place] = variant
-
-    walk_list(slot, lists, position()[2], n_rep, cap, pool_dev, counts, n_blocks == 1, visit)
-    total = jnp.sum(shrunk[...], axis=0).astype(BF16).astype(F32)
-    for i in range(n_rep * cap):
-        spread[pl.ds(i * rank, rank), :] = jnp.where(wanted[...] == variants[i], total, 0.0).astype(BF16)
+    member[...] = jnp.zeros_like(member)
+    for i in range(listed):
+        if n_blocks == 1:
+            name = names[i]
+        else:
+            name = names[lax.rem(me - i // cap + n_rep, n_rep) * cap + i % cap]
+        member[i : i + 1, :] = jnp.where(wanted[...] == name, 1.0, 0.0)
+    total = jnp.sum(shrunk[...], axis=0).astype(BF16)
+    entry = lax.broadcasted_iota(jnp.int32, (member.shape[0], listed * rank), 0)
+    column = lax.broadcasted_iota(jnp.int32, (member.shape[0], listed * rank), 1)
+    to_entry = jnp.where(column // rank == entry, 1.0, 0.0).astype(BF16)
+    part = lax.broadcasted_iota(jnp.int32, (rank, listed * rank), 0)
+    column = lax.broadcasted_iota(jnp.int32, (rank, listed * rank), 1)
+    to_part = jnp.where(lax.rem(column, rank) == part, 1.0, 0.0).astype(BF16)
+    turned = (((0,), (0,)), ((), ()))
+    named = lax.dot_general(member[...].astype(BF16), to_entry, turned, preferred_element_type=F32)
+    copied = lax.dot_general(total, to_part, turned, preferred_element_type=F32)
+    spread = (named * copied).astype(BF16)
     for s in range(n_blocks):
         expand[pl.ds(s * size, size), :] = blocks[s][...]
-    result[...] = lax.dot_general(
-        spread[...], expand[...], (((0,), (0,)), ((), ())), preferred_element_type=F32
-    )
-    chip, core, _ = position()
+    result[...] = jnp.dot(spread, expand[...], preferred_element_type=F32)
     for out, c in ((straight, core), (cross, 1 - core)):
         rows = pl.ds(pl.multiple_of(c * own, own), own)
         base = late_own[rows, :].astype(F32) + late_recv[rows, :].astype(F32)
@@ -356,31 +353,30 @@
     send[:, start:] = result[pl.ds((2 * chip + 1 - core) * own, own), :].astype(BF16)
 
 
-def delta(slot, lists, wanted, shrunk, late, blocks, cut, n_rep, cap, pool_dev, rank, own, before=(), after=()):
+def delta(names, wanted, shrunk, late, blocks, cut, n_rep, cap, rank, own, before=(), after=()):
     rows = wanted.shape[1]
     start, stop = cut
     width = stop - start
-    return pl.pallas_call(
-        functools.partial(delta_kernel, len(blocks), n_rep, cap, pool_dev, rank, len(before)),
+    listed = n_rep * cap
+    return pl.pallas_call(
+        functools.partial(delta_kernel, len(blocks), n_rep, cap, rank, len(before)),
         out_shape=[in_hbm((own, width))] * 2 + [in_hbm((own, stop))] * 2,
         grid=(1,),
-        in_specs=[SMEM] * 2
+        in_specs=[SMEM]
         + [VMEM] * 2
         + [pl.BlockSpec((2 * own, width), lambda i: (0, start // width))] * 2
         + [VMEM] * (len(blocks) + len(before))
         + [ANY] * len(after),
         out_specs=[VMEM] * 4,
         scratch_shapes=[
-            pltpu.VMEM((n_rep * cap * rank, rows), BF16),
-            pltpu.VMEM((n_rep * cap * rank, width), BF16),
+            pltpu.VMEM((-(-listed // 16) * 16, rows), F32),
+            pltpu.VMEM((listed * rank, width), BF16),
             pltpu.VMEM((rows, width), F32),
-            pltpu.SMEM((n_rep * cap,), jnp.int32),
-            pltpu.SMEM((n_rep,), jnp.int32),
         ],
         compiler_params=params(),
         cost_estimate=order(0),
         name="delta",
-    )(*pin(slot, lists, wanted), shrunk, *pin(late[0]), late[1], *pin(blocks[0]), *blocks[1:], *pin(*before), *pin(*after))
+    )(*pin(names, wanted), shrunk, *pin(late[0]), late[1], *pin(blocks[0]), *blocks[1:], *pin(*before), *pin(*after))
 
 
 def gate_kernel(*refs):
@@ -476,8 +472,7 @@
     pool_dev, rank, width = shrink_pool.shape
     cap = pool_dev // 4 + 2
     stream = residual[0]
-    lists = (pool_slot, variant_list)
-    sizes = (cap, pool_dev, rank)
+    sizes = (cap, rank)
     tile = min(1024, width)
     cut = width // 2
     cuts = ((0, cut), (cut, width))
@@ -495,14 +490,16 @@
         return lax.ppermute(x, "rep", [(i, (i + shift) % n_rep) for i in range(n_rep)])
 
     shifts = [s for s in range(1, n_rep) if s != n_rep // 2] + [n_rep // 2]
-    chosen, token = select(pool_slot, variant_list, shrink_pool, (), ((0, width),), n_rep, cap)
+    chosen, token = select(pool_slot, variant_list, shrink_pool, (), ((0, width),), False, n_rep, cap)
     shrink = lax.all_to_all(chosen, "rep", 0, 0, tiled=True).reshape(n_rep * cap * rank, width)
 
     keep0, send0, keep1, send1, token = product_early(features, projection, tile, [token])
     sums = [keep0 + over_core(send0), keep1 + over_core(send1)]
     early = [over_chip(x) for x in sums]
 
-    *chosen, second, token = select(pool_slot, variant_list, expand_pool, cuts[:1], cuts[1:], n_rep, cap, sums)
+    *chosen, second, names, token = select(
+        pool_slot, variant_list, expand_pool, cuts[:1], cuts[1:], True, n_rep, cap, sums
+    )
     first = [chosen[0]] + [None] * (n_rep - 1)
     for s in shifts:
         first[s] = over_rep(chosen[s], s)
@@ -512,10 +509,10 @@
     late = (late_keep, over_core(late_send))
     near_base = (keep, over_core(send))
 
-    part = score(*lists, request_variant, features, shrink, n_rep, *sizes, [token, early[0]])
+    part = score(names, request_variant, features, shrink, rank, [token, early[0]])
     shrunk = lax.all_gather(part, "tp")
 
-    common = (*lists, request_variant, shrunk, late)
+    common = (names, request_variant, shrunk, late)
     straight, cross, *before = delta(*common, first, cuts[0], n_rep, *sizes, own, (), [early[1]])
     far = [over_chip(straight), over_both(cross)]
     straight, cross, mine, send = delta(*common, [second], cuts[1], n_rep, *sizes, own, before, [near_base[1]])

time: 114 us -> 114 us (level)
  no operation moved by 1% of the time
where the time goes in v9:
time: 114 us; the launch traced here: 113 us
  Pallas kernels  70.2 us (62%)
  starting transfers between devices  23.4 us (21%)
  waiting for transfers between devices  8.7 us (8%)
  blocking collectives  5.79 us (5%)
  local copies, waits for them, and re-layouts  2.53 us (2%)
  other arithmetic  2.4 us (2%)
    pallas_call x1, Pallas kernels, product_columns(): pl.pallas_call(kernel, out_shape=[in_hbm((half, width))] * 2 + [in_hbm((2...  18.4 us
    pallas_call x1, Pallas kernels, product_early(): pl.pallas_call(kernel, out_shape=[sds((half // 2, width))] * 4 + [TOKEN],...  11.5 us
    pallas_call x1, Pallas kernels, product(): pl.pallas_call(kernel, out_shape=[in_hbm(shape) if blocks > 1 else sds(sh...  11.4 us
    pallas_call x3, Pallas kernels, finish(): pl.pallas_call(near_kernel if near else far_kernel, out_shape=sds((own, f...  10.8 us
    pallas_call x2, Pallas kernels, delta(): pl.pallas_call(functools.partial(delta_kernel, len(blocks), n_rep, cap, r...  9.47 us
    all_to_all x1, starting transfers between devices, paired(): lax.all_to_all(chosen, 'rep', 0, 0, tiled=True)  6.32 us
    ppermute x3, starting transfers between devices, over_rep(): lax.ppermute(x, 'rep', [(i, (i + shift) % n_rep) for i in range(n_rep)])  5.9 us
    pallas_call x2, Pallas kernels, select(): pl.pallas_call(functools.partial(select_kernel, by_shift, by_target, int(...  5.83 us
  transfers between devices with their start and end apart: 17, of which 4 were waited for; matrix products, arithmetic and copies ran while one was open for 2% of the time, Pallas kernels for 57%

profile of v9, /device:TPU:0, one launch (start us, length us, event | category | flops | bytes accessed | tf_op | source)
XLA Modules:
  0.0 113.2 jit_solution(13805998857296736401)
XLA Ops:
  0.0 2.8 %select.2 = (bf16[4,96,2048]{2,1,0:T(8,128)(2,1)}, f32[8,128]{1,0:T(8,128)}) custom-call(s32[64]{0:T(128)} %slot.3, s32[4,24]{1,0:T(4,128)} %lists.3, bf16[16,16,2048]{2,1,0:T(8,128)(2,1)} %pool.2), custom_call_target="tpu_custom_call" | custom-call | flops 1 | bytes 1 | tf_op jit(solution)/shard_map/select/pallas_call | solution.py:109
  2.8 6.3 %all-to-all-start = ((bf16[4,96,2048]{2,1,0:T(8,128)(2,1)}), bf16[4,96,2048]{2,1,0:T(8,128)(2,1)}, u32[]{:S(2)}, u32[]{:S(2)}) async-start(bf16[4,96,2048]{2,1,0:T(8,128)(2,1)} %get-tuple-element.42), calls=%async_computation | async-start | bytes 3145728 | tf_op jit(solution)/shard_map/all_to_all | solution.py:494
  9.2 11.5 %product.3 = (bf16[192,2048]{1,0:T(8,128)(2,1)S(1)}, bf16[192,2048]{1,0:T(8,128)(2,1)S(1)}, bf16[192,2048]{1,0:T(8,128)(2,1)S(1)}, bf16[192,2048]{1,0:T(8,128)(2,1)S(1)}, f32[8,128]{1,0:T(8,128)}) custom-call(bf16[768,2048]{1,0:T(8,128)(2,1)} %bitcast.6, bf16[2048,8192]{1,0:T(8,128)(2,1)} %weights.5, f32[8,128]{1,0:T(8,128)} %get-tuple-element.36.rest_0_), custom_call_target="tpu_custom_call" | custom-call | flops 1 | bytes 1 | tf_op jit(solution)/shard_map/product/pallas_call | solution.py:147
  21.1 1.8 %collective-permute-done = bf16[192,2048]{1,0:T(8,128)(2,1)S(1)} collective-permute-done((bf16[192,2048]{1,0:T(8,128)(2,1)S(1)}, bf16[192,2048]{1,0:T(8,128)(2,1)S(1)}, u32[]{:S(2)}, u32[]{:S(2)}) %collective-permute-start) | collective-permute-done | bytes 786464 | tf_op jit(solution)/shard_map/ppermute | solution.py:481
  24.1 1.5 %collective-permute-start.2 = (bf16[192,2048]{1,0:T(8,128)(2,1)}, bf16[192,2048]{1,0:T(8,128)(2,1)}, u32[]{:S(2)}, u32[]{:S(2)}) collective-permute-start(bf16[192,2048]{1,0:T(8,128)(2,1)} %add.6.rest_0_), channel_id=1, source_target_pairs={{0,8},{8,0},{4,12},{12,4},{1,9},{9,1},{5,13},{13,5},{2,10},{10,2},... | collective-permute-start | bytes 2359304 | tf_op jit(solution)/shard_map/ppermute | solution.py:484
  26.8 3.0 %select.3 = (bf16[96,1024]{1,0:T(8,128)(2,1)}, bf16[96,1024]{1,0:T(8,128)(2,1)}, bf16[96,1024]{1,0:T(8,128)(2,1)}, bf16[96,1024]{1,0:T(8,128)(2,1)}, bf16[4,96,1...) custom-call(s32[64]{0:T(128)} %slot.3, s32[4,24]{1,0:T(4,128)} %lists.3, bf16[16,16,2048]{2,1,0:T(8,128)(2,1)} %pool.3, ...), custom_call_target="tpu_custom_call" | custom-call | flops 1 | bytes 1 | tf_op jit(solution)/shard_map/select/pallas_call | solution.py:109
  29.8 2.1 %collective-permute-start.4 = (bf16[96,1024]{1,0:T(8,128)(2,1)}, bf16[96,1024]{1,0:T(8,128)(2,1)S(1)}, u32[]{:S(2)}, u32[]{:S(2)}) collective-permute-start(bf16[96,1024]{1,0:T(8,128)(2,1)} %get-tuple-element.49), channel_id=1, source_target_pairs={{0,1},{1,2},{2,3},{3,0},{4,5},{5,6},{6,7},{7,4},{8,9},{9,10},{10,1... | collective-permute-start | bytes 589832 | tf_op jit(solution)/shard_map/ppermute | solution.py:490
  32.4 2.4 %collective-permute-start.5 = (bf16[96,1024]{1,0:T(8,128)(2,1)}, bf16[96,1024]{1,0:T(8,128)(2,1)}, u32[]{:S(2)}, u32[]{:S(2)}) collective-permute-start(bf16[96,1024]{1,0:T(8,128)(2,1)} %get-tuple-element.50), channel_id=1, source_target_pairs={{0,2},{1,3},{2,0},{3,1},{4,6},{5,7},{6,4},{7,5},{8,10},{9,11},{10,... | collective-permute-start | bytes 589832 | tf_op jit(solution)/shard_map/ppermute | solution.py:490
  34.8 1.5 %collective-permute-start.6 = (bf16[96,1024]{1,0:T(8,128)(2,1)}, bf16[96,1024]{1,0:T(8,128)(2,1)}, u32[]{:S(2)}, u32[]{:S(2)}) collective-permute-start(bf16[96,1024]{1,0:T(8,128)(2,1)} %get-tuple-element.51), channel_id=1, source_target_pairs={{0,3},{1,0},{2,1},{3,2},{4,7},{5,4},{6,5},{7,6},{8,11},{9,8},{10,9... | collective-permute-start | bytes 589832 | tf_op jit(solution)/shard_map/ppermute | solution.py:490
  36.3 18.4 %product.4 = (bf16[384,2048]{1,0:T(8,128)(2,1)}, bf16[384,2048]{1,0:T(8,128)(2,1)}, bf16[2,192,2048]{2,1,0:T(8,128)(2,1)}, bf16[2,192,2048]{2,1,0:T(8,128)(2,1)}, f32[8,128]{1,0:T(8,128)}) custom-call(bf16[768,2048]{1,0:T(8,128)(2,1)S(1)} %bitcast.7, bf16[2048,8192]{1,0:T(8,128)(2,1)} %weights.5, bf16[192,2048]{1,0:T(8,128)(2,1)} %add.6.rest_0_, ...), custom_call_target="tpu_custom_call" | custom-call | flops 1 | bytes 1 | tf_op jit(solution)/shard_map/product/pallas_call | solution.py:205
  55.7 4.2 %all-to-all-start.1 = ((bf16[4,96,1024]{2,1,0:T(8,128)(2,1)}), bf16[4,96,1024]{2,1,0:T(8,128)(2,1)}, u32[]{:S(2)}, u32[]{:S(2)}) async-start(bf16[4,96,1024]{2,1,0:T(8,128)(2,1)} %get-tuple-element.47), calls=%async_computation.1 | async-start | bytes 1572864 | tf_op jit(solution)/shard_map/all_to_all | solution.py:506
  60.5 2.8 %score.1 = f32[16,768]{1,0:T(8,128)S(1)} custom-call(s32[24]{0:T(128)} %get-tuple-element.41.names, s32[1,768]{1,0:T(1,128)} %wanted.5, bf16[768,2048]{1,0:T(8,128)(2,1)S(1)} %bitcast.8, bf16[384,2048]{1,0:T(8,128)(2,1)} %bitcast.2.factors, f32[8,128]{1,0:T(8,128)} %get-tuple-element.44.rest_0_, bf16[192,2048]{1,0:T(8,128)(2,1)} %collective-permute-done.2.rest_1_.first), custom_call_target="tpu_custom_call" | custom-call | flops 46000001024 | bytes 1 | tf_op jit(solution)/shard_map/score/pallas_call | solution.py:304
  63.4 5.8 %all-gather = f32[64,768]{1,0:T(8,128)S(1)} all-gather(f32[16,768]{1,0:T(8,128)S(1)} %score.1), channel_id=2, replica_groups=mesh['groups'=2,'tp'=4,'rep'=4] {'tp'}, dimensions={0}, use_global_device_ids=true | all-gather | bytes 245760 | tf_op jit(solution)/shard_map/all_gather | solution.py:513
  69.2 4.8 %delta.2 = (bf16[192,1024]{1,0:T(8,128)(2,1)}, bf16[192,1024]{1,0:T(8,128)(2,1)}, bf16[192,1024]{1,0:T(8,128)(2,1)}, bf16[192,1024]{1,0:T(8,128)(2,1)}) custom-call(s32[24]{0:T(128)} %get-tuple-element.41.names, s32[1,768]{1,0:T(1,128)} %wanted.5, f32[4,16,768]{2,1,0:T(8,128)S(1)} %bitcast.10, bf16[384,2048]{1,0:T(8,128)(2,1)} %get-tuple-element.45.late_own, ...), custom_call_target="tpu_custom_call" | custom-call | flops 1 | bytes 1 | tf_op jit(solution)/shard_map/delta/pallas_call | solution.py:361
  74.0 1.5 %collective-permute-start.12 = (bf16[192,1024]{1,0:T(8,128)(2,1)}, bf16[192,1024]{1,0:T(8,128)(2,1)}, u32[]{:S(2)}, u32[]{:S(2)}) collective-permute-start(bf16[192,1024]{1,0:T(8,128)(2,1)} %get-tuple-element.60), channel_id=1, source_target_pairs={{0,8},{8,0},{4,12},{12,4},{1,9},{9,1},{5,13},{13,5},{2,10},{10,2},... | collective-permute-start | bytes 1179656 | tf_op jit(solution)/shard_map/ppermute | solution.py:484
  75.7 4.3 %all-to-all-done.1 = bf16[4,96,1024]{2,1,0:T(8,128)(2,1)} async-done(((bf16[4,96,1024]{2,1,0:T(8,128)(2,1)}), bf16[4,96,1024]{2,1,0:T(8,128)(2,1)}, u32[]{:S(2)}, u32[]{:S(2)}) %all-to-all-start.1) | async-done | bytes 786464 | tf_op jit(solution)/shard_map/all_to_all | solution.py:506
  80.0 1.4 %copy-done.2 = bf16[384,2048]{1,0:T(8,128)(2,1)S(1)} copy-done((bf16[384,2048]{1,0:T(8,128)(2,1)S(1)}, bf16[384,2048]{1,0:T(8,128)(2,1)}, u32[]{:S(2)}) %copy-start.2) | copy-done | bytes 1572888
  81.4 4.7 %delta.3 = (bf16[192,1024]{1,0:T(8,128)(2,1)}, bf16[192,1024]{1,0:T(8,128)(2,1)}, bf16[192,2048]{1,0:T(8,128)(2,1)}, bf16[192,2048]{1,0:T(8,128)(2,1)}) custom-call(s32[24]{0:T(128)} %get-tuple-element.41.names, s32[1,768]{1,0:T(1,128)} %wanted.5, f32[4,16,768]{2,1,0:T(8,128)S(1)} %bitcast.11, bf16[384,2048]{1,0:T(8,128)(2,1)} %get-tuple-element.45.late_own, ...), custom_call_target="tpu_custom_call" | custom-call | flops 1 | bytes 1 | tf_op jit(solution)/shard_map/delta/pallas_call | solution.py:361
  86.1 1.5 %collective-permute-start.10 = (bf16[192,1024]{1,0:T(8,128)(2,1)}, bf16[192,1024]{1,0:T(8,128)(2,1)}, u32[]{:S(2)}, u32[]{:S(2)}) collective-permute-start(bf16[192,1024]{1,0:T(8,128)(2,1)} %get-tuple-element.58), channel_id=1, source_target_pairs={{0,8},{8,0},{4,12},{12,4},{1,9},{9,1},{5,13},{13,5},{2,10},{10,2},... | collective-permute-start | bytes 1179656 | tf_op jit(solution)/shard_map/ppermute | solution.py:484
  88.2 11.4 %product.5 = (bf16[2,192,2048]{2,1,0:T(8,128)(2,1)}, bf16[2,192,2048]{2,1,0:T(8,128)(2,1)}, f32[8,128]{1,0:T(8,128)}) custom-call(bf16[768,2048]{1,0:T(8,128)(2,1)S(1)} %bitcast.9, bf16[2048,8192]{1,0:T(8,128)(2,1)} %weights.5, bf16[192,2048]{1,0:T(8,128)(2,1)} %get-tuple-element.55.rest_0_.mine), custom_call_target="tpu_custom_call" | custom-call | flops 1 | bytes 1 | tf_op jit(solution)/shard_map/product/pallas_call | solution.py:276
  100.9 5.2 %near.1.rest_0_ = bf16[192,8192]{1,0:T(8,128)(2,1)} custom-call(bf16[192,8192]{1,0:T(8,128)(2,1)} %bitcast.12, bf16[2,192,2048]{2,1,0:T(8,128)(2,1)} %get-tuple-element.65.keep, bf16[2,192,2048]{2,1,0:T(8,128)(2,1)} %collective-permute-done.8.rest_3_.recv, bf16[192,2048]{1,0:T(8,128)(2,1)} %collective-permute-done.2.rest_1_.first, ...), custom_call_target="tpu_custom_call" | custom-call | flops 69000003584 | bytes 1 | tf_op jit(solution)/shard_map/near/pallas_call | solution.py:450
  106.1 2.8 %far.2.rest_0_ = bf16[192,8192]{1,0:T(8,128)(2,1)} custom-call(bf16[192,8192]{1,0:T(8,128)(2,1)} %bitcast.13, bf16[2,192,2048]{2,1,0:T(8,128)(2,1)} %get-tuple-element.56.keep, bf16[2,192,2048]{2,1,0:T(8,128)(2,1)} %collective-permute-done.9.recv, bf16[192,1024]{1,0:T(8,128)(2,1)} %get-tuple-element.63.rest_0_.straight, ...), custom_call_target="tpu_custom_call", output_to_operand_aliasing={{}: (5, {})} | custom-call | flops 69000003584 | bytes 1 | tf_op jit(solution)/shard_map/far/pallas_call | solution.py:450
  108.9 1.5 %collective-permute-done.11.cross = bf16[192,1024]{1,0:T(8,128)(2,1)} collective-permute-done((bf16[192,1024]{1,0:T(8,128)(2,1)}, bf16[192,1024]{1,0:T(8,128)(2,1)}, u32[]{:S(2)}, u32[]{:S(2)}) %collective-permute-start.11) | collective-permute-done | bytes 393248 | tf_op jit(solution)/shard_map/ppermute | solution.py:487
  110.4 2.8 %far.3 = bf16[192,8192]{1,0:T(8,128)(2,1)} custom-call(bf16[192,8192]{1,0:T(8,128)(2,1)} %bitcast.14, bf16[2,192,2048]{2,1,0:T(8,128)(2,1)} %get-tuple-element.56.keep, bf16[2,192,2048]{2,1,0:T(8,128)(2,1)} %collective-permute-done.9.recv, bf16[192,1024]{1,0:T(8,128)(2,1)} %collective-permute-done.10.straight, ...), custom_call_target="tpu_custom_call", output_to_operand_aliasing={{}: (5, {})} | custom-call | flops 69000003584 | bytes 1 | tf_op jit(solution)/shard_map/far/pallas_call | solution.py:450
  (33 shorter events, 7.1 us)
Async XLA Ops:
  2.8 52.9 %all-to-all-start = ((bf16[4,96,2048]{2,1,0:T(8,128)(2,1)}), bf16[4,96,2048]{2,1,0:T(8,128)(2,1)}, u32[]{:S(2)}, u32[]{:S(2)}) async-start(bf16[4,96,2048]{2,1,0:T(8,128)(2,1)} %get-tuple-element.42), calls=%async_computation | async-start | bytes 3145728 | tf_op jit(solution)/shard_map/all_to_all | solution.py:494
  20.6 2.3 %collective-permute-start = (bf16[192,2048]{1,0:T(8,128)(2,1)S(1)}, bf16[192,2048]{1,0:T(8,128)(2,1)S(1)}, u32[]{:S(2)}, u32[]{:S(2)}) collective-permute-start(bf16[192,2048]{1,0:T(8,128)(2,1)S(1)} %get-tuple-element.38), channel_id=1, source_target_pairs={{0,4},{4,0},{8,12},{12,8},{1,5},{5,1},{9,13},{13,9},{2,6},{6,2},{1... | collective-permute-start | bytes 2359304 | tf_op jit(solution)/shard_map/ppermute | solution.py:481
  20.6 5.0 %collective-permute-start.1 = (bf16[192,2048]{1,0:T(8,128)(2,1)S(1)}, bf16[192,2048]{1,0:T(8,128)(2,1)S(1)}, u32[]{:S(2)}, u32[]{:S(2)}) collective-permute-start(bf16[192,2048]{1,0:T(8,128)(2,1)S(1)} %get-tuple-element.40), channel_id=1, source_target_pairs={{0,4},{4,0},{8,12},{12,8},{1,5},{5,1},{9,13},{13,9},{2,6},{6,2},{1... | collective-permute-start | bytes 2359304 | tf_op jit(solution)/shard_map/ppermute | solution.py:481
  24.1 36.0 %collective-permute-start.2 = (bf16[192,2048]{1,0:T(8,128)(2,1)}, bf16[192,2048]{1,0:T(8,128)(2,1)}, u32[]{:S(2)}, u32[]{:S(2)}) collective-permute-start(bf16[192,2048]{1,0:T(8,128)(2,1)} %add.6.rest_0_), channel_id=1, source_target_pairs={{0,8},{8,0},{4,12},{12,4},{1,9},{9,1},{5,13},{13,5},{2,10},{10,2},... | collective-permute-start | bytes 2359304 | tf_op jit(solution)/shard_map/ppermute | solution.py:484
  25.6 10.7 %copy-start = (bf16[1,768,2048]{2,1,0:T(8,128)(2,1)S(1)}, bf16[1,768,2048]{2,1,0:T(8,128)(2,1)}, u32[]{:S(2)}) copy-start(bf16[1,768,2048]{2,1,0:T(8,128)(2,1)} %param.8) | copy-start | bytes 9437188
  29.8 30.1 %collective-permute-start.4 = (bf16[96,1024]{1,0:T(8,128)(2,1)}, bf16[96,1024]{1,0:T(8,128)(2,1)S(1)}, u32[]{:S(2)}, u32[]{:S(2)}) collective-permute-start(bf16[96,1024]{1,0:T(8,128)(2,1)} %get-tuple-element.49), channel_id=1, source_target_pairs={{0,1},{1,2},{2,3},{3,0},{4,5},{5,6},{6,7},{7,4},{8,9},{9,10},{10,1... | collective-permute-start | bytes 589832 | tf_op jit(solution)/shard_map/ppermute | solution.py:490
  31.9 37.3 %collective-permute-start.7 = (bf16[192,2048]{1,0:T(8,128)(2,1)}, bf16[192,2048]{1,0:T(8,128)(2,1)}, u32[]{:S(2)}, u32[]{:S(2)}) collective-permute-start(bf16[192,2048]{1,0:T(8,128)(2,1)} %add.7.rest_1_), channel_id=1, source_target_pairs={{0,8},{8,0},{4,12},{12,4},{1,9},{9,1},{5,13},{13,5},{2,10},{10,2},... | collective-permute-start | bytes 2359304 | tf_op jit(solution)/shard_map/ppermute | solution.py:484
  32.4 36.8 %collective-permute-start.5 = (bf16[96,1024]{1,0:T(8,128)(2,1)}, bf16[96,1024]{1,0:T(8,128)(2,1)}, u32[]{:S(2)}, u32[]{:S(2)}) collective-permute-start(bf16[96,1024]{1,0:T(8,128)(2,1)} %get-tuple-element.50), channel_id=1, source_target_pairs={{0,2},{1,3},{2,0},{3,1},{4,6},{5,7},{6,4},{7,5},{8,10},{9,11},{10,... | collective-permute-start | bytes 589832 | tf_op jit(solution)/shard_map/ppermute | solution.py:490
  34.8 34.4 %collective-permute-start.6 = (bf16[96,1024]{1,0:T(8,128)(2,1)}, bf16[96,1024]{1,0:T(8,128)(2,1)}, u32[]{:S(2)}, u32[]{:S(2)}) collective-permute-start(bf16[96,1024]{1,0:T(8,128)(2,1)} %get-tuple-element.51), channel_id=1, source_target_pairs={{0,3},{1,0},{2,1},{3,2},{4,7},{5,4},{6,5},{7,6},{8,11},{9,8},{10,9... | collective-permute-start | bytes 589832 | tf_op jit(solution)/shard_map/ppermute | solution.py:490
  55.7 24.2 %all-to-all-start.1 = ((bf16[4,96,1024]{2,1,0:T(8,128)(2,1)}), bf16[4,96,1024]{2,1,0:T(8,128)(2,1)}, u32[]{:S(2)}, u32[]{:S(2)}) async-start(bf16[4,96,1024]{2,1,0:T(8,128)(2,1)} %get-tuple-element.47), calls=%async_computation.1 | async-start | bytes 1572864 | tf_op jit(solution)/shard_map/all_to_all | solution.py:506
  60.0 9.2 %collective-permute-start.3 = (bf16[384,2048]{1,0:T(8,128)(2,1)}, bf16[384,2048]{1,0:T(8,128)(2,1)S(1)}, u32[]{:S(2)}, u32[]{:S(2)}) collective-permute-start(bf16[384,2048]{1,0:T(8,128)(2,1)} %get-tuple-element.46), channel_id=1, source_target_pairs={{0,4},{4,0},{8,12},{12,8},{1,5},{5,1},{9,13},{13,9},{2,6},{6,2},{1... | collective-permute-start | bytes 4718600 | tf_op jit(solution)/shard_map/ppermute | solution.py:481
  60.0 19.9 %collective-permute-start.8 = (bf16[2,192,2048]{2,1,0:T(8,128)(2,1)}, bf16[2,192,2048]{2,1,0:T(8,128)(2,1)}, u32[]{:S(2)}, u32[]{:S(2)}) collective-permute-start(bf16[2,192,2048]{2,1,0:T(8,128)(2,1)} %get-tuple-element.54), channel_id=1, source_target_pairs={{0,4},{4,0},{8,12},{12,8},{1,5},{5,1},{9,13},{13,9},{2,6},{6,2},{1... | collective-permute-start | bytes 4718600 | tf_op jit(solution)/shard_map/ppermute | solution.py:481
  69.2 4.8 %copy-start.1 = (bf16[384,2048]{1,0:T(8,128)(2,1)}, bf16[384,2048]{1,0:T(8,128)(2,1)S(1)}, u32[]{:S(2)}) copy-start(bf16[384,2048]{1,0:T(8,128)(2,1)S(1)} %collective-permute-done.3.late_recv) | copy-start | bytes 4718596
  74.0 25.6 %collective-permute-start.12 = (bf16[192,1024]{1,0:T(8,128)(2,1)}, bf16[192,1024]{1,0:T(8,128)(2,1)}, u32[]{:S(2)}, u32[]{:S(2)}) collective-permute-start(bf16[192,1024]{1,0:T(8,128)(2,1)} %get-tuple-element.60), channel_id=1, source_target_pairs={{0,8},{8,0},{4,12},{12,4},{1,9},{9,1},{5,13},{13,5},{2,10},{10,2},... | collective-permute-start | bytes 1179656 | tf_op jit(solution)/shard_map/ppermute | solution.py:484
  75.5 24.2 %collective-permute-start.13 = (bf16[192,1024]{1,0:T(8,128)(2,1)}, bf16[192,1024]{1,0:T(8,128)(2,1)}, u32[]{:S(2)}, u32[]{:S(2)}) collective-permute-start(bf16[192,1024]{1,0:T(8,128)(2,1)} %get-tuple-element.61), channel_id=1, source_target_pairs={{0,12},{12,0},{4,8},{8,4},{1,13},{13,1},{5,9},{9,5},{2,14},{14,2},... | collective-permute-start | bytes 1179656 | tf_op jit(solution)/shard_map/ppermute | solution.py:487
  80.0 1.4 %copy-start.2 = (bf16[384,2048]{1,0:T(8,128)(2,1)S(1)}, bf16[384,2048]{1,0:T(8,128)(2,1)}, u32[]{:S(2)}) copy-start(bf16[384,2048]{1,0:T(8,128)(2,1)} %copy-done.1) | copy-start | bytes 4718596
  86.1 22.8 %collective-permute-start.10 = (bf16[192,1024]{1,0:T(8,128)(2,1)}, bf16[192,1024]{1,0:T(8,128)(2,1)}, u32[]{:S(2)}, u32[]{:S(2)}) collective-permute-start(bf16[192,1024]{1,0:T(8,128)(2,1)} %get-tuple-element.58), channel_id=1, source_target_pairs={{0,8},{8,0},{4,12},{12,4},{1,9},{9,1},{5,13},{13,5},{2,10},{10,2},... | collective-permute-start | bytes 1179656 | tf_op jit(solution)/shard_map/ppermute | solution.py:484
  87.6 22.8 %collective-permute-start.11 = (bf16[192,1024]{1,0:T(8,128)(2,1)}, bf16[192,1024]{1,0:T(8,128)(2,1)}, u32[]{:S(2)}, u32[]{:S(2)}) collective-permute-start(bf16[192,1024]{1,0:T(8,128)(2,1)} %get-tuple-element.59), channel_id=1, source_target_pairs={{0,12},{12,0},{4,8},{8,4},{1,13},{13,1},{5,9},{9,5},{2,14},{14,2},... | collective-permute-start | bytes 1179656 | tf_op jit(solution)/shard_map/ppermute | solution.py:487
  87.6 12.2 %collective-permute-start.14 = (bf16[192,2048]{1,0:T(8,128)(2,1)}, bf16[192,2048]{1,0:T(8,128)(2,1)}, u32[]{:S(2)}, u32[]{:S(2)}) collective-permute-start(bf16[192,2048]{1,0:T(8,128)(2,1)} %get-tuple-element.66), channel_id=1, source_target_pairs={{0,4},{4,0},{8,12},{12,8},{1,5},{5,1},{9,13},{13,9},{2,6},{6,2},{1... | collective-permute-start | bytes 2359304 | tf_op jit(solution)/shard_map/ppermute | solution.py:481
  99.6 6.4 %collective-permute-start.9 = (bf16[2,192,2048]{2,1,0:T(8,128)(2,1)}, bf16[2,192,2048]{2,1,0:T(8,128)(2,1)}, u32[]{:S(2)}, u32[]{:S(2)}) collective-permute-start(bf16[2,192,2048]{2,1,0:T(8,128)(2,1)} %get-tuple-element.57), channel_id=1, source_target_pairs={{0,4},{4,0},{8,12},{12,8},{1,5},{5,1},{9,13},{13,9},{2,6},{6,2},{1... | collective-permute-start | bytes 4718600 | tf_op jit(solution)/shard_map/ppermute | solution.py:481
  99.7 1.1 %copy-start.3 = (bf16[192,2048]{1,0:T(8,128)(2,1)S(1)}, bf16[192,2048]{1,0:T(8,128)(2,1)}, u32[]{:S(2)}) copy-start(bf16[192,2048]{1,0:T(8,128)(2,1)} %get-tuple-element.55.rest_0_.mine) | copy-start | bytes 2359300

commit v10 on v9

--- a/solution.py
+++ b/solution.py
@@ -62,8 +62,10 @@
 
 
 def select_kernel(by_shift, by_target, named, n_rep, cap, pool_dev, rank, slot, lists, pool, *rest):
-    token, idx, counts = rest[-3:]
-    outs = rest[: -3]
+    token, idx, counts, sems = rest[-4:]
+    outs = rest[:-4]
+    direct = not by_shift
+    copies = []
     outs = outs[-(n_rep * len(by_shift) + len(by_target) + named) :]
     token[...] = jnp.zeros_like(token)
     me = lax.axis_index("rep")
@@ -73,17 +75,25 @@
         for k in range(cap + 1):
             idx[k] = 0
         count = jnp.int32(0)
-        for l in range(lists.shape[1]):
-            place = slot[lists[target, l]] - base
+        for place in [slot[lists[target, l]] - base for l in range(lists.shape[1])]:
             idx[jnp.minimum(count, cap)] = place
             count = count + jnp.where((place >= 0) & (place < pool_dev), 1, 0)
         for k in range(cap):
             entry = jnp.clip(idx[k], 0, pool_dev - 1)
             rows = pl.ds(k * rank, rank)
+            if direct:
+                copy = pltpu.make_async_copy(
+                    pool.at[entry], outs[0].at[target, rows, :], sems.at[shift * cap + k]
+                )
+                copy.start()
+                copies.append(copy)
+                continue
             for c, (start, stop) in enumerate(by_shift):
                 outs[c * n_rep + shift][rows, :] = pool[entry, :, start:stop]
             for c, (start, stop) in enumerate(by_target):
                 outs[len(by_shift) * n_rep + c][target, rows, :] = pool[entry, :, start:stop]
+    for copy in copies:
+        copy.wait()
     if named:
         names = outs[-1]
         for i in range(n_rep * cap):
@@ -102,7 +112,7 @@
     pool_dev, rank, width = pool.shape
     shapes = [in_hbm((cap * rank, stop - start)) for start, stop in by_shift for _ in range(n_rep)]
     shapes += [in_hbm((n_rep, cap * rank, stop - start)) for start, stop in by_target]
-    specs = [VMEM] * len(shapes)
+    specs = [VMEM if by_shift else ANY] * len(shapes)
     if named:
         shapes.append(in_hbm((n_rep * cap,), jnp.int32))
         specs.append(SMEM)
@@ -111,7 +121,11 @@
         out_shape=[*shapes, TOKEN],
         in_specs=[SMEM, SMEM, VMEM] + [ANY] * len(after),
         out_specs=[*specs, VMEM],
-        scratch_shapes=[pltpu.SMEM((cap + 1,), jnp.int32), pltpu.SMEM((n_rep,), jnp.int32)],
+        scratch_shapes=[
+            pltpu.SMEM((cap + 1,), jnp.int32),
+            pltpu.SMEM((n_rep,), jnp.int32),
+            pltpu.SemaphoreType.DMA((n_rep * cap,)),
+        ],
         compiler_params=params(16),
         cost_estimate=order(0),
         name="select",
@@ -313,70 +327,79 @@
     )(*pin(names, wanted), features, *pin(factors), *pin(*after))
 
 
-def delta_kernel(n_blocks, n_rep, cap, rank, n_before, names, wanted, shrunk, late_own, late_recv, *rest):
+def delta_kernel(n_blocks, n_before, n_rep, cap, rank, names, wanted, shrunk, late_own, late_recv, *rest):
     blocks, before = rest[:n_blocks], rest[n_blocks : n_blocks + n_before]
-    straight, cross, mine, send, member, expand, result = rest[-7:]
+    straight, cross = rest[-7:-5] if before else rest[-5:-3]
+    member, expand, result = rest[-3:]
     chip, core, me = position()
     listed = n_rep * cap
-    size = listed * rank // n_blocks
-    own, width = straight.shape
-    member[...] = jnp.zeros_like(member)
-    for i in range(listed):
-        if n_blocks == 1:
-            name = names[i]
-        else:
-            name = names[lax.rem(me - i // cap + n_rep, n_rep) * cap + i % cap]
-        member[i : i + 1, :] = jnp.where(wanted[...] == name, 1.0, 0.0)
-    total = jnp.sum(shrunk[...], axis=0).astype(BF16)
-    entry = lax.broadcasted_iota(jnp.int32, (member.shape[0], listed * rank), 0)
-    column = lax.broadcasted_iota(jnp.int32, (member.shape[0], listed * rank), 1)
-    to_entry = jnp.where(column // rank == entry, 1.0, 0.0).astype(BF16)
-    part = lax.broadcasted_iota(jnp.int32, (rank, listed * rank), 0)
-    column = lax.broadcasted_iota(jnp.int32, (rank, listed * rank), 1)
-    to_part = jnp.where(lax.rem(column, rank) == part, 1.0, 0.0).astype(BF16)
-    turned = (((0,), (0,)), ((), ()))
-    named = lax.dot_general(member[...].astype(BF16), to_entry, turned, preferred_element_type=F32)
-    copied = lax.dot_general(total, to_part, turned, preferred_element_type=F32)
-    spread = (named * copied).astype(BF16)
-    for s in range(n_blocks):
-        expand[pl.ds(s * size, size), :] = blocks[s][...]
-    result[...] = jnp.dot(spread, expand[...], preferred_element_type=F32)
+    half = late_own.shape[0]
+    own = half // 2
+
+    def product_of(factors, rows):
+        columns = pl.ds(pl.multiple_of(rows * half, half), half)
+        asked = wanted[:, columns]
+        member[...] = jnp.zeros_like(member)
+        for i in range(listed):
+            if len(factors) == 1:
+                name = names[i]
+            else:
+                name = names[lax.rem(me - i // cap + n_rep, n_rep) * cap + i % cap]
+            member[i : i + 1, :] = jnp.where(asked == name, 1.0, 0.0)
+        total = jnp.sum(shrunk[:, :, columns], axis=0).astype(BF16)
+        entry = lax.broadcasted_iota(jnp.int32, (member.shape[0], listed * rank), 0)
+        column = lax.broadcasted_iota(jnp.int32, (member.shape[0], listed * rank), 1)
+        to_entry = jnp.where(column // rank == entry, 1.0, 0.0).astype(BF16)
+        part = lax.broadcasted_iota(jnp.int32, (rank, listed * rank), 0)
+        column = lax.broadcasted_iota(jnp.int32, (rank, listed * rank), 1)
+        to_part = jnp.where(lax.rem(column, rank) == part, 1.0, 0.0).astype(BF16)
+        turned = (((0,), (0,)), ((), ()))
+        named = lax.dot_general(member[...].astype(BF16), to_entry, turned, preferred_element_type=F32)
+        copied = lax.dot_general(total, to_part, turned, preferred_element_type=F32)
+        size = listed * rank // len(factors)
+        for s, factor in enumerate(factors):
+            expand[pl.ds(s * size, size), :] = factor[...]
+        result[...] = jnp.dot((named * copied).astype(BF16), expand[...], preferred_element_type=F32)
+
+    product_of(blocks, 1 - chip)
     for out, c in ((straight, core), (cross, 1 - core)):
         rows = pl.ds(pl.multiple_of(c * own, own), own)
         base = late_own[rows, :].astype(F32) + late_recv[rows, :].astype(F32)
-        out[...] = (base + result[pl.ds((2 - 2 * chip + c) * own, own), :]).astype(BF16)
-    start = mine.shape[1] - width
+        out[...] = (base + result[rows, :]).astype(BF16)
     if before:
-        mine[:, :start] = before[0][...]
-        send[:, :start] = before[1][...]
-    mine[:, start:] = result[pl.ds((2 * chip + core) * own, own), :].astype(BF16)
-    send[:, start:] = result[pl.ds((2 * chip + 1 - core) * own, own), :].astype(BF16)
+        mine, send = rest[-5], rest[-4]
+        width = straight.shape[1]
+        for start, factors in ((0, before), (mine.shape[1] - width, blocks)):
+            product_of(factors, chip)
+            for out, c in ((mine, core), (send, 1 - core)):
+                rows = pl.ds(pl.multiple_of(c * own, own), own)
+                out[:, start : start + width] = result[rows, :].astype(BF16)
 
 
 def delta(names, wanted, shrunk, late, blocks, cut, n_rep, cap, rank, own, before=(), after=()):
-    rows = wanted.shape[1]
     start, stop = cut
     width = stop - start
     listed = n_rep * cap
-    return pl.pallas_call(
-        functools.partial(delta_kernel, len(blocks), n_rep, cap, rank, len(before)),
-        out_shape=[in_hbm((own, width))] * 2 + [in_hbm((own, stop))] * 2,
+    shapes = [in_hbm((own, width))] * 2 + ([in_hbm((own, stop))] * 2 if before else [])
+    return pl.pallas_call(
+        functools.partial(delta_kernel, len(blocks), len(before), n_rep, cap, rank),
+        out_shape=shapes,
         grid=(1,),
         in_specs=[SMEM]
         + [VMEM] * 2
         + [pl.BlockSpec((2 * own, width), lambda i: (0, start // width))] * 2
         + [VMEM] * (len(blocks) + len(before))
         + [ANY] * len(after),
-        out_specs=[VMEM] * 4,
+        out_specs=[VMEM] * len(shapes),
         scratch_shapes=[
-            pltpu.VMEM((-(-listed // 16) * 16, rows), F32),
+            pltpu.VMEM((-(-listed // 16) * 16, 2 * own), F32),
             pltpu.VMEM((listed * rank, width), BF16),
-            pltpu.VMEM((rows, width), F32),
+            pltpu.VMEM((2 * own, width), F32),
         ],
         compiler_params=params(),
         cost_estimate=order(0),
         name="delta",
-    )(*pin(names, wanted), shrunk, *pin(late[0]), late[1], *pin(blocks[0]), *blocks[1:], *pin(*before), *pin(*after))
+    )(*pin(names, wanted), shrunk, *pin(late[0]), *(pin(late[1]) if before else late[1:]), *pin(*blocks, *before, *after))
 
 
 def gate_kernel(*refs):
@@ -513,9 +536,9 @@
     shrunk = lax.all_gather(part, "tp")
 
     common = (names, request_variant, shrunk, late)
-    straight, cross, *before = delta(*common, first, cuts[0], n_rep, *sizes, own, (), [early[1]])
+    straight, cross = delta(*common, first, cuts[0], n_rep, *sizes, own, (), [early[1]])
     far = [over_chip(straight), over_both(cross)]
-    straight, cross, mine, send = delta(*common, [second], cuts[1], n_rep, *sizes, own, before, [near_base[1]])
+    straight, cross, mine, send = delta(*common, [second], cuts[1], n_rep, *sizes, own, first, [near_base[1], straight])
     last = [over_chip(straight), over_both(cross)]
     theirs = over_core(send)
     keep, send, token = product(features, projection, False, True, 0, 2 * width, tile, 2, [mine])

time: 114 us -> 114 us (level)
  local copies, waits for them, and re-layouts: 2.53 us -> 1.12 us
    unnamed x8, local copies, waits for them, and re-layouts: 2.53 us -> 1.12 us
    ppermute x2, starting transfers between devices: 0.19 us -> 1.47 us  [over_both(): return lax.ppermute(x, 'tp', [(0, 3), (3, 0), (1, 2), (2, 1)])]
where the time goes in v10:
time: 114 us; the launch traced here: 113 us
  Pallas kernels  70.9 us (62%)
  starting transfers between devices  23.7 us (21%)
  waiting for transfers between devices  9.02 us (8%)
  blocking collectives  5.79 us (5%)
  other arithmetic  2.34 us (2%)
    pallas_call x1, Pallas kernels, product_columns(): pl.pallas_call(kernel, out_shape=[in_hbm((half, width))] * 2 + [in_hbm((2...  18.3 us
    pallas_call x1, Pallas kernels, product_early(): pl.pallas_call(kernel, out_shape=[sds((half // 2, width))] * 4 + [TOKEN],...  11.5 us
    pallas_call x1, Pallas kernels, product(): pl.pallas_call(kernel, out_shape=[in_hbm(shape) if blocks > 1 else sds(sh...  11.4 us
    pallas_call x3, Pallas kernels, finish(): pl.pallas_call(near_kernel if near else far_kernel, out_shape=sds((own, f...  10.8 us
    pallas_call x2, Pallas kernels, delta(): pl.pallas_call(functools.partial(delta_kernel, len(blocks), len(before),...  9.54 us
    pallas_call x2, Pallas kernels, select(): pl.pallas_call(functools.partial(select_kernel, by_shift, by_target, int(...  6.54 us
    all_to_all x1, starting transfers between devices, paired(): lax.all_to_all(chosen, 'rep', 0, 0, tiled=True)  6.33 us
    ppermute x3, starting transfers between devices, over_rep(): lax.ppermute(x, 'rep', [(i, (i + shift) % n_rep) for i in range(n_rep)])  5.9 us
  transfers between devices with their start and end apart: 17, of which 4 were waited for; matrix products, arithmetic and copies ran while one was open for 2% of the time, Pallas kernels for 57%

profile of v10, /device:TPU:0, one launch (start us, length us, event | category | flops | bytes accessed | tf_op | source)
XLA Modules:
  0.0 113.0 jit_solution(10526300985041329087)
XLA Ops:
  0.0 3.3 %select.2 = (bf16[4,96,2048]{2,1,0:T(8,128)(2,1)}, f32[8,128]{1,0:T(8,128)}) custom-call(s32[64]{0:T(128)} %slot.3, s32[4,24]{1,0:T(4,128)} %lists.3, bf16[16,16,2048]{2,1,0:T(8,128)(2,1)} %pool.2), custom_call_target="tpu_custom_call" | custom-call | flops 1 | bytes 1 | tf_op jit(solution)/shard_map/select/pallas_call | solution.py:119
  3.3 6.3 %all-to-all-start = ((bf16[4,96,2048]{2,1,0:T(8,128)(2,1)}), bf16[4,96,2048]{2,1,0:T(8,128)(2,1)}, u32[]{:S(2)}, u32[]{:S(2)}) async-start(bf16[4,96,2048]{2,1,0:T(8,128)(2,1)} %get-tuple-element.40), calls=%async_computation | async-start | bytes 3145728 | tf_op jit(solution)/shard_map/all_to_all | solution.py:517
  9.6 11.5 %product.3 = (bf16[192,2048]{1,0:T(8,128)(2,1)S(1)}, bf16[192,2048]{1,0:T(8,128)(2,1)S(1)}, bf16[192,2048]{1,0:T(8,128)(2,1)S(1)}, bf16[192,2048]{1,0:T(8,128)(2,1)S(1)}, f32[8,128]{1,0:T(8,128)}) custom-call(bf16[768,2048]{1,0:T(8,128)(2,1)} %bitcast.6, bf16[2048,8192]{1,0:T(8,128)(2,1)} %weights.5, f32[8,128]{1,0:T(8,128)} %get-tuple-element.34.rest_0_), custom_call_target="tpu_custom_call" | custom-call | flops 1 | bytes 1 | tf_op jit(solution)/shard_map/product/pallas_call | solution.py:161
  21.6 1.8 %collective-permute-done = bf16[192,2048]{1,0:T(8,128)(2,1)S(1)} collective-permute-done((bf16[192,2048]{1,0:T(8,128)(2,1)S(1)}, bf16[192,2048]{1,0:T(8,128)(2,1)S(1)}, u32[]{:S(2)}, u32[]{:S(2)}) %collective-permute-start) | collective-permute-done | bytes 786464 | tf_op jit(solution)/shard_map/ppermute | solution.py:504
  24.5 1.5 %collective-permute-start.2 = (bf16[192,2048]{1,0:T(8,128)(2,1)}, bf16[192,2048]{1,0:T(8,128)(2,1)}, u32[]{:S(2)}, u32[]{:S(2)}) collective-permute-start(bf16[192,2048]{1,0:T(8,128)(2,1)} %add.6.rest_0_), channel_id=1, source_target_pairs={{0,8},{8,0},{4,12},{12,4},{1,9},{9,1},{5,13},{13,5},{2,10},{10,2},... | collective-permute-start | bytes 2359304 | tf_op jit(solution)/shard_map/ppermute | solution.py:507
  26.0 1.2 %add.7.rest_1_ = bf16[192,2048]{1,0:T(8,128)(2,1)} add(bf16[192,2048]{1,0:T(8,128)(2,1)S(1)} %get-tuple-element.37, bf16[192,2048]{1,0:T(8,128)(2,1)S(1)} %collective-permute-done.1) | non-fusion elementwise | flops 393216 | bytes 2359296 | tf_op jit(solution)/shard_map/add | solution.py:520
  27.2 3.3 %select.3 = (bf16[96,1024]{1,0:T(8,128)(2,1)}, bf16[96,1024]{1,0:T(8,128)(2,1)}, bf16[96,1024]{1,0:T(8,128)(2,1)}, bf16[96,1024]{1,0:T(8,128)(2,1)}, bf16[4,96,1...) custom-call(s32[64]{0:T(128)} %slot.3, s32[4,24]{1,0:T(4,128)} %lists.3, bf16[16,16,2048]{2,1,0:T(8,128)(2,1)} %pool.3, ...), custom_call_target="tpu_custom_call" | custom-call | flops 1 | bytes 1 | tf_op jit(solution)/shard_map/select/pallas_call | solution.py:119
  30.5 2.1 %collective-permute-start.4 = (bf16[96,1024]{1,0:T(8,128)(2,1)}, bf16[96,1024]{1,0:T(8,128)(2,1)S(1)}, u32[]{:S(2)}, u32[]{:S(2)}) collective-permute-start(bf16[96,1024]{1,0:T(8,128)(2,1)} %get-tuple-element.47), channel_id=1, source_target_pairs={{0,1},{1,2},{2,3},{3,0},{4,5},{5,6},{6,7},{7,4},{8,9},{9,10},{10,1... | collective-permute-start | bytes 589832 | tf_op jit(solution)/shard_map/ppermute | solution.py:513
  33.1 2.4 %collective-permute-start.5 = (bf16[96,1024]{1,0:T(8,128)(2,1)}, bf16[96,1024]{1,0:T(8,128)(2,1)}, u32[]{:S(2)}, u32[]{:S(2)}) collective-permute-start(bf16[96,1024]{1,0:T(8,128)(2,1)} %get-tuple-element.48), channel_id=1, source_target_pairs={{0,2},{1,3},{2,0},{3,1},{4,6},{5,7},{6,4},{7,5},{8,10},{9,11},{10,... | collective-permute-start | bytes 589832 | tf_op jit(solution)/shard_map/ppermute | solution.py:513
  35.5 1.5 %collective-permute-start.6 = (bf16[96,1024]{1,0:T(8,128)(2,1)}, bf16[96,1024]{1,0:T(8,128)(2,1)}, u32[]{:S(2)}, u32[]{:S(2)}) collective-permute-start(bf16[96,1024]{1,0:T(8,128)(2,1)} %get-tuple-element.49), channel_id=1, source_target_pairs={{0,3},{1,0},{2,1},{3,2},{4,7},{5,4},{6,5},{7,6},{8,11},{9,8},{10,9... | collective-permute-start | bytes 589832 | tf_op jit(solution)/shard_map/ppermute | solution.py:513
  36.9 18.3 %product.4 = (bf16[384,2048]{1,0:T(8,128)(2,1)}, bf16[384,2048]{1,0:T(8,128)(2,1)}, bf16[2,192,2048]{2,1,0:T(8,128)(2,1)}, bf16[2,192,2048]{2,1,0:T(8,128)(2,1)}, f32[8,128]{1,0:T(8,128)}) custom-call(bf16[768,2048]{1,0:T(8,128)(2,1)S(1)} %bitcast.7, bf16[2048,8192]{1,0:T(8,128)(2,1)} %weights.5, bf16[192,2048]{1,0:T(8,128)(2,1)} %add.6.rest_0_, ...), custom_call_target="tpu_custom_call" | custom-call | flops 1 | bytes 1 | tf_op jit(solution)/shard_map/product/pallas_call | solution.py:219
  56.2 4.2 %all-to-all-start.1 = ((bf16[4,96,1024]{2,1,0:T(8,128)(2,1)}), bf16[4,96,1024]{2,1,0:T(8,128)(2,1)}, u32[]{:S(2)}, u32[]{:S(2)}) async-start(bf16[4,96,1024]{2,1,0:T(8,128)(2,1)} %get-tuple-element.45), calls=%async_computation.1 | async-start | bytes 1572864 | tf_op jit(solution)/shard_map/all_to_all | solution.py:529
  61.0 2.9 %score.1 = f32[16,768]{1,0:T(8,128)S(1)} custom-call(s32[24]{0:T(128)} %get-tuple-element.39.names, s32[1,768]{1,0:T(1,128)} %wanted.5, bf16[768,2048]{1,0:T(8,128)(2,1)S(1)} %bitcast.8, bf16[384,2048]{1,0:T(8,128)(2,1)} %bitcast.2.factors, f32[8,128]{1,0:T(8,128)} %get-tuple-element.42.rest_0_, bf16[192,2048]{1,0:T(8,128)(2,1)} %collective-permute-done.2.rest_1_.first), custom_call_target="tpu_custom_call" | custom-call | flops 46000001024 | bytes 1 | tf_op jit(solution)/shard_map/score/pallas_call | solution.py:318
  63.9 5.8 %all-gather = f32[64,768]{1,0:T(8,128)S(1)} all-gather(f32[16,768]{1,0:T(8,128)S(1)} %score.1), channel_id=2, replica_groups=mesh['groups'=2,'tp'=4,'rep'=4] {'tp'}, dimensions={0}, use_global_device_ids=true | all-gather | bytes 245760 | tf_op jit(solution)/shard_map/all_gather | solution.py:536
  69.7 4.0 %delta.2 = (bf16[192,1024]{1,0:T(8,128)(2,1)}, bf16[192,1024]{1,0:T(8,128)(2,1)}) custom-call(s32[24]{0:T(128)} %get-tuple-element.39.names, s32[1,768]{1,0:T(1,128)} %wanted.5, f32[4,16,768]{2,1,0:T(8,128)S(1)} %bitcast.10, bf16[384,2048]{1,0:T(8,128)(2,1)} %get-tuple-element.43.late_own, bf16[384,2048]{1,0:T(8,128)(2,1)S(1)} %collective-permute-done.3.late_recv, ...), custom_call_target="tpu_custom_call" | custom-call | flops 1 | bytes 1 | tf_op jit(solution)/shard_map/delta/pallas_call | solution.py:384
  73.7 1.5 %collective-permute-start.13 = (bf16[192,1024]{1,0:T(8,128)(2,1)}, bf16[192,1024]{1,0:T(8,128)(2,1)}, u32[]{:S(2)}, u32[]{:S(2)}) collective-permute-start(bf16[192,1024]{1,0:T(8,128)(2,1)} %get-tuple-element.57), channel_id=1, source_target_pairs={{0,12},{12,0},{4,8},{8,4},{1,13},{13,1},{5,9},{9,5},{2,14},{14,2},... | collective-permute-start | bytes 1179656 | tf_op jit(solution)/shard_map/ppermute | solution.py:510
  75.6 4.8 %all-to-all-done.1 = bf16[4,96,1024]{2,1,0:T(8,128)(2,1)} async-done(((bf16[4,96,1024]{2,1,0:T(8,128)(2,1)}), bf16[4,96,1024]{2,1,0:T(8,128)(2,1)}, u32[]{:S(2)}, u32[]{:S(2)}) %all-to-all-start.1) | async-done | bytes 786464 | tf_op jit(solution)/shard_map/all_to_all | solution.py:529
  80.4 5.6 %delta.3 = (bf16[192,1024]{1,0:T(8,128)(2,1)}, bf16[192,1024]{1,0:T(8,128)(2,1)}, bf16[192,2048]{1,0:T(8,128)(2,1)}, bf16[192,2048]{1,0:T(8,128)(2,1)}) custom-call(s32[24]{0:T(128)} %get-tuple-element.39.names, s32[1,768]{1,0:T(1,128)} %wanted.5, f32[4,16,768]{2,1,0:T(8,128)S(1)} %bitcast.11, bf16[384,2048]{1,0:T(8,128)(2,1)} %get-tuple-element.43.late_own, ...), custom_call_target="tpu_custom_call" | custom-call | flops 1 | bytes 1 | tf_op jit(solution)/shard_map/delta/pallas_call | solution.py:384
  86.0 1.5 %collective-permute-start.10 = (bf16[192,1024]{1,0:T(8,128)(2,1)}, bf16[192,1024]{1,0:T(8,128)(2,1)}, u32[]{:S(2)}, u32[]{:S(2)}) collective-permute-start(bf16[192,1024]{1,0:T(8,128)(2,1)} %get-tuple-element.55), channel_id=1, source_target_pairs={{0,8},{8,0},{4,12},{12,4},{1,9},{9,1},{5,13},{13,5},{2,10},{10,2},... | collective-permute-start | bytes 1179656 | tf_op jit(solution)/shard_map/ppermute | solution.py:507
  88.1 11.4 %product.5 = (bf16[2,192,2048]{2,1,0:T(8,128)(2,1)}, bf16[2,192,2048]{2,1,0:T(8,128)(2,1)}, f32[8,128]{1,0:T(8,128)}) custom-call(bf16[768,2048]{1,0:T(8,128)(2,1)S(1)} %bitcast.9, bf16[2048,8192]{1,0:T(8,128)(2,1)} %weights.5, bf16[192,2048]{1,0:T(8,128)(2,1)} %get-tuple-element.52.rest_0_.mine), custom_call_target="tpu_custom_call" | custom-call | flops 1 | bytes 1 | tf_op jit(solution)/shard_map/product/pallas_call | solution.py:290
  100.7 5.2 %near.1.rest_0_ = bf16[192,8192]{1,0:T(8,128)(2,1)} custom-call(bf16[192,8192]{1,0:T(8,128)(2,1)} %bitcast.12, bf16[2,192,2048]{2,1,0:T(8,128)(2,1)} %get-tuple-element.61.keep, bf16[2,192,2048]{2,1,0:T(8,128)(2,1)} %collective-permute-done.7.rest_5_.recv, bf16[192,2048]{1,0:T(8,128)(2,1)} %collective-permute-done.2.rest_1_.first, ...), custom_call_target="tpu_custom_call" | custom-call | flops 69000003584 | bytes 1 | tf_op jit(solution)/shard_map/near/pallas_call | solution.py:473
  105.9 2.8 %far.2.rest_0_ = bf16[192,8192]{1,0:T(8,128)(2,1)} custom-call(bf16[192,8192]{1,0:T(8,128)(2,1)} %bitcast.13, bf16[2,192,2048]{2,1,0:T(8,128)(2,1)} %get-tuple-element.53.keep, bf16[2,192,2048]{2,1,0:T(8,128)(2,1)} %collective-permute-done.9.recv, bf16[192,1024]{1,0:T(8,128)(2,1)} %get-tuple-element.59.rest_0_.straight, ...), custom_call_target="tpu_custom_call", output_to_operand_aliasing={{}: (5, {})} | custom-call | flops 69000003584 | bytes 1 | tf_op jit(solution)/shard_map/far/pallas_call | solution.py:473
  108.7 1.5 %collective-permute-done.11.cross = bf16[192,1024]{1,0:T(8,128)(2,1)} collective-permute-done((bf16[192,1024]{1,0:T(8,128)(2,1)}, bf16[192,1024]{1,0:T(8,128)(2,1)}, u32[]{:S(2)}, u32[]{:S(2)}) %collective-permute-start.11) | collective-permute-done | bytes 393248 | tf_op jit(solution)/shard_map/ppermute | solution.py:510
  110.2 2.8 %far.3 = bf16[192,8192]{1,0:T(8,128)(2,1)} custom-call(bf16[192,8192]{1,0:T(8,128)(2,1)} %bitcast.14, bf16[2,192,2048]{2,1,0:T(8,128)(2,1)} %get-tuple-element.53.keep, bf16[2,192,2048]{2,1,0:T(8,128)(2,1)} %collective-permute-done.9.recv, bf16[192,1024]{1,0:T(8,128)(2,1)} %collective-permute-done.10.straight, ...), custom_call_target="tpu_custom_call", output_to_operand_aliasing={{}: (5, {})} | custom-call | flops 69000003584 | bytes 1 | tf_op jit(solution)/shard_map/far/pallas_call | solution.py:473
  (33 shorter events, 6.0 us)
Async XLA Ops:
  3.3 52.9 %all-to-all-start = ((bf16[4,96,2048]{2,1,0:T(8,128)(2,1)}), bf16[4,96,2048]{2,1,0:T(8,128)(2,1)}, u32[]{:S(2)}, u32[]{:S(2)}) async-start(bf16[4,96,2048]{2,1,0:T(8,128)(2,1)} %get-tuple-element.40), calls=%async_computation | async-start | bytes 3145728 | tf_op jit(solution)/shard_map/all_to_all | solution.py:517
  21.1 2.3 %collective-permute-start = (bf16[192,2048]{1,0:T(8,128)(2,1)S(1)}, bf16[192,2048]{1,0:T(8,128)(2,1)S(1)}, u32[]{:S(2)}, u32[]{:S(2)}) collective-permute-start(bf16[192,2048]{1,0:T(8,128)(2,1)S(1)} %get-tuple-element.36), channel_id=1, source_target_pairs={{0,4},{4,0},{8,12},{12,8},{1,5},{5,1},{9,13},{13,9},{2,6},{6,2},{1... | collective-permute-start | bytes 2359304 | tf_op jit(solution)/shard_map/ppermute | solution.py:504
  21.1 5.0 %collective-permute-start.1 = (bf16[192,2048]{1,0:T(8,128)(2,1)S(1)}, bf16[192,2048]{1,0:T(8,128)(2,1)S(1)}, u32[]{:S(2)}, u32[]{:S(2)}) collective-permute-start(bf16[192,2048]{1,0:T(8,128)(2,1)S(1)} %get-tuple-element.38), channel_id=1, source_target_pairs={{0,4},{4,0},{8,12},{12,8},{1,5},{5,1},{9,13},{13,9},{2,6},{6,2},{1... | collective-permute-start | bytes 2359304 | tf_op jit(solution)/shard_map/ppermute | solution.py:504
  24.5 36.0 %collective-permute-start.2 = (bf16[192,2048]{1,0:T(8,128)(2,1)}, bf16[192,2048]{1,0:T(8,128)(2,1)}, u32[]{:S(2)}, u32[]{:S(2)}) collective-permute-start(bf16[192,2048]{1,0:T(8,128)(2,1)} %add.6.rest_0_), channel_id=1, source_target_pairs={{0,8},{8,0},{4,12},{12,4},{1,9},{9,1},{5,13},{13,5},{2,10},{10,2},... | collective-permute-start | bytes 2359304 | tf_op jit(solution)/shard_map/ppermute | solution.py:507
  26.0 10.9 %copy-start = (bf16[1,768,2048]{2,1,0:T(8,128)(2,1)S(1)}, bf16[1,768,2048]{2,1,0:T(8,128)(2,1)}, u32[]{:S(2)}) copy-start(bf16[1,768,2048]{2,1,0:T(8,128)(2,1)} %param.8) | copy-start | bytes 9437188
  30.5 29.9 %collective-permute-start.4 = (bf16[96,1024]{1,0:T(8,128)(2,1)}, bf16[96,1024]{1,0:T(8,128)(2,1)S(1)}, u32[]{:S(2)}, u32[]{:S(2)}) collective-permute-start(bf16[96,1024]{1,0:T(8,128)(2,1)} %get-tuple-element.47), channel_id=1, source_target_pairs={{0,1},{1,2},{2,3},{3,0},{4,5},{5,6},{6,7},{7,4},{8,9},{9,10},{10,1... | collective-permute-start | bytes 589832 | tf_op jit(solution)/shard_map/ppermute | solution.py:513
  32.6 37.1 %collective-permute-start.8 = (bf16[192,2048]{1,0:T(8,128)(2,1)}, bf16[192,2048]{1,0:T(8,128)(2,1)}, u32[]{:S(2)}, u32[]{:S(2)}) collective-permute-start(bf16[192,2048]{1,0:T(8,128)(2,1)} %add.7.rest_1_), channel_id=1, source_target_pairs={{0,8},{8,0},{4,12},{12,4},{1,9},{9,1},{5,13},{13,5},{2,10},{10,2},... | collective-permute-start | bytes 2359304 | tf_op jit(solution)/shard_map/ppermute | solution.py:507
  33.1 36.6 %collective-permute-start.5 = (bf16[96,1024]{1,0:T(8,128)(2,1)}, bf16[96,1024]{1,0:T(8,128)(2,1)}, u32[]{:S(2)}, u32[]{:S(2)}) collective-permute-start(bf16[96,1024]{1,0:T(8,128)(2,1)} %get-tuple-element.48), channel_id=1, source_target_pairs={{0,2},{1,3},{2,0},{3,1},{4,6},{5,7},{6,4},{7,5},{8,10},{9,11},{10,... | collective-permute-start | bytes 589832 | tf_op jit(solution)/shard_map/ppermute | solution.py:513
  35.5 34.2 %collective-permute-start.6 = (bf16[96,1024]{1,0:T(8,128)(2,1)}, bf16[96,1024]{1,0:T(8,128)(2,1)}, u32[]{:S(2)}, u32[]{:S(2)}) collective-permute-start(bf16[96,1024]{1,0:T(8,128)(2,1)} %get-tuple-element.49), channel_id=1, source_target_pairs={{0,3},{1,0},{2,1},{3,2},{4,7},{5,4},{6,5},{7,6},{8,11},{9,8},{10,9... | collective-permute-start | bytes 589832 | tf_op jit(solution)/shard_map/ppermute | solution.py:513
  56.2 24.2 %all-to-all-start.1 = ((bf16[4,96,1024]{2,1,0:T(8,128)(2,1)}), bf16[4,96,1024]{2,1,0:T(8,128)(2,1)}, u32[]{:S(2)}, u32[]{:S(2)}) async-start(bf16[4,96,1024]{2,1,0:T(8,128)(2,1)} %get-tuple-element.45), calls=%async_computation.1 | async-start | bytes 1572864 | tf_op jit(solution)/shard_map/all_to_all | solution.py:529
  60.4 3.5 %copy-start.3 = (bf16[96,1024]{1,0:T(8,128)(2,1)}, bf16[96,1024]{1,0:T(8,128)(2,1)S(1)}, u32[]{:S(2)}) copy-start(bf16[96,1024]{1,0:T(8,128)(2,1)S(1)} %collective-permute-done.4.rest_1_.rest_2_) | copy-start | bytes 589828
  60.4 9.3 %collective-permute-start.3 = (bf16[384,2048]{1,0:T(8,128)(2,1)}, bf16[384,2048]{1,0:T(8,128)(2,1)S(1)}, u32[]{:S(2)}, u32[]{:S(2)}) collective-permute-start(bf16[384,2048]{1,0:T(8,128)(2,1)} %get-tuple-element.44), channel_id=1, source_target_pairs={{0,4},{4,0},{8,12},{12,8},{1,5},{5,1},{9,13},{13,9},{2,6},{6,2},{1... | collective-permute-start | bytes 4718600 | tf_op jit(solution)/shard_map/ppermute | solution.py:504
  60.5 19.9 %collective-permute-start.7 = (bf16[2,192,2048]{2,1,0:T(8,128)(2,1)}, bf16[2,192,2048]{2,1,0:T(8,128)(2,1)}, u32[]{:S(2)}, u32[]{:S(2)}) collective-permute-start(bf16[2,192,2048]{2,1,0:T(8,128)(2,1)} %get-tuple-element.50), channel_id=1, source_target_pairs={{0,4},{4,0},{8,12},{12,8},{1,5},{5,1},{9,13},{13,9},{2,6},{6,2},{1... | collective-permute-start | bytes 4718600 | tf_op jit(solution)/shard_map/ppermute | solution.py:504
  69.7 4.0 %copy-start.1 = (bf16[384,2048]{1,0:T(8,128)(2,1)}, bf16[384,2048]{1,0:T(8,128)(2,1)S(1)}, u32[]{:S(2)}) copy-start(bf16[384,2048]{1,0:T(8,128)(2,1)S(1)} %collective-permute-done.3.late_recv) | copy-start | bytes 4718596
  73.7 25.8 %collective-permute-start.13 = (bf16[192,1024]{1,0:T(8,128)(2,1)}, bf16[192,1024]{1,0:T(8,128)(2,1)}, u32[]{:S(2)}, u32[]{:S(2)}) collective-permute-start(bf16[192,1024]{1,0:T(8,128)(2,1)} %get-tuple-element.57), channel_id=1, source_target_pairs={{0,12},{12,0},{4,8},{8,4},{1,13},{13,1},{5,9},{9,5},{2,14},{14,2},... | collective-permute-start | bytes 1179656 | tf_op jit(solution)/shard_map/ppermute | solution.py:510
  75.1 24.4 %collective-permute-start.12 = (bf16[192,1024]{1,0:T(8,128)(2,1)}, bf16[192,1024]{1,0:T(8,128)(2,1)}, u32[]{:S(2)}, u32[]{:S(2)}) collective-permute-start(bf16[192,1024]{1,0:T(8,128)(2,1)} %get-tuple-element.51.rest_6_), channel_id=1, source_target_pairs={{0,8},{8,0},{4,12},{12,4},{1,9},{9,1},{5,13},{13,5},{2,10},{10,2},... | collective-permute-start | bytes 1179656 | tf_op jit(solution)/shard_map/ppermute | solution.py:507
  86.0 22.7 %collective-permute-start.10 = (bf16[192,1024]{1,0:T(8,128)(2,1)}, bf16[192,1024]{1,0:T(8,128)(2,1)}, u32[]{:S(2)}, u32[]{:S(2)}) collective-permute-start(bf16[192,1024]{1,0:T(8,128)(2,1)} %get-tuple-element.55), channel_id=1, source_target_pairs={{0,8},{8,0},{4,12},{12,4},{1,9},{9,1},{5,13},{13,5},{2,10},{10,2},... | collective-permute-start | bytes 1179656 | tf_op jit(solution)/shard_map/ppermute | solution.py:507
  87.5 22.7 %collective-permute-start.11 = (bf16[192,1024]{1,0:T(8,128)(2,1)}, bf16[192,1024]{1,0:T(8,128)(2,1)}, u32[]{:S(2)}, u32[]{:S(2)}) collective-permute-start(bf16[192,1024]{1,0:T(8,128)(2,1)} %get-tuple-element.56), channel_id=1, source_target_pairs={{0,12},{12,0},{4,8},{8,4},{1,13},{13,1},{5,9},{9,5},{2,14},{14,2},... | collective-permute-start | bytes 1179656 | tf_op jit(solution)/shard_map/ppermute | solution.py:510
  87.5 12.1 %collective-permute-start.14 = (bf16[192,2048]{1,0:T(8,128)(2,1)}, bf16[192,2048]{1,0:T(8,128)(2,1)}, u32[]{:S(2)}, u32[]{:S(2)}) collective-permute-start(bf16[192,2048]{1,0:T(8,128)(2,1)} %get-tuple-element.62), channel_id=1, source_target_pairs={{0,4},{4,0},{8,12},{12,8},{1,5},{5,1},{9,13},{13,9},{2,6},{6,2},{1... | collective-permute-start | bytes 2359304 | tf_op jit(solution)/shard_map/ppermute | solution.py:504
  99.5 6.4 %collective-permute-start.9 = (bf16[2,192,2048]{2,1,0:T(8,128)(2,1)}, bf16[2,192,2048]{2,1,0:T(8,128)(2,1)}, u32[]{:S(2)}, u32[]{:S(2)}) collective-permute-start(bf16[2,192,2048]{2,1,0:T(8,128)(2,1)} %get-tuple-element.54), channel_id=1, source_target_pairs={{0,4},{4,0},{8,12},{12,8},{1,5},{5,1},{9,13},{13,9},{2,6},{6,2},{1... | collective-permute-start | bytes 4718600 | tf_op jit(solution)/shard_map/ppermute | solution.py:504
  99.6 1.1 %copy-start.2 = (bf16[192,2048]{1,0:T(8,128)(2,1)S(1)}, bf16[192,2048]{1,0:T(8,128)(2,1)}, u32[]{:S(2)}) copy-start(bf16[192,2048]{1,0:T(8,128)(2,1)} %get-tuple-element.52.rest_0_.mine) | copy-start | bytes 2359300

commit v11 on v10

--- a/solution.py
+++ b/solution.py
@@ -62,10 +62,8 @@
 
 
 def select_kernel(by_shift, by_target, named, n_rep, cap, pool_dev, rank, slot, lists, pool, *rest):
-    token, idx, counts, sems = rest[-4:]
-    outs = rest[:-4]
-    direct = not by_shift
-    copies = []
+    token, idx, counts = rest[-3:]
+    outs = rest[: -3]
     outs = outs[-(n_rep * len(by_shift) + len(by_target) + named) :]
     token[...] = jnp.zeros_like(token)
     me = lax.axis_index("rep")
@@ -75,25 +73,17 @@
         for k in range(cap + 1):
             idx[k] = 0
         count = jnp.int32(0)
-        for place in [slot[lists[target, l]] - base for l in range(lists.shape[1])]:
+        for l in range(lists.shape[1]):
+            place = slot[lists[target, l]] - base
             idx[jnp.minimum(count, cap)] = place
             count = count + jnp.where((place >= 0) & (place < pool_dev), 1, 0)
         for k in range(cap):
             entry = jnp.clip(idx[k], 0, pool_dev - 1)
             rows = pl.ds(k * rank, rank)
-            if direct:
-                copy = pltpu.make_async_copy(
-                    pool.at[entry], outs[0].at[target, rows, :], sems.at[shift * cap + k]
-                )
-                copy.start()
-                copies.append(copy)
-                continue
             for c, (start, stop) in enumerate(by_shift):
                 outs[c * n_rep + shift][rows, :] = pool[entry, :, start:stop]
             for c, (start, stop) in enumerate(by_target):
                 outs[len(by_shift) * n_rep + c][target, rows, :] = pool[entry, :, start:stop]
-    for copy in copies:
-        copy.wait()
     if named:
         names = outs[-1]
         for i in range(n_rep * cap):
@@ -112,7 +102,7 @@
     pool_dev, rank, width = pool.shape
     shapes = [in_hbm((cap * rank, stop - start)) for start, stop in by_shift for _ in range(n_rep)]
     shapes += [in_hbm((n_rep, cap * rank, stop - start)) for start, stop in by_target]
-    specs = [VMEM if by_shift else ANY] * len(shapes)
+    specs = [VMEM] * len(shapes)
     if named:
         shapes.append(in_hbm((n_rep * cap,), jnp.int32))
         specs.append(SMEM)
@@ -121,11 +111,7 @@
         out_shape=[*shapes, TOKEN],
         in_specs=[SMEM, SMEM, VMEM] + [ANY] * len(after),
         out_specs=[*specs, VMEM],
-        scratch_shapes=[
-            pltpu.SMEM((cap + 1,), jnp.int32),
-            pltpu.SMEM((n_rep,), jnp.int32),
-            pltpu.SemaphoreType.DMA((n_rep * cap,)),
-        ],
+        scratch_shapes=[pltpu.SMEM((cap + 1,), jnp.int32), pltpu.SMEM((n_rep,), jnp.int32)],
         compiler_params=params(16),
         cost_estimate=order(0),
         name="select",

time: 114 us -> 113 us (level)
  no operation moved by 1% of the time
where the time goes in v11:
time: 113 us
  Pallas kernels  70.2 us (62%)
  starting transfers between devices  23.7 us (21%)
  waiting for transfers between devices  9.24 us (8%)
  blocking collectives  5.79 us (5%)
  other arithmetic  2.34 us (2%)
    pallas_call x1, Pallas kernels, product_columns(): pl.pallas_call(kernel, out_shape=[in_hbm((half, width))] * 2 + [in_hbm((2...  18.3 us
    pallas_call x1, Pallas kernels, product_early(): pl.pallas_call(kernel, out_shape=[sds((half // 2, width))] * 4 + [TOKEN],...  11.5 us
    pallas_call x1, Pallas kernels, product(): pl.pallas_call(kernel, out_shape=[in_hbm(shape) if blocks > 1 else sds(sh...  11.4 us
    pallas_call x3, Pallas kernels, finish(): pl.pallas_call(near_kernel if near else far_kernel, out_shape=sds((own, f...  10.8 us
    pallas_call x2, Pallas kernels, delta(): pl.pallas_call(functools.partial(delta_kernel, len(blocks), len(before),...  9.54 us
    all_to_all x1, starting transfers between devices, paired(): lax.all_to_all(chosen, 'rep', 0, 0, tiled=True)  6.32 us
    ppermute x3, starting transfers between devices, over_rep(): lax.ppermute(x, 'rep', [(i, (i + shift) % n_rep) for i in range(n_rep)])  5.9 us
    pallas_call x2, Pallas kernels, select(): pl.pallas_call(functools.partial(select_kernel, by_shift, by_target, int(...  5.89 us
  transfers between devices with their start and end apart: 17, of which 4 were waited for; matrix products, arithmetic and copies ran while one was open for 2% of the time, Pallas kernels for 57%

profile of v11, /device:TPU:0, one launch (start us, length us, event | category | flops | bytes accessed | tf_op | source)
XLA Modules:
  0.0 112.5 jit_solution(17109717155524665726)
XLA Ops:
  0.0 2.8 %select.2 = (bf16[4,96,2048]{2,1,0:T(8,128)(2,1)}, f32[8,128]{1,0:T(8,128)}) custom-call(s32[64]{0:T(128)} %slot.3, s32[4,24]{1,0:T(4,128)} %lists.3, bf16[16,16,2048]{2,1,0:T(8,128)(2,1)} %pool.2), custom_call_target="tpu_custom_call" | custom-call | flops 1 | bytes 1 | tf_op jit(solution)/shard_map/select/pallas_call | solution.py:109
  2.8 6.3 %all-to-all-start = ((bf16[4,96,2048]{2,1,0:T(8,128)(2,1)}), bf16[4,96,2048]{2,1,0:T(8,128)(2,1)}, u32[]{:S(2)}, u32[]{:S(2)}) async-start(bf16[4,96,2048]{2,1,0:T(8,128)(2,1)} %get-tuple-element.40), calls=%async_computation | async-start | bytes 3145728 | tf_op jit(solution)/shard_map/all_to_all | solution.py:503
  9.2 11.5 %product.3 = (bf16[192,2048]{1,0:T(8,128)(2,1)S(1)}, bf16[192,2048]{1,0:T(8,128)(2,1)S(1)}, bf16[192,2048]{1,0:T(8,128)(2,1)S(1)}, bf16[192,2048]{1,0:T(8,128)(2,1)S(1)}, f32[8,128]{1,0:T(8,128)}) custom-call(bf16[768,2048]{1,0:T(8,128)(2,1)} %bitcast.6, bf16[2048,8192]{1,0:T(8,128)(2,1)} %weights.5, f32[8,128]{1,0:T(8,128)} %get-tuple-element.34.rest_0_), custom_call_target="tpu_custom_call" | custom-call | flops 1 | bytes 1 | tf_op jit(solution)/shard_map/product/pallas_call | solution.py:147
  21.1 1.8 %collective-permute-done = bf16[192,2048]{1,0:T(8,128)(2,1)S(1)} collective-permute-done((bf16[192,2048]{1,0:T(8,128)(2,1)S(1)}, bf16[192,2048]{1,0:T(8,128)(2,1)S(1)}, u32[]{:S(2)}, u32[]{:S(2)}) %collective-permute-start) | collective-permute-done | bytes 786464 | tf_op jit(solution)/shard_map/ppermute | solution.py:490
  24.1 1.5 %collective-permute-start.2 = (bf16[192,2048]{1,0:T(8,128)(2,1)}, bf16[192,2048]{1,0:T(8,128)(2,1)}, u32[]{:S(2)}, u32[]{:S(2)}) collective-permute-start(bf16[192,2048]{1,0:T(8,128)(2,1)} %add.6.rest_0_), channel_id=1, source_target_pairs={{0,8},{8,0},{4,12},{12,4},{1,9},{9,1},{5,13},{13,5},{2,10},{10,2},... | collective-permute-start | bytes 2359304 | tf_op jit(solution)/shard_map/ppermute | solution.py:493
  25.6 1.2 %add.7.rest_1_ = bf16[192,2048]{1,0:T(8,128)(2,1)} add(bf16[192,2048]{1,0:T(8,128)(2,1)S(1)} %get-tuple-element.37, bf16[192,2048]{1,0:T(8,128)(2,1)S(1)} %collective-permute-done.1) | non-fusion elementwise | flops 393216 | bytes 2359296 | tf_op jit(solution)/shard_map/add | solution.py:506
  26.8 3.1 %select.3 = (bf16[96,1024]{1,0:T(8,128)(2,1)}, bf16[96,1024]{1,0:T(8,128)(2,1)}, bf16[96,1024]{1,0:T(8,128)(2,1)}, bf16[96,1024]{1,0:T(8,128)(2,1)}, bf16[4,96,1...) custom-call(s32[64]{0:T(128)} %slot.3, s32[4,24]{1,0:T(4,128)} %lists.3, bf16[16,16,2048]{2,1,0:T(8,128)(2,1)} %pool.3, ...), custom_call_target="tpu_custom_call" | custom-call | flops 1 | bytes 1 | tf_op jit(solution)/shard_map/select/pallas_call | solution.py:109
  29.8 2.1 %collective-permute-start.4 = (bf16[96,1024]{1,0:T(8,128)(2,1)}, bf16[96,1024]{1,0:T(8,128)(2,1)S(1)}, u32[]{:S(2)}, u32[]{:S(2)}) collective-permute-start(bf16[96,1024]{1,0:T(8,128)(2,1)} %get-tuple-element.47), channel_id=1, source_target_pairs={{0,1},{1,2},{2,3},{3,0},{4,5},{5,6},{6,7},{7,4},{8,9},{9,10},{10,1... | collective-permute-start | bytes 589832 | tf_op jit(solution)/shard_map/ppermute | solution.py:499
  32.4 2.4 %collective-permute-start.5 = (bf16[96,1024]{1,0:T(8,128)(2,1)}, bf16[96,1024]{1,0:T(8,128)(2,1)}, u32[]{:S(2)}, u32[]{:S(2)}) collective-permute-start(bf16[96,1024]{1,0:T(8,128)(2,1)} %get-tuple-element.48), channel_id=1, source_target_pairs={{0,2},{1,3},{2,0},{3,1},{4,6},{5,7},{6,4},{7,5},{8,10},{9,11},{10,... | collective-permute-start | bytes 589832 | tf_op jit(solution)/shard_map/ppermute | solution.py:499
  34.8 1.5 %collective-permute-start.6 = (bf16[96,1024]{1,0:T(8,128)(2,1)}, bf16[96,1024]{1,0:T(8,128)(2,1)}, u32[]{:S(2)}, u32[]{:S(2)}) collective-permute-start(bf16[96,1024]{1,0:T(8,128)(2,1)} %get-tuple-element.49), channel_id=1, source_target_pairs={{0,3},{1,0},{2,1},{3,2},{4,7},{5,4},{6,5},{7,6},{8,11},{9,8},{10,9... | collective-permute-start | bytes 589832 | tf_op jit(solution)/shard_map/ppermute | solution.py:499
  36.3 18.3 %product.4 = (bf16[384,2048]{1,0:T(8,128)(2,1)}, bf16[384,2048]{1,0:T(8,128)(2,1)}, bf16[2,192,2048]{2,1,0:T(8,128)(2,1)}, bf16[2,192,2048]{2,1,0:T(8,128)(2,1)}, f32[8,128]{1,0:T(8,128)}) custom-call(bf16[768,2048]{1,0:T(8,128)(2,1)S(1)} %bitcast.7, bf16[2048,8192]{1,0:T(8,128)(2,1)} %weights.5, bf16[192,2048]{1,0:T(8,128)(2,1)} %add.6.rest_0_, ...), custom_call_target="tpu_custom_call" | custom-call | flops 1 | bytes 1 | tf_op jit(solution)/shard_map/product/pallas_call | solution.py:205
  55.7 4.2 %all-to-all-start.1 = ((bf16[4,96,1024]{2,1,0:T(8,128)(2,1)}), bf16[4,96,1024]{2,1,0:T(8,128)(2,1)}, u32[]{:S(2)}, u32[]{:S(2)}) async-start(bf16[4,96,1024]{2,1,0:T(8,128)(2,1)} %get-tuple-element.45), calls=%async_computation.1 | async-start | bytes 1572864 | tf_op jit(solution)/shard_map/all_to_all | solution.py:515
  60.5 2.9 %score.1 = f32[16,768]{1,0:T(8,128)S(1)} custom-call(s32[24]{0:T(128)} %get-tuple-element.39.names, s32[1,768]{1,0:T(1,128)} %wanted.5, bf16[768,2048]{1,0:T(8,128)(2,1)S(1)} %bitcast.8, bf16[384,2048]{1,0:T(8,128)(2,1)} %bitcast.2.factors, f32[8,128]{1,0:T(8,128)} %get-tuple-element.42.rest_0_, bf16[192,2048]{1,0:T(8,128)(2,1)} %collective-permute-done.2.rest_1_.first), custom_call_target="tpu_custom_call" | custom-call | flops 46000001024 | bytes 1 | tf_op jit(solution)/shard_map/score/pallas_call | solution.py:304
  63.4 5.8 %all-gather = f32[64,768]{1,0:T(8,128)S(1)} all-gather(f32[16,768]{1,0:T(8,128)S(1)} %score.1), channel_id=2, replica_groups=mesh['groups'=2,'tp'=4,'rep'=4] {'tp'}, dimensions={0}, use_global_device_ids=true | all-gather | bytes 245760 | tf_op jit(solution)/shard_map/all_gather | solution.py:522
  69.2 4.0 %delta.2 = (bf16[192,1024]{1,0:T(8,128)(2,1)}, bf16[192,1024]{1,0:T(8,128)(2,1)}) custom-call(s32[24]{0:T(128)} %get-tuple-element.39.names, s32[1,768]{1,0:T(1,128)} %wanted.5, f32[4,16,768]{2,1,0:T(8,128)S(1)} %bitcast.10, bf16[384,2048]{1,0:T(8,128)(2,1)} %get-tuple-element.43.late_own, bf16[384,2048]{1,0:T(8,128)(2,1)S(1)} %collective-permute-done.3.late_recv, ...), custom_call_target="tpu_custom_call" | custom-call | flops 1 | bytes 1 | tf_op jit(solution)/shard_map/delta/pallas_call | solution.py:370
  73.2 1.5 %collective-permute-start.13 = (bf16[192,1024]{1,0:T(8,128)(2,1)}, bf16[192,1024]{1,0:T(8,128)(2,1)}, u32[]{:S(2)}, u32[]{:S(2)}) collective-permute-start(bf16[192,1024]{1,0:T(8,128)(2,1)} %get-tuple-element.57), channel_id=1, source_target_pairs={{0,12},{12,0},{4,8},{8,4},{1,13},{13,1},{5,9},{9,5},{2,14},{14,2},... | collective-permute-start | bytes 1179656 | tf_op jit(solution)/shard_map/ppermute | solution.py:496
  75.2 4.8 %all-to-all-done.1 = bf16[4,96,1024]{2,1,0:T(8,128)(2,1)} async-done(((bf16[4,96,1024]{2,1,0:T(8,128)(2,1)}), bf16[4,96,1024]{2,1,0:T(8,128)(2,1)}, u32[]{:S(2)}, u32[]{:S(2)}) %all-to-all-start.1) | async-done | bytes 786464 | tf_op jit(solution)/shard_map/all_to_all | solution.py:515
  80.0 5.6 %delta.3 = (bf16[192,1024]{1,0:T(8,128)(2,1)}, bf16[192,1024]{1,0:T(8,128)(2,1)}, bf16[192,2048]{1,0:T(8,128)(2,1)}, bf16[192,2048]{1,0:T(8,128)(2,1)}) custom-call(s32[24]{0:T(128)} %get-tuple-element.39.names, s32[1,768]{1,0:T(1,128)} %wanted.5, f32[4,16,768]{2,1,0:T(8,128)S(1)} %bitcast.11, bf16[384,2048]{1,0:T(8,128)(2,1)} %get-tuple-element.43.late_own, ...), custom_call_target="tpu_custom_call" | custom-call | flops 1 | bytes 1 | tf_op jit(solution)/shard_map/delta/pallas_call | solution.py:370
  85.5 1.5 %collective-permute-start.10 = (bf16[192,1024]{1,0:T(8,128)(2,1)}, bf16[192,1024]{1,0:T(8,128)(2,1)}, u32[]{:S(2)}, u32[]{:S(2)}) collective-permute-start(bf16[192,1024]{1,0:T(8,128)(2,1)} %get-tuple-element.55), channel_id=1, source_target_pairs={{0,8},{8,0},{4,12},{12,4},{1,9},{9,1},{5,13},{13,5},{2,10},{10,2},... | collective-permute-start | bytes 1179656 | tf_op jit(solution)/shard_map/ppermute | solution.py:493
  87.7 11.4 %product.5 = (bf16[2,192,2048]{2,1,0:T(8,128)(2,1)}, bf16[2,192,2048]{2,1,0:T(8,128)(2,1)}, f32[8,128]{1,0:T(8,128)}) custom-call(bf16[768,2048]{1,0:T(8,128)(2,1)S(1)} %bitcast.9, bf16[2048,8192]{1,0:T(8,128)(2,1)} %weights.5, bf16[192,2048]{1,0:T(8,128)(2,1)} %get-tuple-element.52.rest_0_.mine), custom_call_target="tpu_custom_call" | custom-call | flops 1 | bytes 1 | tf_op jit(solution)/shard_map/product/pallas_call | solution.py:276
  100.2 5.2 %near.1.rest_0_ = bf16[192,8192]{1,0:T(8,128)(2,1)} custom-call(bf16[192,8192]{1,0:T(8,128)(2,1)} %bitcast.12, bf16[2,192,2048]{2,1,0:T(8,128)(2,1)} %get-tuple-element.61.keep, bf16[2,192,2048]{2,1,0:T(8,128)(2,1)} %collective-permute-done.7.rest_5_.recv, bf16[192,2048]{1,0:T(8,128)(2,1)} %collective-permute-done.2.rest_1_.first, ...), custom_call_target="tpu_custom_call" | custom-call | flops 69000003584 | bytes 1 | tf_op jit(solution)/shard_map/near/pallas_call | solution.py:459
  105.4 2.8 %far.2.rest_0_ = bf16[192,8192]{1,0:T(8,128)(2,1)} custom-call(bf16[192,8192]{1,0:T(8,128)(2,1)} %bitcast.13, bf16[2,192,2048]{2,1,0:T(8,128)(2,1)} %get-tuple-element.53.keep, bf16[2,192,2048]{2,1,0:T(8,128)(2,1)} %collective-permute-done.9.recv, bf16[192,1024]{1,0:T(8,128)(2,1)} %get-tuple-element.59.rest_0_.straight, ...), custom_call_target="tpu_custom_call", output_to_operand_aliasing={{}: (5, {})} | custom-call | flops 69000003584 | bytes 1 | tf_op jit(solution)/shard_map/far/pallas_call | solution.py:459
  108.3 1.5 %collective-permute-done.11.cross = bf16[192,1024]{1,0:T(8,128)(2,1)} collective-permute-done((bf16[192,1024]{1,0:T(8,128)(2,1)}, bf16[192,1024]{1,0:T(8,128)(2,1)}, u32[]{:S(2)}, u32[]{:S(2)}) %collective-permute-start.11) | collective-permute-done | bytes 393248 | tf_op jit(solution)/shard_map/ppermute | solution.py:496
  109.8 2.8 %far.3 = bf16[192,8192]{1,0:T(8,128)(2,1)} custom-call(bf16[192,8192]{1,0:T(8,128)(2,1)} %bitcast.14, bf16[2,192,2048]{2,1,0:T(8,128)(2,1)} %get-tuple-element.53.keep, bf16[2,192,2048]{2,1,0:T(8,128)(2,1)} %collective-permute-done.9.recv, bf16[192,1024]{1,0:T(8,128)(2,1)} %collective-permute-done.10.straight, ...), custom_call_target="tpu_custom_call", output_to_operand_aliasing={{}: (5, {})} | custom-call | flops 69000003584 | bytes 1 | tf_op jit(solution)/shard_map/far/pallas_call | solution.py:459
  (33 shorter events, 6.2 us)
Async XLA Ops:
  2.8 52.9 %all-to-all-start = ((bf16[4,96,2048]{2,1,0:T(8,128)(2,1)}), bf16[4,96,2048]{2,1,0:T(8,128)(2,1)}, u32[]{:S(2)}, u32[]{:S(2)}) async-start(bf16[4,96,2048]{2,1,0:T(8,128)(2,1)} %get-tuple-element.40), calls=%async_computation | async-start | bytes 3145728 | tf_op jit(solution)/shard_map/all_to_all | solution.py:503
  20.6 2.3 %collective-permute-start = (bf16[192,2048]{1,0:T(8,128)(2,1)S(1)}, bf16[192,2048]{1,0:T(8,128)(2,1)S(1)}, u32[]{:S(2)}, u32[]{:S(2)}) collective-permute-start(bf16[192,2048]{1,0:T(8,128)(2,1)S(1)} %get-tuple-element.36), channel_id=1, source_target_pairs={{0,4},{4,0},{8,12},{12,8},{1,5},{5,1},{9,13},{13,9},{2,6},{6,2},{1... | collective-permute-start | bytes 2359304 | tf_op jit(solution)/shard_map/ppermute | solution.py:490
  20.6 5.0 %collective-permute-start.1 = (bf16[192,2048]{1,0:T(8,128)(2,1)S(1)}, bf16[192,2048]{1,0:T(8,128)(2,1)S(1)}, u32[]{:S(2)}, u32[]{:S(2)}) collective-permute-start(bf16[192,2048]{1,0:T(8,128)(2,1)S(1)} %get-tuple-element.38), channel_id=1, source_target_pairs={{0,4},{4,0},{8,12},{12,8},{1,5},{5,1},{9,13},{13,9},{2,6},{6,2},{1... | collective-permute-start | bytes 2359304 | tf_op jit(solution)/shard_map/ppermute | solution.py:490
  24.1 36.0 %collective-permute-start.2 = (bf16[192,2048]{1,0:T(8,128)(2,1)}, bf16[192,2048]{1,0:T(8,128)(2,1)}, u32[]{:S(2)}, u32[]{:S(2)}) collective-permute-start(bf16[192,2048]{1,0:T(8,128)(2,1)} %add.6.rest_0_), channel_id=1, source_target_pairs={{0,8},{8,0},{4,12},{12,4},{1,9},{9,1},{5,13},{13,5},{2,10},{10,2},... | collective-permute-start | bytes 2359304 | tf_op jit(solution)/shard_map/ppermute | solution.py:493
  25.6 10.7 %copy-start = (bf16[1,768,2048]{2,1,0:T(8,128)(2,1)S(1)}, bf16[1,768,2048]{2,1,0:T(8,128)(2,1)}, u32[]{:S(2)}) copy-start(bf16[1,768,2048]{2,1,0:T(8,128)(2,1)} %param.8) | copy-start | bytes 9437188
  29.8 30.1 %collective-permute-start.4 = (bf16[96,1024]{1,0:T(8,128)(2,1)}, bf16[96,1024]{1,0:T(8,128)(2,1)S(1)}, u32[]{:S(2)}, u32[]{:S(2)}) collective-permute-start(bf16[96,1024]{1,0:T(8,128)(2,1)} %get-tuple-element.47), channel_id=1, source_target_pairs={{0,1},{1,2},{2,3},{3,0},{4,5},{5,6},{6,7},{7,4},{8,9},{9,10},{10,1... | collective-permute-start | bytes 589832 | tf_op jit(solution)/shard_map/ppermute | solution.py:499
  31.9 37.3 %collective-permute-start.8 = (bf16[192,2048]{1,0:T(8,128)(2,1)}, bf16[192,2048]{1,0:T(8,128)(2,1)}, u32[]{:S(2)}, u32[]{:S(2)}) collective-permute-start(bf16[192,2048]{1,0:T(8,128)(2,1)} %add.7.rest_1_), channel_id=1, source_target_pairs={{0,8},{8,0},{4,12},{12,4},{1,9},{9,1},{5,13},{13,5},{2,10},{10,2},... | collective-permute-start | bytes 2359304 | tf_op jit(solution)/shard_map/ppermute | solution.py:493
  32.4 36.8 %collective-permute-start.5 = (bf16[96,1024]{1,0:T(8,128)(2,1)}, bf16[96,1024]{1,0:T(8,128)(2,1)}, u32[]{:S(2)}, u32[]{:S(2)}) collective-permute-start(bf16[96,1024]{1,0:T(8,128)(2,1)} %get-tuple-element.48), channel_id=1, source_target_pairs={{0,2},{1,3},{2,0},{3,1},{4,6},{5,7},{6,4},{7,5},{8,10},{9,11},{10,... | collective-permute-start | bytes 589832 | tf_op jit(solution)/shard_map/ppermute | solution.py:499
  34.8 34.4 %collective-permute-start.6 = (bf16[96,1024]{1,0:T(8,128)(2,1)}, bf16[96,1024]{1,0:T(8,128)(2,1)}, u32[]{:S(2)}, u32[]{:S(2)}) collective-permute-start(bf16[96,1024]{1,0:T(8,128)(2,1)} %get-tuple-element.49), channel_id=1, source_target_pairs={{0,3},{1,0},{2,1},{3,2},{4,7},{5,4},{6,5},{7,6},{8,11},{9,8},{10,9... | collective-permute-start | bytes 589832 | tf_op jit(solution)/shard_map/ppermute | solution.py:499
  55.7 24.2 %all-to-all-start.1 = ((bf16[4,96,1024]{2,1,0:T(8,128)(2,1)}), bf16[4,96,1024]{2,1,0:T(8,128)(2,1)}, u32[]{:S(2)}, u32[]{:S(2)}) async-start(bf16[4,96,1024]{2,1,0:T(8,128)(2,1)} %get-tuple-element.45), calls=%async_computation.1 | async-start | bytes 1572864 | tf_op jit(solution)/shard_map/all_to_all | solution.py:515
  60.0 3.5 %copy-start.3 = (bf16[96,1024]{1,0:T(8,128)(2,1)}, bf16[96,1024]{1,0:T(8,128)(2,1)S(1)}, u32[]{:S(2)}) copy-start(bf16[96,1024]{1,0:T(8,128)(2,1)S(1)} %collective-permute-done.4.rest_1_.rest_2_) | copy-start | bytes 589828
  60.0 9.3 %collective-permute-start.3 = (bf16[384,2048]{1,0:T(8,128)(2,1)}, bf16[384,2048]{1,0:T(8,128)(2,1)S(1)}, u32[]{:S(2)}, u32[]{:S(2)}) collective-permute-start(bf16[384,2048]{1,0:T(8,128)(2,1)} %get-tuple-element.44), channel_id=1, source_target_pairs={{0,4},{4,0},{8,12},{12,8},{1,5},{5,1},{9,13},{13,9},{2,6},{6,2},{1... | collective-permute-start | bytes 4718600 | tf_op jit(solution)/shard_map/ppermute | solution.py:490
  60.1 19.9 %collective-permute-start.7 = (bf16[2,192,2048]{2,1,0:T(8,128)(2,1)}, bf16[2,192,2048]{2,1,0:T(8,128)(2,1)}, u32[]{:S(2)}, u32[]{:S(2)}) collective-permute-start(bf16[2,192,2048]{2,1,0:T(8,128)(2,1)} %get-tuple-element.50), channel_id=1, source_target_pairs={{0,4},{4,0},{8,12},{12,8},{1,5},{5,1},{9,13},{13,9},{2,6},{6,2},{1... | collective-permute-start | bytes 4718600 | tf_op jit(solution)/shard_map/ppermute | solution.py:490
  69.2 4.0 %copy-start.1 = (bf16[384,2048]{1,0:T(8,128)(2,1)}, bf16[384,2048]{1,0:T(8,128)(2,1)S(1)}, u32[]{:S(2)}) copy-start(bf16[384,2048]{1,0:T(8,128)(2,1)S(1)} %collective-permute-done.3.late_recv) | copy-start | bytes 4718596
  73.2 25.8 %collective-permute-start.13 = (bf16[192,1024]{1,0:T(8,128)(2,1)}, bf16[192,1024]{1,0:T(8,128)(2,1)}, u32[]{:S(2)}, u32[]{:S(2)}) collective-permute-start(bf16[192,1024]{1,0:T(8,128)(2,1)} %get-tuple-element.57), channel_id=1, source_target_pairs={{0,12},{12,0},{4,8},{8,4},{1,13},{13,1},{5,9},{9,5},{2,14},{14,2},... | collective-permute-start | bytes 1179656 | tf_op jit(solution)/shard_map/ppermute | solution.py:496
  74.7 24.4 %collective-permute-start.12 = (bf16[192,1024]{1,0:T(8,128)(2,1)}, bf16[192,1024]{1,0:T(8,128)(2,1)}, u32[]{:S(2)}, u32[]{:S(2)}) collective-permute-start(bf16[192,1024]{1,0:T(8,128)(2,1)} %get-tuple-element.51.rest_6_), channel_id=1, source_target_pairs={{0,8},{8,0},{4,12},{12,4},{1,9},{9,1},{5,13},{13,5},{2,10},{10,2},... | collective-permute-start | bytes 1179656 | tf_op jit(solution)/shard_map/ppermute | solution.py:493
  85.5 22.7 %collective-permute-start.10 = (bf16[192,1024]{1,0:T(8,128)(2,1)}, bf16[192,1024]{1,0:T(8,128)(2,1)}, u32[]{:S(2)}, u32[]{:S(2)}) collective-permute-start(bf16[192,1024]{1,0:T(8,128)(2,1)} %get-tuple-element.55), channel_id=1, source_target_pairs={{0,8},{8,0},{4,12},{12,4},{1,9},{9,1},{5,13},{13,5},{2,10},{10,2},... | collective-permute-start | bytes 1179656 | tf_op jit(solution)/shard_map/ppermute | solution.py:493
  87.1 22.7 %collective-permute-start.11 = (bf16[192,1024]{1,0:T(8,128)(2,1)}, bf16[192,1024]{1,0:T(8,128)(2,1)}, u32[]{:S(2)}, u32[]{:S(2)}) collective-permute-start(bf16[192,1024]{1,0:T(8,128)(2,1)} %get-tuple-element.56), channel_id=1, source_target_pairs={{0,12},{12,0},{4,8},{8,4},{1,13},{13,1},{5,9},{9,5},{2,14},{14,2},... | collective-permute-start | bytes 1179656 | tf_op jit(solution)/shard_map/ppermute | solution.py:496
  87.1 12.1 %collective-permute-start.14 = (bf16[192,2048]{1,0:T(8,128)(2,1)}, bf16[192,2048]{1,0:T(8,128)(2,1)}, u32[]{:S(2)}, u32[]{:S(2)}) collective-permute-start(bf16[192,2048]{1,0:T(8,128)(2,1)} %get-tuple-element.62), channel_id=1, source_target_pairs={{0,4},{4,0},{8,12},{12,8},{1,5},{5,1},{9,13},{13,9},{2,6},{6,2},{1... | collective-permute-start | bytes 2359304 | tf_op jit(solution)/shard_map/ppermute | solution.py:490
  99.1 6.4 %collective-permute-start.9 = (bf16[2,192,2048]{2,1,0:T(8,128)(2,1)}, bf16[2,192,2048]{2,1,0:T(8,128)(2,1)}, u32[]{:S(2)}, u32[]{:S(2)}) collective-permute-start(bf16[2,192,2048]{2,1,0:T(8,128)(2,1)} %get-tuple-element.54), channel_id=1, source_target_pairs={{0,4},{4,0},{8,12},{12,8},{1,5},{5,1},{9,13},{13,9},{2,6},{6,2},{1... | collective-permute-start | bytes 4718600 | tf_op jit(solution)/shard_map/ppermute | solution.py:490
  99.1 1.1 %copy-start.2 = (bf16[192,2048]{1,0:T(8,128)(2,1)S(1)}, bf16[192,2048]{1,0:T(8,128)(2,1)}, u32[]{:S(2)}) copy-start(bf16[192,2048]{1,0:T(8,128)(2,1)} %get-tuple-element.52.rest_0_.mine) | copy-start | bytes 2359300

commit v12 on v11

--- a/solution.py
+++ b/solution.py
@@ -61,10 +61,22 @@
 TOKEN = in_hbm((8, 128), F32)
 
 
+def asked_entries(names, wanted, member, place, listed, rank):
+    member[...] = jnp.zeros_like(member)
+    for i in range(listed):
+        member[i : i + 1, :] = jnp.where(wanted == names[place(i)], 1.0, 0.0)
+    entry = lax.broadcasted_iota(jnp.int32, (member.shape[0], listed * rank), 0)
+    column = lax.broadcasted_iota(jnp.int32, (member.shape[0], listed * rank), 1)
+    to_entry = jnp.where(column // rank == entry, 1.0, 0.0).astype(BF16)
+    return lax.dot_general(
+        member[...].astype(BF16), to_entry, (((0,), (0,)), ((), ())), preferred_element_type=F32
+    )
+
+
 def select_kernel(by_shift, by_target, named, n_rep, cap, pool_dev, rank, slot, lists, pool, *rest):
-    token, idx, counts = rest[-3:]
-    outs = rest[: -3]
-    outs = outs[-(n_rep * len(by_shift) + len(by_target) + named) :]
+    token, idx, counts, member = rest[-4:]
+    outs = rest[:-4]
+    outs = outs[-(n_rep * len(by_shift) + len(by_target) + 2 * named) :]
     token[...] = jnp.zeros_like(token)
     me = lax.axis_index("rep")
     base = me * pool_dev
@@ -85,7 +97,7 @@
             for c, (start, stop) in enumerate(by_target):
                 outs[len(by_shift) * n_rep + c][target, rows, :] = pool[entry, :, start:stop]
     if named:
-        names = outs[-1]
+        names, asked, wanted = outs[-2], outs[-1], rest[0]
         for i in range(n_rep * cap):
             names[i] = -1
         for s in range(n_rep):
@@ -97,25 +109,36 @@
             counts[owner] = k + 1
             names[owner * cap + jnp.minimum(k, cap - 1)] = variant
 
-
-def select(slot, lists, pool, by_shift, by_target, named, n_rep, cap, after=()):
+        def place(i):
+            return lax.rem(me - i // cap + n_rep, n_rep) * cap + i % cap
+
+        asked[...] = asked_entries(names, wanted[...], member, place, n_rep * cap, rank).astype(BF16)
+
+
+def select(slot, lists, pool, by_shift, by_target, wanted, n_rep, cap, after=()):
     pool_dev, rank, width = pool.shape
     shapes = [in_hbm((cap * rank, stop - start)) for start, stop in by_shift for _ in range(n_rep)]
     shapes += [in_hbm((n_rep, cap * rank, stop - start)) for start, stop in by_target]
     specs = [VMEM] * len(shapes)
-    if named:
-        shapes.append(in_hbm((n_rep * cap,), jnp.int32))
-        specs.append(SMEM)
-    return pl.pallas_call(
-        functools.partial(select_kernel, by_shift, by_target, int(named), n_rep, cap, pool_dev, rank),
+    rows = 128
+    for x in wanted:
+        rows = x.shape[1]
+        shapes += [in_hbm((n_rep * cap,), jnp.int32), in_hbm((rows, n_rep * cap * rank))]
+        specs += [SMEM, VMEM]
+    return pl.pallas_call(
+        functools.partial(select_kernel, by_shift, by_target, len(wanted), n_rep, cap, pool_dev, rank),
         out_shape=[*shapes, TOKEN],
-        in_specs=[SMEM, SMEM, VMEM] + [ANY] * len(after),
+        in_specs=[SMEM, SMEM, VMEM] + [VMEM] * len(wanted) + [ANY] * len(after),
         out_specs=[*specs, VMEM],
-        scratch_shapes=[pltpu.SMEM((cap + 1,), jnp.int32), pltpu.SMEM((n_rep,), jnp.int32)],
+        scratch_shapes=[
+            pltpu.SMEM((cap + 1,), jnp.int32),
+            pltpu.SMEM((n_rep,), jnp.int32),
+            pltpu.VMEM((-(-n_rep * cap // 16) * 16, rows), F32),
+        ],
         compiler_params=params(16),
         cost_estimate=order(0),
         name="select",
-    )(*pin(slot, lists, pool), *pin(*after))
+    )(*pin(slot, lists, pool, *wanted), *pin(*after))
 
 
 def product_early_kernel(per, pos, features, weights, keep0, send0, keep1, send1, token):
@@ -313,7 +336,7 @@
     )(*pin(names, wanted), features, *pin(factors), *pin(*after))
 
 
-def delta_kernel(n_blocks, n_before, n_rep, cap, rank, names, wanted, shrunk, late_own, late_recv, *rest):
+def delta_kernel(n_blocks, n_before, known, n_rep, cap, rank, names, wanted, shrunk, late_own, late_recv, *rest):
     blocks, before = rest[:n_blocks], rest[n_blocks : n_blocks + n_before]
     straight, cross = rest[-7:-5] if before else rest[-5:-3]
     member, expand, result = rest[-3:]
@@ -322,32 +345,29 @@
     half = late_own.shape[0]
     own = half // 2
 
-    def product_of(factors, rows):
+    def product_of(factors, rows, known=None):
         columns = pl.ds(pl.multiple_of(rows * half, half), half)
-        asked = wanted[:, columns]
-        member[...] = jnp.zeros_like(member)
-        for i in range(listed):
-            if len(factors) == 1:
-                name = names[i]
-            else:
-                name = names[lax.rem(me - i // cap + n_rep, n_rep) * cap + i % cap]
-            member[i : i + 1, :] = jnp.where(asked == name, 1.0, 0.0)
+        if known is None:
+            by_owner = len(factors) == 1
+
+            def place(i):
+                return i if by_owner else lax.rem(me - i // cap + n_rep, n_rep) * cap + i % cap
+
+            named = asked_entries(names, wanted[:, columns], member, place, listed, rank)
+        else:
+            named = known[...].astype(F32)
         total = jnp.sum(shrunk[:, :, columns], axis=0).astype(BF16)
-        entry = lax.broadcasted_iota(jnp.int32, (member.shape[0], listed * rank), 0)
-        column = lax.broadcasted_iota(jnp.int32, (member.shape[0], listed * rank), 1)
-        to_entry = jnp.where(column // rank == entry, 1.0, 0.0).astype(BF16)
         part = lax.broadcasted_iota(jnp.int32, (rank, listed * rank), 0)
         column = lax.broadcasted_iota(jnp.int32, (rank, listed * rank), 1)
         to_part = jnp.where(lax.rem(column, rank) == part, 1.0, 0.0).astype(BF16)
         turned = (((0,), (0,)), ((), ()))
-        named = lax.dot_general(member[...].astype(BF16), to_entry, turned, preferred_element_type=F32)
         copied = lax.dot_general(total, to_part, turned, preferred_element_type=F32)
         size = listed * rank // len(factors)
         for s, factor in enumerate(factors):
             expand[pl.ds(s * size, size), :] = factor[...]
         result[...] = jnp.dot((named * copied).astype(BF16), expand[...], preferred_element_type=F32)
 
-    product_of(blocks, 1 - chip)
+    product_of(blocks, 1 - chip, rest[n_blocks + n_before] if known else None)
     for out, c in ((straight, core), (cross, 1 - core)):
         rows = pl.ds(pl.multiple_of(c * own, own), own)
         base = late_own[rows, :].astype(F32) + late_recv[rows, :].astype(F32)
@@ -362,19 +382,20 @@
                 out[:, start : start + width] = result[rows, :].astype(BF16)
 
 
-def delta(names, wanted, shrunk, late, blocks, cut, n_rep, cap, rank, own, before=(), after=()):
+def delta(names, wanted, shrunk, late, blocks, cut, n_rep, cap, rank, own, before=(), after=(), asked=()):
     start, stop = cut
     width = stop - start
     listed = n_rep * cap
     shapes = [in_hbm((own, width))] * 2 + ([in_hbm((own, stop))] * 2 if before else [])
     return pl.pallas_call(
-        functools.partial(delta_kernel, len(blocks), len(before), n_rep, cap, rank),
+        functools.partial(delta_kernel, len(blocks), len(before), len(asked), n_rep, cap, rank),
         out_shape=shapes,
         grid=(1,),
         in_specs=[SMEM]
         + [VMEM] * 2
         + [pl.BlockSpec((2 * own, width), lambda i: (0, start // width))] * 2
         + [VMEM] * (len(blocks) + len(before))
+        + [pl.BlockSpec((2 * own, listed * rank), lambda i: (1 - position()[0], 0))] * len(asked)
         + [ANY] * len(after),
         out_specs=[VMEM] * len(shapes),
         scratch_shapes=[
@@ -385,7 +406,7 @@
         compiler_params=params(),
         cost_estimate=order(0),
         name="delta",
-    )(*pin(names, wanted), shrunk, *pin(late[0]), *(pin(late[1]) if before else late[1:]), *pin(*blocks, *before, *after))
+    )(*pin(names, wanted), shrunk, *pin(late[0]), *(pin(late[1]) if before else late[1:]), *pin(*blocks, *before, *asked, *after))
 
 
 def gate_kernel(*refs):
@@ -499,15 +520,15 @@
         return lax.ppermute(x, "rep", [(i, (i + shift) % n_rep) for i in range(n_rep)])
 
     shifts = [s for s in range(1, n_rep) if s != n_rep // 2] + [n_rep // 2]
-    chosen, token = select(pool_slot, variant_list, shrink_pool, (), ((0, width),), False, n_rep, cap)
+    chosen, token = select(pool_slot, variant_list, shrink_pool, (), ((0, width),), (), n_rep, cap)
     shrink = lax.all_to_all(chosen, "rep", 0, 0, tiled=True).reshape(n_rep * cap * rank, width)
 
     keep0, send0, keep1, send1, token = product_early(features, projection, tile, [token])
     sums = [keep0 + over_core(send0), keep1 + over_core(send1)]
     early = [over_chip(x) for x in sums]
 
-    *chosen, second, names, token = select(
-        pool_slot, variant_list, expand_pool, cuts[:1], cuts[1:], True, n_rep, cap, sums
+    *chosen, second, names, asked, token = select(
+        pool_slot, variant_list, expand_pool, cuts[:1], cuts[1:], [request_variant], n_rep, cap, sums
     )
     first = [chosen[0]] + [None] * (n_rep - 1)
     for s in shifts:
@@ -522,7 +543,7 @@
     shrunk = lax.all_gather(part, "tp")
 
     common = (names, request_variant, shrunk, late)
-    straight, cross = delta(*common, first, cuts[0], n_rep, *sizes, own, (), [early[1]])
+    straight, cross = delta(*common, first, cuts[0], n_rep, *sizes, own, (), [early[1]], [asked])
     far = [over_chip(straight), over_both(cross)]
     straight, cross, mine, send = delta(*common, [second], cuts[1], n_rep, *sizes, own, first, [near_base[1], straight])
     last = [over_chip(straight), over_both(cross)]

time: 113 us -> 113 us (level)
  transfers between devices with their start and end apart: 17 -> 17, of which waited for: 4 -> 4; matrix products, arithmetic and copies ran while one was open for 2% -> 2% of each run, Pallas kernels for 57% -> 58%
where the time goes in v12:
time: 113 us
  Pallas kernels  70.7 us (63%)
  starting transfers between devices  23.6 us (21%)
  waiting for transfers between devices  8.78 us (8%)
  blocking collectives  5.79 us (5%)
  other arithmetic  2.4 us (2%)
    pallas_call x1, Pallas kernels, product_columns(): pl.pallas_call(kernel, out_shape=[in_hbm((half, width))] * 2 + [in_hbm((2...  18.3 us
    pallas_call x1, Pallas kernels, product_early(): pl.pallas_call(kernel, out_shape=[sds((half // 2, width))] * 4 + [TOKEN],...  11.5 us
    pallas_call x1, Pallas kernels, product(): pl.pallas_call(kernel, out_shape=[in_hbm(shape) if blocks > 1 else sds(sh...  11.4 us
    pallas_call x3, Pallas kernels, finish(): pl.pallas_call(near_kernel if near else far_kernel, out_shape=sds((own, f...  10.8 us
    pallas_call x2, Pallas kernels, delta(): pl.pallas_call(functools.partial(delta_kernel, len(blocks), len(before),...  9.58 us
    all_to_all x1, starting transfers between devices, paired(): lax.all_to_all(chosen, 'rep', 0, 0, tiled=True)  6.32 us
    pallas_call x2, Pallas kernels, select(): pl.pallas_call(functools.partial(select_kernel, by_shift, by_target, len(...  6.24 us
    ppermute x3, starting transfers between devices, over_rep(): lax.ppermute(x, 'rep', [(i, (i + shift) % n_rep) for i in range(n_rep)])  5.9 us
  transfers between devices with their start and end apart: 17, of which 4 were waited for; matrix products, arithmetic and copies ran while one was open for 2% of the time, Pallas kernels for 58%

profile of v12, /device:TPU:0, one launch (start us, length us, event | category | flops | bytes accessed | tf_op | source)
XLA Modules:
  0.0 112.5 jit_solution(2395446773383571079)
XLA Ops:
  0.0 2.8 %select.2 = (bf16[4,96,2048]{2,1,0:T(8,128)(2,1)}, f32[8,128]{1,0:T(8,128)}) custom-call(s32[64]{0:T(128)} %slot.3, s32[4,24]{1,0:T(4,128)} %lists.3, bf16[16,16,2048]{2,1,0:T(8,128)(2,1)} %pool.2), custom_call_target="tpu_custom_call" | custom-call | flops 1 | bytes 1 | tf_op jit(solution)/shard_map/select/pallas_call | solution.py:128
  2.8 6.3 %all-to-all-start = ((bf16[4,96,2048]{2,1,0:T(8,128)(2,1)}), bf16[4,96,2048]{2,1,0:T(8,128)(2,1)}, u32[]{:S(2)}, u32[]{:S(2)}) async-start(bf16[4,96,2048]{2,1,0:T(8,128)(2,1)} %get-tuple-element.41), calls=%async_computation | async-start | bytes 3145728 | tf_op jit(solution)/shard_map/all_to_all | solution.py:524
  9.2 11.5 %product.3 = (bf16[192,2048]{1,0:T(8,128)(2,1)S(1)}, bf16[192,2048]{1,0:T(8,128)(2,1)S(1)}, bf16[192,2048]{1,0:T(8,128)(2,1)S(1)}, bf16[192,2048]{1,0:T(8,128)(2,1)S(1)}, f32[8,128]{1,0:T(8,128)}) custom-call(bf16[768,2048]{1,0:T(8,128)(2,1)} %bitcast.6, bf16[2048,8192]{1,0:T(8,128)(2,1)} %weights.5, f32[8,128]{1,0:T(8,128)} %get-tuple-element.35.rest_0_), custom_call_target="tpu_custom_call" | custom-call | flops 1 | bytes 1 | tf_op jit(solution)/shard_map/product/pallas_call | solution.py:170
  21.1 1.8 %collective-permute-done = bf16[192,2048]{1,0:T(8,128)(2,1)S(1)} collective-permute-done((bf16[192,2048]{1,0:T(8,128)(2,1)S(1)}, bf16[192,2048]{1,0:T(8,128)(2,1)S(1)}, u32[]{:S(2)}, u32[]{:S(2)}) %collective-permute-start) | collective-permute-done | bytes 786464 | tf_op jit(solution)/shard_map/ppermute | solution.py:511
  24.1 1.5 %collective-permute-start.2 = (bf16[192,2048]{1,0:T(8,128)(2,1)}, bf16[192,2048]{1,0:T(8,128)(2,1)}, u32[]{:S(2)}, u32[]{:S(2)}) collective-permute-start(bf16[192,2048]{1,0:T(8,128)(2,1)} %add.6.rest_1_.rest_0_), channel_id=1, source_target_pairs={{0,8},{8,0},{4,12},{12,4},{1,9},{9,1},{5,13},{13,5},{2,10},{10,2},... | collective-permute-start | bytes 2359304 | tf_op jit(solution)/shard_map/ppermute | solution.py:514
  25.6 1.2 %add.7.rest_2_.rest_1_ = bf16[192,2048]{1,0:T(8,128)(2,1)} add(bf16[192,2048]{1,0:T(8,128)(2,1)S(1)} %get-tuple-element.38, bf16[192,2048]{1,0:T(8,128)(2,1)S(1)} %collective-permute-done.1) | non-fusion elementwise | flops 393216 | bytes 2359296 | tf_op jit(solution)/shard_map/add | solution.py:527
  26.8 3.4 %select.3 = (bf16[96,1024]{1,0:T(8,128)(2,1)}, bf16[96,1024]{1,0:T(8,128)(2,1)}, bf16[96,1024]{1,0:T(8,128)(2,1)}, bf16[96,1024]{1,0:T(8,128)(2,1)}, bf16[4,96,1...) custom-call(s32[64]{0:T(128)} %slot.3, s32[4,24]{1,0:T(4,128)} %lists.3, ...), custom_call_target="tpu_custom_call" | custom-call | flops 1 | bytes 1 | tf_op jit(solution)/shard_map/select/pallas_call | solution.py:128
  30.3 2.1 %collective-permute-start.4 = (bf16[96,1024]{1,0:T(8,128)(2,1)}, bf16[96,1024]{1,0:T(8,128)(2,1)S(1)}, u32[]{:S(2)}, u32[]{:S(2)}) collective-permute-start(bf16[96,1024]{1,0:T(8,128)(2,1)} %get-tuple-element.48), channel_id=1, source_target_pairs={{0,1},{1,2},{2,3},{3,0},{4,5},{5,6},{6,7},{7,4},{8,9},{9,10},{10,1... | collective-permute-start | bytes 589832 | tf_op jit(solution)/shard_map/ppermute | solution.py:520
  32.8 2.4 %collective-permute-start.5 = (bf16[96,1024]{1,0:T(8,128)(2,1)}, bf16[96,1024]{1,0:T(8,128)(2,1)}, u32[]{:S(2)}, u32[]{:S(2)}) collective-permute-start(bf16[96,1024]{1,0:T(8,128)(2,1)} %get-tuple-element.49), channel_id=1, source_target_pairs={{0,2},{1,3},{2,0},{3,1},{4,6},{5,7},{6,4},{7,5},{8,10},{9,11},{10,... | collective-permute-start | bytes 589832 | tf_op jit(solution)/shard_map/ppermute | solution.py:520
  35.2 1.5 %collective-permute-start.6 = (bf16[96,1024]{1,0:T(8,128)(2,1)}, bf16[96,1024]{1,0:T(8,128)(2,1)}, u32[]{:S(2)}, u32[]{:S(2)}) collective-permute-start(bf16[96,1024]{1,0:T(8,128)(2,1)} %get-tuple-element.50), channel_id=1, source_target_pairs={{0,3},{1,0},{2,1},{3,2},{4,7},{5,4},{6,5},{7,6},{8,11},{9,8},{10,9... | collective-permute-start | bytes 589832 | tf_op jit(solution)/shard_map/ppermute | solution.py:520
  36.7 18.3 %product.4 = (bf16[384,2048]{1,0:T(8,128)(2,1)}, bf16[384,2048]{1,0:T(8,128)(2,1)}, bf16[2,192,2048]{2,1,0:T(8,128)(2,1)}, bf16[2,192,2048]{2,1,0:T(8,128)(2,1)}, f32[8,128]{1,0:T(8,128)}) custom-call(bf16[768,2048]{1,0:T(8,128)(2,1)S(1)} %bitcast.7, bf16[2048,8192]{1,0:T(8,128)(2,1)} %weights.5, bf16[192,2048]{1,0:T(8,128)(2,1)} %add.6.rest_1_.rest_0_, ...), custom_call_target="tpu_custom_call" | custom-call | flops 1 | bytes 1 | tf_op jit(solution)/shard_map/product/pallas_call | solution.py:228
  55.7 4.2 %all-to-all-start.1 = ((bf16[4,96,1024]{2,1,0:T(8,128)(2,1)}), bf16[4,96,1024]{2,1,0:T(8,128)(2,1)}, u32[]{:S(2)}, u32[]{:S(2)}) async-start(bf16[4,96,1024]{2,1,0:T(8,128)(2,1)} %get-tuple-element.46), calls=%async_computation.1 | async-start | bytes 1572864 | tf_op jit(solution)/shard_map/all_to_all | solution.py:536
  60.5 2.9 %score.1 = f32[16,768]{1,0:T(8,128)S(1)} custom-call(s32[24]{0:T(128)} %get-tuple-element.40.names, s32[1,768]{1,0:T(1,128)} %wanted.5, bf16[768,2048]{1,0:T(8,128)(2,1)S(1)} %bitcast.8, bf16[384,2048]{1,0:T(8,128)(2,1)} %bitcast.2.factors, f32[8,128]{1,0:T(8,128)} %get-tuple-element.43.rest_0_, bf16[192,2048]{1,0:T(8,128)(2,1)} %collective-permute-done.2.rest_1_.first), custom_call_target="tpu_custom_call" | custom-call | flops 46000001024 | bytes 1 | tf_op jit(solution)/shard_map/score/pallas_call | solution.py:327
  63.4 5.8 %all-gather = f32[64,768]{1,0:T(8,128)S(1)} all-gather(f32[16,768]{1,0:T(8,128)S(1)} %score.1), channel_id=2, replica_groups=mesh['groups'=2,'tp'=4,'rep'=4] {'tp'}, dimensions={0}, use_global_device_ids=true | all-gather | bytes 245760 | tf_op jit(solution)/shard_map/all_gather | solution.py:543
  69.2 4.0 %delta.2 = (bf16[192,1024]{1,0:T(8,128)(2,1)}, bf16[192,1024]{1,0:T(8,128)(2,1)}) custom-call(s32[24]{0:T(128)} %get-tuple-element.40.names, s32[1,768]{1,0:T(1,128)} %wanted.5, f32[4,16,768]{2,1,0:T(8,128)S(1)} %bitcast.10, bf16[384,2048]{1,0:T(8,128)(2,1)} %get-tuple-element.44.late_own, bf16[384,2048]{1,0:T(8,128)(2,1)S(1)} %collective-permute-done.3.late_recv, ...), custom_call_target="tpu_custom_call" | custom-call | flops 1 | bytes 1 | tf_op jit(solution)/shard_map/delta/pallas_call | solution.py:390
  73.2 1.5 %collective-permute-start.13 = (bf16[192,1024]{1,0:T(8,128)(2,1)}, bf16[192,1024]{1,0:T(8,128)(2,1)}, u32[]{:S(2)}, u32[]{:S(2)}) collective-permute-start(bf16[192,1024]{1,0:T(8,128)(2,1)} %get-tuple-element.59), channel_id=1, source_target_pairs={{0,12},{12,0},{4,8},{8,4},{1,13},{13,1},{5,9},{9,5},{2,14},{14,2},... | collective-permute-start | bytes 1179656 | tf_op jit(solution)/shard_map/ppermute | solution.py:517
  75.2 4.8 %all-to-all-done.1 = bf16[4,96,1024]{2,1,0:T(8,128)(2,1)} async-done(((bf16[4,96,1024]{2,1,0:T(8,128)(2,1)}), bf16[4,96,1024]{2,1,0:T(8,128)(2,1)}, u32[]{:S(2)}, u32[]{:S(2)}) %all-to-all-start.1) | async-done | bytes 786464 | tf_op jit(solution)/shard_map/all_to_all | solution.py:536
  80.0 5.6 %delta.3 = (bf16[192,1024]{1,0:T(8,128)(2,1)}, bf16[192,1024]{1,0:T(8,128)(2,1)}, bf16[192,2048]{1,0:T(8,128)(2,1)}, bf16[192,2048]{1,0:T(8,128)(2,1)}) custom-call(s32[24]{0:T(128)} %get-tuple-element.40.names, s32[1,768]{1,0:T(1,128)} %wanted.5, f32[4,16,768]{2,1,0:T(8,128)S(1)} %bitcast.11, bf16[384,2048]{1,0:T(8,128)(2,1)} %get-tuple-element.44.late_own, ...), custom_call_target="tpu_custom_call" | custom-call | flops 1 | bytes 1 | tf_op jit(solution)/shard_map/delta/pallas_call | solution.py:390
  85.6 1.5 %collective-permute-start.10 = (bf16[192,1024]{1,0:T(8,128)(2,1)}, bf16[192,1024]{1,0:T(8,128)(2,1)}, u32[]{:S(2)}, u32[]{:S(2)}) collective-permute-start(bf16[192,1024]{1,0:T(8,128)(2,1)} %get-tuple-element.57), channel_id=1, source_target_pairs={{0,8},{8,0},{4,12},{12,4},{1,9},{9,1},{5,13},{13,5},{2,10},{10,2},... | collective-permute-start | bytes 1179656 | tf_op jit(solution)/shard_map/ppermute | solution.py:514
  87.7 11.4 %product.5 = (bf16[2,192,2048]{2,1,0:T(8,128)(2,1)}, bf16[2,192,2048]{2,1,0:T(8,128)(2,1)}, f32[8,128]{1,0:T(8,128)}) custom-call(bf16[768,2048]{1,0:T(8,128)(2,1)S(1)} %bitcast.9, bf16[2048,8192]{1,0:T(8,128)(2,1)} %weights.5, bf16[192,2048]{1,0:T(8,128)(2,1)} %get-tuple-element.54.rest_0_.mine), custom_call_target="tpu_custom_call" | custom-call | flops 1 | bytes 1 | tf_op jit(solution)/shard_map/product/pallas_call | solution.py:299
  100.3 5.2 %near.1.rest_0_ = bf16[192,8192]{1,0:T(8,128)(2,1)} custom-call(bf16[192,8192]{1,0:T(8,128)(2,1)} %bitcast.12, bf16[2,192,2048]{2,1,0:T(8,128)(2,1)} %get-tuple-element.63.keep, bf16[2,192,2048]{2,1,0:T(8,128)(2,1)} %collective-permute-done.7.rest_5_.recv, bf16[192,2048]{1,0:T(8,128)(2,1)} %collective-permute-done.2.rest_1_.first, ...), custom_call_target="tpu_custom_call" | custom-call | flops 69000003584 | bytes 1 | tf_op jit(solution)/shard_map/near/pallas_call | solution.py:480
  105.5 2.8 %far.2.rest_0_ = bf16[192,8192]{1,0:T(8,128)(2,1)} custom-call(bf16[192,8192]{1,0:T(8,128)(2,1)} %bitcast.13, bf16[2,192,2048]{2,1,0:T(8,128)(2,1)} %get-tuple-element.55.keep, bf16[2,192,2048]{2,1,0:T(8,128)(2,1)} %collective-permute-done.9.recv, bf16[192,1024]{1,0:T(8,128)(2,1)} %get-tuple-element.61.rest_0_.straight, ...), custom_call_target="tpu_custom_call", output_to_operand_aliasing={{}: (5, {})} | custom-call | flops 69000003584 | bytes 1 | tf_op jit(solution)/shard_map/far/pallas_call | solution.py:480
  108.3 1.4 %collective-permute-done.11.cross = bf16[192,1024]{1,0:T(8,128)(2,1)} collective-permute-done((bf16[192,1024]{1,0:T(8,128)(2,1)}, bf16[192,1024]{1,0:T(8,128)(2,1)}, u32[]{:S(2)}, u32[]{:S(2)}) %collective-permute-start.11) | collective-permute-done | bytes 393248 | tf_op jit(solution)/shard_map/ppermute | solution.py:517
  109.8 2.8 %far.3 = bf16[192,8192]{1,0:T(8,128)(2,1)} custom-call(bf16[192,8192]{1,0:T(8,128)(2,1)} %bitcast.14, bf16[2,192,2048]{2,1,0:T(8,128)(2,1)} %get-tuple-element.55.keep, bf16[2,192,2048]{2,1,0:T(8,128)(2,1)} %collective-permute-done.9.recv, bf16[192,1024]{1,0:T(8,128)(2,1)} %collective-permute-done.10.straight, ...), custom_call_target="tpu_custom_call", output_to_operand_aliasing={{}: (5, {})} | custom-call | flops 69000003584 | bytes 1 | tf_op jit(solution)/shard_map/far/pallas_call | solution.py:480
  (33 shorter events, 5.8 us)
Async XLA Ops:
  2.8 52.9 %all-to-all-start = ((bf16[4,96,2048]{2,1,0:T(8,128)(2,1)}), bf16[4,96,2048]{2,1,0:T(8,128)(2,1)}, u32[]{:S(2)}, u32[]{:S(2)}) async-start(bf16[4,96,2048]{2,1,0:T(8,128)(2,1)} %get-tuple-element.41), calls=%async_computation | async-start | bytes 3145728 | tf_op jit(solution)/shard_map/all_to_all | solution.py:524
  20.6 2.3 %collective-permute-start = (bf16[192,2048]{1,0:T(8,128)(2,1)S(1)}, bf16[192,2048]{1,0:T(8,128)(2,1)S(1)}, u32[]{:S(2)}, u32[]{:S(2)}) collective-permute-start(bf16[192,2048]{1,0:T(8,128)(2,1)S(1)} %get-tuple-element.37), channel_id=1, source_target_pairs={{0,4},{4,0},{8,12},{12,8},{1,5},{5,1},{9,13},{13,9},{2,6},{6,2},{1... | collective-permute-start | bytes 2359304 | tf_op jit(solution)/shard_map/ppermute | solution.py:511
  20.6 5.0 %collective-permute-start.1 = (bf16[192,2048]{1,0:T(8,128)(2,1)S(1)}, bf16[192,2048]{1,0:T(8,128)(2,1)S(1)}, u32[]{:S(2)}, u32[]{:S(2)}) collective-permute-start(bf16[192,2048]{1,0:T(8,128)(2,1)S(1)} %get-tuple-element.39), channel_id=1, source_target_pairs={{0,4},{4,0},{8,12},{12,8},{1,5},{5,1},{9,13},{13,9},{2,6},{6,2},{1... | collective-permute-start | bytes 2359304 | tf_op jit(solution)/shard_map/ppermute | solution.py:511
  24.1 36.0 %collective-permute-start.2 = (bf16[192,2048]{1,0:T(8,128)(2,1)}, bf16[192,2048]{1,0:T(8,128)(2,1)}, u32[]{:S(2)}, u32[]{:S(2)}) collective-permute-start(bf16[192,2048]{1,0:T(8,128)(2,1)} %add.6.rest_1_.rest_0_), channel_id=1, source_target_pairs={{0,8},{8,0},{4,12},{12,4},{1,9},{9,1},{5,13},{13,5},{2,10},{10,2},... | collective-permute-start | bytes 2359304 | tf_op jit(solution)/shard_map/ppermute | solution.py:514
  25.6 11.1 %copy-start = (bf16[1,768,2048]{2,1,0:T(8,128)(2,1)S(1)}, bf16[1,768,2048]{2,1,0:T(8,128)(2,1)}, u32[]{:S(2)}) copy-start(bf16[1,768,2048]{2,1,0:T(8,128)(2,1)} %param.8) | copy-start | bytes 9437188
  30.3 29.7 %collective-permute-start.4 = (bf16[96,1024]{1,0:T(8,128)(2,1)}, bf16[96,1024]{1,0:T(8,128)(2,1)S(1)}, u32[]{:S(2)}, u32[]{:S(2)}) collective-permute-start(bf16[96,1024]{1,0:T(8,128)(2,1)} %get-tuple-element.48), channel_id=1, source_target_pairs={{0,1},{1,2},{2,3},{3,0},{4,5},{5,6},{6,7},{7,4},{8,9},{9,10},{10,1... | collective-permute-start | bytes 589832 | tf_op jit(solution)/shard_map/ppermute | solution.py:520
  32.3 36.9 %collective-permute-start.8 = (bf16[192,2048]{1,0:T(8,128)(2,1)}, bf16[192,2048]{1,0:T(8,128)(2,1)}, u32[]{:S(2)}, u32[]{:S(2)}) collective-permute-start(bf16[192,2048]{1,0:T(8,128)(2,1)} %add.7.rest_2_.rest_1_), channel_id=1, source_target_pairs={{0,8},{8,0},{4,12},{12,4},{1,9},{9,1},{5,13},{13,5},{2,10},{10,2},... | collective-permute-start | bytes 2359304 | tf_op jit(solution)/shard_map/ppermute | solution.py:514
  32.8 36.4 %collective-permute-start.5 = (bf16[96,1024]{1,0:T(8,128)(2,1)}, bf16[96,1024]{1,0:T(8,128)(2,1)}, u32[]{:S(2)}, u32[]{:S(2)}) collective-permute-start(bf16[96,1024]{1,0:T(8,128)(2,1)} %get-tuple-element.49), channel_id=1, source_target_pairs={{0,2},{1,3},{2,0},{3,1},{4,6},{5,7},{6,4},{7,5},{8,10},{9,11},{10,... | collective-permute-start | bytes 589832 | tf_op jit(solution)/shard_map/ppermute | solution.py:520
  35.2 34.0 %collective-permute-start.6 = (bf16[96,1024]{1,0:T(8,128)(2,1)}, bf16[96,1024]{1,0:T(8,128)(2,1)}, u32[]{:S(2)}, u32[]{:S(2)}) collective-permute-start(bf16[96,1024]{1,0:T(8,128)(2,1)} %get-tuple-element.50), channel_id=1, source_target_pairs={{0,3},{1,0},{2,1},{3,2},{4,7},{5,4},{6,5},{7,6},{8,11},{9,8},{10,9... | collective-permute-start | bytes 589832 | tf_op jit(solution)/shard_map/ppermute | solution.py:520
  55.7 24.2 %all-to-all-start.1 = ((bf16[4,96,1024]{2,1,0:T(8,128)(2,1)}), bf16[4,96,1024]{2,1,0:T(8,128)(2,1)}, u32[]{:S(2)}, u32[]{:S(2)}) async-start(bf16[4,96,1024]{2,1,0:T(8,128)(2,1)} %get-tuple-element.46), calls=%async_computation.1 | async-start | bytes 1572864 | tf_op jit(solution)/shard_map/all_to_all | solution.py:536
  60.0 3.5 %copy-start.3 = (bf16[96,1024]{1,0:T(8,128)(2,1)}, bf16[96,1024]{1,0:T(8,128)(2,1)S(1)}, u32[]{:S(2)}) copy-start(bf16[96,1024]{1,0:T(8,128)(2,1)S(1)} %collective-permute-done.4.rest_1_.rest_2_) | copy-start | bytes 589828
  60.0 9.3 %collective-permute-start.3 = (bf16[384,2048]{1,0:T(8,128)(2,1)}, bf16[384,2048]{1,0:T(8,128)(2,1)S(1)}, u32[]{:S(2)}, u32[]{:S(2)}) collective-permute-start(bf16[384,2048]{1,0:T(8,128)(2,1)} %get-tuple-element.45), channel_id=1, source_target_pairs={{0,4},{4,0},{8,12},{12,8},{1,5},{5,1},{9,13},{13,9},{2,6},{6,2},{1... | collective-permute-start | bytes 4718600 | tf_op jit(solution)/shard_map/ppermute | solution.py:511
  60.1 19.9 %collective-permute-start.7 = (bf16[2,192,2048]{2,1,0:T(8,128)(2,1)}, bf16[2,192,2048]{2,1,0:T(8,128)(2,1)}, u32[]{:S(2)}, u32[]{:S(2)}) collective-permute-start(bf16[2,192,2048]{2,1,0:T(8,128)(2,1)} %get-tuple-element.51), channel_id=1, source_target_pairs={{0,4},{4,0},{8,12},{12,8},{1,5},{5,1},{9,13},{13,9},{2,6},{6,2},{1... | collective-permute-start | bytes 4718600 | tf_op jit(solution)/shard_map/ppermute | solution.py:511
  69.2 4.0 %copy-start.1 = (bf16[384,2048]{1,0:T(8,128)(2,1)}, bf16[384,2048]{1,0:T(8,128)(2,1)S(1)}, u32[]{:S(2)}) copy-start(bf16[384,2048]{1,0:T(8,128)(2,1)S(1)} %collective-permute-done.3.late_recv) | copy-start | bytes 4718596
  73.2 25.9 %collective-permute-start.13 = (bf16[192,1024]{1,0:T(8,128)(2,1)}, bf16[192,1024]{1,0:T(8,128)(2,1)}, u32[]{:S(2)}, u32[]{:S(2)}) collective-permute-start(bf16[192,1024]{1,0:T(8,128)(2,1)} %get-tuple-element.59), channel_id=1, source_target_pairs={{0,12},{12,0},{4,8},{8,4},{1,13},{13,1},{5,9},{9,5},{2,14},{14,2},... | collective-permute-start | bytes 1179656 | tf_op jit(solution)/shard_map/ppermute | solution.py:517
  74.7 24.5 %collective-permute-start.12 = (bf16[192,1024]{1,0:T(8,128)(2,1)}, bf16[192,1024]{1,0:T(8,128)(2,1)}, u32[]{:S(2)}, u32[]{:S(2)}) collective-permute-start(bf16[192,1024]{1,0:T(8,128)(2,1)} %get-tuple-element.53.rest_6_), channel_id=1, source_target_pairs={{0,8},{8,0},{4,12},{12,4},{1,9},{9,1},{5,13},{13,5},{2,10},{10,2},... | collective-permute-start | bytes 1179656 | tf_op jit(solution)/shard_map/ppermute | solution.py:514
  85.6 22.7 %collective-permute-start.10 = (bf16[192,1024]{1,0:T(8,128)(2,1)}, bf16[192,1024]{1,0:T(8,128)(2,1)}, u32[]{:S(2)}, u32[]{:S(2)}) collective-permute-start(bf16[192,1024]{1,0:T(8,128)(2,1)} %get-tuple-element.57), channel_id=1, source_target_pairs={{0,8},{8,0},{4,12},{12,4},{1,9},{9,1},{5,13},{13,5},{2,10},{10,2},... | collective-permute-start | bytes 1179656 | tf_op jit(solution)/shard_map/ppermute | solution.py:514
  87.1 22.6 %collective-permute-start.11 = (bf16[192,1024]{1,0:T(8,128)(2,1)}, bf16[192,1024]{1,0:T(8,128)(2,1)}, u32[]{:S(2)}, u32[]{:S(2)}) collective-permute-start(bf16[192,1024]{1,0:T(8,128)(2,1)} %get-tuple-element.58), channel_id=1, source_target_pairs={{0,12},{12,0},{4,8},{8,4},{1,13},{13,1},{5,9},{9,5},{2,14},{14,2},... | collective-permute-start | bytes 1179656 | tf_op jit(solution)/shard_map/ppermute | solution.py:517
  87.1 12.1 %collective-permute-start.14 = (bf16[192,2048]{1,0:T(8,128)(2,1)}, bf16[192,2048]{1,0:T(8,128)(2,1)}, u32[]{:S(2)}, u32[]{:S(2)}) collective-permute-start(bf16[192,2048]{1,0:T(8,128)(2,1)} %get-tuple-element.64), channel_id=1, source_target_pairs={{0,4},{4,0},{8,12},{12,8},{1,5},{5,1},{9,13},{13,9},{2,6},{6,2},{1... | collective-permute-start | bytes 2359304 | tf_op jit(solution)/shard_map/ppermute | solution.py:511
  99.1 6.4 %collective-permute-start.9 = (bf16[2,192,2048]{2,1,0:T(8,128)(2,1)}, bf16[2,192,2048]{2,1,0:T(8,128)(2,1)}, u32[]{:S(2)}, u32[]{:S(2)}) collective-permute-start(bf16[2,192,2048]{2,1,0:T(8,128)(2,1)} %get-tuple-element.56), channel_id=1, source_target_pairs={{0,4},{4,0},{8,12},{12,8},{1,5},{5,1},{9,13},{13,9},{2,6},{6,2},{1... | collective-permute-start | bytes 4718600 | tf_op jit(solution)/shard_map/ppermute | solution.py:511
  99.2 1.1 %copy-start.2 = (bf16[192,2048]{1,0:T(8,128)(2,1)S(1)}, bf16[192,2048]{1,0:T(8,128)(2,1)}, u32[]{:S(2)}) copy-start(bf16[192,2048]{1,0:T(8,128)(2,1)} %get-tuple-element.54.rest_0_.mine) | copy-start | bytes 2359300

commit v13 on v12

--- a/solution.py
+++ b/solution.py
@@ -442,7 +442,7 @@
     out[...] = total.astype(BF16)
 
 
-def finish(out, residual, base, start, stop, near, pieces, after=()):
+def finish(out, residual, base, start, stop, near, pieces, after=(), pinned=True):
     own, full = residual.shape
     width = full // 4
     size = stop - start
@@ -471,7 +471,8 @@
     part = pl.BlockSpec((1, own, tile), lambda b, j, pos: (b, 0, skip + j))
     specs = [part, part, *(by_block if near else []), by_core(0), by_core(1)]
     specs = specs + [ANY] * len(after)
-    operands = [*pin(residual, *base), *pieces, *pin(*after)]
+    fixed = pin(residual, *base) if pinned else [residual, *base]
+    operands = [*fixed, *pieces, *pin(*after)]
     aliases = {}
     if out is not None:
         specs = specs + [ANY]
@@ -553,7 +554,7 @@
     far = gate(far, [token])
     out = finish(None, stream, near_base, 0, width, True, [*early, mine, theirs], far)
     out = finish(out, stream, far_base, *cuts[0], False, far)
-    out = finish(out, stream, far_base, *cuts[1], False, last)
+    out = finish(out, stream, far_base, *cuts[1], False, last, pinned=False)
     return out[None]
 
 

time: 113 us -> 113 us (level)
  no operation moved by 1% of the time
where the time goes in v13:
time: 113 us; the launch traced here: 112 us
  Pallas kernels  70.7 us (63%)
  starting transfers between devices  23.6 us (21%)
  waiting for transfers between devices  8.58 us (8%)
  blocking collectives  5.79 us (5%)
  other arithmetic  2.39 us (2%)
    pallas_call x1, Pallas kernels, product_columns(): pl.pallas_call(kernel, out_shape=[in_hbm((half, width))] * 2 + [in_hbm((2...  18.4 us
    pallas_call x1, Pallas kernels, product_early(): pl.pallas_call(kernel, out_shape=[sds((half // 2, width))] * 4 + [TOKEN],...  11.5 us
    pallas_call x1, Pallas kernels, product(): pl.pallas_call(kernel, out_shape=[in_hbm(shape) if blocks > 1 else sds(sh...  11.4 us
    pallas_call x3, Pallas kernels, finish(): pl.pallas_call(near_kernel if near else far_kernel, out_shape=sds((own, f...  10.7 us
    pallas_call x2, Pallas kernels, delta(): pl.pallas_call(functools.partial(delta_kernel, len(blocks), len(before),...  9.65 us
    all_to_all x1, starting transfers between devices, paired(): lax.all_to_all(chosen, 'rep', 0, 0, tiled=True)  6.32 us
    pallas_call x2, Pallas kernels, select(): pl.pallas_call(functools.partial(select_kernel, by_shift, by_target, len(...  6.27 us
    ppermute x3, starting transfers between devices, over_rep(): lax.ppermute(x, 'rep', [(i, (i + shift) % n_rep) for i in range(n_rep)])  5.9 us
  transfers between devices with their start and end apart: 17, of which 4 were waited for; matrix products, arithmetic and copies ran while one was open for 2% of the time, Pallas kernels for 58%

profile of v13, /device:TPU:0, one launch (start us, length us, event | category | flops | bytes accessed | tf_op | source)
XLA Modules:
  0.0 112.4 jit_solution(114349392525843977)
XLA Ops:
  0.0 2.8 %select.2 = (bf16[4,96,2048]{2,1,0:T(8,128)(2,1)}, f32[8,128]{1,0:T(8,128)}) custom-call(s32[64]{0:T(128)} %slot.3, s32[4,24]{1,0:T(4,128)} %lists.3, bf16[16,16,2048]{2,1,0:T(8,128)(2,1)} %pool.2), custom_call_target="tpu_custom_call" | custom-call | flops 1 | bytes 1 | tf_op jit(solution)/shard_map/select/pallas_call | solution.py:128
  2.8 6.3 %all-to-all-start = ((bf16[4,96,2048]{2,1,0:T(8,128)(2,1)}), bf16[4,96,2048]{2,1,0:T(8,128)(2,1)}, u32[]{:S(2)}, u32[]{:S(2)}) async-start(bf16[4,96,2048]{2,1,0:T(8,128)(2,1)} %get-tuple-element.41), calls=%async_computation | async-start | bytes 3145728 | tf_op jit(solution)/shard_map/all_to_all | solution.py:525
  9.2 11.5 %product.3 = (bf16[192,2048]{1,0:T(8,128)(2,1)S(1)}, bf16[192,2048]{1,0:T(8,128)(2,1)S(1)}, bf16[192,2048]{1,0:T(8,128)(2,1)S(1)}, bf16[192,2048]{1,0:T(8,128)(2,1)S(1)}, f32[8,128]{1,0:T(8,128)}) custom-call(bf16[768,2048]{1,0:T(8,128)(2,1)} %bitcast.6, bf16[2048,8192]{1,0:T(8,128)(2,1)} %weights.5, f32[8,128]{1,0:T(8,128)} %get-tuple-element.35.rest_0_), custom_call_target="tpu_custom_call" | custom-call | flops 1 | bytes 1 | tf_op jit(solution)/shard_map/product/pallas_call | solution.py:170
  21.1 1.8 %collective-permute-done = bf16[192,2048]{1,0:T(8,128)(2,1)S(1)} collective-permute-done((bf16[192,2048]{1,0:T(8,128)(2,1)S(1)}, bf16[192,2048]{1,0:T(8,128)(2,1)S(1)}, u32[]{:S(2)}, u32[]{:S(2)}) %collective-permute-start) | collective-permute-done | bytes 786464 | tf_op jit(solution)/shard_map/ppermute | solution.py:512
  24.1 1.5 %collective-permute-start.2 = (bf16[192,2048]{1,0:T(8,128)(2,1)}, bf16[192,2048]{1,0:T(8,128)(2,1)}, u32[]{:S(2)}, u32[]{:S(2)}) collective-permute-start(bf16[192,2048]{1,0:T(8,128)(2,1)} %add.6.rest_1_.rest_0_), channel_id=1, source_target_pairs={{0,8},{8,0},{4,12},{12,4},{1,9},{9,1},{5,13},{13,5},{2,10},{10,2},... | collective-permute-start | bytes 2359304 | tf_op jit(solution)/shard_map/ppermute | solution.py:515
  25.6 1.2 %add.7.rest_2_.rest_1_ = bf16[192,2048]{1,0:T(8,128)(2,1)} add(bf16[192,2048]{1,0:T(8,128)(2,1)S(1)} %get-tuple-element.38, bf16[192,2048]{1,0:T(8,128)(2,1)S(1)} %collective-permute-done.1) | non-fusion elementwise | flops 393216 | bytes 2359296 | tf_op jit(solution)/shard_map/add | solution.py:528
  26.8 3.4 %select.3 = (bf16[96,1024]{1,0:T(8,128)(2,1)}, bf16[96,1024]{1,0:T(8,128)(2,1)}, bf16[96,1024]{1,0:T(8,128)(2,1)}, bf16[96,1024]{1,0:T(8,128)(2,1)}, bf16[4,96,1...) custom-call(s32[64]{0:T(128)} %slot.3, s32[4,24]{1,0:T(4,128)} %lists.3, ...), custom_call_target="tpu_custom_call" | custom-call | flops 1 | bytes 1 | tf_op jit(solution)/shard_map/select/pallas_call | solution.py:128
  30.3 2.1 %collective-permute-start.4 = (bf16[96,1024]{1,0:T(8,128)(2,1)}, bf16[96,1024]{1,0:T(8,128)(2,1)S(1)}, u32[]{:S(2)}, u32[]{:S(2)}) collective-permute-start(bf16[96,1024]{1,0:T(8,128)(2,1)} %get-tuple-element.48), channel_id=1, source_target_pairs={{0,1},{1,2},{2,3},{3,0},{4,5},{5,6},{6,7},{7,4},{8,9},{9,10},{10,1... | collective-permute-start | bytes 589832 | tf_op jit(solution)/shard_map/ppermute | solution.py:521
  32.8 2.4 %collective-permute-start.5 = (bf16[96,1024]{1,0:T(8,128)(2,1)}, bf16[96,1024]{1,0:T(8,128)(2,1)}, u32[]{:S(2)}, u32[]{:S(2)}) collective-permute-start(bf16[96,1024]{1,0:T(8,128)(2,1)} %get-tuple-element.49), channel_id=1, source_target_pairs={{0,2},{1,3},{2,0},{3,1},{4,6},{5,7},{6,4},{7,5},{8,10},{9,11},{10,... | collective-permute-start | bytes 589832 | tf_op jit(solution)/shard_map/ppermute | solution.py:521
  35.2 1.5 %collective-permute-start.6 = (bf16[96,1024]{1,0:T(8,128)(2,1)}, bf16[96,1024]{1,0:T(8,128)(2,1)}, u32[]{:S(2)}, u32[]{:S(2)}) collective-permute-start(bf16[96,1024]{1,0:T(8,128)(2,1)} %get-tuple-element.50), channel_id=1, source_target_pairs={{0,3},{1,0},{2,1},{3,2},{4,7},{5,4},{6,5},{7,6},{8,11},{9,8},{10,9... | collective-permute-start | bytes 589832 | tf_op jit(solution)/shard_map/ppermute | solution.py:521
  36.7 18.4 %product.4 = (bf16[384,2048]{1,0:T(8,128)(2,1)}, bf16[384,2048]{1,0:T(8,128)(2,1)}, bf16[2,192,2048]{2,1,0:T(8,128)(2,1)}, bf16[2,192,2048]{2,1,0:T(8,128)(2,1)}, f32[8,128]{1,0:T(8,128)}) custom-call(bf16[768,2048]{1,0:T(8,128)(2,1)S(1)} %bitcast.7, bf16[2048,8192]{1,0:T(8,128)(2,1)} %weights.5, bf16[192,2048]{1,0:T(8,128)(2,1)} %add.6.rest_1_.rest_0_, ...), custom_call_target="tpu_custom_call" | custom-call | flops 1 | bytes 1 | tf_op jit(solution)/shard_map/product/pallas_call | solution.py:228
  55.7 4.2 %all-to-all-start.1 = ((bf16[4,96,1024]{2,1,0:T(8,128)(2,1)}), bf16[4,96,1024]{2,1,0:T(8,128)(2,1)}, u32[]{:S(2)}, u32[]{:S(2)}) async-start(bf16[4,96,1024]{2,1,0:T(8,128)(2,1)} %get-tuple-element.46), calls=%async_computation.1 | async-start | bytes 1572864 | tf_op jit(solution)/shard_map/all_to_all | solution.py:537
  60.5 2.9 %score.1 = f32[16,768]{1,0:T(8,128)S(1)} custom-call(s32[24]{0:T(128)} %get-tuple-element.40.names, s32[1,768]{1,0:T(1,128)} %wanted.5, bf16[768,2048]{1,0:T(8,128)(2,1)S(1)} %bitcast.8, bf16[384,2048]{1,0:T(8,128)(2,1)} %bitcast.2.factors, f32[8,128]{1,0:T(8,128)} %get-tuple-element.43.rest_0_, bf16[192,2048]{1,0:T(8,128)(2,1)} %collective-permute-done.2.rest_1_.first), custom_call_target="tpu_custom_call" | custom-call | flops 46000001024 | bytes 1 | tf_op jit(solution)/shard_map/score/pallas_call | solution.py:327
  63.4 5.8 %all-gather = f32[64,768]{1,0:T(8,128)S(1)} all-gather(f32[16,768]{1,0:T(8,128)S(1)} %score.1), channel_id=2, replica_groups=mesh['groups'=2,'tp'=4,'rep'=4] {'tp'}, dimensions={0}, use_global_device_ids=true | all-gather | bytes 245760 | tf_op jit(solution)/shard_map/all_gather | solution.py:544
  69.2 4.0 %delta.2 = (bf16[192,1024]{1,0:T(8,128)(2,1)}, bf16[192,1024]{1,0:T(8,128)(2,1)}) custom-call(s32[24]{0:T(128)} %get-tuple-element.40.names, s32[1,768]{1,0:T(1,128)} %wanted.5, f32[4,16,768]{2,1,0:T(8,128)S(1)} %bitcast.10, bf16[384,2048]{1,0:T(8,128)(2,1)} %get-tuple-element.44.late_own, bf16[384,2048]{1,0:T(8,128)(2,1)S(1)} %collective-permute-done.3.late_recv, ...), custom_call_target="tpu_custom_call" | custom-call | flops 1 | bytes 1 | tf_op jit(solution)/shard_map/delta/pallas_call | solution.py:390
  73.2 1.5 %collective-permute-start.13 = (bf16[192,1024]{1,0:T(8,128)(2,1)}, bf16[192,1024]{1,0:T(8,128)(2,1)}, u32[]{:S(2)}, u32[]{:S(2)}) collective-permute-start(bf16[192,1024]{1,0:T(8,128)(2,1)} %get-tuple-element.59), channel_id=1, source_target_pairs={{0,12},{12,0},{4,8},{8,4},{1,13},{13,1},{5,9},{9,5},{2,14},{14,2},... | collective-permute-start | bytes 1179656 | tf_op jit(solution)/shard_map/ppermute | solution.py:518
  75.2 4.8 %all-to-all-done.1 = bf16[4,96,1024]{2,1,0:T(8,128)(2,1)} async-done(((bf16[4,96,1024]{2,1,0:T(8,128)(2,1)}), bf16[4,96,1024]{2,1,0:T(8,128)(2,1)}, u32[]{:S(2)}, u32[]{:S(2)}) %all-to-all-start.1) | async-done | bytes 786464 | tf_op jit(solution)/shard_map/all_to_all | solution.py:537
  80.0 5.6 %delta.3 = (bf16[192,1024]{1,0:T(8,128)(2,1)}, bf16[192,1024]{1,0:T(8,128)(2,1)}, bf16[192,2048]{1,0:T(8,128)(2,1)}, bf16[192,2048]{1,0:T(8,128)(2,1)}) custom-call(s32[24]{0:T(128)} %get-tuple-element.40.names, s32[1,768]{1,0:T(1,128)} %wanted.5, f32[4,16,768]{2,1,0:T(8,128)S(1)} %bitcast.11, bf16[384,2048]{1,0:T(8,128)(2,1)} %get-tuple-element.44.late_own, ...), custom_call_target="tpu_custom_call" | custom-call | flops 1 | bytes 1 | tf_op jit(solution)/shard_map/delta/pallas_call | solution.py:390
  85.6 1.5 %collective-permute-start.10 = (bf16[192,1024]{1,0:T(8,128)(2,1)}, bf16[192,1024]{1,0:T(8,128)(2,1)}, u32[]{:S(2)}, u32[]{:S(2)}) collective-permute-start(bf16[192,1024]{1,0:T(8,128)(2,1)} %get-tuple-element.57), channel_id=1, source_target_pairs={{0,8},{8,0},{4,12},{12,4},{1,9},{9,1},{5,13},{13,5},{2,10},{10,2},... | collective-permute-start | bytes 1179656 | tf_op jit(solution)/shard_map/ppermute | solution.py:515
  87.7 11.4 %product.5 = (bf16[2,192,2048]{2,1,0:T(8,128)(2,1)}, bf16[2,192,2048]{2,1,0:T(8,128)(2,1)}, f32[8,128]{1,0:T(8,128)}) custom-call(bf16[768,2048]{1,0:T(8,128)(2,1)S(1)} %bitcast.9, bf16[2048,8192]{1,0:T(8,128)(2,1)} %weights.5, bf16[192,2048]{1,0:T(8,128)(2,1)} %get-tuple-element.54.rest_0_.mine), custom_call_target="tpu_custom_call" | custom-call | flops 1 | bytes 1 | tf_op jit(solution)/shard_map/product/pallas_call | solution.py:299
  100.3 5.2 %near.1.rest_0_ = bf16[192,8192]{1,0:T(8,128)(2,1)} custom-call(bf16[192,8192]{1,0:T(8,128)(2,1)} %bitcast.12, bf16[2,192,2048]{2,1,0:T(8,128)(2,1)} %get-tuple-element.63.keep, bf16[2,192,2048]{2,1,0:T(8,128)(2,1)} %collective-permute-done.7.rest_5_.recv, bf16[192,2048]{1,0:T(8,128)(2,1)} %collective-permute-done.2.rest_1_.first, ...), custom_call_target="tpu_custom_call" | custom-call | flops 69000003584 | bytes 1 | tf_op jit(solution)/shard_map/near/pallas_call | solution.py:481
  105.5 2.9 %far.2.rest_0_ = bf16[192,8192]{1,0:T(8,128)(2,1)} custom-call(bf16[192,8192]{1,0:T(8,128)(2,1)} %bitcast.13, bf16[2,192,2048]{2,1,0:T(8,128)(2,1)} %get-tuple-element.55.keep, bf16[2,192,2048]{2,1,0:T(8,128)(2,1)} %collective-permute-done.9.recv, bf16[192,1024]{1,0:T(8,128)(2,1)} %get-tuple-element.61.rest_0_.straight, ...), custom_call_target="tpu_custom_call", output_to_operand_aliasing={{}: (5, {})} | custom-call | flops 69000003584 | bytes 1 | tf_op jit(solution)/shard_map/far/pallas_call | solution.py:481
  108.5 1.3 %collective-permute-done.11.cross = bf16[192,1024]{1,0:T(8,128)(2,1)} collective-permute-done((bf16[192,1024]{1,0:T(8,128)(2,1)}, bf16[192,1024]{1,0:T(8,128)(2,1)}, u32[]{:S(2)}, u32[]{:S(2)}) %collective-permute-start.11) | collective-permute-done | bytes 393248 | tf_op jit(solution)/shard_map/ppermute | solution.py:518
  109.8 2.6 %far.3 = bf16[192,8192]{1,0:T(8,128)(2,1)} custom-call(bf16[192,8192]{1,0:T(8,128)(2,1)} %bitcast.14, bf16[2,192,2048]{2,1,0:T(8,128)(2,1)S(1)} %copy-done.3, bf16[2,192,2048]{2,1,0:T(8,128)(2,1)} %collective-permute-done.9.recv, bf16[192,1024]{1,0:T(8,128)(2,1)} %collective-permute-done.10.straight, ...), custom_call_target="tpu_custom_call", output_to_operand_aliasing={{}: (5, {})} | custom-call | flops 69000003584 | bytes 1 | tf_op jit(solution)/shard_map/far/pallas_call | solution.py:481
  (35 shorter events, 5.7 us)
Async XLA Ops:
  2.8 52.9 %all-to-all-start = ((bf16[4,96,2048]{2,1,0:T(8,128)(2,1)}), bf16[4,96,2048]{2,1,0:T(8,128)(2,1)}, u32[]{:S(2)}, u32[]{:S(2)}) async-start(bf16[4,96,2048]{2,1,0:T(8,128)(2,1)} %get-tuple-element.41), calls=%async_computation | async-start | bytes 3145728 | tf_op jit(solution)/shard_map/all_to_all | solution.py:525
  20.6 2.3 %collective-permute-start = (bf16[192,2048]{1,0:T(8,128)(2,1)S(1)}, bf16[192,2048]{1,0:T(8,128)(2,1)S(1)}, u32[]{:S(2)}, u32[]{:S(2)}) collective-permute-start(bf16[192,2048]{1,0:T(8,128)(2,1)S(1)} %get-tuple-element.37), channel_id=1, source_target_pairs={{0,4},{4,0},{8,12},{12,8},{1,5},{5,1},{9,13},{13,9},{2,6},{6,2},{1... | collective-permute-start | bytes 2359304 | tf_op jit(solution)/shard_map/ppermute | solution.py:512
  20.6 5.0 %collective-permute-start.1 = (bf16[192,2048]{1,0:T(8,128)(2,1)S(1)}, bf16[192,2048]{1,0:T(8,128)(2,1)S(1)}, u32[]{:S(2)}, u32[]{:S(2)}) collective-permute-start(bf16[192,2048]{1,0:T(8,128)(2,1)S(1)} %get-tuple-element.39), channel_id=1, source_target_pairs={{0,4},{4,0},{8,12},{12,8},{1,5},{5,1},{9,13},{13,9},{2,6},{6,2},{1... | collective-permute-start | bytes 2359304 | tf_op jit(solution)/shard_map/ppermute | solution.py:512
  24.1 35.9 %collective-permute-start.2 = (bf16[192,2048]{1,0:T(8,128)(2,1)}, bf16[192,2048]{1,0:T(8,128)(2,1)}, u32[]{:S(2)}, u32[]{:S(2)}) collective-permute-start(bf16[192,2048]{1,0:T(8,128)(2,1)} %add.6.rest_1_.rest_0_), channel_id=1, source_target_pairs={{0,8},{8,0},{4,12},{12,4},{1,9},{9,1},{5,13},{13,5},{2,10},{10,2},... | collective-permute-start | bytes 2359304 | tf_op jit(solution)/shard_map/ppermute | solution.py:515
  25.6 11.1 %copy-start = (bf16[1,768,2048]{2,1,0:T(8,128)(2,1)S(1)}, bf16[1,768,2048]{2,1,0:T(8,128)(2,1)}, u32[]{:S(2)}) copy-start(bf16[1,768,2048]{2,1,0:T(8,128)(2,1)} %param.8) | copy-start | bytes 9437188
  30.3 29.7 %collective-permute-start.4 = (bf16[96,1024]{1,0:T(8,128)(2,1)}, bf16[96,1024]{1,0:T(8,128)(2,1)S(1)}, u32[]{:S(2)}, u32[]{:S(2)}) collective-permute-start(bf16[96,1024]{1,0:T(8,128)(2,1)} %get-tuple-element.48), channel_id=1, source_target_pairs={{0,1},{1,2},{2,3},{3,0},{4,5},{5,6},{6,7},{7,4},{8,9},{9,10},{10,1... | collective-permute-start | bytes 589832 | tf_op jit(solution)/shard_map/ppermute | solution.py:521
  32.3 36.9 %collective-permute-start.8 = (bf16[192,2048]{1,0:T(8,128)(2,1)}, bf16[192,2048]{1,0:T(8,128)(2,1)}, u32[]{:S(2)}, u32[]{:S(2)}) collective-permute-start(bf16[192,2048]{1,0:T(8,128)(2,1)} %add.7.rest_2_.rest_1_), channel_id=1, source_target_pairs={{0,8},{8,0},{4,12},{12,4},{1,9},{9,1},{5,13},{13,5},{2,10},{10,2},... | collective-permute-start | bytes 2359304 | tf_op jit(solution)/shard_map/ppermute | solution.py:515
  32.8 36.3 %collective-permute-start.5 = (bf16[96,1024]{1,0:T(8,128)(2,1)}, bf16[96,1024]{1,0:T(8,128)(2,1)}, u32[]{:S(2)}, u32[]{:S(2)}) collective-permute-start(bf16[96,1024]{1,0:T(8,128)(2,1)} %get-tuple-element.49), channel_id=1, source_target_pairs={{0,2},{1,3},{2,0},{3,1},{4,6},{5,7},{6,4},{7,5},{8,10},{9,11},{10,... | collective-permute-start | bytes 589832 | tf_op jit(solution)/shard_map/ppermute | solution.py:521
  35.2 34.0 %collective-permute-start.6 = (bf16[96,1024]{1,0:T(8,128)(2,1)}, bf16[96,1024]{1,0:T(8,128)(2,1)}, u32[]{:S(2)}, u32[]{:S(2)}) collective-permute-start(bf16[96,1024]{1,0:T(8,128)(2,1)} %get-tuple-element.50), channel_id=1, source_target_pairs={{0,3},{1,0},{2,1},{3,2},{4,7},{5,4},{6,5},{7,6},{8,11},{9,8},{10,9... | collective-permute-start | bytes 589832 | tf_op jit(solution)/shard_map/ppermute | solution.py:521
  55.7 24.2 %all-to-all-start.1 = ((bf16[4,96,1024]{2,1,0:T(8,128)(2,1)}), bf16[4,96,1024]{2,1,0:T(8,128)(2,1)}, u32[]{:S(2)}, u32[]{:S(2)}) async-start(bf16[4,96,1024]{2,1,0:T(8,128)(2,1)} %get-tuple-element.46), calls=%async_computation.1 | async-start | bytes 1572864 | tf_op jit(solution)/shard_map/all_to_all | solution.py:537
  59.9 3.5 %copy-start.4 = (bf16[96,1024]{1,0:T(8,128)(2,1)}, bf16[96,1024]{1,0:T(8,128)(2,1)S(1)}, u32[]{:S(2)}) copy-start(bf16[96,1024]{1,0:T(8,128)(2,1)S(1)} %collective-permute-done.4.rest_1_.rest_2_) | copy-start | bytes 589828
  59.9 9.3 %collective-permute-start.3 = (bf16[384,2048]{1,0:T(8,128)(2,1)}, bf16[384,2048]{1,0:T(8,128)(2,1)S(1)}, u32[]{:S(2)}, u32[]{:S(2)}) collective-permute-start(bf16[384,2048]{1,0:T(8,128)(2,1)} %get-tuple-element.45), channel_id=1, source_target_pairs={{0,4},{4,0},{8,12},{12,8},{1,5},{5,1},{9,13},{13,9},{2,6},{6,2},{1... | collective-permute-start | bytes 4718600 | tf_op jit(solution)/shard_map/ppermute | solution.py:512
  60.0 19.9 %collective-permute-start.7 = (bf16[2,192,2048]{2,1,0:T(8,128)(2,1)}, bf16[2,192,2048]{2,1,0:T(8,128)(2,1)}, u32[]{:S(2)}, u32[]{:S(2)}) collective-permute-start(bf16[2,192,2048]{2,1,0:T(8,128)(2,1)} %get-tuple-element.51), channel_id=1, source_target_pairs={{0,4},{4,0},{8,12},{12,8},{1,5},{5,1},{9,13},{13,9},{2,6},{6,2},{1... | collective-permute-start | bytes 4718600 | tf_op jit(solution)/shard_map/ppermute | solution.py:512
  69.2 4.0 %copy-start.1 = (bf16[384,2048]{1,0:T(8,128)(2,1)}, bf16[384,2048]{1,0:T(8,128)(2,1)S(1)}, u32[]{:S(2)}) copy-start(bf16[384,2048]{1,0:T(8,128)(2,1)S(1)} %collective-permute-done.3.late_recv) | copy-start | bytes 4718596
  73.2 25.9 %collective-permute-start.13 = (bf16[192,1024]{1,0:T(8,128)(2,1)}, bf16[192,1024]{1,0:T(8,128)(2,1)}, u32[]{:S(2)}, u32[]{:S(2)}) collective-permute-start(bf16[192,1024]{1,0:T(8,128)(2,1)} %get-tuple-element.59), channel_id=1, source_target_pairs={{0,12},{12,0},{4,8},{8,4},{1,13},{13,1},{5,9},{9,5},{2,14},{14,2},... | collective-permute-start | bytes 1179656 | tf_op jit(solution)/shard_map/ppermute | solution.py:518
  74.7 24.5 %collective-permute-start.12 = (bf16[192,1024]{1,0:T(8,128)(2,1)}, bf16[192,1024]{1,0:T(8,128)(2,1)}, u32[]{:S(2)}, u32[]{:S(2)}) collective-permute-start(bf16[192,1024]{1,0:T(8,128)(2,1)} %get-tuple-element.53.rest_6_), channel_id=1, source_target_pairs={{0,8},{8,0},{4,12},{12,4},{1,9},{9,1},{5,13},{13,5},{2,10},{10,2},... | collective-permute-start | bytes 1179656 | tf_op jit(solution)/shard_map/ppermute | solution.py:515
  85.6 22.8 %collective-permute-start.10 = (bf16[192,1024]{1,0:T(8,128)(2,1)}, bf16[192,1024]{1,0:T(8,128)(2,1)}, u32[]{:S(2)}, u32[]{:S(2)}) collective-permute-start(bf16[192,1024]{1,0:T(8,128)(2,1)} %get-tuple-element.57), channel_id=1, source_target_pairs={{0,8},{8,0},{4,12},{12,4},{1,9},{9,1},{5,13},{13,5},{2,10},{10,2},... | collective-permute-start | bytes 1179656 | tf_op jit(solution)/shard_map/ppermute | solution.py:515
  87.1 22.7 %collective-permute-start.11 = (bf16[192,1024]{1,0:T(8,128)(2,1)}, bf16[192,1024]{1,0:T(8,128)(2,1)}, u32[]{:S(2)}, u32[]{:S(2)}) collective-permute-start(bf16[192,1024]{1,0:T(8,128)(2,1)} %get-tuple-element.58), channel_id=1, source_target_pairs={{0,12},{12,0},{4,8},{8,4},{1,13},{13,1},{5,9},{9,5},{2,14},{14,2},... | collective-permute-start | bytes 1179656 | tf_op jit(solution)/shard_map/ppermute | solution.py:518
  87.1 12.1 %collective-permute-start.14 = (bf16[192,2048]{1,0:T(8,128)(2,1)}, bf16[192,2048]{1,0:T(8,128)(2,1)}, u32[]{:S(2)}, u32[]{:S(2)}) collective-permute-start(bf16[192,2048]{1,0:T(8,128)(2,1)} %get-tuple-element.64), channel_id=1, source_target_pairs={{0,4},{4,0},{8,12},{12,8},{1,5},{5,1},{9,13},{13,9},{2,6},{6,2},{1... | collective-permute-start | bytes 2359304 | tf_op jit(solution)/shard_map/ppermute | solution.py:512
  99.1 6.4 %collective-permute-start.9 = (bf16[2,192,2048]{2,1,0:T(8,128)(2,1)}, bf16[2,192,2048]{2,1,0:T(8,128)(2,1)}, u32[]{:S(2)}, u32[]{:S(2)}) collective-permute-start(bf16[2,192,2048]{2,1,0:T(8,128)(2,1)} %get-tuple-element.56), channel_id=1, source_target_pairs={{0,4},{4,0},{8,12},{12,8},{1,5},{5,1},{9,13},{13,9},{2,6},{6,2},{1... | collective-permute-start | bytes 4718600 | tf_op jit(solution)/shard_map/ppermute | solution.py:512
  99.2 1.1 %copy-start.2 = (bf16[192,2048]{1,0:T(8,128)(2,1)S(1)}, bf16[192,2048]{1,0:T(8,128)(2,1)}, u32[]{:S(2)}) copy-start(bf16[192,2048]{1,0:T(8,128)(2,1)} %get-tuple-element.54.rest_0_.mine) | copy-start | bytes 2359300
  105.5 4.3 %copy-start.3 = (bf16[2,192,2048]{2,1,0:T(8,128)(2,1)S(1)}, bf16[2,192,2048]{2,1,0:T(8,128)(2,1)}, u32[]{:S(2)}) copy-start(bf16[2,192,2048]{2,1,0:T(8,128)(2,1)} %get-tuple-element.55.keep) | copy-start | bytes 4718596

commit v14 on v13

--- a/solution.py
+++ b/solution.py
@@ -406,7 +406,7 @@
         compiler_params=params(),
         cost_estimate=order(0),
         name="delta",
-    )(*pin(names, wanted), shrunk, *pin(late[0]), *(pin(late[1]) if before else late[1:]), *pin(*blocks, *before, *asked, *after))
+    )(*pin(names, wanted), shrunk, *(pin(*late, *blocks) if before else [*late, blocks[0], *pin(*blocks[1:])]), *pin(*before), *asked, *pin(*after))
 
 
 def gate_kernel(*refs):

time: 113 us -> 113 us (level)
  no operation moved by 1% of the time
where the time goes in v14:
time: 113 us; the launch traced here: 112 us
  Pallas kernels  70.4 us (62%)
  starting transfers between devices  23.7 us (21%)
  waiting for transfers between devices  8.73 us (8%)
  blocking collectives  5.79 us (5%)
  other arithmetic  2.34 us (2%)
    pallas_call x1, Pallas kernels, product_columns(): pl.pallas_call(kernel, out_shape=[in_hbm((half, width))] * 2 + [in_hbm((2...  18.3 us
    pallas_call x1, Pallas kernels, product_early(): pl.pallas_call(kernel, out_shape=[sds((half // 2, width))] * 4 + [TOKEN],...  11.5 us
    pallas_call x1, Pallas kernels, product(): pl.pallas_call(kernel, out_shape=[in_hbm(shape) if blocks > 1 else sds(sh...  11.4 us
    pallas_call x3, Pallas kernels, finish(): pl.pallas_call(near_kernel if near else far_kernel, out_shape=sds((own, f...  10.7 us
    pallas_call x2, Pallas kernels, delta(): pl.pallas_call(functools.partial(delta_kernel, len(blocks), len(before),...  9.23 us
    all_to_all x1, starting transfers between devices, paired(): lax.all_to_all(chosen, 'rep', 0, 0, tiled=True)  6.32 us
    pallas_call x2, Pallas kernels, select(): pl.pallas_call(functools.partial(select_kernel, by_shift, by_target, len(...  6.27 us
    ppermute x3, starting transfers between devices, over_rep(): lax.ppermute(x, 'rep', [(i, (i + shift) % n_rep) for i in range(n_rep)])  5.9 us
  transfers between devices with their start and end apart: 17, of which 4 were waited for; matrix products, arithmetic and copies ran while one was open for 2% of the time, Pallas kernels for 58%

profile of v14, /device:TPU:0, one launch (start us, length us, event | category | flops | bytes accessed | tf_op | source)
XLA Modules:
  0.0 112.2 jit_solution(18149530555062857738)
XLA Ops:
  0.0 2.8 %select.2 = (bf16[4,96,2048]{2,1,0:T(8,128)(2,1)}, f32[8,128]{1,0:T(8,128)}) custom-call(s32[64]{0:T(128)} %slot.3, s32[4,24]{1,0:T(4,128)} %lists.3, bf16[16,16,2048]{2,1,0:T(8,128)(2,1)} %pool.2), custom_call_target="tpu_custom_call" | custom-call | flops 1 | bytes 1 | tf_op jit(solution)/shard_map/select/pallas_call | solution.py:128
  2.8 6.3 %all-to-all-start = ((bf16[4,96,2048]{2,1,0:T(8,128)(2,1)}), bf16[4,96,2048]{2,1,0:T(8,128)(2,1)}, u32[]{:S(2)}, u32[]{:S(2)}) async-start(bf16[4,96,2048]{2,1,0:T(8,128)(2,1)} %get-tuple-element.41), calls=%async_computation | async-start | bytes 3145728 | tf_op jit(solution)/shard_map/all_to_all | solution.py:525
  9.2 11.5 %product.3 = (bf16[192,2048]{1,0:T(8,128)(2,1)S(1)}, bf16[192,2048]{1,0:T(8,128)(2,1)S(1)}, bf16[192,2048]{1,0:T(8,128)(2,1)S(1)}, bf16[192,2048]{1,0:T(8,128)(2,1)S(1)}, f32[8,128]{1,0:T(8,128)}) custom-call(bf16[768,2048]{1,0:T(8,128)(2,1)} %bitcast.6, bf16[2048,8192]{1,0:T(8,128)(2,1)} %weights.5, f32[8,128]{1,0:T(8,128)} %get-tuple-element.35.rest_0_), custom_call_target="tpu_custom_call" | custom-call | flops 1 | bytes 1 | tf_op jit(solution)/shard_map/product/pallas_call | solution.py:170
  21.1 1.8 %collective-permute-done = bf16[192,2048]{1,0:T(8,128)(2,1)S(1)} collective-permute-done((bf16[192,2048]{1,0:T(8,128)(2,1)S(1)}, bf16[192,2048]{1,0:T(8,128)(2,1)S(1)}, u32[]{:S(2)}, u32[]{:S(2)}) %collective-permute-start) | collective-permute-done | bytes 786464 | tf_op jit(solution)/shard_map/ppermute | solution.py:512
  24.1 1.5 %collective-permute-start.2 = (bf16[192,2048]{1,0:T(8,128)(2,1)}, bf16[192,2048]{1,0:T(8,128)(2,1)}, u32[]{:S(2)}, u32[]{:S(2)}) collective-permute-start(bf16[192,2048]{1,0:T(8,128)(2,1)} %add.6.rest_1_.rest_0_), channel_id=1, source_target_pairs={{0,8},{8,0},{4,12},{12,4},{1,9},{9,1},{5,13},{13,5},{2,10},{10,2},... | collective-permute-start | bytes 2359304 | tf_op jit(solution)/shard_map/ppermute | solution.py:515
  25.6 1.2 %add.7.rest_2_.rest_1_ = bf16[192,2048]{1,0:T(8,128)(2,1)} add(bf16[192,2048]{1,0:T(8,128)(2,1)S(1)} %get-tuple-element.38, bf16[192,2048]{1,0:T(8,128)(2,1)S(1)} %collective-permute-done.1) | non-fusion elementwise | flops 393216 | bytes 2359296 | tf_op jit(solution)/shard_map/add | solution.py:528
  26.8 3.4 %select.3 = (bf16[96,1024]{1,0:T(8,128)(2,1)}, bf16[96,1024]{1,0:T(8,128)(2,1)}, bf16[96,1024]{1,0:T(8,128)(2,1)}, bf16[96,1024]{1,0:T(8,128)(2,1)}, bf16[4,96,1...) custom-call(s32[64]{0:T(128)} %slot.3, s32[4,24]{1,0:T(4,128)} %lists.3, ...), custom_call_target="tpu_custom_call" | custom-call | flops 1 | bytes 1 | tf_op jit(solution)/shard_map/select/pallas_call | solution.py:128
  30.2 2.1 %collective-permute-start.4 = (bf16[96,1024]{1,0:T(8,128)(2,1)}, bf16[96,1024]{1,0:T(8,128)(2,1)S(1)}, u32[]{:S(2)}, u32[]{:S(2)}) collective-permute-start(bf16[96,1024]{1,0:T(8,128)(2,1)} %get-tuple-element.48), channel_id=1, source_target_pairs={{0,1},{1,2},{2,3},{3,0},{4,5},{5,6},{6,7},{7,4},{8,9},{9,10},{10,1... | collective-permute-start | bytes 589832 | tf_op jit(solution)/shard_map/ppermute | solution.py:521
  32.8 2.4 %collective-permute-start.5 = (bf16[96,1024]{1,0:T(8,128)(2,1)}, bf16[96,1024]{1,0:T(8,128)(2,1)}, u32[]{:S(2)}, u32[]{:S(2)}) collective-permute-start(bf16[96,1024]{1,0:T(8,128)(2,1)} %get-tuple-element.49), channel_id=1, source_target_pairs={{0,2},{1,3},{2,0},{3,1},{4,6},{5,7},{6,4},{7,5},{8,10},{9,11},{10,... | collective-permute-start | bytes 589832 | tf_op jit(solution)/shard_map/ppermute | solution.py:521
  35.2 1.5 %collective-permute-start.6 = (bf16[96,1024]{1,0:T(8,128)(2,1)}, bf16[96,1024]{1,0:T(8,128)(2,1)}, u32[]{:S(2)}, u32[]{:S(2)}) collective-permute-start(bf16[96,1024]{1,0:T(8,128)(2,1)} %get-tuple-element.50), channel_id=1, source_target_pairs={{0,3},{1,0},{2,1},{3,2},{4,7},{5,4},{6,5},{7,6},{8,11},{9,8},{10,9... | collective-permute-start | bytes 589832 | tf_op jit(solution)/shard_map/ppermute | solution.py:521
  36.6 18.3 %product.4 = (bf16[384,2048]{1,0:T(8,128)(2,1)}, bf16[384,2048]{1,0:T(8,128)(2,1)}, bf16[2,192,2048]{2,1,0:T(8,128)(2,1)}, bf16[2,192,2048]{2,1,0:T(8,128)(2,1)}, f32[8,128]{1,0:T(8,128)}) custom-call(bf16[768,2048]{1,0:T(8,128)(2,1)S(1)} %bitcast.7, bf16[2048,8192]{1,0:T(8,128)(2,1)} %weights.5, bf16[192,2048]{1,0:T(8,128)(2,1)} %add.6.rest_1_.rest_0_, ...), custom_call_target="tpu_custom_call" | custom-call | flops 1 | bytes 1 | tf_op jit(solution)/shard_map/product/pallas_call | solution.py:228
  55.7 4.2 %all-to-all-start.1 = ((bf16[4,96,1024]{2,1,0:T(8,128)(2,1)}), bf16[4,96,1024]{2,1,0:T(8,128)(2,1)}, u32[]{:S(2)}, u32[]{:S(2)}) async-start(bf16[4,96,1024]{2,1,0:T(8,128)(2,1)} %get-tuple-element.46), calls=%async_computation.1 | async-start | bytes 1572864 | tf_op jit(solution)/shard_map/all_to_all | solution.py:537
  60.5 3.0 %score.1 = f32[16,768]{1,0:T(8,128)S(1)} custom-call(s32[24]{0:T(128)} %get-tuple-element.40.names, s32[1,768]{1,0:T(1,128)} %wanted.5, bf16[768,2048]{1,0:T(8,128)(2,1)S(1)} %bitcast.8, bf16[384,2048]{1,0:T(8,128)(2,1)} %bitcast.2.factors, f32[8,128]{1,0:T(8,128)} %get-tuple-element.43.rest_0_, bf16[192,2048]{1,0:T(8,128)(2,1)} %collective-permute-done.2.rest_1_.first), custom_call_target="tpu_custom_call" | custom-call | flops 46000001024 | bytes 1 | tf_op jit(solution)/shard_map/score/pallas_call | solution.py:327
  63.6 5.8 %all-gather = f32[64,768]{1,0:T(8,128)S(1)} all-gather(f32[16,768]{1,0:T(8,128)S(1)} %score.1), channel_id=2, replica_groups=mesh['groups'=2,'tp'=4,'rep'=4] {'tp'}, dimensions={0}, use_global_device_ids=true | all-gather | bytes 245760 | tf_op jit(solution)/shard_map/all_gather | solution.py:544
  69.4 3.6 %delta.2 = (bf16[192,1024]{1,0:T(8,128)(2,1)}, bf16[192,1024]{1,0:T(8,128)(2,1)}) custom-call(s32[24]{0:T(128)} %get-tuple-element.40.names, s32[1,768]{1,0:T(1,128)} %wanted.5, f32[4,16,768]{2,1,0:T(8,128)S(1)} %bitcast.10, bf16[384,2048]{1,0:T(8,128)(2,1)S(1)} %copy-done.1, bf16[384,2048]{1,0:T(8,128)(2,1)S(1)} %collective-permute-done.3.late_recv, ...), custom_call_target="tpu_custom_call" | custom-call | flops 1 | bytes 1 | tf_op jit(solution)/shard_map/delta/pallas_call | solution.py:390
  73.1 1.5 %collective-permute-start.13 = (bf16[192,1024]{1,0:T(8,128)(2,1)}, bf16[192,1024]{1,0:T(8,128)(2,1)}, u32[]{:S(2)}, u32[]{:S(2)}) collective-permute-start(bf16[192,1024]{1,0:T(8,128)(2,1)} %get-tuple-element.59), channel_id=1, source_target_pairs={{0,12},{12,0},{4,8},{8,4},{1,13},{13,1},{5,9},{9,5},{2,14},{14,2},... | collective-permute-start | bytes 1179656 | tf_op jit(solution)/shard_map/ppermute | solution.py:518
  75.0 4.9 %all-to-all-done.1 = bf16[4,96,1024]{2,1,0:T(8,128)(2,1)} async-done(((bf16[4,96,1024]{2,1,0:T(8,128)(2,1)}), bf16[4,96,1024]{2,1,0:T(8,128)(2,1)}, u32[]{:S(2)}, u32[]{:S(2)}) %all-to-all-start.1) | async-done | bytes 786464 | tf_op jit(solution)/shard_map/all_to_all | solution.py:537
  80.0 5.6 %delta.3 = (bf16[192,1024]{1,0:T(8,128)(2,1)}, bf16[192,1024]{1,0:T(8,128)(2,1)}, bf16[192,2048]{1,0:T(8,128)(2,1)}, bf16[192,2048]{1,0:T(8,128)(2,1)}) custom-call(s32[24]{0:T(128)} %get-tuple-element.40.names, s32[1,768]{1,0:T(1,128)} %wanted.5, f32[4,16,768]{2,1,0:T(8,128)S(1)} %bitcast.11, bf16[384,2048]{1,0:T(8,128)(2,1)} %get-tuple-element.44.late_own, ...), custom_call_target="tpu_custom_call" | custom-call | flops 1 | bytes 1 | tf_op jit(solution)/shard_map/delta/pallas_call | solution.py:390
  85.5 1.5 %collective-permute-start.10 = (bf16[192,1024]{1,0:T(8,128)(2,1)}, bf16[192,1024]{1,0:T(8,128)(2,1)}, u32[]{:S(2)}, u32[]{:S(2)}) collective-permute-start(bf16[192,1024]{1,0:T(8,128)(2,1)} %get-tuple-element.57), channel_id=1, source_target_pairs={{0,8},{8,0},{4,12},{12,4},{1,9},{9,1},{5,13},{13,5},{2,10},{10,2},... | collective-permute-start | bytes 1179656 | tf_op jit(solution)/shard_map/ppermute | solution.py:515
  87.7 11.4 %product.5 = (bf16[2,192,2048]{2,1,0:T(8,128)(2,1)}, bf16[2,192,2048]{2,1,0:T(8,128)(2,1)}, f32[8,128]{1,0:T(8,128)}) custom-call(bf16[768,2048]{1,0:T(8,128)(2,1)S(1)} %bitcast.9, bf16[2048,8192]{1,0:T(8,128)(2,1)} %weights.5, bf16[192,2048]{1,0:T(8,128)(2,1)} %get-tuple-element.54.rest_0_.mine), custom_call_target="tpu_custom_call" | custom-call | flops 1 | bytes 1 | tf_op jit(solution)/shard_map/product/pallas_call | solution.py:299
  100.3 5.2 %near.1.rest_0_ = bf16[192,8192]{1,0:T(8,128)(2,1)} custom-call(bf16[192,8192]{1,0:T(8,128)(2,1)} %bitcast.12, bf16[2,192,2048]{2,1,0:T(8,128)(2,1)} %get-tuple-element.63.keep, bf16[2,192,2048]{2,1,0:T(8,128)(2,1)} %collective-permute-done.7.rest_5_.recv, bf16[192,2048]{1,0:T(8,128)(2,1)} %collective-permute-done.2.rest_1_.first, ...), custom_call_target="tpu_custom_call" | custom-call | flops 69000003584 | bytes 1 | tf_op jit(solution)/shard_map/near/pallas_call | solution.py:481
  105.5 2.9 %far.2.rest_0_ = bf16[192,8192]{1,0:T(8,128)(2,1)} custom-call(bf16[192,8192]{1,0:T(8,128)(2,1)} %bitcast.13, bf16[2,192,2048]{2,1,0:T(8,128)(2,1)} %get-tuple-element.55.keep, bf16[2,192,2048]{2,1,0:T(8,128)(2,1)} %collective-permute-done.9.recv, bf16[192,1024]{1,0:T(8,128)(2,1)} %get-tuple-element.61.rest_0_.straight, ...), custom_call_target="tpu_custom_call", output_to_operand_aliasing={{}: (5, {})} | custom-call | flops 69000003584 | bytes 1 | tf_op jit(solution)/shard_map/far/pallas_call | solution.py:481
  108.4 1.2 %collective-permute-done.11.cross = bf16[192,1024]{1,0:T(8,128)(2,1)} collective-permute-done((bf16[192,1024]{1,0:T(8,128)(2,1)}, bf16[192,1024]{1,0:T(8,128)(2,1)}, u32[]{:S(2)}, u32[]{:S(2)}) %collective-permute-start.11) | collective-permute-done | bytes 393248 | tf_op jit(solution)/shard_map/ppermute | solution.py:518
  109.6 2.6 %far.3 = bf16[192,8192]{1,0:T(8,128)(2,1)} custom-call(bf16[192,8192]{1,0:T(8,128)(2,1)} %bitcast.14, bf16[2,192,2048]{2,1,0:T(8,128)(2,1)S(1)} %copy-done.6, bf16[2,192,2048]{2,1,0:T(8,128)(2,1)} %collective-permute-done.9.recv, bf16[192,1024]{1,0:T(8,128)(2,1)} %collective-permute-done.10.straight, ...), custom_call_target="tpu_custom_call", output_to_operand_aliasing={{}: (5, {})} | custom-call | flops 69000003584 | bytes 1 | tf_op jit(solution)/shard_map/far/pallas_call | solution.py:481
  (41 shorter events, 5.8 us)
Async XLA Ops:
  2.8 52.9 %all-to-all-start = ((bf16[4,96,2048]{2,1,0:T(8,128)(2,1)}), bf16[4,96,2048]{2,1,0:T(8,128)(2,1)}, u32[]{:S(2)}, u32[]{:S(2)}) async-start(bf16[4,96,2048]{2,1,0:T(8,128)(2,1)} %get-tuple-element.41), calls=%async_computation | async-start | bytes 3145728 | tf_op jit(solution)/shard_map/all_to_all | solution.py:525
  20.6 2.3 %collective-permute-start = (bf16[192,2048]{1,0:T(8,128)(2,1)S(1)}, bf16[192,2048]{1,0:T(8,128)(2,1)S(1)}, u32[]{:S(2)}, u32[]{:S(2)}) collective-permute-start(bf16[192,2048]{1,0:T(8,128)(2,1)S(1)} %get-tuple-element.37), channel_id=1, source_target_pairs={{0,4},{4,0},{8,12},{12,8},{1,5},{5,1},{9,13},{13,9},{2,6},{6,2},{1... | collective-permute-start | bytes 2359304 | tf_op jit(solution)/shard_map/ppermute | solution.py:512
  20.6 5.0 %collective-permute-start.1 = (bf16[192,2048]{1,0:T(8,128)(2,1)S(1)}, bf16[192,2048]{1,0:T(8,128)(2,1)S(1)}, u32[]{:S(2)}, u32[]{:S(2)}) collective-permute-start(bf16[192,2048]{1,0:T(8,128)(2,1)S(1)} %get-tuple-element.39), channel_id=1, source_target_pairs={{0,4},{4,0},{8,12},{12,8},{1,5},{5,1},{9,13},{13,9},{2,6},{6,2},{1... | collective-permute-start | bytes 2359304 | tf_op jit(solution)/shard_map/ppermute | solution.py:512
  24.1 36.0 %collective-permute-start.2 = (bf16[192,2048]{1,0:T(8,128)(2,1)}, bf16[192,2048]{1,0:T(8,128)(2,1)}, u32[]{:S(2)}, u32[]{:S(2)}) collective-permute-start(bf16[192,2048]{1,0:T(8,128)(2,1)} %add.6.rest_1_.rest_0_), channel_id=1, source_target_pairs={{0,8},{8,0},{4,12},{12,4},{1,9},{9,1},{5,13},{13,5},{2,10},{10,2},... | collective-permute-start | bytes 2359304 | tf_op jit(solution)/shard_map/ppermute | solution.py:515
  25.6 11.0 %copy-start = (bf16[1,768,2048]{2,1,0:T(8,128)(2,1)S(1)}, bf16[1,768,2048]{2,1,0:T(8,128)(2,1)}, u32[]{:S(2)}) copy-start(bf16[1,768,2048]{2,1,0:T(8,128)(2,1)} %param.8) | copy-start | bytes 9437188
  30.2 29.7 %collective-permute-start.4 = (bf16[96,1024]{1,0:T(8,128)(2,1)}, bf16[96,1024]{1,0:T(8,128)(2,1)S(1)}, u32[]{:S(2)}, u32[]{:S(2)}) collective-permute-start(bf16[96,1024]{1,0:T(8,128)(2,1)} %get-tuple-element.48), channel_id=1, source_target_pairs={{0,1},{1,2},{2,3},{3,0},{4,5},{5,6},{6,7},{7,4},{8,9},{9,10},{10,1... | collective-permute-start | bytes 589832 | tf_op jit(solution)/shard_map/ppermute | solution.py:521
  32.3 37.1 %collective-permute-start.8 = (bf16[192,2048]{1,0:T(8,128)(2,1)}, bf16[192,2048]{1,0:T(8,128)(2,1)}, u32[]{:S(2)}, u32[]{:S(2)}) collective-permute-start(bf16[192,2048]{1,0:T(8,128)(2,1)} %add.7.rest_2_.rest_1_), channel_id=1, source_target_pairs={{0,8},{8,0},{4,12},{12,4},{1,9},{9,1},{5,13},{13,5},{2,10},{10,2},... | collective-permute-start | bytes 2359304 | tf_op jit(solution)/shard_map/ppermute | solution.py:515
  32.8 36.5 %collective-permute-start.5 = (bf16[96,1024]{1,0:T(8,128)(2,1)}, bf16[96,1024]{1,0:T(8,128)(2,1)}, u32[]{:S(2)}, u32[]{:S(2)}) collective-permute-start(bf16[96,1024]{1,0:T(8,128)(2,1)} %get-tuple-element.49), channel_id=1, source_target_pairs={{0,2},{1,3},{2,0},{3,1},{4,6},{5,7},{6,4},{7,5},{8,10},{9,11},{10,... | collective-permute-start | bytes 589832 | tf_op jit(solution)/shard_map/ppermute | solution.py:521
  35.2 34.2 %collective-permute-start.6 = (bf16[96,1024]{1,0:T(8,128)(2,1)}, bf16[96,1024]{1,0:T(8,128)(2,1)}, u32[]{:S(2)}, u32[]{:S(2)}) collective-permute-start(bf16[96,1024]{1,0:T(8,128)(2,1)} %get-tuple-element.50), channel_id=1, source_target_pairs={{0,3},{1,0},{2,1},{3,2},{4,7},{5,4},{6,5},{7,6},{8,11},{9,8},{10,9... | collective-permute-start | bytes 589832 | tf_op jit(solution)/shard_map/ppermute | solution.py:521
  55.7 24.2 %all-to-all-start.1 = ((bf16[4,96,1024]{2,1,0:T(8,128)(2,1)}), bf16[4,96,1024]{2,1,0:T(8,128)(2,1)}, u32[]{:S(2)}, u32[]{:S(2)}) async-start(bf16[4,96,1024]{2,1,0:T(8,128)(2,1)} %get-tuple-element.46), calls=%async_computation.1 | async-start | bytes 1572864 | tf_op jit(solution)/shard_map/all_to_all | solution.py:537
  60.0 3.6 %copy-start.7 = (bf16[96,1024]{1,0:T(8,128)(2,1)}, bf16[96,1024]{1,0:T(8,128)(2,1)S(1)}, u32[]{:S(2)}) copy-start(bf16[96,1024]{1,0:T(8,128)(2,1)S(1)} %collective-permute-done.4.rest_1_.rest_2_) | copy-start | bytes 589828
  60.0 9.4 %collective-permute-start.3 = (bf16[384,2048]{1,0:T(8,128)(2,1)}, bf16[384,2048]{1,0:T(8,128)(2,1)S(1)}, u32[]{:S(2)}, u32[]{:S(2)}) collective-permute-start(bf16[384,2048]{1,0:T(8,128)(2,1)} %get-tuple-element.45), channel_id=1, source_target_pairs={{0,4},{4,0},{8,12},{12,8},{1,5},{5,1},{9,13},{13,9},{2,6},{6,2},{1... | collective-permute-start | bytes 4718600 | tf_op jit(solution)/shard_map/ppermute | solution.py:512
  60.1 19.9 %collective-permute-start.7 = (bf16[2,192,2048]{2,1,0:T(8,128)(2,1)}, bf16[2,192,2048]{2,1,0:T(8,128)(2,1)}, u32[]{:S(2)}, u32[]{:S(2)}) collective-permute-start(bf16[2,192,2048]{2,1,0:T(8,128)(2,1)} %get-tuple-element.51), channel_id=1, source_target_pairs={{0,4},{4,0},{8,12},{12,8},{1,5},{5,1},{9,13},{13,9},{2,6},{6,2},{1... | collective-permute-start | bytes 4718600 | tf_op jit(solution)/shard_map/ppermute | solution.py:512
  60.5 8.8 %copy-start.1 = (bf16[384,2048]{1,0:T(8,128)(2,1)S(1)}, bf16[384,2048]{1,0:T(8,128)(2,1)}, u32[]{:S(2)}) copy-start(bf16[384,2048]{1,0:T(8,128)(2,1)} %get-tuple-element.44.late_own) | copy-start | bytes 4718596
  60.5 8.9 %copy-start.3 = (bf16[96,1024]{1,0:T(8,128)(2,1)S(1)}, bf16[96,1024]{1,0:T(8,128)(2,1)}, u32[]{:S(2)}) copy-start(bf16[96,1024]{1,0:T(8,128)(2,1)} %get-tuple-element.47.rest_0_.rest_1_) | copy-start | bytes 589828
  60.5 8.9 %copy-start.5 = (bf16[768,384]{1,0:T(8,128)(2,1)S(1)}, bf16[768,384]{1,0:T(8,128)(2,1)}, u32[]{:S(2)}) copy-start(bf16[768,384]{1,0:T(8,128)(2,1)} %get-tuple-element.52.rest_4_) | copy-start | bytes 1769476
  69.4 3.7 %copy-start.2 = (bf16[384,2048]{1,0:T(8,128)(2,1)}, bf16[384,2048]{1,0:T(8,128)(2,1)S(1)}, u32[]{:S(2)}) copy-start(bf16[384,2048]{1,0:T(8,128)(2,1)S(1)} %collective-permute-done.3.late_recv) | copy-start | bytes 4718596
  73.1 26.0 %collective-permute-start.13 = (bf16[192,1024]{1,0:T(8,128)(2,1)}, bf16[192,1024]{1,0:T(8,128)(2,1)}, u32[]{:S(2)}, u32[]{:S(2)}) collective-permute-start(bf16[192,1024]{1,0:T(8,128)(2,1)} %get-tuple-element.59), channel_id=1, source_target_pairs={{0,12},{12,0},{4,8},{8,4},{1,13},{13,1},{5,9},{9,5},{2,14},{14,2},... | collective-permute-start | bytes 1179656 | tf_op jit(solution)/shard_map/ppermute | solution.py:518
  74.5 24.6 %collective-permute-start.12 = (bf16[192,1024]{1,0:T(8,128)(2,1)}, bf16[192,1024]{1,0:T(8,128)(2,1)}, u32[]{:S(2)}, u32[]{:S(2)}) collective-permute-start(bf16[192,1024]{1,0:T(8,128)(2,1)} %get-tuple-element.53.rest_6_), channel_id=1, source_target_pairs={{0,8},{8,0},{4,12},{12,4},{1,9},{9,1},{5,13},{13,5},{2,10},{10,2},... | collective-permute-start | bytes 1179656 | tf_op jit(solution)/shard_map/ppermute | solution.py:515
  85.5 22.8 %collective-permute-start.10 = (bf16[192,1024]{1,0:T(8,128)(2,1)}, bf16[192,1024]{1,0:T(8,128)(2,1)}, u32[]{:S(2)}, u32[]{:S(2)}) collective-permute-start(bf16[192,1024]{1,0:T(8,128)(2,1)} %get-tuple-element.57), channel_id=1, source_target_pairs={{0,8},{8,0},{4,12},{12,4},{1,9},{9,1},{5,13},{13,5},{2,10},{10,2},... | collective-permute-start | bytes 1179656 | tf_op jit(solution)/shard_map/ppermute | solution.py:515
  87.1 22.5 %collective-permute-start.11 = (bf16[192,1024]{1,0:T(8,128)(2,1)}, bf16[192,1024]{1,0:T(8,128)(2,1)}, u32[]{:S(2)}, u32[]{:S(2)}) collective-permute-start(bf16[192,1024]{1,0:T(8,128)(2,1)} %get-tuple-element.58), channel_id=1, source_target_pairs={{0,12},{12,0},{4,8},{8,4},{1,13},{13,1},{5,9},{9,5},{2,14},{14,2},... | collective-permute-start | bytes 1179656 | tf_op jit(solution)/shard_map/ppermute | solution.py:518
  87.1 12.1 %collective-permute-start.14 = (bf16[192,2048]{1,0:T(8,128)(2,1)}, bf16[192,2048]{1,0:T(8,128)(2,1)}, u32[]{:S(2)}, u32[]{:S(2)}) collective-permute-start(bf16[192,2048]{1,0:T(8,128)(2,1)} %get-tuple-element.64), channel_id=1, source_target_pairs={{0,4},{4,0},{8,12},{12,8},{1,5},{5,1},{9,13},{13,9},{2,6},{6,2},{1... | collective-permute-start | bytes 2359304 | tf_op jit(solution)/shard_map/ppermute | solution.py:512
  99.1 6.4 %collective-permute-start.9 = (bf16[2,192,2048]{2,1,0:T(8,128)(2,1)}, bf16[2,192,2048]{2,1,0:T(8,128)(2,1)}, u32[]{:S(2)}, u32[]{:S(2)}) collective-permute-start(bf16[2,192,2048]{2,1,0:T(8,128)(2,1)} %get-tuple-element.56), channel_id=1, source_target_pairs={{0,4},{4,0},{8,12},{12,8},{1,5},{5,1},{9,13},{13,9},{2,6},{6,2},{1... | collective-permute-start | bytes 4718600 | tf_op jit(solution)/shard_map/ppermute | solution.py:512
  105.5 4.1 %copy-start.6 = (bf16[2,192,2048]{2,1,0:T(8,128)(2,1)S(1)}, bf16[2,192,2048]{2,1,0:T(8,128)(2,1)}, u32[]{:S(2)}) copy-start(bf16[2,192,2048]{2,1,0:T(8,128)(2,1)} %get-tuple-element.55.keep) | copy-start | bytes 4718596
  (1 other events, 1.1 us)
